TPU v7x, 32 devices: a whole 2x2x4 slice. The times are simulated.
32 devices in a mesh: head: 4 (over y, x), blk: 8 (over z, core).
Axes of the slice: x: 2, y: 2, z: 4, core: 2. Of those that a mesh axis runs over, the one named last changes fastest.
Arguments:
- inputs: bfloat16 [4096, 2048], P(('blk', 'head')), may hold values from -6 to 6
- dealing: int32 [4096], replicated, may hold values from 0 to 4095, each once
- lengths: int32 [3], replicated, may hold values from 1024 to 2048, as said below
- input_gain: bfloat16 [2048], P(('head', 'blk')), may hold values from 0.099609375 to 1.8984375
- w_query: bfloat16 [2048, 2048], P(None, ('head', 'blk')), may hold values from -0.125 to 0.125
- w_key: bfloat16 [2048, 1024], P(None, ('head', 'blk')), may hold values from -0.125 to 0.125
- w_value: bfloat16 [2048, 1024], P(None, ('head', 'blk')), may hold values from -0.125 to 0.125
- query_gain: bfloat16 [128], P(('head', 'blk')), may hold values from 0.099609375 to 1.8984375
- key_gain: bfloat16 [128], P(('head', 'blk')), may hold values from 0.099609375 to 1.8984375
- w_out: bfloat16 [2048, 2048], P(('head', 'blk')), may hold values from -2 to 2
- hidden_gain: bfloat16 [2048], P('blk'), may hold values from 0.099609375 to 1.8984375
- w_gate: bfloat16 [2048, 6144], P(None, ('head', 'blk')), may hold values from -0.125 to 0.125
- w_up: bfloat16 [2048, 6144], P(None, ('head', 'blk')), may hold values from -0.125 to 0.125
- w_down: bfloat16 [6144, 2048], P(('head', 'blk')), may hold values from -0.3125 to 0.3125
- cotangent: bfloat16 [4096, 2048], P('blk'), may hold values from -6 to 6
Outputs:
- layer_out: bfloat16 [4096, 2048], P(('blk', 'head'))
- grad_input: float32 [4096, 2048], P(('blk', 'head'))
- grad_input_gain: float32 [2048], P(('head', 'blk'))
- grad_query: float32 [2048, 2048], P(None, ('head', 'blk'))
- grad_key: float32 [2048, 1024], P(None, ('head', 'blk'))
- grad_value: float32 [2048, 1024], P(None, ('head', 'blk'))
- grad_query_gain: float32 [128], P(('head', 'blk'))
- grad_key_gain: float32 [128], P(('head', 'blk'))
- grad_out: float32 [2048, 2048], P(('head', 'blk'))
- grad_hidden_gain: float32 [2048], P('blk')
- grad_gate: float32 [2048, 6144], P(None, ('head', 'blk'))
- grad_up: float32 [2048, 6144], P(None, ('head', 'blk'))
- grad_down: float32 [6144, 2048], P(('head', 'blk'))
Inputs may be any that keep to these rules, and one draw needn't show every extreme that they name: 3 lengths that sum to 4096; one of them is 2048, at a place drawn from the seed. `dealing`: a permutation of the packed tokens.
All inputs are finite; a program needn't handle non-finite values.
Results may differ from a plain program's by a relative error of at most 0.04.
Values may be sent and summed in bfloat16 or wider, within the bound.
No kernel may reach another device: no remote copies, remote signals or barrier semaphores. Data moves between devices by JAX's collectives and lax.ppermute only.
A program may use at most 256 MiB of HBM per device.

v0:
```python
import math

import jax
import jax.numpy as jnp
from jax import lax
from jax.sharding import PartitionSpec as P

QH = 16
KVH = 8
HD = 128


EPSILON = 1e-06
ROPE_BASE = 1000000.0
CONTRACT_ROWS = (((0,), (0,)), ((), ()))
CONTRACT_COLS = (((1,), (1,)), ((), ()))


def shifted(value, axis, steps):
    count = lax.axis_size(axis)
    pairs = [(source, (source + steps) % count) for source in range(count)]
    return lax.ppermute(value, axis, pairs)


def rms_scale(values):
    return lax.rsqrt(jnp.mean(values * values, axis=-1, keepdims=True) + EPSILON)


def norm_rope(projected, gain, cosine, sine):
    heads = projected.reshape(projected.shape[0], -1, HD)
    normed = heads * rms_scale(heads) * gain
    half_dim = HD // 2
    turned = jnp.concatenate([-normed[..., half_dim:], normed[..., :half_dim]], axis=-1)
    rotated = normed * cosine[:, None, :] + turned * sine[:, None, :]
    return rotated.reshape(projected.shape)


def rope_tables(places):
    half_dim = HD // 2
    ladder = jnp.arange(half_dim, dtype=jnp.float32)
    rates = jnp.exp(ladder * (-2.0 * math.log(ROPE_BASE) / HD))
    angles = places.astype(jnp.float32)[:, None] * rates[None, :]
    angles = jnp.concatenate([angles, angles], axis=1)
    return (jnp.cos(angles), jnp.sin(angles))


def token_starts(anchors, lengths):
    ends = jnp.cumsum(lengths)
    seq_starts = ends - lengths
    inside = seq_starts[None, :] <= anchors[:, None]
    return jnp.max(jnp.where(inside, seq_starts[None, :], 0), axis=1)


def row_outer(left, right):
    return lax.dot_general(left, right, CONTRACT_ROWS, preferred_element_type=jnp.float32)


def col_inner(left, right):
    return lax.dot_general(left, right, CONTRACT_COLS, preferred_element_type=jnp.float32)


def norm_back(upstream, source, scale_rows, gain):
    scaled = upstream * gain
    return scale_rows * scaled - source * scale_rows**3 * jnp.mean(
        scaled * source, axis=-1, keepdims=True
    )


def rope_pull(projected, gain, cosine, sine, upstream):

    def rope_map(raw_input, gain_input):
        return norm_rope(raw_input, gain_input, cosine, sine)

    unused, pullback = jax.vjp(rope_map, projected, gain)
    return pullback(upstream)


def local(
    inputs,
    dealing,
    lengths,
    input_gain,
    w_query,
    w_key,
    w_value,
    query_gain,
    key_gain,
    w_out,
    hidden_gain,
    w_gate,
    w_up,
    w_down,
    cotangent,
):
    head_count = lax.axis_size("head")
    cycle_count = lax.axis_size("blk")
    head_place = lax.axis_index("head")
    cycle_place = lax.axis_index("blk")
    own_rows = inputs.shape[0]
    group_rows = own_rows * head_count
    score_scale = HD ** (-0.5)
    group_size = QH // KVH
    full_query, full_key, full_value, gain_one, gain_query, gain_key = (
        lax.all_gather(w_query, ("head", "blk"), axis=1, tiled=True),
        lax.all_gather(w_key, ("head", "blk"), axis=1, tiled=True),
        lax.all_gather(w_value, ("head", "blk"), axis=1, tiled=True),
        lax.all_gather(input_gain, ("head", "blk"), axis=0, tiled=True),
        lax.all_gather(query_gain, ("head", "blk"), axis=0, tiled=True),
        lax.all_gather(key_gain, ("head", "blk"), axis=0, tiled=True),
    )
    out_rows, gate_cols, up_cols, down_rows, gain_two = (
        lax.all_gather(w_out, "blk", axis=0, tiled=True),
        lax.all_gather(w_gate, "blk", axis=1, tiled=True),
        lax.all_gather(w_up, "blk", axis=1, tiled=True),
        lax.all_gather(w_down, "blk", axis=0, tiled=True),
        lax.all_gather(hidden_gain, "blk", axis=0, tiled=True),
    )
    input_norm = gain_one.astype(jnp.float32)
    hidden_norm = gain_two.astype(jnp.float32)
    query_norm = gain_query.astype(jnp.float32)
    key_norm = gain_key.astype(jnp.float32)
    token_values = inputs.astype(jnp.float32)
    scale_one = rms_scale(token_values)
    normed = (token_values * scale_one * input_norm).astype(jnp.bfloat16)
    query_raw = jnp.dot(normed, full_query, preferred_element_type=jnp.float32).astype(jnp.bfloat16)
    key_raw = jnp.dot(normed, full_key, preferred_element_type=jnp.float32).astype(jnp.bfloat16)
    value_raw = jnp.dot(normed, full_value, preferred_element_type=jnp.float32).astype(jnp.bfloat16)
    query_heads, key_heads, value_heads = (
        lax.all_to_all(query_raw, "head", split_axis=1, concat_axis=0, tiled=True),
        lax.all_to_all(key_raw, "head", split_axis=1, concat_axis=0, tiled=True),
        lax.all_to_all(value_raw, "head", split_axis=1, concat_axis=0, tiled=True),
    )
    group_anchors = lax.dynamic_slice_in_dim(dealing, cycle_place * group_rows, group_rows)
    group_starts = token_starts(group_anchors, lengths)
    cosine, sine = rope_tables(group_anchors - group_starts)
    query_input = query_heads.astype(jnp.float32)
    key_input = key_heads.astype(jnp.float32)
    query = norm_rope(query_input, query_norm, cosine, sine).astype(jnp.bfloat16)
    keys = norm_rope(key_input, key_norm, cosine, sine).astype(jnp.bfloat16)
    local_heads = keys.shape[1] // HD
    query_grid = query.reshape(group_rows, local_heads, group_size, HD)

    def source_anchors(cycle_step):
        source = (cycle_place - cycle_step) % cycle_count
        return lax.dynamic_slice_in_dim(dealing, source * group_rows, group_rows)

    def block_scores(key_block, cycle_step):
        key_grid = key_block.reshape(group_rows, local_heads, HD)
        raw_scores = (
            jnp.einsum("qkgd,tkd->qkgt", query_grid, key_grid, preferred_element_type=jnp.float32)
            * score_scale
        )
        anchors = source_anchors(cycle_step)
        allowed = (anchors[None, :] <= group_anchors[:, None]) & (
            anchors[None, :] >= group_starts[:, None]
        )
        return (raw_scores, allowed[:, None, None, :])

    def add_stats(key_block, cycle_step, row_peak, total_sum):
        raw_scores, allowed = block_scores(key_block, cycle_step)
        new_peak = jnp.maximum(row_peak, jnp.max(jnp.where(allowed, raw_scores, -1e30), axis=-1))
        lifted = jnp.where(allowed, jnp.exp(raw_scores - new_peak[..., None]), 0.0)
        return (new_peak, total_sum * jnp.exp(row_peak - new_peak) + jnp.sum(lifted, axis=-1))

    def cycle_visit(carry, cycle_step):
        key_block, value_block, row_peak, total_sum = carry
        row_peak, total_sum = add_stats(key_block, cycle_step, row_peak, total_sum)
        next_key, next_value = shifted((key_block, value_block), "blk", 1)
        return ((next_key, next_value, row_peak, total_sum), (key_block, value_block))

    floor_stats = jnp.full((group_rows, local_heads, group_size), -1e30, jnp.float32)
    cycle_start = (keys, value_heads, floor_stats, jnp.zeros_like(floor_stats))
    (last_key, last_value, row_peak, total_sum), (seen_keys, seen_values) = lax.scan(
        cycle_visit, cycle_start, jnp.arange(cycle_count - 1, dtype=jnp.int32)
    )
    row_peak, total_sum = add_stats(last_key, cycle_count - 1, row_peak, total_sum)
    seen_keys = jnp.concatenate([seen_keys, last_key[None]], axis=0)
    seen_values = jnp.concatenate([seen_values, last_value[None]], axis=0)
    log_total = row_peak + jnp.log(total_sum)
    cycle_steps = jnp.arange(cycle_count, dtype=jnp.int32)

    def add_values(carry, stored):
        mixed_sum, extra_sum = carry
        cycle_step, key_block, value_block = stored
        raw_scores, allowed = block_scores(key_block, cycle_step)
        probs = jnp.where(allowed, jnp.exp(raw_scores - log_total[..., None]), 0.0)
        weights = probs.astype(jnp.bfloat16)
        remainder = (probs - weights.astype(jnp.float32)).astype(jnp.bfloat16)
        value_grid = value_block.reshape(group_rows, local_heads, HD)
        mixed_sum = mixed_sum + jnp.einsum(
            "qkgt,tkd->qkgd", weights, value_grid, preferred_element_type=jnp.float32
        )
        extra_sum = extra_sum + jnp.einsum(
            "qkgt,tkd->qkgd", remainder, value_grid, preferred_element_type=jnp.float32
        )
        return ((mixed_sum, extra_sum), None)

    empty_heads = jnp.zeros((group_rows, local_heads, group_size, HD), jnp.float32)
    (mixed_sum, extra_sum), unused_values = lax.scan(
        add_values, (empty_heads, empty_heads), (cycle_steps, seen_keys, seen_values)
    )
    mixed = mixed_sum.reshape(group_rows, -1).astype(jnp.bfloat16)
    branch = jnp.dot(mixed, out_rows, preferred_element_type=jnp.float32)
    own_part = lax.dynamic_update_slice_in_dim(
        jnp.zeros_like(branch), token_values, head_place * own_rows, 0
    )
    middle = lax.psum(branch + own_part, "head")
    scale_two = rms_scale(middle)
    hidden_in = (middle * scale_two * hidden_norm).astype(jnp.bfloat16)
    gate = jnp.dot(hidden_in, gate_cols, preferred_element_type=jnp.float32)
    up_proj = jnp.dot(hidden_in, up_cols, preferred_element_type=jnp.float32)
    activated = (jax.nn.silu(gate) * up_proj).astype(jnp.bfloat16)
    feed_out = lax.psum_scatter(
        jnp.dot(activated, down_rows, preferred_element_type=jnp.float32),
        "head",
        scatter_dimension=0,
        tiled=True,
    )
    middle_own = lax.dynamic_slice_in_dim(middle, head_place * own_rows, own_rows, 0)
    layer_out = (middle_own + feed_out).astype(jnp.bfloat16)
    act_grad = col_inner(cotangent, down_rows)
    grad_down = row_outer(activated, cotangent)
    sigmoid_gate = jax.nn.sigmoid(gate)
    silu_gate = jax.nn.silu(gate)
    gate_grad = (act_grad * up_proj * sigmoid_gate * (1.0 + gate * (1.0 - sigmoid_gate))).astype(
        jnp.bfloat16
    )
    up_grad = (act_grad * silu_gate).astype(jnp.bfloat16)
    grad_gate = row_outer(hidden_in, gate_grad)
    grad_up = row_outer(hidden_in, up_grad)
    hidden_part = col_inner(gate_grad, gate_cols) + col_inner(up_grad, up_cols)
    hidden_grad = lax.psum(hidden_part, "head")
    grad_hidden_gain = jnp.sum(hidden_grad * middle * scale_two, axis=0)
    middle_grad = cotangent.astype(jnp.float32) + norm_back(
        hidden_grad, middle, scale_two, hidden_norm
    )
    branch_grad = middle_grad.astype(jnp.bfloat16)
    grad_out = row_outer(mixed, branch_grad)
    mixed_grad = col_inner(branch_grad, out_rows).astype(jnp.bfloat16)
    grad_grid = mixed_grad.reshape(group_rows, local_heads, group_size, HD)
    row_delta = jnp.sum(grad_grid.astype(jnp.float32) * (mixed_sum + extra_sum), axis=-1)

    def back_visit(carry, stored):
        query_acc, key_acc, value_acc = carry
        cycle_step, key_block, value_block = stored
        raw_scores, allowed = block_scores(key_block, cycle_step)
        probs = jnp.where(allowed, jnp.exp(raw_scores - log_total[..., None]), 0.0)
        key_grid = key_block.reshape(group_rows, local_heads, HD)
        value_grid = value_block.reshape(group_rows, local_heads, HD)
        value_acc = value_acc + jnp.einsum(
            "qkgt,qkgd->tkd",
            probs.astype(jnp.bfloat16),
            grad_grid,
            preferred_element_type=jnp.float32,
        ).reshape(group_rows, -1)
        prob_grad = jnp.einsum(
            "qkgd,tkd->qkgt", grad_grid, value_grid, preferred_element_type=jnp.float32
        )
        score_grad = (probs * (prob_grad - row_delta[..., None])).astype(jnp.bfloat16)
        query_acc = (
            query_acc
            + jnp.einsum("qkgt,tkd->qkgd", score_grad, key_grid, preferred_element_type=jnp.float32)
            * score_scale
        )
        key_acc = (
            key_acc
            + jnp.einsum(
                "qkgt,qkgd->tkd", score_grad, query_grid, preferred_element_type=jnp.float32
            ).reshape(group_rows, -1)
            * score_scale
        )
        key_acc, value_acc = shifted((key_acc, value_acc), "blk", 1)
        return ((query_acc, key_acc, value_acc), None)

    pair_zero = jnp.zeros((group_rows, local_heads * HD), jnp.float32)
    (query_acc, key_acc, value_acc), unused_back = lax.scan(
        back_visit, (empty_heads, pair_zero, pair_zero), (cycle_steps, seen_keys, seen_values)
    )
    query_raw_grad, grad_query_gain = rope_pull(
        query_input, query_norm, cosine, sine, query_acc.reshape(group_rows, -1)
    )
    key_raw_grad, grad_key_gain = rope_pull(key_input, key_norm, cosine, sine, key_acc)
    query_send = query_raw_grad.astype(jnp.bfloat16)
    key_send = key_raw_grad.astype(jnp.bfloat16)
    value_send = value_acc.astype(jnp.bfloat16)
    query_back, key_back, value_back = (
        lax.all_to_all(query_send, "head", split_axis=0, concat_axis=1, tiled=True),
        lax.all_to_all(key_send, "head", split_axis=0, concat_axis=1, tiled=True),
        lax.all_to_all(value_send, "head", split_axis=0, concat_axis=1, tiled=True),
    )
    normed_grad = (
        col_inner(query_back, full_query)
        + col_inner(key_back, full_key)
        + col_inner(value_back, full_value)
    )
    grad_gain_part = jnp.sum(normed_grad * token_values * scale_one, axis=0)
    middle_own_grad = lax.dynamic_slice_in_dim(middle_grad, head_place * own_rows, own_rows, 0)
    grad_input = middle_own_grad + norm_back(normed_grad, token_values, scale_one, input_norm)
    query_whole = row_outer(normed, query_back)
    key_whole = row_outer(normed, key_back)
    value_whole = row_outer(normed, value_back)
    grad_query, grad_key, grad_value, grad_input_gain, grad_query_gain, grad_key_gain = (
        lax.psum_scatter(query_whole, ("head", "blk"), scatter_dimension=1, tiled=True),
        lax.psum_scatter(key_whole, ("head", "blk"), scatter_dimension=1, tiled=True),
        lax.psum_scatter(value_whole, ("head", "blk"), scatter_dimension=1, tiled=True),
        lax.psum_scatter(grad_gain_part, ("head", "blk"), scatter_dimension=0, tiled=True),
        lax.psum_scatter(grad_query_gain, ("head", "blk"), scatter_dimension=0, tiled=True),
        lax.psum_scatter(grad_key_gain, ("head", "blk"), scatter_dimension=0, tiled=True),
    )
    grad_out, grad_gate, grad_up, grad_down, grad_hidden_gain = (
        lax.psum_scatter(grad_out, "blk", scatter_dimension=0, tiled=True),
        lax.psum_scatter(grad_gate, "blk", scatter_dimension=1, tiled=True),
        lax.psum_scatter(grad_up, "blk", scatter_dimension=1, tiled=True),
        lax.psum_scatter(grad_down, "blk", scatter_dimension=0, tiled=True),
        lax.psum_scatter(grad_hidden_gain, "blk", scatter_dimension=0, tiled=True),
    )
    return (
        layer_out,
        grad_input,
        grad_input_gain,
        grad_query,
        grad_key,
        grad_value,
        grad_query_gain,
        grad_key_gain,
        grad_out,
        grad_hidden_gain,
        grad_gate,
        grad_up,
        grad_down,
    )


def solution(mesh):
    return jax.shard_map(
        local,
        mesh=mesh,
        in_specs=(
            P(("blk", "head"), None),
            P(),
            P(),
            P(("head", "blk")),
            P(None, ("head", "blk")),
            P(None, ("head", "blk")),
            P(None, ("head", "blk")),
            P(("head", "blk")),
            P(("head", "blk")),
            P(("head", "blk"), None),
            P("blk"),
            P(None, ("head", "blk")),
            P(None, ("head", "blk")),
            P(("head", "blk"), None),
            P("blk", None),
        ),
        out_specs=(
            P(("blk", "head"), None),
            P(("blk", "head"), None),
            P(("head", "blk")),
            P(None, ("head", "blk")),
            P(None, ("head", "blk")),
            P(None, ("head", "blk")),
            P(("head", "blk")),
            P(("head", "blk")),
            P(("head", "blk"), None),
            P("blk"),
            P(None, ("head", "blk")),
            P(None, ("head", "blk")),
            P(("head", "blk"), None),
        ),
        check_vma=False,
    )
```

profile of v0, /device:TPU:0, one launch (start us, length us, event | category | flops | bytes accessed | tf_op | source)
XLA Modules:
  0.0 2074.7 jit_solution(10102535283136231635)
XLA Ops:
  12.6 42.1 %all-reduce.12 = (bf16[2048]{0:T(1024)(128)(2,1)S(1)}, bf16[128]{0:T(256)(128)(2,1)S(1)}, bf16[128]{0:T(256)(128)(2,1)S(1)}) all-reduce(bf16[2048]{0:T(1024)(128)(2,1)S(1)} %dynamic-update-slice.1, bf16[128]{0:T(256)(128)(2,1)S(1)} %dynamic-update-slice.2, ...), channel_id=1, replica_groups=mesh['head'=4,'blk'=8] {'head','blk'}, use_global_device_ids=true, to_apply=%add.4 | all-reduce | flops 2304 | bytes 9216
  63.0 12.9 all-gather.9.cloned.1.call-done
  84.0 55.8 %all-gather.11.cloned.1.call-done = bf16[2048,1024]{0,1:T(8,128)(2,1)} async-done(((bf16[2048,32]{0,1:T(8,128)(2,1)}), bf16[2048,1024]{0,1:T(8,128)(2,1)}) %all-gather.11.cloned.1.call-update) | async-done | bytes 4194320 | tf_op jit(solution)/shard_map/all_gather | solution.py:106
  147.5 71.2 %all-gather.13.cloned.1.call-done = bf16[2048,2048]{0,1:T(8,128)(2,1)} async-done(((bf16[2048,64]{0,1:T(8,128)(2,1)}), bf16[2048,2048]{0,1:T(8,128)(2,1)}) %all-gather.13.cloned.1.call-update) | async-done | bytes 8388624 | tf_op jit(solution)/shard_map/all_gather | solution.py:104
  218.7 6.3 convolution_convert_fusion
  232.0 6.0 all-to-all-done.2
  252.9 73.4 %while.55 = (s32[]{:T(128)}, bf16[512,256]{1,0:T(8,128)(2,1)S(1)}, bf16[512,256]{1,0:T(8,128)(2,1)S(1)}, f32[512,2,2]{0,2,1:T(2,128)S(1)}, f32[512,2,2]{0,2,1:T(...) while((s32[]{:T(128)}, bf16[512,256]{1,0:T(8,128)(2,1)S(1)}, ...), condition=%wide.region_8.9_spmd.clone, body=%wide.region_5.8_spmd.clone.sunk | while | flops 276572192 | bytes 15845835 | solution.py:173
  331.0 107.6 %while.56 = (s32[]{:T(128)}, f32[512,2,2,128]{0,3,2,1:T(8,128)}, f32[512,2,2,128]{0,3,2,1:T(8,128)}, bf16[8,512,256]{1,2,0:T(8,128)(2,1)}, s32[8]{0:T(128)S(1)},...) while((s32[]{:T(128)}, f32[512,2,2,128]{0,3,2,1:T(8,128)}, ...), condition=%wide.region_12.13_spmd.clone, body=%wide.region_11.12_spmd.clone.sunk | while | flops 818675712 | bytes 45115844 | solution.py:199
  449.3 8.4 all-gather
  457.7 91.9 %all-reduce.16.cloned.1.call-done = f32[512,2048]{1,0:T(8,128)} async-done(((f32[512,2048]{1,0:T(8,128)}), f32[512,2048]{1,0:T(8,128)}) %all-reduce.16.cloned.1.call-update) | async-done | bytes 4194320 | tf_op jit(solution)/shard_map/psum | solution.py:207
  554.9 61.2 %all-gather.17.cloned.1.call-done = bf16[2048,1536]{0,1:T(8,128)(2,1)} async-done(((bf16[2048,192]{0,1:T(8,128)(2,1)}), bf16[2048,1536]{0,1:T(8,128)(2,1)}) %all-gather.17.cloned.1.call-update) | async-done | bytes 6291472 | tf_op jit(solution)/shard_map/all_gather | solution.py:113
  616.1 8.5 fusion.87
  624.6 56.7 %all-gather.19.cloned.1.call-done = bf16[2048,1536]{0,1:T(8,128)(2,1)} async-done(((bf16[2048,192]{0,1:T(8,128)(2,1)}), bf16[2048,1536]{0,1:T(8,128)(2,1)}) %all-gather.19.cloned.1.call-update) | async-done | bytes 6291472 | tf_op jit(solution)/shard_map/all_gather | solution.py:114
  681.3 8.6 fusion.88
  689.8 56.6 %all-gather.21.cloned.1.call-done = bf16[1536,2048]{1,0:T(8,128)(2,1)} async-done(((bf16[192,2048]{1,0:T(8,128)(2,1)}), bf16[1536,2048]{1,0:T(8,128)(2,1)}) %all-gather.21.cloned.1.call-update) | async-done | bytes 6291472 | tf_op jit(solution)/shard_map/all_gather | solution.py:115
  746.4 9.7 multiply_convert_fusion.1
  756.2 7.5 fusion.90
  768.8 7.8 fusion.89
  776.7 94.7 %all-reduce.18.cloned.1.call-done = f32[512,2048]{1,0:T(8,128)} async-done(((f32[512,2048]{1,0:T(8,128)}), f32[512,2048]{1,0:T(8,128)}) %all-reduce.18.cloned.1.call-update) | async-done | bytes 4194320 | tf_op jit(solution)/shard_map/psum | solution.py:232
  893.7 271.7 %while.57 = (s32[]{:T(128)}, f32[512,2,2,128]{0,3,2,1:T(8,128)}, f32[512,256]{0,1:T(8,128)}, f32[512,256]{0,1:T(8,128)}, bf16[8,512,256]{1,2,0:T(8,128)(2,1)}, /...) while((s32[]{:T(128)}, f32[512,2,2,128]{0,3,2,1:T(8,128)}, ...), condition=%wide.region_20.21_spmd.clone, body=%wide.region_19.20_spmd.clone.sunk | while | flops 1354629120 | bytes 52988428 | solution.py:276
  919.6 5.6 collective-permute-done.3
  946.0 15.9 collective-permute-done.2
  961.9 16.9 collective-permute-done.3
  1004.4 5.6 collective-permute-done.3
  1030.4 5.0 collective-permute-done.2
  1035.5 5.6 collective-permute-done.3
  1061.5 5.0 collective-permute-done.2
  1066.5 5.6 collective-permute-done.3
  1092.6 5.0 collective-permute-done.2
  1097.6 5.6 collective-permute-done.3
  1123.7 5.0 collective-permute-done.2
  1128.7 5.6 collective-permute-done.3
  1159.8 5.6 collective-permute-done.3
  1173.3 8.9 all_to_all.96
  1188.0 8.8 all_to_all.97
  1203.3 8.0 fusion.92
  1211.4 7.8 fusion.93
  1220.8 7.9 fusion.94
  1240.6 10.1 all_to_all.98
  1250.6 8.2 fusion.72
  1260.7 14.3 all-reduce.10
  1283.8 38.3 %all-reduce.11 = (f32[2048]{0:T(1024)S(1)}, f32[128]{0:T(128)S(1)}, f32[128]{0:T(128)S(1)}) all-reduce(f32[2048]{0:T(1024)S(1)} %get-tuple-element.838, f32[128]{0:T(128)S(1)} %get-tuple-element.836, f32[128]{0:T(128)S(1)} %get-tuple-element.840), channel_id=3, replica_groups=mesh['head'=4,'blk'=8] {'head','blk'}, use_global_device_ids=true, to_apply=%region_25.26.clone | all-reduce | flops 2304 | bytes 18432
  1328.9 7.7 reduce-scatter.13.cloned.1.call-done
  1336.6 153.0 %reduce-scatter.15.cloned.1.call-done = f32[2048,32]{0,1:T(8,128)} async-done(((f32[2048,1024]{0,1:T(8,128)}), f32[2048,32]{0,1:T(8,128)}) %reduce-scatter.15.cloned.1.call-update) | async-done | bytes 262160 | tf_op jit(solution)/shard_map/reduce_scatter | solution.py:305
  1489.6 129.7 %reduce-scatter.19.cloned.1.call-done = f32[2048,192]{0,1:T(8,128)} async-done(((f32[2048,1536]{0,1:T(8,128)}), f32[2048,192]{0,1:T(8,128)}) %reduce-scatter.19.cloned.1.call-update) | async-done | bytes 1572880 | tf_op jit(solution)/shard_map/reduce_scatter | solution.py:312
  1619.3 130.4 %reduce-scatter.21.cloned.1.call-done = f32[2048,192]{0,1:T(8,128)} async-done(((f32[2048,1536]{0,1:T(8,128)}), f32[2048,192]{0,1:T(8,128)}) %reduce-scatter.21.cloned.1.call-update) | async-done | bytes 1572880 | tf_op jit(solution)/shard_map/reduce_scatter | solution.py:313
  1749.7 130.5 %reduce-scatter.23.cloned.1.call-done = f32[192,2048]{1,0:T(8,128)} async-done(((f32[1536,2048]{1,0:T(8,128)}), f32[192,2048]{1,0:T(8,128)}) %reduce-scatter.23.cloned.1.call-update) | async-done | bytes 1572880 | tf_op jit(solution)/shard_map/reduce_scatter | solution.py:314
  1880.2 187.8 %reduce-scatter.11.cloned.1.call-done = f32[2048,64]{0,1:T(8,128)} async-done(((f32[2048,2048]{0,1:T(8,128)}), f32[2048,64]{0,1:T(8,128)}) %reduce-scatter.11.cloned.1.call-update) | async-done | bytes 524304 | tf_op jit(solution)/shard_map/reduce_scatter | solution.py:303
  (645 shorter events, 491.9 us)
Async XLA Ops:
  7.2 68.8 %all-gather.9.cloned.1.call-start = ((), (), s32[]{:S(2)}) async-start(), calls=%async_computation.14 | async-start | bytes 4325376 | tf_op jit(solution)/shard_map/all_gather | solution.py:105
  7.9 131.8 %all-gather.11.cloned.1.call-start = ((), (), s32[]{:S(2)}) async-start(), calls=%async_computation.15 | async-start | bytes 4325376 | tf_op jit(solution)/shard_map/all_gather | solution.py:106
  8.7 210.1 %all-gather.13.cloned.1.call-start = ((), (), s32[]{:S(2)}) async-start(), calls=%async_computation.16 | async-start | bytes 8650752 | tf_op jit(solution)/shard_map/all_gather | solution.py:104
  9.4 430.5 %all-gather.15.cloned.1.call-start = ((), (), s32[]{:S(2)}) async-start(), calls=%async_computation.17 | async-start | bytes 2359296 | tf_op jit(solution)/shard_map/all_gather | solution.py:112
  80.5 63.7 %all-to-all-start = ((bf16[128,4,256]{2,0,1:T(8,128)(2,1)}), bf16[128,4,256]{2,0,1:T(8,128)(2,1)S(1)}, u32[]{:S(2)}, u32[]{:S(2)}) async-start(bf16[128,4,256]{2,0,1:T(8,128)(2,1)} %bitcast.232), calls=%async_computation | async-start | bytes 524288 | tf_op jit(solution)/shard_map/all_to_all | solution.py:130
  225.9 12.2 all-to-all-start.2
  238.1 14.8 all-to-all-start.1
  241.5 308.2 %all-reduce.16.cloned.1.call-start = ((), (), s32[]{:S(2)}) async-start(), calls=%async_computation.18 | async-start | bytes 8388608 | tf_op jit(solution)/shard_map/psum | solution.py:207
  252.9 7.6 collective-permute-start
  253.0 10.4 collective-permute-start.1
  263.4 7.6 collective-permute-start
  263.5 10.4 collective-permute-start.1
  274.0 10.4 collective-permute-start.1
  284.4 10.4 collective-permute-start.1
  294.8 7.6 collective-permute-start
  294.9 10.4 collective-permute-start.1
  305.3 7.6 collective-permute-start
  305.4 10.4 collective-permute-start.1
  315.8 7.6 collective-permute-start
  315.9 10.4 collective-permute-start.1
  447.2 168.9 %all-gather.17.cloned.1.call-start = ((), (), s32[]{:S(2)}) async-start(), calls=%async_computation.19 | async-start | bytes 7077888 | tf_op jit(solution)/shard_map/all_gather | solution.py:113
  447.7 233.5 %all-gather.19.cloned.1.call-start = ((), (), s32[]{:S(2)}) async-start(), calls=%async_computation.20 | async-start | bytes 7077888 | tf_op jit(solution)/shard_map/all_gather | solution.py:114
  448.5 297.9 %all-gather.21.cloned.1.call-start = ((), (), s32[]{:S(2)}) async-start(), calls=%async_computation.21 | async-start | bytes 7077888 | tf_op jit(solution)/shard_map/all_gather | solution.py:115
  449.2 422.2 %all-reduce.18.cloned.1.call-start = ((), (), s32[]{:S(2)}) async-start(), calls=%async_computation.23 | async-start | bytes 8388608 | tf_op jit(solution)/shard_map/psum | solution.py:232
  768.8 557.7 %reduce-scatter.9.cloned.1.call-start = ((), (), s32[]{:S(2)}) async-start(), calls=%async_computation.22 | async-start | bytes 5242880 | tf_op jit(solution)/shard_map/reduce_scatter | solution.py:213
  776.7 552.3 %reduce-scatter.17.cloned.1.call-start = ((), (), s32[]{:S(2)}) async-start(), calls=%async_computation.27 | async-start | bytes 4718592 | tf_op jit(solution)/shard_map/reduce_scatter | solution.py:311
  885.3 451.3 %reduce-scatter.13.cloned.1.call-start = ((), (), s32[]{:S(2)}) async-start(), calls=%async_computation.25 | async-start | bytes 8650752 | tf_op jit(solution)/shard_map/reduce_scatter | solution.py:304
  908.9 10.7 collective-permute-start.2
  911.9 13.3 collective-permute-start.3
  940.0 21.9 %collective-permute-start.2 = (f32[512,256]{0,1:T(8,128)}, f32[512,256]{0,1:T(8,128)}, u32[]{:S(2)}, u32[]{:S(2)}) collective-permute-start(f32[512,256]{0,1:T(8,128)} %bitcast_add_fusion.5), channel_id=1, source_target_pairs={{0,1},{1,2},{2,3},{3,4},{4,5},{5,6},{6,7},{7,0},{8,9},{9,10},{10,1... | collective-permute-start | bytes 1572872 | tf_op jit(solution)/shard_map/while/body/eval_jaxpr/ppermute | solution.py:22
  943.0 35.8 %collective-permute-start.3 = (f32[512,256]{0,1:T(8,128)}, f32[512,256]{0,1:T(8,128)}, u32[]{:S(2)}, u32[]{:S(2)}) collective-permute-start(f32[512,256]{0,1:T(8,128)} %bitcast_add_fusion.6), channel_id=1, source_target_pairs={{0,1},{1,2},{2,3},{3,4},{4,5},{5,6},{6,7},{7,0},{8,9},{9,10},{10,1... | collective-permute-start | bytes 1572872 | tf_op jit(solution)/shard_map/while/body/eval_jaxpr/ppermute | solution.py:22
  993.7 10.7 collective-permute-start.2
  996.7 13.3 collective-permute-start.3
  1024.7 10.7 collective-permute-start.2
  1027.7 13.3 collective-permute-start.3
  1055.8 10.7 collective-permute-start.2
  1058.8 13.3 collective-permute-start.3
  1086.9 10.7 collective-permute-start.2
  1089.9 13.3 collective-permute-start.3
  1118.0 10.7 collective-permute-start.2
  1121.0 13.3 collective-permute-start.3
  1149.1 10.7 collective-permute-start.2
  1152.1 13.3 collective-permute-start.3
  1186.8 302.8 %reduce-scatter.15.cloned.1.call-start = ((), (), s32[]{:S(2)}) async-start(), calls=%async_computation.26 | async-start | bytes 8650752 | tf_op jit(solution)/shard_map/reduce_scatter | solution.py:305
  1201.7 417.5 %reduce-scatter.19.cloned.1.call-start = ((), (), s32[]{:S(2)}) async-start(), calls=%async_computation.28 | async-start | bytes 14155776 | tf_op jit(solution)/shard_map/reduce_scatter | solution.py:312
  1211.3 538.4 %reduce-scatter.21.cloned.1.call-start = ((), (), s32[]{:S(2)}) async-start(), calls=%async_computation.29 | async-start | bytes 14155776 | tf_op jit(solution)/shard_map/reduce_scatter | solution.py:313
  1219.2 660.9 %reduce-scatter.23.cloned.1.call-start = ((), (), s32[]{:S(2)}) async-start(), calls=%async_computation.30 | async-start | bytes 14155776 | tf_op jit(solution)/shard_map/reduce_scatter | solution.py:314
  1228.7 839.3 %reduce-scatter.11.cloned.1.call-start = ((), (), s32[]{:S(2)}) async-start(), calls=%async_computation.24 | async-start | bytes 17301504 | tf_op jit(solution)/shard_map/reduce_scatter | solution.py:303
  (93 other events, 1718.8 us)
Sparse Core Ops, SparseCore 0:
  11.0 64.8 all-gather.8
  78.9 60.7 all-gather.10
  142.7 75.9 all-gather.12
  220.2 27.7 all-gather.14
  447.3 102.3 all-reduce.15
  551.3 64.7 all-gather.16
  617.8 63.3 all-gather.18
  683.0 63.3 all-gather.20
  768.9 102.4 all-reduce.17
  874.2 52.6 reduce-scatter.8
  930.0 61.2 reduce-scatter.16
  1186.9 149.6 reduce-scatter.12
  1339.6 149.9 reduce-scatter.14
  1492.4 126.8 reduce-scatter.18
  1622.1 127.5 reduce-scatter.20
  1752.5 127.5 reduce-scatter.22
  1883.0 184.9 reduce-scatter.10
where the time goes:
time: 2090 us; the launch traced here: 2070 us
  waiting for transfers between devices  1390 us (67%)
  matrix products  290 us (14%)
  blocking collectives  131 us (6%)
  local copies, waits for them, and re-layouts  116 us (6%)
  other arithmetic  99.4 us (5%)
    reduce_scatter x1, waiting for transfers between devices, local(): lax.psum_scatter(query_whole, ('head', 'blk'), scatter_dimension=1, tiled...  188 us
    reduce_scatter x1, waiting for transfers between devices, local(): lax.psum_scatter(value_whole, ('head', 'blk'), scatter_dimension=1, tiled...  153 us
    ppermute x30, waiting for transfers between devices, shifted(): return lax.ppermute(value, axis, pairs)  139 us
    reduce_scatter x1, waiting for transfers between devices, local(): lax.psum_scatter(grad_down, 'blk', scatter_dimension=0, tiled=True)  130 us
    reduce_scatter x1, waiting for transfers between devices, local(): lax.psum_scatter(grad_up, 'blk', scatter_dimension=1, tiled=True)  130 us
    reduce_scatter x1, waiting for transfers between devices, local(): lax.psum_scatter(grad_gate, 'blk', scatter_dimension=1, tiled=True)  130 us
    psum x1, waiting for transfers between devices, local(): hidden_grad = lax.psum(hidden_part, 'head')  94.7 us
    unnamed x3, blocking collectives  94.7 us
  transfers between devices with their start and end apart: 50, of which 45 were waited for; matrix products, arithmetic and copies ran while one was open for 22% of the time, Pallas kernels for 0%

commit v1 on v0

v1 whole, which is shorter than its diff:
```python
import functools
import math

import jax
import jax.numpy as jnp
from jax import lax
from jax.experimental import pallas as pl
from jax.experimental.pallas import tpu as pltpu
from jax.sharding import PartitionSpec as P

QH = 16
KVH = 8
HD = 128
HALF = HD // 2
EPSILON = 1e-06
ROPE_BASE = 1000000.0
SCORE_SCALE = HD ** (-0.5)
EXP2_SCALE = SCORE_SCALE * math.log2(math.e)
CONTRACT_ROWS = (((0,), (0,)), ((), ()))
CONTRACT_COLS = (((1,), (1,)), ((), ()))
BF16 = jnp.bfloat16
F32 = jnp.float32
VMEM_LIMIT = 40 * 1024 * 1024


def dot(left, right):
    return jnp.dot(left, right, preferred_element_type=F32)


def row_outer(left, right):
    return lax.dot_general(left, right, CONTRACT_ROWS, preferred_element_type=F32)


def col_inner(left, right):
    return lax.dot_general(left, right, CONTRACT_COLS, preferred_element_type=F32)


def rms_scale(values):
    return lax.rsqrt(jnp.mean(values * values, axis=-1, keepdims=True) + EPSILON)


def norm_back(upstream, source, scale_rows, gain):
    scaled = upstream * gain
    return scale_rows * scaled - source * scale_rows**3 * jnp.mean(
        scaled * source, axis=-1, keepdims=True
    )


def core_swap(value):
    count = lax.axis_size("blk")
    return lax.ppermute(value, "blk", [(i, i ^ 1) for i in range(count)])


def chip_shift(value, steps=1, flip=0):
    count = lax.axis_size("blk")
    return lax.ppermute(
        value, "blk", [(i, ((i + 2 * steps) % count) ^ flip) for i in range(count)]
    )


def column_gather(value):
    chips = lax.axis_size("blk") // 2
    blocks = []
    for step in range(chips):
        blocks.append(jnp.concatenate([value, core_swap(value)], axis=0))
        if step < chips - 1:
            value = chip_shift(value)
    return blocks


def column_scatter(part_of):
    chips = lax.axis_size("blk") // 2
    arrived = None
    for step in list(range(1, chips)) + [0]:
        part = part_of(step)
        rows = part.shape[0] // 2
        total = part[:rows] + core_swap(part[rows:].astype(BF16)).astype(F32)
        if arrived is not None:
            total = total + arrived.astype(F32)
        if step:
            arrived = chip_shift(total.astype(BF16))
    return total


def head_bits():
    count = lax.axis_size("head")
    return [1 << i for i in range(count.bit_length() - 1)]


def head_flip(value, bit):
    count = lax.axis_size("head")
    return lax.ppermute(value, "head", [(i, i ^ bit) for i in range(count)])


def head_gather(value, backwards):
    pieces = {0: value}
    bits = head_bits()
    for bit in bits[::-1] if backwards else bits:
        for place in sorted(pieces):
            pieces[place ^ bit] = head_flip(pieces[place], bit)
    return [pieces[i] for i in range(len(pieces))]


def head_scatter(parts, backwards):
    pieces = dict(enumerate(parts))
    bits = head_bits()
    for bit in bits if backwards else bits[::-1]:
        for place in sorted(pieces):
            if place & bit:
                gone = head_flip(pieces.pop(place).astype(BF16), bit)
                pieces[place ^ bit] = pieces[place ^ bit] + gone.astype(F32)
    return pieces[0]


def sum_everywhere(value):
    for bit in head_bits():
        value = value + head_flip(value, bit)
    count = lax.axis_size("blk")
    for shift in range(count.bit_length() - 1):
        bit = 1 << shift
        value = value + lax.ppermute(value, "blk", [(i, i ^ bit) for i in range(count)])
    return value


def pick(stack, index):
    return lax.dynamic_index_in_dim(stack, index, 0, keepdims=False)


def token_starts(anchors, lengths):
    ends = jnp.cumsum(lengths)
    seq_starts = ends - lengths
    inside = seq_starts[None, :] <= anchors[:, None]
    return jnp.max(jnp.where(inside, seq_starts[None, :], 0), axis=1)


def rope_tables(places):
    ladder = jnp.arange(HALF, dtype=F32)
    rates = jnp.exp(ladder * (-2.0 * math.log(ROPE_BASE) / HD))
    angles = rates[:, None] * places.astype(F32)[None, :]
    return (jnp.cos(angles), jnp.sin(angles))


def rope_forward(raw, gain, cosine, sine):
    heads = raw.astype(F32)
    scale = lax.rsqrt(jnp.mean(heads * heads, axis=-2, keepdims=True) + EPSILON)
    normed = heads * scale * gain[:, None]
    low, high = normed[..., :HALF, :], normed[..., HALF:, :]
    return jnp.concatenate([low * cosine - high * sine, high * cosine + low * sine], axis=-2)


def rope_backward(raw, gain, cosine, sine, upstream):
    heads = raw.astype(F32)
    scale = lax.rsqrt(jnp.mean(heads * heads, axis=-2, keepdims=True) + EPSILON)
    low, high = upstream[..., :HALF, :], upstream[..., HALF:, :]
    turned = jnp.concatenate([low * cosine + high * sine, high * cosine - low * sine], axis=-2)
    gain_grad = jnp.sum(turned * heads * scale, axis=-1)
    scaled = turned * gain[:, None]
    back = scale * scaled - heads * scale**3 * jnp.mean(scaled * heads, axis=-2, keepdims=True)
    return back, gain_grad


def attend_kernel(chunk, q_ref, k_ref, v_ref, qpos_ref, qlow_ref, kpos_ref, out_ref, log_ref):
    rows = q_ref.shape[0]
    query = q_ref[...]
    qpos = qpos_ref[...]
    qlow = qlow_ref[...]

    def body(i, total):
        at = pl.multiple_of(i * chunk, chunk)
        scores = col_inner(query, k_ref[pl.ds(at, chunk), :])
        kpos = kpos_ref[:, pl.ds(at, chunk)]
        allowed = (kpos <= qpos) & (kpos >= qlow)
        lifted = jnp.where(allowed, jnp.exp2(scores * EXP2_SCALE), 0.0).astype(BF16)
        values = jnp.concatenate(
            [v_ref[pl.ds(at, chunk), :], jnp.ones((chunk, HD), BF16)], axis=1
        )
        return total + dot(lifted, values)

    total = lax.fori_loop(
        0, k_ref.shape[0] // chunk, body, jnp.zeros((rows, 2 * HD), F32), unroll=True
    )
    weight = total[:, HD:]
    out_ref[...] = total[:, :HD] / weight
    log_ref[...] = jnp.log2(weight).T[:8, :]


def attend(query, keys, values, qpos, qlow, kpos):
    rows, tokens = query.shape[0], keys.shape[0]
    own = qpos.shape[0]
    block = 256
    wrap = own // block
    cost = pl.CostEstimate(
        flops=4 * rows * tokens * HD, bytes_accessed=4 * tokens * HD, transcendentals=rows * tokens
    )
    return pl.pallas_call(
        functools.partial(attend_kernel, min(1024, tokens)),
        grid=(rows // block,),
        in_specs=[
            pl.BlockSpec((block, HD), lambda i: (i, 0)),
            pl.BlockSpec((tokens, HD), lambda i: (0, 0)),
            pl.BlockSpec((tokens, HD), lambda i: (0, 0)),
            pl.BlockSpec((block, 1), lambda i: (i % wrap, 0)),
            pl.BlockSpec((block, 1), lambda i: (i % wrap, 0)),
            pl.BlockSpec((1, tokens), lambda i: (0, 0)),
        ],
        out_specs=[
            pl.BlockSpec((block, HD), lambda i: (i, 0)),
            pl.BlockSpec((8, block), lambda i: (0, i)),
        ],
        out_shape=[
            jax.ShapeDtypeStruct((rows, HD), F32),
            jax.ShapeDtypeStruct((8, rows), F32),
        ],
        compiler_params=pltpu.CompilerParams(vmem_limit_bytes=VMEM_LIMIT),
        cost_estimate=cost,
    )(query, keys, values, qpos[:, None], qlow[:, None], kpos[None, :])


def attend_back_kernel(
    chunk, own, q_ref, g_ref, o_ref, log_ref, qpos_ref, qlow_ref, k_ref, v_ref, kpos_ref,
    dq_ref, dk_ref, dv_ref, delta_ref,
):
    rows = q_ref.shape[0]

    @pl.when(pl.program_id(0) == 0)
    def _():
        dq_ref[...] = jnp.zeros_like(dq_ref)
        for i in range(rows // chunk):
            at = pl.ds(i * chunk, chunk)
            product = g_ref[at, :].astype(F32) * o_ref[at, :]
            sums = jnp.sum(product.T, axis=0, keepdims=True)
            delta_ref[:, at] = jnp.broadcast_to(sums, (8, chunk))

    keys = k_ref[...]
    values = v_ref[...]
    kpos = kpos_ref[...]
    key_sum = jnp.zeros(keys.shape, F32)
    value_sum = jnp.zeros(keys.shape, F32)
    for i in range(rows // chunk):
        at = pl.ds(i * chunk, chunk)
        place = pl.ds((i * chunk) % own, chunk)
        query = q_ref[at, :]
        upstream = g_ref[at, :]
        scores = col_inner(keys, query)
        allowed = (kpos <= qpos_ref[:, place]) & (kpos >= qlow_ref[:, place])
        probs = jnp.where(allowed, jnp.exp2(scores * EXP2_SCALE - log_ref[0:1, at]), 0.0)
        prob_grad = col_inner(values, upstream)
        score_grad = (probs * (prob_grad - delta_ref[0:1, at])).astype(BF16)
        value_sum = value_sum + dot(probs.astype(BF16), upstream)
        key_sum = key_sum + dot(score_grad, query)
        dq_ref[at, :] += row_outer(score_grad, keys) * SCORE_SCALE
    dk_ref[...] = key_sum * SCORE_SCALE
    dv_ref[...] = value_sum


def attend_back(query, upstream, out, logs, qpos, qlow, keys, values, kpos):
    rows, tokens = query.shape[0], keys.shape[0]
    own = qpos.shape[0]
    block = 512
    cost = pl.CostEstimate(
        flops=10 * rows * tokens * HD, bytes_accessed=8 * tokens * HD, transcendentals=rows * tokens
    )
    whole = lambda i: (0, 0)
    return pl.pallas_call(
        functools.partial(attend_back_kernel, 512, own),
        grid=(tokens // block,),
        in_specs=[
            pl.BlockSpec((rows, HD), whole),
            pl.BlockSpec((rows, HD), whole),
            pl.BlockSpec((rows, HD), whole),
            pl.BlockSpec((8, rows), whole),
            pl.BlockSpec((1, own), whole),
            pl.BlockSpec((1, own), whole),
            pl.BlockSpec((block, HD), lambda i: (i, 0)),
            pl.BlockSpec((block, HD), lambda i: (i, 0)),
            pl.BlockSpec((block, 1), lambda i: (i, 0)),
        ],
        out_specs=[
            pl.BlockSpec((rows, HD), whole),
            pl.BlockSpec((block, HD), lambda i: (i, 0)),
            pl.BlockSpec((block, HD), lambda i: (i, 0)),
        ],
        out_shape=[
            jax.ShapeDtypeStruct((rows, HD), F32),
            jax.ShapeDtypeStruct((tokens, HD), F32),
            jax.ShapeDtypeStruct((tokens, HD), F32),
        ],
        scratch_shapes=[pltpu.VMEM((8, rows), F32)],
        compiler_params=pltpu.CompilerParams(vmem_limit_bytes=VMEM_LIMIT),
        cost_estimate=cost,
    )(query, upstream, out, logs, qpos[None, :], qlow[None, :], keys, values, kpos[:, None])


def local(
    inputs,
    dealing,
    lengths,
    input_gain,
    w_query,
    w_key,
    w_value,
    query_gain,
    key_gain,
    w_out,
    hidden_gain,
    w_gate,
    w_up,
    w_down,
    cotangent,
):
    heads, blks = lax.axis_size("head"), lax.axis_size("blk")
    head, blk = lax.axis_index("head"), lax.axis_index("blk")
    shards = heads * blks
    chips = blks // 2
    chip, core = blk // 2, blk % 2
    shard = head * blks + blk
    rows, width = inputs.shape
    column = rows * blks
    pair = 2 * rows
    per_device = QH // blks
    query_rows, key_rows = w_query.shape[1], w_key.shape[1]
    qkv_rows = query_rows + 2 * key_rows
    in_pair = shards // KVH == heads and blks == 2 * heads

    gains = jnp.zeros((2 * width + 2 * HD,), F32)
    hidden_part = jnp.where(head == 0, hidden_gain.astype(F32), 0.0)
    for at, part in (
        (shard * input_gain.shape[0], input_gain),
        (width + blk * hidden_gain.shape[0], hidden_part),
        (2 * width + shard * query_gain.shape[0], query_gain),
        (2 * width + HD + shard * key_gain.shape[0], key_gain),
    ):
        gains = lax.dynamic_update_slice(gains, part.astype(F32), (at,))
    gains = sum_everywhere(gains.reshape(-1, 128)).reshape(-1)
    input_norm = gains[:width]
    hidden_norm = gains[width : 2 * width]
    query_norm = gains[2 * width : 2 * width + HD]
    key_norm = gains[2 * width + HD :]

    query_pieces = head_gather(w_query.T, False)
    key_value_pieces = head_gather(jnp.concatenate([w_key.T, w_value.T], axis=0), True)
    qkv_weights = jnp.concatenate(
        [part for pieces in zip(query_pieces, key_value_pieces) for part in pieces], axis=0
    )
    full_out = lax.all_gather(w_out, ("head", "blk"), axis=0, tiled=True)
    gate_weights = jnp.concatenate(head_gather(w_gate.T, False), axis=0)
    up_weights = jnp.concatenate(head_gather(w_up.T, True), axis=0)
    half_down = w_down.shape[0] // 2
    down_low = head_gather(w_down[:half_down], False)
    down_high = head_gather(w_down[half_down:], True)
    down_weights = jnp.concatenate(
        [part for pieces in zip(down_low, down_high) for part in pieces], axis=0
    )

    deals = dealing.reshape(blks, heads, rows)
    deals = jnp.concatenate(
        [
            lax.dynamic_index_in_dim(deals, ((chip - step) % chips) * 2 + (core ^ flip), 0)
            for step in range(chips)
            for flip in range(2)
        ],
        axis=0,
    )
    key_places = jnp.concatenate(
        [
            lax.dynamic_index_in_dim(deals, head ^ place, 1, keepdims=False).reshape(-1)
            for place in range(heads)
        ]
    )
    query_places = key_places[:column]
    query_starts = token_starts(query_places, lengths)
    cosine, sine = rope_tables(query_places - query_starts)

    token_blocks = column_gather(inputs)
    normed_blocks = []
    raw_blocks = []
    for block in token_blocks:
        values = block.astype(F32)
        normed = (values * rms_scale(values) * input_norm).astype(BF16)
        normed_blocks.append(normed)
        raw_blocks.append(col_inner(qkv_weights, normed).astype(BF16))
    normed_column = jnp.concatenate(normed_blocks, axis=0)
    raw = jnp.concatenate(raw_blocks, axis=1).reshape(heads, qkv_rows, column)

    def from_member(piece, flip):
        piece = lax.ppermute(piece, "blk", [(i, i ^ flip) for i in range(blks)])
        if flip & 1:
            cuts = [piece[..., i * rows : (i + 1) * rows] for i in range(blks)]
            piece = jnp.concatenate([cuts[i ^ 1] for i in range(blks)], axis=-1)
        if flip & 2:
            later = jnp.concatenate([piece[..., pair:], piece[..., :pair]], axis=-1)
            sooner = jnp.concatenate([piece[..., -pair:], piece[..., :-pair]], axis=-1)
            piece = jnp.where(chip % 2 == 0, later, sooner)
        return piece

    if in_pair:
        member = blk % heads
        mine = pick(raw, head ^ member)
        arrived = jnp.stack(
            [mine]
            + [
                from_member(pick(raw, head ^ member ^ flip), flip)
                for flip in range(1, heads)
            ]
        )
        quarters = jnp.stack([pick(arrived, member ^ place) for place in range(heads)])
        query_raw = quarters[:, :query_rows].reshape(per_device, HD, column)
        key_raw = quarters[:, query_rows : query_rows + key_rows].reshape(HD, column)
        value_raw = quarters[:, query_rows + key_rows :].reshape(HD, column)
        unit_blk = [(unit % 2) * heads + unit // 2 for unit in range(blks)]
    else:
        by_head = jnp.stack([pick(raw, head ^ place) for place in range(heads)])
        every = jnp.swapaxes(lax.all_gather(by_head, "blk", axis=0), 0, 1)
        every = every.reshape(shards, qkv_rows, column)
        query_all = every[:, :query_rows].reshape(QH, HD, column)
        key_all = every[:, query_rows : query_rows + key_rows].reshape(KVH, HD, column)
        value_all = every[:, query_rows + key_rows :].reshape(KVH, HD, column)
        query_raw = lax.dynamic_slice_in_dim(query_all, blk * per_device, per_device, 0)
        key_raw = pick(key_all, blk * KVH // blks)
        value_raw = pick(value_all, blk * KVH // blks)
        unit_blk = list(range(blks))

    query = rope_forward(query_raw, query_norm, cosine, sine).astype(BF16)
    keys = rope_forward(key_raw, key_norm, cosine, sine).astype(BF16)
    query = jnp.swapaxes(query, 1, 2).reshape(per_device * column, HD)
    all_keys = jnp.concatenate(head_gather(keys.T, False), axis=0)
    all_values = jnp.concatenate(head_gather(value_raw.T, True), axis=0)

    heads_out, logs = attend(query, all_keys, all_values, query_places, query_starts, key_places)

    def head_blocks(step, flip):
        block = heads_out.reshape(per_device, blks, rows, HD)[:, 2 * step + flip]
        return jnp.swapaxes(block, 0, 1).reshape(rows, per_device * HD).astype(BF16)

    mixed_parts = jnp.stack(
        [
            head_blocks(step, flip)
            if step + flip == 0
            else chip_shift(head_blocks(step, flip), -step, flip)
            for step in range(chips)
            for flip in range(2)
        ]
    )
    mixed = jnp.concatenate(
        [
            pick(mixed_parts, ((source // 2 - chip) % chips) * 2 + ((source % 2) ^ core))
            for source in unit_blk
        ],
        axis=1,
    )
    token_values = inputs.astype(F32)
    middle = token_values + dot(mixed, full_out)
    scale_two = rms_scale(middle)
    hidden_in = (middle * scale_two * hidden_norm).astype(BF16)

    own_cotangent = lax.dynamic_slice_in_dim(cotangent, head * rows, rows, 0)
    cotangent_blocks = column_gather(own_cotangent)
    act_grads = [col_inner(block, down_weights) for block in cotangent_blocks]
    hidden_blocks = column_gather(hidden_in)
    activated_blocks, gate_grads, up_grads = [], [], []
    for block, act_grad in zip(hidden_blocks, act_grads):
        gate = col_inner(block, gate_weights)
        up_proj = col_inner(block, up_weights)
        sigmoid_gate = jax.nn.sigmoid(gate)
        silu_gate = gate * sigmoid_gate
        activated_blocks.append((silu_gate * up_proj).astype(BF16))
        gate_grads.append(
            (act_grad * up_proj * sigmoid_gate * (1.0 + gate * (1.0 - sigmoid_gate))).astype(BF16)
        )
        up_grads.append((act_grad * silu_gate).astype(BF16))
    hidden_grad = column_scatter(
        lambda step: dot(gate_grads[step], gate_weights) + dot(up_grads[step], up_weights)
    )
    feed_out = column_scatter(lambda step: dot(activated_blocks[step], down_weights))
    layer_out = (middle + feed_out).astype(BF16)

    hidden_gain_grad = jnp.sum(hidden_grad * middle * scale_two, axis=0)
    middle_grad = own_cotangent.astype(F32) + norm_back(hidden_grad, middle, scale_two, hidden_norm)
    branch_grad = middle_grad.astype(BF16)
    grad_out = lax.psum_scatter(
        row_outer(mixed, branch_grad).astype(BF16), ("head", "blk"), scatter_dimension=0, tiled=True
    ).astype(F32)
    mixed_grad = col_inner(branch_grad, full_out).astype(BF16)
    mixed_grad = jnp.swapaxes(mixed_grad.reshape(rows, blks, per_device * HD), 0, 1)
    blk_unit = [unit_blk.index(place) for place in range(blks)]
    unit_of = jnp.asarray(blk_unit, jnp.int32)

    def tokens_to_heads(step, flip):
        target = ((chip + step) % chips) * 2 + (core ^ flip)
        part = pick(mixed_grad, pick(unit_of, target))
        return part if step + flip == 0 else chip_shift(part, step, flip)

    upstream = jnp.concatenate(
        [tokens_to_heads(step, flip) for step in range(chips) for flip in range(2)], axis=0
    )
    upstream = jnp.swapaxes(upstream.reshape(column, per_device, HD), 0, 1)
    query_grad, key_grads, value_grads = attend_back(
        query,
        upstream.reshape(per_device * column, HD),
        heads_out,
        logs,
        query_places,
        query_starts,
        all_keys,
        all_values,
        key_places,
    )

    hidden_column = jnp.concatenate(hidden_blocks, axis=0)
    cotangent_column = jnp.concatenate(cotangent_blocks, axis=0)
    grad_gate = row_outer(jnp.concatenate(gate_grads, axis=0), hidden_column)
    grad_up = row_outer(jnp.concatenate(up_grads, axis=0), hidden_column)
    grad_down = row_outer(jnp.concatenate(activated_blocks, axis=0), cotangent_column)
    grad_gate = head_scatter(grad_gate.reshape((heads, -1, width)), False).T
    grad_up = head_scatter(grad_up.reshape((heads, -1, width)), True).T
    grad_down = grad_down.reshape((heads, 2, half_down, width))
    grad_down = jnp.concatenate(
        [head_scatter(grad_down[:, 0], False), head_scatter(grad_down[:, 1], True)], axis=0
    )

    key_grad = head_scatter(key_grads.reshape(heads, column, HD), False).T
    value_grad = head_scatter(value_grads.reshape(heads, column, HD), True).T
    query_grad = jnp.swapaxes(query_grad.reshape(per_device, column, HD), 1, 2)
    query_raw_grad, query_gain_grad = rope_backward(
        query_raw, query_norm, cosine, sine, query_grad
    )
    key_raw_grad, key_gain_grad = rope_backward(key_raw, key_norm, cosine, sine, key_grad)
    query_raw_grad = query_raw_grad.astype(BF16)
    key_raw_grad = key_raw_grad.astype(BF16)
    value_raw_grad = value_grad.astype(BF16)
    if in_pair:
        quarters = jnp.concatenate(
            [
                query_raw_grad.reshape(heads, query_rows, column),
                key_raw_grad.reshape(heads, key_rows, column),
                value_raw_grad.reshape(heads, key_rows, column),
            ],
            axis=1,
        )
        arrived = jnp.stack(
            [pick(quarters, member)]
            + [from_member(pick(quarters, member ^ flip), flip) for flip in range(1, heads)]
        )
        raw_grad = jnp.concatenate(
            [pick(arrived, head ^ member ^ place) for place in range(heads)], axis=0
        )
    else:
        def spread(part, count, index):
            empty = jnp.zeros((count,) + part.shape[1:], BF16)
            return lax.dynamic_update_slice_in_dim(empty, part, index, 0)

        every = jnp.concatenate(
            [
                spread(query_raw_grad, QH, blk * per_device).reshape(shards, query_rows, column),
                spread(key_raw_grad[None], KVH, blk * KVH // blks).reshape(
                    shards, key_rows, column
                ),
                spread(value_raw_grad[None], KVH, blk * KVH // blks).reshape(
                    shards, key_rows, column
                ),
            ],
            axis=1,
        ).reshape(heads, blks, qkv_rows, column)
        by_head = lax.psum_scatter(
            jnp.swapaxes(every, 0, 1), "blk", scatter_dimension=0, tiled=False
        )
        raw_grad = jnp.concatenate(
            [pick(by_head, head ^ place) for place in range(heads)], axis=0
        )

    qkv_grad = dot(raw_grad, normed_column)
    input_gain_grad = jnp.sum(qkv_grad * qkv_weights.astype(F32), axis=0) / input_norm
    normed_grad = column_scatter(
        lambda step: row_outer(raw_grad[:, step * pair : (step + 1) * pair], qkv_weights)
    )
    grad_input = middle_grad + norm_back(
        normed_grad, token_values, rms_scale(token_values), input_norm
    )
    qkv_grad = qkv_grad.reshape(heads, qkv_rows, width)
    grad_query = head_scatter(qkv_grad[:, :query_rows], False)
    grad_key_value = head_scatter(qkv_grad[:, query_rows:], True)

    sums = jnp.concatenate(
        [
            input_gain_grad,
            hidden_gain_grad,
            jnp.sum(query_gain_grad, axis=0),
            key_gain_grad,
        ]
    )
    sums = sum_everywhere(sums.reshape(-1, 128)).reshape(-1)

    def own_part(at, size):
        return lax.dynamic_slice_in_dim(sums, at, size)

    return (
        layer_out,
        grad_input,
        own_part(shard * input_gain.shape[0], input_gain.shape[0]),
        grad_query.T,
        grad_key_value[:key_rows].T,
        grad_key_value[key_rows:].T,
        own_part(2 * width + shard * query_gain.shape[0], query_gain.shape[0]),
        own_part(2 * width + HD + shard * key_gain.shape[0], key_gain.shape[0]),
        grad_out,
        own_part(width + blk * hidden_gain.shape[0], hidden_gain.shape[0]),
        grad_gate,
        grad_up,
        grad_down,
    )


def solution(mesh):
    return jax.shard_map(
        local,
        mesh=mesh,
        in_specs=(
            P(("blk", "head"), None),
            P(),
            P(),
            P(("head", "blk")),
            P(None, ("head", "blk")),
            P(None, ("head", "blk")),
            P(None, ("head", "blk")),
            P(("head", "blk")),
            P(("head", "blk")),
            P(("head", "blk"), None),
            P("blk"),
            P(None, ("head", "blk")),
            P(None, ("head", "blk")),
            P(("head", "blk"), None),
            P("blk", None),
        ),
        out_specs=(
            P(("blk", "head"), None),
            P(("blk", "head"), None),
            P(("head", "blk")),
            P(None, ("head", "blk")),
            P(None, ("head", "blk")),
            P(None, ("head", "blk")),
            P(("head", "blk")),
            P(("head", "blk")),
            P(("head", "blk"), None),
            P("blk"),
            P(None, ("head", "blk")),
            P(None, ("head", "blk")),
            P(("head", "blk"), None),
        ),
        check_vma=False,
    )
```

time: 2090 us -> 739 us (0.35)
  waiting for transfers between devices: 1390 us -> 357 us
  matrix products: 290 us -> 73.9 us
  blocking collectives: 131 us -> 0 us
  starting transfers between devices: 15.6 us -> 81.9 us
  local copies, waits for them, and re-layouts: 116 us -> 71.6 us
  Pallas kernels: 0 us -> 43.1 us
  other arithmetic: 99.4 us -> 70.5 us
    reduce_scatter x8 -> x1, waiting for transfers between devices: 739 us -> 0.01 us  [local(): lax.psum_scatter(row_outer(mixed, branch_grad).astype(BF16), ('head', 'bl...]
    all_gather x7 -> x1, waiting for transfers between devices: 314 us -> 0.02 us  [local(): full_out = lax.all_gather(w_out, ('head', 'blk'), axis=0, tiled=True)]
    ppermute x30 -> x120, waiting for transfers between devices: 139 us -> 357 us  [the longest x32 174 us: chip_shift(): lax.ppermute(value, 'blk', [(i, (i + 2 * steps) % count ^ flip) for i in...]
    dot_general x93 -> x39, matrix products: 290 us -> 73.9 us  [the longest x17 30.2 us: col_inner(): lax.dot_general(left, right, CONTRACT_COLS, preferred_element_type=F32)]
    psum x2 -> x0, waiting for transfers between devices: 187 us -> none  [the longest x1 94.7 us: local(): hidden_grad = lax.psum(hidden_part, 'head')]
    unnamed x3 -> x0, blocking collectives: 94.7 us -> none
    ppermute x30 -> x120, starting transfers between devices: 4.63 us -> 81.8 us  [the longest x52 50 us: head_flip(): return lax.ppermute(value, 'head', [(i, i ^ bit) for i in range(count)])]
    dynamic_slice x71 -> x8, local copies, waits for them, and re-layouts: 61.6 us -> 2.74 us  [the longest x3 1.81 us: own_part(): return lax.dynamic_slice_in_dim(sums, at, size)]
  transfers between devices with their start and end apart: 50 -> 122, of which waited for: 45 -> 57; matrix products, arithmetic and copies ran while one was open for 22% -> 27% of each run, Pallas kernels for 0% -> 6%
where the time goes in v1:
time: 739 us; the launch traced here: 731 us
  waiting for transfers between devices  357 us (48%)
  starting transfers between devices  81.9 us (11%)
  matrix products  73.9 us (10%)
  local copies, waits for them, and re-layouts  71.6 us (10%)
  other arithmetic  70.5 us (10%)
  Pallas kernels  43.1 us (6%)
  between operations  33.2 us (4%)
    ppermute x32, waiting for transfers between devices, chip_shift(): lax.ppermute(value, 'blk', [(i, (i + 2 * steps) % count ^ flip) for i in...  174 us
    ppermute x52, waiting for transfers between devices, head_flip(): return lax.ppermute(value, 'head', [(i, i ^ bit) for i in range(count)])  161 us
    ppermute x52, starting transfers between devices, head_flip(): return lax.ppermute(value, 'head', [(i, i ^ bit) for i in range(count)])  50 us
    unnamed x294, local copies, waits for them, and re-layouts  37.6 us
    dot_general x17, matrix products, col_inner(): lax.dot_general(left, right, CONTRACT_COLS, preferred_element_type=F32)  30.2 us
    pallas_call x1, Pallas kernels, attend_back(): pl.pallas_call(functools.partial(attend_back_kernel, 512, own), grid=(tok...  29.3 us
    dot_general x8, matrix products, row_outer(): lax.dot_general(left, right, CONTRACT_ROWS, preferred_element_type=F32)  22.8 us
    dot_general x14, matrix products, dot(): return jnp.dot(left, right, preferred_element_type=F32)  20.9 us
  transfers between devices with their start and end apart: 122, of which 57 were waited for; matrix products, arithmetic and copies ran while one was open for 27% of the time, Pallas kernels for 6%

profile of v1, /device:TPU:0, one launch (start us, length us, event | category | flops | bytes accessed | tf_op | source)
XLA Modules:
  0.0 731.0 jit_solution(12601071778323298263)
XLA Ops:
  26.1 3.5 collective-permute-done.8
  68.4 15.1 %collective-permute-done.41 = bf16[96,2048]{1,0:T(8,128)(2,1)S(1)} collective-permute-done((bf16[96,2048]{1,0:T(8,128)(2,1)}, bf16[96,2048]{1,0:T(8,128)(2,1)S(1)}, u32[]{:S(2)}, u32[]{:S(2)}) %collective-permute-start.41) | collective-permute-done | bytes 393248 | tf_op jit(solution)/shard_map/ppermute | solution.py:92
  85.6 10.3 %collective-permute-done.42 = bf16[96,2048]{1,0:T(8,128)(2,1)S(1)} collective-permute-done((bf16[96,2048]{1,0:T(8,128)(2,1)}, bf16[96,2048]{1,0:T(8,128)(2,1)S(1)}, u32[]{:S(2)}, u32[]{:S(2)}) %collective-permute-start.42) | collective-permute-done | bytes 393248 | tf_op jit(solution)/shard_map/ppermute | solution.py:92
  102.4 5.4 collective-permute-done.4
  111.3 6.9 collective-permute-done.62
  120.5 13.7 %collective-permute-done.5 = bf16[64,2048]{1,0:T(8,128)(2,1)S(1)} collective-permute-done((bf16[64,2048]{1,0:T(8,128)(2,1)S(1)}, bf16[64,2048]{1,0:T(8,128)(2,1)S(1)}, u32[]{:S(2)}, u32[]{:S(2)}) %collective-permute-start.5) | collective-permute-done | bytes 262176 | tf_op jit(solution)/shard_map/ppermute | solution.py:92
  135.1 5.9 collective-permute-done.46
  143.1 3.7 collective-permute-done.14
  149.1 14.3 %collective-permute-done.63 = bf16[128,2048]{1,0:T(8,128)(2,1)S(1)} collective-permute-done((bf16[128,2048]{1,0:T(8,128)(2,1)S(1)}, bf16[128,2048]{1,0:T(8,128)(2,1)S(1)}, u32[]{:S(2)}, u32[]{:S(2)}) %collective-permute-start.63) | collective-permute-done | bytes 524320 | tf_op jit(solution)/shard_map/ppermute | solution.py:56
  165.1 5.3 collective-permute-done.16
  175.1 6.8 collective-permute-done.64
  195.1 12.9 %collective-permute-done.40 = bf16[192,2048]{1,0:T(8,128)(2,1)} collective-permute-done((bf16[192,2048]{1,0:T(8,128)(2,1)}, bf16[192,2048]{1,0:T(8,128)(2,1)}, u32[]{:S(2)}, u32[]{:S(2)}) %collective-permute-start.40) | collective-permute-done | bytes 786464 | tf_op jit(solution)/shard_map/ppermute | solution.py:92
  211.5 8.4 %collective-permute-done.19 = bf16[128,1024]{1,0:T(8,128)(2,1)S(1)} collective-permute-done((bf16[128,1024]{1,0:T(8,128)(2,1)S(1)}, bf16[128,1024]{1,0:T(8,128)(2,1)S(1)}, u32[]{:S(2)}, u32[]{:S(2)}) %collective-permute-start.19) | collective-permute-done | bytes 262176 | tf_op jit(solution)/shard_map/ppermute | solution.py:386
  239.9 3.6 collective-permute-done.26
  246.7 4.9 collective-permute-done.23
  252.7 13.8 %shard_map.255 = (f32[2048,128]{1,0:T(8,128)S(1)}, f32[8,2048]{1,0:T(8,128)S(1)}) custom-call(bf16[2048,128]{1,0:T(8,128)(2,1)S(1)} %bitcast.373, bf16[4096,128]{1,0:T(8,128)(2,1)S(1)} %pad_maximum_fusion.10.k_ref, bf16[4096,128]{1,0:T(8,128)(2,1)S(1)} %pad_maximum_fusion.11.v_ref, s32[1024,1]{1,0:T(8,128)S(1)} %copy.130.qpos_ref, ...), custom_call_target="tpu_custom_call" | custom-call | flops 4294967296 | bytes 2097152 | tf_op jit(solution)/shard_map/pallas_call | solution.py:195
  267.1 3.9 collective-permute-start.28
  276.2 3.3 collective-permute-done.30
  282.2 4.7 collective-permute-done.32
  287.5 4.9 multiply_reduce_fusion.3
  301.8 3.5 fusion.120
  311.7 5.2 collective-permute-done.48
  324.7 10.4 %collective-permute-done.49 = bf16[128,2048]{1,0:T(8,128)(2,1)S(1)} collective-permute-done((bf16[128,2048]{1,0:T(8,128)(2,1)S(1)}, bf16[128,2048]{1,0:T(8,128)(2,1)S(1)}, u32[]{:S(2)}, u32[]{:S(2)}) %collective-permute-start.49) | collective-permute-done | bytes 524320 | tf_op jit(solution)/shard_map/ppermute | solution.py:56
  346.2 7.3 collective-permute-done.50
  364.0 3.5 fusion.42
  367.5 5.1 fusion.178
  372.6 5.6 fusion.177
  395.6 8.8 %collective-permute-done.58 = bf16[128,2048]{1,0:T(8,128)(2,1)S(1)} collective-permute-done((bf16[128,2048]{1,0:T(8,128)(2,1)S(1)}, bf16[128,2048]{1,0:T(8,128)(2,1)S(1)}, u32[]{:S(2)}, u32[]{:S(2)}) %collective-permute-start.58) | collective-permute-done | bytes 524320 | tf_op jit(solution)/shard_map/ppermute | solution.py:56
  405.0 9.6 %collective-permute-done.72 = bf16[128,2048]{1,0:T(8,128)(2,1)S(1)} collective-permute-done((bf16[128,2048]{1,0:T(8,128)(2,1)S(1)}, bf16[128,2048]{1,0:T(8,128)(2,1)S(1)}, u32[]{:S(2)}, u32[]{:S(2)}) %collective-permute-start.72) | collective-permute-done | bytes 524320 | tf_op jit(solution)/shard_map/ppermute | solution.py:56
  416.8 7.5 %collective-permute-done.112 = bf16[192,2048]{1,0:T(8,128)(2,1)S(1)} collective-permute-done((bf16[192,2048]{1,0:T(8,128)(2,1)S(1)}, bf16[192,2048]{1,0:T(8,128)(2,1)S(1)}, u32[]{:S(2)}, u32[]{:S(2)}) %collective-permute-start.112) | collective-permute-done | bytes 786464 | tf_op jit(solution)/shard_map/ppermute | solution.py:92
  425.8 15.8 %collective-permute-done.109 = bf16[192,2048]{1,0:T(8,128)(2,1)S(1)} collective-permute-done((bf16[192,2048]{1,0:T(8,128)(2,1)S(1)}, bf16[192,2048]{1,0:T(8,128)(2,1)S(1)}, u32[]{:S(2)}, u32[]{:S(2)}) %collective-permute-start.109) | collective-permute-done | bytes 786464 | tf_op jit(solution)/shard_map/ppermute | solution.py:92
  444.7 8.9 %collective-permute-done.116 = bf16[96,2048]{1,0:T(8,128)(2,1)S(1)} collective-permute-done((bf16[96,2048]{1,0:T(8,128)(2,1)S(1)}, bf16[96,2048]{1,0:T(8,128)(2,1)S(1)}, u32[]{:S(2)}, u32[]{:S(2)}) %collective-permute-start.116) | collective-permute-done | bytes 393248 | tf_op jit(solution)/shard_map/ppermute | solution.py:92
  455.5 13.8 %collective-permute-done.73 = bf16[128,2048]{1,0:T(8,128)(2,1)S(1)} collective-permute-done((bf16[128,2048]{1,0:T(8,128)(2,1)S(1)}, bf16[128,2048]{1,0:T(8,128)(2,1)S(1)}, u32[]{:S(2)}, u32[]{:S(2)}) %collective-permute-start.73) | collective-permute-done | bytes 524320 | tf_op jit(solution)/shard_map/ppermute | solution.py:56
  474.6 5.6 convolution_convert_fusion
  480.2 6.3 convolution_convert_fusion.1
  489.5 6.7 collective-permute-done.75
  496.4 7.0 collective-permute-done.76
  503.5 6.9 collective-permute-done.77
  510.6 7.7 %collective-permute-done.78 = bf16[128,256]{1,0:T(8,128)(2,1)S(1)} collective-permute-done((bf16[128,256]{1,0:T(8,128)(2,1)S(1)}, bf16[128,256]{1,0:T(8,128)(2,1)S(1)}, u32[]{:S(2)}, u32[]{:S(2)}) %collective-permute-start.78) | collective-permute-done | bytes 65568 | tf_op jit(solution)/shard_map/ppermute | solution.py:56
  519.7 4.3 collective-permute-done.79
  526.1 3.4 collective-permute-done.80
  538.1 29.3 %shard_map.256 = (f32[2048,128]{1,0:T(8,128)S(1)}, f32[4096,128]{1,0:T(8,128)S(1)}, f32[4096,128]{1,0:T(8,128)S(1)}) custom-call(bf16[2048,128]{1,0:T(8,128)(2,1)S(1)} %bitcast.374, bf16[2048,128]{1,0:T(8,128)(2,1)S(1)} %bitcast.375, f32[2048,128]{1,0:T(8,128)S(1)} %get-tuple-element.18.o_ref, f32[8,2048]{1,0:T(8,128)S(1)} %get-tuple-element.19.log_ref, ...), custom_call_target="tpu_custom_call" | custom-call | flops 10737418240 | bytes 4194304 | tf_op jit(solution)/shard_map/pallas_call | solution.py:264
  585.6 6.3 collective-permute-done.82
  603.5 30.0 %collective-permute-done.83 = bf16[1024,128]{1,0:T(8,128)(2,1)S(1)} collective-permute-done((bf16[1024,128]{1,0:T(8,128)(2,1)S(1)}, bf16[1024,128]{1,0:T(8,128)(2,1)S(1)}, u32[]{:S(2)}, u32[]{:S(2)}) %collective-permute-start.83) | collective-permute-done | bytes 262176 | tf_op jit(solution)/shard_map/ppermute | solution.py:92
  647.4 5.3 collective-permute-done.88
  680.2 12.6 %collective-permute-done.94 = bf16[128,2048]{1,0:T(8,128)(2,1)S(1)} collective-permute-done((bf16[128,2048]{1,0:T(8,128)(2,1)S(1)}, bf16[128,2048]{1,0:T(8,128)(2,1)S(1)}, u32[]{:S(2)}, u32[]{:S(2)}) %collective-permute-start.94) | collective-permute-done | bytes 524320 | tf_op jit(solution)/shard_map/ppermute | solution.py:56
  696.5 10.4 %collective-permute-done.95 = bf16[128,2048]{1,0:T(8,128)(2,1)S(1)} collective-permute-done((bf16[128,2048]{1,0:T(8,128)(2,1)S(1)}, bf16[128,2048]{1,0:T(8,128)(2,1)S(1)}, u32[]{:S(2)}, u32[]{:S(2)}) %collective-permute-start.95) | collective-permute-done | bytes 524320 | tf_op jit(solution)/shard_map/ppermute | solution.py:56
  708.9 11.2 %collective-permute-done.96 = bf16[128,2048]{1,0:T(8,128)(2,1)S(1)} collective-permute-done((bf16[128,2048]{1,0:T(8,128)(2,1)S(1)}, bf16[128,2048]{1,0:T(8,128)(2,1)S(1)}, u32[]{:S(2)}, u32[]{:S(2)}) %collective-permute-start.96) | collective-permute-done | bytes 524320 | tf_op jit(solution)/shard_map/ppermute | solution.py:56
  (731 shorter events, 288.7 us)
Async XLA Ops:
  7.2 280.3 %all-gather.2.cloned.1.call-start = ((), (), s32[]{:S(2)}) async-start(), calls=%async_computation.1 | async-start | bytes 8650752 | tf_op jit(solution)/shard_map/all_gather | solution.py:345
  7.2 112.7 %collective-permute-start.12 = (bf16[128,2048]{1,0:T(8,128)(2,1)}, bf16[128,2048]{1,0:T(8,128)(2,1)S(1)}, u32[]{:S(2)}, u32[]{:S(2)}) collective-permute-start(bf16[128,2048]{1,0:T(8,128)(2,1)} %param.16), channel_id=1, source_target_pairs={{0,2},{1,3},{2,4},{3,5},{4,6},{5,7},{6,0},{7,1},{8,10},{9,11},{10,... | collective-permute-start | bytes 1572872 | tf_op jit(solution)/shard_map/ppermute | solution.py:56
  10.3 99.1 %collective-permute-start.6 = (bf16[128,2048]{1,0:T(8,128)(2,1)}, bf16[128,2048]{1,0:T(8,128)(2,1)}, u32[]{:S(2)}, u32[]{:S(2)}) collective-permute-start(bf16[128,2048]{1,0:T(8,128)(2,1)} %param.16), channel_id=1, source_target_pairs={{0,1},{1,0},{2,3},{3,2},{4,5},{5,4},{6,7},{7,6},{8,9},{9,8},{10,11... | collective-permute-start | bytes 1572872 | tf_op jit(solution)/shard_map/ppermute | solution.py:51
  10.3 48.9 %collective-permute-start = (bf16[64,2048]{1,0:T(8,128)(2,1)}, bf16[64,2048]{1,0:T(8,128)(2,1)S(1)}, u32[]{:S(2)}, u32[]{:S(2)}) collective-permute-start(bf16[64,2048]{1,0:T(8,128)(2,1)} %bitcast.415), channel_id=1, source_target_pairs={{0,8},{8,0},{16,24},{24,16},{1,9},{9,1},{17,25},{25,17},{2,10},{10... | collective-permute-start | bytes 786440 | tf_op jit(solution)/shard_map/ppermute | solution.py:92
  11.8 53.8 %collective-permute-start.2 = (bf16[64,2048]{1,0:T(8,128)(2,1)}, bf16[64,2048]{1,0:T(8,128)(2,1)S(1)}, u32[]{:S(2)}, u32[]{:S(2)}) collective-permute-start(bf16[64,2048]{1,0:T(8,128)(2,1)} %bitcast.416), channel_id=1, source_target_pairs={{0,16},{8,24},{16,0},{24,8},{1,17},{9,25},{17,1},{25,9},{2,18},{10... | collective-permute-start | bytes 786440 | tf_op jit(solution)/shard_map/ppermute | solution.py:92
  16.9 705.0 %reduce-scatter.2.cloned.1.call-start = ((), (), s32[]{:S(2)}) async-start(), calls=%async_computation.2 | async-start | bytes 8650752 | tf_op jit(solution)/shard_map/reduce_scatter | solution.py:480
  34.7 21.6 %collective-permute-start.11 = (f32[34,128]{1,0:T(8,128)S(1)}, f32[34,128]{1,0:T(8,128)S(1)}, u32[]{:S(2)}, u32[]{:S(2)}) collective-permute-start(f32[34,128]{1,0:T(8,128)S(1)} %add.641), channel_id=1, source_target_pairs={{0,4},{1,5},{2,6},{3,7},{4,0},{5,1},{6,2},{7,3},{8,12},{9,13},{10,... | collective-permute-start | bytes 52232 | tf_op jit(solution)/shard_map/ppermute | solution.py:121
  63.4 20.0 %collective-permute-start.41 = (bf16[96,2048]{1,0:T(8,128)(2,1)}, bf16[96,2048]{1,0:T(8,128)(2,1)S(1)}, u32[]{:S(2)}, u32[]{:S(2)}) collective-permute-start(bf16[96,2048]{1,0:T(8,128)(2,1)} %get-tuple-element.94), channel_id=1, source_target_pairs={{0,8},{8,0},{16,24},{24,16},{1,9},{9,1},{17,25},{25,17},{2,10},{10... | collective-permute-start | bytes 1179656 | tf_op jit(solution)/shard_map/ppermute | solution.py:92
  65.6 31.1 %collective-permute-start.43 = (bf16[96,2048]{1,0:T(8,128)(2,1)}, bf16[96,2048]{1,0:T(8,128)(2,1)S(1)}, u32[]{:S(2)}, u32[]{:S(2)}) collective-permute-start(bf16[96,2048]{1,0:T(8,128)(2,1)} %get-tuple-element.94), channel_id=1, source_target_pairs={{0,16},{8,24},{16,0},{24,8},{1,17},{9,25},{17,1},{25,9},{2,18},{10... | collective-permute-start | bytes 1179656 | tf_op jit(solution)/shard_map/ppermute | solution.py:92
  66.5 29.4 %collective-permute-start.42 = (bf16[96,2048]{1,0:T(8,128)(2,1)}, bf16[96,2048]{1,0:T(8,128)(2,1)S(1)}, u32[]{:S(2)}, u32[]{:S(2)}) collective-permute-start(bf16[96,2048]{1,0:T(8,128)(2,1)} %get-tuple-element.93), channel_id=1, source_target_pairs={{0,8},{8,0},{16,24},{24,16},{1,9},{9,1},{17,25},{25,17},{2,10},{10... | collective-permute-start | bytes 1179656 | tf_op jit(solution)/shard_map/ppermute | solution.py:92
  96.7 21.5 %collective-permute-start.62 = (bf16[128,2048]{1,0:T(8,128)(2,1)S(1)}, bf16[128,2048]{1,0:T(8,128)(2,1)S(1)}, u32[]{:S(2)}, u32[]{:S(2)}) collective-permute-start(bf16[128,2048]{1,0:T(8,128)(2,1)S(1)} %get-tuple-element.34), channel_id=1, source_target_pairs={{0,2},{1,3},{2,4},{3,5},{4,6},{5,7},{6,0},{7,1},{8,10},{9,11},{10,... | collective-permute-start | bytes 1572872 | tf_op jit(solution)/shard_map/ppermute | solution.py:56
  101.6 71.6 %collective-permute-start.39 = (bf16[192,2048]{1,0:T(8,128)(2,1)}, bf16[192,2048]{1,0:T(8,128)(2,1)}, u32[]{:S(2)}, u32[]{:S(2)}) collective-permute-start(bf16[192,2048]{1,0:T(8,128)(2,1)} %bitcast.78), channel_id=1, source_target_pairs={{0,16},{8,24},{16,0},{24,8},{1,17},{9,25},{17,1},{25,9},{2,18},{10... | collective-permute-start | bytes 2359304 | tf_op jit(solution)/shard_map/ppermute | solution.py:92
  107.9 66.8 %collective-permute-start.35 = (bf16[192,2048]{1,0:T(8,128)(2,1)}, bf16[192,2048]{1,0:T(8,128)(2,1)}, u32[]{:S(2)}, u32[]{:S(2)}) collective-permute-start(bf16[192,2048]{1,0:T(8,128)(2,1)} %bitcast.77), channel_id=1, source_target_pairs={{0,8},{8,0},{16,24},{24,16},{1,9},{9,1},{17,25},{25,17},{2,10},{10... | collective-permute-start | bytes 2359304 | tf_op jit(solution)/shard_map/ppermute | solution.py:92
  109.4 24.8 %collective-permute-start.5 = (bf16[64,2048]{1,0:T(8,128)(2,1)S(1)}, bf16[64,2048]{1,0:T(8,128)(2,1)S(1)}, u32[]{:S(2)}, u32[]{:S(2)}) collective-permute-start(bf16[64,2048]{1,0:T(8,128)(2,1)S(1)} %collective-permute-done.3), channel_id=1, source_target_pairs={{0,8},{8,0},{16,24},{24,16},{1,9},{9,1},{17,25},{25,17},{2,10},{10... | collective-permute-start | bytes 786440 | tf_op jit(solution)/shard_map/ppermute | solution.py:92
  120.0 21.0 %collective-permute-start.46 = (bf16[96,2048]{1,0:T(8,128)(2,1)S(1)}, bf16[96,2048]{1,0:T(8,128)(2,1)S(1)}, u32[]{:S(2)}, u32[]{:S(2)}) collective-permute-start(bf16[96,2048]{1,0:T(8,128)(2,1)S(1)} %collective-permute-done.44), channel_id=1, source_target_pairs={{0,8},{8,0},{16,24},{24,16},{1,9},{9,1},{17,25},{25,17},{2,10},{10... | collective-permute-start | bytes 1179656 | tf_op jit(solution)/shard_map/ppermute | solution.py:92
  146.7 23.7 %collective-permute-start.16 = (bf16[128,2048]{1,0:T(8,128)(2,1)S(1)}, bf16[128,2048]{1,0:T(8,128)(2,1)S(1)}, u32[]{:S(2)}, u32[]{:S(2)}) collective-permute-start(bf16[128,2048]{1,0:T(8,128)(2,1)S(1)} %collective-permute-done.14), channel_id=1, source_target_pairs={{0,2},{1,3},{2,4},{3,5},{4,6},{5,7},{6,0},{7,1},{8,10},{9,11},{10,... | collective-permute-start | bytes 1572872 | tf_op jit(solution)/shard_map/ppermute | solution.py:56
  147.0 23.4 %collective-permute-start.15 = (bf16[128,2048]{1,0:T(8,128)(2,1)S(1)}, bf16[128,2048]{1,0:T(8,128)(2,1)S(1)}, u32[]{:S(2)}, u32[]{:S(2)}) collective-permute-start(bf16[128,2048]{1,0:T(8,128)(2,1)S(1)} %collective-permute-done.14), channel_id=1, source_target_pairs={{0,1},{1,0},{2,3},{3,2},{4,5},{5,4},{6,7},{7,6},{8,9},{9,8},{10,11... | collective-permute-start | bytes 1572872 | tf_op jit(solution)/shard_map/ppermute | solution.py:51
  170.8 24.3 %collective-permute-start.38 = (bf16[192,2048]{1,0:T(8,128)(2,1)}, bf16[192,2048]{1,0:T(8,128)(2,1)}, u32[]{:S(2)}, u32[]{:S(2)}) collective-permute-start(bf16[192,2048]{1,0:T(8,128)(2,1)} %bitcast.78), channel_id=1, source_target_pairs={{0,8},{8,0},{16,24},{24,16},{1,9},{9,1},{17,25},{25,17},{2,10},{10... | collective-permute-start | bytes 2359304 | tf_op jit(solution)/shard_map/ppermute | solution.py:92
  173.2 122.6 %collective-permute-start.36 = (bf16[192,2048]{1,0:T(8,128)(2,1)}, bf16[192,2048]{1,0:T(8,128)(2,1)}, u32[]{:S(2)}, u32[]{:S(2)}) collective-permute-start(bf16[192,2048]{1,0:T(8,128)(2,1)} %bitcast.77), channel_id=1, source_target_pairs={{0,16},{8,24},{16,0},{24,8},{1,17},{9,25},{17,1},{25,9},{2,18},{10... | collective-permute-start | bytes 2359304 | tf_op jit(solution)/shard_map/ppermute | solution.py:92
  174.6 33.3 %collective-permute-start.40 = (bf16[192,2048]{1,0:T(8,128)(2,1)}, bf16[192,2048]{1,0:T(8,128)(2,1)}, u32[]{:S(2)}, u32[]{:S(2)}) collective-permute-start(bf16[192,2048]{1,0:T(8,128)(2,1)} %collective-permute-done.39), channel_id=1, source_target_pairs={{0,8},{8,0},{16,24},{24,16},{1,9},{9,1},{17,25},{25,17},{2,10},{10... | collective-permute-start | bytes 2359304 | tf_op jit(solution)/shard_map/ppermute | solution.py:92
  182.0 113.8 %collective-permute-start.37 = (bf16[192,2048]{1,0:T(8,128)(2,1)}, bf16[192,2048]{1,0:T(8,128)(2,1)}, u32[]{:S(2)}, u32[]{:S(2)}) collective-permute-start(bf16[192,2048]{1,0:T(8,128)(2,1)} %collective-permute-done.35), channel_id=1, source_target_pairs={{0,16},{8,24},{16,0},{24,8},{1,17},{9,25},{17,1},{25,9},{2,18},{10... | collective-permute-start | bytes 2359304 | tf_op jit(solution)/shard_map/ppermute | solution.py:92
  236.7 62.2 %collective-permute-start.65 = (bf16[128,2048]{1,0:T(8,128)(2,1)}, bf16[128,2048]{1,0:T(8,128)(2,1)}, u32[]{:S(2)}, u32[]{:S(2)}) collective-permute-start(bf16[128,2048]{1,0:T(8,128)(2,1)} %copy-done.66), channel_id=1, source_target_pairs={{0,1},{1,0},{2,3},{3,2},{4,5},{5,4},{6,7},{7,6},{8,9},{9,8},{10,11... | collective-permute-start | bytes 1572872 | tf_op jit(solution)/shard_map/ppermute | solution.py:51
  310.1 161.0 %collective-permute-start.47 = (bf16[128,2048]{1,0:T(8,128)(2,1)}, bf16[128,2048]{1,0:T(8,128)(2,1)}, u32[]{:S(2)}, u32[]{:S(2)}) collective-permute-start(bf16[128,2048]{1,0:T(8,128)(2,1)} %slice.742), channel_id=1, source_target_pairs={{0,1},{1,0},{2,3},{3,2},{4,5},{5,4},{6,7},{7,6},{8,9},{9,8},{10,11... | collective-permute-start | bytes 1572872 | tf_op jit(solution)/shard_map/ppermute | solution.py:51
  340.1 44.1 %collective-permute-start.57 = (bf16[128,2048]{1,0:T(8,128)(2,1)}, bf16[128,2048]{1,0:T(8,128)(2,1)}, u32[]{:S(2)}, u32[]{:S(2)}) collective-permute-start(bf16[128,2048]{1,0:T(8,128)(2,1)} %fusion.68), channel_id=1, source_target_pairs={{0,2},{1,3},{2,4},{3,5},{4,6},{5,7},{6,0},{7,1},{8,10},{9,11},{10,... | collective-permute-start | bytes 1572872 | tf_op jit(solution)/shard_map/ppermute | solution.py:56
  343.9 40.9 %collective-permute-start.54 = (bf16[128,2048]{1,0:T(8,128)(2,1)}, bf16[128,2048]{1,0:T(8,128)(2,1)}, u32[]{:S(2)}, u32[]{:S(2)}) collective-permute-start(bf16[128,2048]{1,0:T(8,128)(2,1)} %slice.740), channel_id=1, source_target_pairs={{0,1},{1,0},{2,3},{3,2},{4,5},{5,4},{6,7},{7,6},{8,9},{9,8},{10,11... | collective-permute-start | bytes 1572872 | tf_op jit(solution)/shard_map/ppermute | solution.py:51
  344.9 45.1 %collective-permute-start.71 = (bf16[128,2048]{1,0:T(8,128)(2,1)}, bf16[128,2048]{1,0:T(8,128)(2,1)}, u32[]{:S(2)}, u32[]{:S(2)}) collective-permute-start(bf16[128,2048]{1,0:T(8,128)(2,1)} %fusion.62), channel_id=1, source_target_pairs={{0,2},{1,3},{2,4},{3,5},{4,6},{5,7},{6,0},{7,1},{8,10},{9,11},{10,... | collective-permute-start | bytes 1572872 | tf_op jit(solution)/shard_map/ppermute | solution.py:56
  355.6 34.5 %collective-permute-start.68 = (bf16[128,2048]{1,0:T(8,128)(2,1)}, bf16[128,2048]{1,0:T(8,128)(2,1)}, u32[]{:S(2)}, u32[]{:S(2)}) collective-permute-start(bf16[128,2048]{1,0:T(8,128)(2,1)} %slice.736), channel_id=1, source_target_pairs={{0,1},{1,0},{2,3},{3,2},{4,5},{5,4},{6,7},{7,6},{8,9},{9,8},{10,11... | collective-permute-start | bytes 1572872 | tf_op jit(solution)/shard_map/ppermute | solution.py:51
  391.5 23.1 %collective-permute-start.72 = (bf16[128,2048]{1,0:T(8,128)(2,1)S(1)}, bf16[128,2048]{1,0:T(8,128)(2,1)S(1)}, u32[]{:S(2)}, u32[]{:S(2)}) collective-permute-start(bf16[128,2048]{1,0:T(8,128)(2,1)S(1)} %fusion.64), channel_id=1, source_target_pairs={{0,2},{1,3},{2,4},{3,5},{4,6},{5,7},{6,0},{7,1},{8,10},{9,11},{10,... | collective-permute-start | bytes 1572872 | tf_op jit(solution)/shard_map/ppermute | solution.py:56
  395.5 20.5 %collective-permute-start.66 = (bf16[128,2048]{1,0:T(8,128)(2,1)S(1)}, bf16[128,2048]{1,0:T(8,128)(2,1)S(1)}, u32[]{:S(2)}, u32[]{:S(2)}) collective-permute-start(bf16[128,2048]{1,0:T(8,128)(2,1)S(1)} %slice.737), channel_id=1, source_target_pairs={{0,1},{1,0},{2,3},{3,2},{4,5},{5,4},{6,7},{7,6},{8,9},{9,8},{10,11... | collective-permute-start | bytes 1572872 | tf_op jit(solution)/shard_map/ppermute | solution.py:51
  404.4 50.7 %collective-permute-start.61 = (bf16[128,2048]{1,0:T(8,128)(2,1)S(1)}, bf16[128,2048]{1,0:T(8,128)(2,1)S(1)}, u32[]{:S(2)}, u32[]{:S(2)}) collective-permute-start(bf16[128,2048]{1,0:T(8,128)(2,1)S(1)} %copy-done.72), channel_id=1, source_target_pairs={{0,1},{1,0},{2,3},{3,2},{4,5},{5,4},{6,7},{7,6},{8,9},{9,8},{10,11... | collective-permute-start | bytes 1572872 | tf_op jit(solution)/shard_map/ppermute | solution.py:51
  404.4 20.0 %collective-permute-start.112 = (bf16[192,2048]{1,0:T(8,128)(2,1)S(1)}, bf16[192,2048]{1,0:T(8,128)(2,1)S(1)}, u32[]{:S(2)}, u32[]{:S(2)}) collective-permute-start(bf16[192,2048]{1,0:T(8,128)(2,1)S(1)} %get-tuple-element.48), channel_id=1, source_target_pairs={{0,8},{8,0},{16,24},{24,16},{1,9},{9,1},{17,25},{25,17},{2,10},{10... | collective-permute-start | bytes 2359304 | tf_op jit(solution)/shard_map/ppermute | solution.py:92
  414.6 28.5 %collective-permute-start.114 = (bf16[96,2048]{1,0:T(8,128)(2,1)S(1)}, bf16[96,2048]{1,0:T(8,128)(2,1)S(1)}, u32[]{:S(2)}, u32[]{:S(2)}) collective-permute-start(bf16[96,2048]{1,0:T(8,128)(2,1)S(1)} %get-tuple-element.43), channel_id=1, source_target_pairs={{0,16},{8,24},{16,0},{24,8},{1,17},{9,25},{17,1},{25,9},{2,18},{10... | collective-permute-start | bytes 1179656 | tf_op jit(solution)/shard_map/ppermute | solution.py:92
  416.0 25.5 %collective-permute-start.109 = (bf16[192,2048]{1,0:T(8,128)(2,1)S(1)}, bf16[192,2048]{1,0:T(8,128)(2,1)S(1)}, u32[]{:S(2)}, u32[]{:S(2)}) collective-permute-start(bf16[192,2048]{1,0:T(8,128)(2,1)S(1)} %get-tuple-element.50), channel_id=1, source_target_pairs={{0,16},{8,24},{16,0},{24,8},{1,17},{9,25},{17,1},{25,9},{2,18},{10... | collective-permute-start | bytes 2359304 | tf_op jit(solution)/shard_map/ppermute | solution.py:92
  424.3 20.4 %collective-permute-start.118 = (bf16[96,2048]{1,0:T(8,128)(2,1)S(1)}, bf16[96,2048]{1,0:T(8,128)(2,1)S(1)}, u32[]{:S(2)}, u32[]{:S(2)}) collective-permute-start(bf16[96,2048]{1,0:T(8,128)(2,1)S(1)} %get-tuple-element.44), channel_id=1, source_target_pairs={{0,8},{8,0},{16,24},{24,16},{1,9},{9,1},{17,25},{25,17},{2,10},{10... | collective-permute-start | bytes 1179656 | tf_op jit(solution)/shard_map/ppermute | solution.py:92
  443.0 138.4 %collective-permute-start.117 = (bf16[96,2048]{1,0:T(8,128)(2,1)}, bf16[96,2048]{1,0:T(8,128)(2,1)}, u32[]{:S(2)}, u32[]{:S(2)}) collective-permute-start(bf16[96,2048]{1,0:T(8,128)(2,1)} %get-tuple-element.45), channel_id=1, source_target_pairs={{0,8},{8,0},{16,24},{24,16},{1,9},{9,1},{17,25},{25,17},{2,10},{10... | collective-permute-start | bytes 1179656 | tf_op jit(solution)/shard_map/ppermute | solution.py:92
  444.7 27.1 %collective-permute-start.59 = (bf16[128,2048]{1,0:T(8,128)(2,1)S(1)}, bf16[128,2048]{1,0:T(8,128)(2,1)S(1)}, u32[]{:S(2)}, u32[]{:S(2)}) collective-permute-start(bf16[128,2048]{1,0:T(8,128)(2,1)S(1)} %fusion.72), channel_id=1, source_target_pairs={{0,2},{1,3},{2,4},{3,5},{4,6},{5,7},{6,0},{7,1},{8,10},{9,11},{10,... | collective-permute-start | bytes 1572872 | tf_op jit(solution)/shard_map/ppermute | solution.py:56
  455.1 139.1 %collective-permute-start.111 = (bf16[192,2048]{1,0:T(8,128)(2,1)}, bf16[192,2048]{1,0:T(8,128)(2,1)}, u32[]{:S(2)}, u32[]{:S(2)}) collective-permute-start(bf16[192,2048]{1,0:T(8,128)(2,1)} %get-tuple-element.47), channel_id=1, source_target_pairs={{0,8},{8,0},{16,24},{24,16},{1,9},{9,1},{17,25},{25,17},{2,10},{10... | collective-permute-start | bytes 2359304 | tf_op jit(solution)/shard_map/ppermute | solution.py:92
  469.2 170.9 %collective-permute-start.108 = (bf16[192,2048]{1,0:T(8,128)(2,1)}, bf16[192,2048]{1,0:T(8,128)(2,1)}, u32[]{:S(2)}, u32[]{:S(2)}) collective-permute-start(bf16[192,2048]{1,0:T(8,128)(2,1)} %get-tuple-element.49), channel_id=1, source_target_pairs={{0,16},{8,24},{16,0},{24,8},{1,17},{9,25},{17,1},{25,9},{2,18},{10... | collective-permute-start | bytes 2359304 | tf_op jit(solution)/shard_map/ppermute | solution.py:92
  471.1 111.0 %collective-permute-start.119 = (bf16[96,2048]{1,0:T(8,128)(2,1)}, bf16[96,2048]{1,0:T(8,128)(2,1)}, u32[]{:S(2)}, u32[]{:S(2)}) collective-permute-start(bf16[96,2048]{1,0:T(8,128)(2,1)} %get-tuple-element.40), channel_id=1, source_target_pairs={{0,16},{8,24},{16,0},{24,8},{1,17},{9,25},{17,1},{25,9},{2,18},{10... | collective-permute-start | bytes 1179656 | tf_op jit(solution)/shard_map/ppermute | solution.py:92
  529.6 67.0 %collective-permute-start.113 = (bf16[192,2048]{1,0:T(8,128)(2,1)}, bf16[192,2048]{1,0:T(8,128)(2,1)}, u32[]{:S(2)}, u32[]{:S(2)}) collective-permute-start(bf16[192,2048]{1,0:T(8,128)(2,1)} %fusion.20), channel_id=1, source_target_pairs={{0,16},{8,24},{16,0},{24,8},{1,17},{9,25},{17,1},{25,9},{2,18},{10... | collective-permute-start | bytes 2359304 | tf_op jit(solution)/shard_map/ppermute | solution.py:92
  591.8 48.3 %collective-permute-start.110 = (bf16[192,2048]{1,0:T(8,128)(2,1)}, bf16[192,2048]{1,0:T(8,128)(2,1)}, u32[]{:S(2)}, u32[]{:S(2)}) collective-permute-start(bf16[192,2048]{1,0:T(8,128)(2,1)} %fusion.23), channel_id=1, source_target_pairs={{0,8},{8,0},{16,24},{24,16},{1,9},{9,1},{17,25},{25,17},{2,10},{10... | collective-permute-start | bytes 2359304 | tf_op jit(solution)/shard_map/ppermute | solution.py:92
  594.2 42.3 %collective-permute-start.84 = (bf16[1024,128]{1,0:T(8,128)(2,1)}, bf16[1024,128]{1,0:T(8,128)(2,1)}, u32[]{:S(2)}, u32[]{:S(2)}) collective-permute-start(bf16[1024,128]{1,0:T(8,128)(2,1)} %get-tuple-element.81), channel_id=1, source_target_pairs={{0,8},{8,0},{16,24},{24,16},{1,9},{9,1},{17,25},{25,17},{2,10},{10... | collective-permute-start | bytes 786440 | tf_op jit(solution)/shard_map/ppermute | solution.py:92
  596.5 37.0 %collective-permute-start.83 = (bf16[1024,128]{1,0:T(8,128)(2,1)S(1)}, bf16[1024,128]{1,0:T(8,128)(2,1)S(1)}, u32[]{:S(2)}, u32[]{:S(2)}) collective-permute-start(bf16[1024,128]{1,0:T(8,128)(2,1)S(1)} %add_convert_fusion.2), channel_id=1, source_target_pairs={{0,8},{8,0},{16,24},{24,16},{1,9},{9,1},{17,25},{25,17},{2,10},{10... | collective-permute-start | bytes 786440 | tf_op jit(solution)/shard_map/ppermute | solution.py:92
  601.9 34.7 %collective-permute-start.86 = (bf16[1024,128]{1,0:T(8,128)(2,1)}, bf16[1024,128]{1,0:T(8,128)(2,1)}, u32[]{:S(2)}, u32[]{:S(2)}) collective-permute-start(bf16[1024,128]{1,0:T(8,128)(2,1)} %add_convert_fusion.1), channel_id=1, source_target_pairs={{0,16},{8,24},{16,0},{24,8},{1,17},{9,25},{17,1},{25,9},{2,18},{10... | collective-permute-start | bytes 786440 | tf_op jit(solution)/shard_map/ppermute | solution.py:92
  669.9 25.0 %collective-permute-start.103 = (bf16[64,2048]{1,0:T(8,128)(2,1)S(1)}, bf16[64,2048]{1,0:T(8,128)(2,1)S(1)}, u32[]{:S(2)}, u32[]{:S(2)}) collective-permute-start(bf16[64,2048]{1,0:T(8,128)(2,1)S(1)} %get-tuple-element.53), channel_id=1, source_target_pairs={{0,16},{8,24},{16,0},{24,8},{1,17},{9,25},{17,1},{25,9},{2,18},{10... | collective-permute-start | bytes 786440 | tf_op jit(solution)/shard_map/ppermute | solution.py:92
  670.8 25.2 %collective-permute-start.105 = (bf16[64,2048]{1,0:T(8,128)(2,1)S(1)}, bf16[64,2048]{1,0:T(8,128)(2,1)S(1)}, u32[]{:S(2)}, u32[]{:S(2)}) collective-permute-start(bf16[64,2048]{1,0:T(8,128)(2,1)S(1)} %get-tuple-element.51), channel_id=1, source_target_pairs={{0,8},{8,0},{16,24},{24,16},{1,9},{9,1},{17,25},{25,17},{2,10},{10... | collective-permute-start | bytes 786440 | tf_op jit(solution)/shard_map/ppermute | solution.py:92
  679.1 17.4 %collective-permute-start.91 = (bf16[128,2048]{1,0:T(8,128)(2,1)S(1)}, bf16[128,2048]{1,0:T(8,128)(2,1)S(1)}, u32[]{:S(2)}, u32[]{:S(2)}) collective-permute-start(bf16[128,2048]{1,0:T(8,128)(2,1)S(1)} %slice.733), channel_id=1, source_target_pairs={{0,1},{1,0},{2,3},{3,2},{4,5},{5,4},{6,7},{7,6},{8,9},{9,8},{10,11... | collective-permute-start | bytes 1572872 | tf_op jit(solution)/shard_map/ppermute | solution.py:51
  679.2 16.9 %collective-permute-start.107 = (bf16[64,2048]{1,0:T(8,128)(2,1)S(1)}, bf16[64,2048]{1,0:T(8,128)(2,1)S(1)}, u32[]{:S(2)}, u32[]{:S(2)}) collective-permute-start(bf16[64,2048]{1,0:T(8,128)(2,1)S(1)} %fusion.129), channel_id=1, source_target_pairs={{0,16},{8,24},{16,0},{24,8},{1,17},{9,25},{17,1},{25,9},{2,18},{10... | collective-permute-start | bytes 786440 | tf_op jit(solution)/shard_map/ppermute | solution.py:92
  (170 other events, 2145.4 us)
Sparse Core Ops, SparseCore 0:
  17.0 97.1 all-gather.1
  480.3 151.6 reduce-scatter.1

commit v2 on v1

v2 whole, which is shorter than its diff:
```python
import functools
import math

import jax
import jax.numpy as jnp
import numpy as np
from jax import lax
from jax.experimental import pallas as pl
from jax.experimental.pallas import tpu as pltpu
from jax.sharding import PartitionSpec as P

QH = 16
KVH = 8
HD = 128
HALF = HD // 2
EPSILON = 1e-06
ROPE_BASE = 1000000.0
SCORE_SCALE = HD ** (-0.5)
EXP2_SCALE = SCORE_SCALE * math.log2(math.e)
CONTRACT_ROWS = (((0,), (0,)), ((), ()))
CONTRACT_COLS = (((1,), (1,)), ((), ()))
BF16 = jnp.bfloat16
F32 = jnp.float32
VMEM_LIMIT = 40 * 1024 * 1024


def dot(left, right):
    return jnp.dot(left, right, preferred_element_type=F32)


def row_outer(left, right):
    return lax.dot_general(left, right, CONTRACT_ROWS, preferred_element_type=F32)


def col_inner(left, right):
    return lax.dot_general(left, right, CONTRACT_COLS, preferred_element_type=F32)


def rms_scale(values):
    return lax.rsqrt(jnp.mean(values * values, axis=-1, keepdims=True) + EPSILON)


def norm_back(upstream, source, scale_rows, gain):
    scaled = upstream * gain
    return scale_rows * scaled - source * scale_rows**3 * jnp.mean(
        scaled * source, axis=-1, keepdims=True
    )


def head_bits():
    count = lax.axis_size("head")
    return [1 << i for i in range(count.bit_length() - 1)]


def head_move(bit):
    count = lax.axis_size("head")
    return ("head", [(i, i ^ bit) for i in range(count)], bit)


def blk_move(steps, flip, link):
    count = lax.axis_size("blk")
    return ("blk", [(i, ((i + 2 * steps) % count) ^ flip) for i in range(count)], link)


def swap_move():
    return blk_move(0, 1, None)


def ring_move():
    return blk_move(1, 0, "z")


def member_move(flip):
    count = lax.axis_size("blk")
    return ("blk", [(i, i ^ flip) for i in range(count)], "z" if flip > 1 else None)


class Job:
    def __init__(self, steps):
        self.steps = steps
        self.wanted = None
        self.result = None
        self.advance(None)

    def advance(self, got):
        try:
            self.wanted = self.steps.send(got)
        except StopIteration as end:
            self.wanted = None
            self.result = end.value


class Wire:
    def __init__(self, token):
        self.token = token
        self.jobs = []

    def add(self, steps):
        job = Job(steps)
        self.jobs.append(job)
        return job

    def tie(self, *arrays):
        *arrays, self.token = lax.optimization_barrier(arrays + (self.token,))
        return arrays

    def phase(self, items, behind=False, riders=()):
        items = list(items)
        count = len(items)
        taken = []
        for job in (self.jobs if behind else []) + list(riders):
            if job.wanted is not None:
                taken.append((job, len(items), len(items) + len(job.wanted)))
                items.extend(job.wanted)
        if not items:
            return []
        values = self.tie(*[value for value, move in items])
        outs = self.tie(
            *[lax.ppermute(value, move[0], move[1]) for value, (same, move) in zip(values, items)]
        )
        for job, start, end in taken:
            job.advance(outs[start:end])
        self.jobs = [job for job in self.jobs if job.wanted is not None]
        return outs[:count]

    def drive(self, steps, hooks=(), riders=()):
        job = Job(steps)
        riders = list(riders)
        hooks = list(hooks)
        while job.wanted is not None or any(rider.wanted is not None for rider in riders):
            got = self.phase(job.wanted or [], riders=riders)
            if job.wanted is not None:
                job.advance(got)
            if hooks:
                riders.extend(hooks.pop(0)() or [])
        return job.result


def column_gather(value, blocks=None):
    chips = lax.axis_size("blk") // 2
    blocks = [] if blocks is None else blocks
    for step in range(chips):
        items = [(value, swap_move())]
        if step < chips - 1:
            items.append((value, ring_move()))
        got = yield items
        blocks.append([value, got[0]])
        value = got[-1]
    return blocks


def join_blocks(blocks):
    return [jnp.concatenate(block, axis=0) for block in blocks]


def column_scatter(part_of, apart=False):
    chips = lax.axis_size("blk") // 2
    order = list(range(1, chips)) + [0]

    def halves(step):
        part = part_of(step)
        rows = part.shape[0] // 2
        return part[:rows], part[rows:]

    own, other = halves(order[0])
    got = yield [(other.astype(BF16), swap_move())]
    total = own + got[0].astype(F32)
    for step in order[1:]:
        if apart:
            got = yield [(total.astype(BF16), ring_move())]
            own, other = halves(step)
            got = got + (yield [(other.astype(BF16), swap_move())])
            apart = False
        else:
            own, other = halves(step)
            got = yield [(total.astype(BF16), ring_move()), (other.astype(BF16), swap_move())]
        total = own + got[1].astype(F32) + got[0].astype(F32)
    return total


def plane_steps(backwards):
    bits = head_bits()
    order = bits[::-1] if backwards else bits
    steps = []
    for weight in range(1, len(bits) + 1):
        step = []
        for place in range(1 << len(bits)):
            if bin(place).count("1") == weight:
                last = [bit for bit in order if place & bit][-1]
                step.append((place, place ^ last, last))
        steps.append(step)
    return steps


def plane_gather(value, backwards):
    pieces = {0: value}
    for step in plane_steps(backwards):
        got = yield [(pieces[source], head_move(bit)) for place, source, bit in step]
        for (place, source, bit), piece in zip(step, got):
            pieces[place] = piece
    return [pieces[i] for i in range(len(pieces))]


def plane_scatter(parts, backwards):
    pieces = list(parts)
    for step in plane_steps(backwards)[::-1]:
        got = yield [(pieces[place].astype(BF16), head_move(bit)) for place, source, bit in step]
        for (place, source, bit), piece in zip(step, got):
            pieces[source] = pieces[source] + piece.astype(F32)
    return pieces[0]


def sum_everywhere(value):
    chips = lax.axis_size("blk") // 2
    for moves in (
        [head_move(flip) for flip in range(1, lax.axis_size("head"))],
        [swap_move()],
        [blk_move(steps, 0, None) for steps in range(1, chips)],
    ):
        got = yield [(value, move) for move in moves]
        for part in got:
            value = value + part
    return value


def pick(stack, index):
    return lax.dynamic_index_in_dim(stack, index, 0, keepdims=False)


def token_starts(anchors, lengths):
    ends = jnp.cumsum(lengths)
    seq_starts = ends - lengths
    inside = seq_starts[None, :] <= anchors[:, None]
    return jnp.max(jnp.where(inside, seq_starts[None, :], 0), axis=1)


def rope_tables(places):
    ladder = jnp.arange(HALF, dtype=F32)
    rates = jnp.exp(ladder * (-2.0 * math.log(ROPE_BASE) / HD))
    angles = rates[:, None] * places.astype(F32)[None, :]
    return (jnp.cos(angles), jnp.sin(angles))


def rope_forward(raw, gain, cosine, sine):
    heads = raw.astype(F32)
    scale = lax.rsqrt(jnp.mean(heads * heads, axis=-2, keepdims=True) + EPSILON)
    normed = heads * scale * gain[:, None]
    low, high = normed[..., :HALF, :], normed[..., HALF:, :]
    return jnp.concatenate([low * cosine - high * sine, high * cosine + low * sine], axis=-2)


def rope_backward(raw, gain, cosine, sine, upstream):
    heads = raw.astype(F32)
    scale = lax.rsqrt(jnp.mean(heads * heads, axis=-2, keepdims=True) + EPSILON)
    low, high = upstream[..., :HALF, :], upstream[..., HALF:, :]
    turned = jnp.concatenate([low * cosine + high * sine, high * cosine - low * sine], axis=-2)
    gain_grad = jnp.sum(turned * heads * scale, axis=-1)
    scaled = turned * gain[:, None]
    back = scale * scaled - heads * scale**3 * jnp.mean(scaled * heads, axis=-2, keepdims=True)
    return back, gain_grad


def small_call(kernel, outs, scalars, arrays, scratch=()):
    vmem = pl.BlockSpec(memory_space=pltpu.VMEM)
    return pl.pallas_call(
        kernel,
        in_specs=[pl.BlockSpec(memory_space=pltpu.SMEM)] + [vmem] * len(arrays),
        out_specs=[vmem] * len(outs),
        out_shape=[jax.ShapeDtypeStruct(shape, dtype) for shape, dtype in outs],
        scratch_shapes=[pltpu.VMEM(shape, dtype) for shape, dtype in scratch],
        compiler_params=pltpu.CompilerParams(vmem_limit_bytes=VMEM_LIMIT),
        cost_estimate=pl.CostEstimate(
            flops=0,
            bytes_accessed=3 * sum(array.size * array.dtype.itemsize for array in arrays),
            transcendentals=0,
        ),
    )(scalars, *arrays)


def table_kernel(blocks, sequences, index_ref, deal_ref, rate_ref, key_ref, start_ref, cos_ref, sin_ref):
    heads, column = key_ref.shape
    rows = column // blocks
    for place in range(heads):
        for block in range(blocks):
            row = deal_ref[pl.ds(index_ref[place * blocks + block], 1), :]
            key_ref[place : place + 1, block * rows : (block + 1) * rows] = row
    own = key_ref[0:1, :]
    starts = jnp.zeros_like(own)
    first = jnp.int32(0)
    for sequence in range(sequences - 1):
        first = first + index_ref[heads * blocks + sequence]
        starts = jnp.where(own >= first, first, starts)
    start_ref[...] = starts
    angles = rate_ref[:, :1] * (own - starts).astype(F32)
    cos_ref[...] = jnp.cos(angles)
    sin_ref[...] = jnp.sin(angles)


def tables(index, lengths, deals, column, heads):
    rates = np.exp(
        np.arange(HALF, dtype=np.float32) * np.float32(-2.0 * math.log(ROPE_BASE) / HD)
    ).astype(np.float32)
    return small_call(
        functools.partial(table_kernel, column // deals.shape[1], lengths.shape[0]),
        [
            ((heads, column), jnp.int32),
            ((1, column), jnp.int32),
            ((HALF, column), F32),
            ((HALF, column), F32),
        ],
        jnp.concatenate([index, lengths]),
        [deals, jnp.asarray(np.broadcast_to(rates[:, None], (HALF, 128)))],
    )


def put_in_order(out_ref, scalar_ref, pieces, rows, finish):
    base = scalar_ref[0]
    for flip, piece in enumerate(pieces):
        value = piece[...]
        column = value.shape[1]
        if flip & 1:
            cuts = [value[:, i * rows : (i + 1) * rows] for i in range(column // rows)]
            value = jnp.concatenate([cuts[i ^ 1] for i in range(column // rows)], axis=1)
        at = pl.ds(base ^ flip, 1)
        if flip & 2:
            pair = 2 * rows

            @pl.when(scalar_ref[1] == 0)
            def _(at=at, value=value, pair=pair):
                out_ref[at] = jnp.concatenate([value[:, pair:], value[:, :pair]], axis=1)[None]

            @pl.when(scalar_ref[1] != 0)
            def _(at=at, value=value, pair=pair):
                out_ref[at] = jnp.concatenate([value[:, -pair:], value[:, :-pair]], axis=1)[None]

        else:
            out_ref[at] = value[None]
    finish()


def join_members(base, odd, pieces, rows):
    count = len(pieces)

    def kernel(scalar_ref, *refs):
        put_in_order(refs[count], scalar_ref, refs[:count], rows, lambda: None)

    return small_call(
        kernel,
        [((count,) + pieces[0].shape, BF16)],
        jnp.stack([base, odd]).astype(jnp.int32),
        pieces,
    )[0]


def split_blocks(base, blocks, count):
    size = blocks[0].shape[0] // count
    width = blocks[0].shape[1]

    def kernel(scalar_ref, *refs):
        for flip in range(count):
            start = pl.multiple_of((scalar_ref[0] ^ flip) * size, size)
            for index in range(len(blocks)):
                refs[len(blocks) + flip][:, index * width : (index + 1) * width] = refs[index][
                    pl.ds(start, size), :
                ]

    return small_call(
        kernel,
        [((size, width * len(blocks)), BF16)] * count,
        base.reshape(1).astype(jnp.int32),
        blocks,
    )


def rope_kernel(rows, query_rows, key_rows, scalar_ref, *refs):
    pieces = refs[:-6]
    cos_ref, sin_ref, gain_ref, raw_ref, query_ref, pair_ref = refs[-6:]
    count, column = len(pieces), cos_ref.shape[1]
    put_in_order(raw_ref, scalar_ref, pieces, rows, lambda: None)
    cosine, sine = cos_ref[...], sin_ref[...]

    def rotate(parts, gain):
        heads = jnp.concatenate(parts, axis=0).astype(F32)
        scale = lax.rsqrt(jnp.mean(heads * heads, axis=0, keepdims=True) + EPSILON)
        normed = heads * scale * gain
        low, high = normed[:HALF], normed[HALF:]
        turned = jnp.concatenate([low * cosine - high * sine, high * cosine + low * sine], axis=0)
        return turned.T.astype(BF16)

    per_head = HD // query_rows
    for head in range(count // per_head):
        parts = [raw_ref[head * per_head + i, :query_rows, :] for i in range(per_head)]
        query_ref[head * column : (head + 1) * column, :] = rotate(parts, gain_ref[:, 0:1])
    parts = [raw_ref[i, query_rows : query_rows + key_rows, :] for i in range(count)]
    pair_ref[:, :HD] = rotate(parts, gain_ref[:, 1:2])
    parts = [raw_ref[i, query_rows + key_rows :, :] for i in range(count)]
    pair_ref[:, HD:] = jnp.concatenate(parts, axis=0).astype(F32).T.astype(BF16)


def rope_members(base, odd, pieces, cosine, sine, gains, rows, query_rows, key_rows):
    count, column = len(pieces), cosine.shape[1]
    return small_call(
        functools.partial(rope_kernel, rows, query_rows, key_rows),
        [
            ((count,) + pieces[0].shape, BF16),
            ((count * query_rows // HD * column, HD), BF16),
            ((column, 2 * HD), BF16),
        ],
        jnp.stack([base, odd]).astype(jnp.int32),
        list(pieces) + [cosine, sine, gains],
    )


def mixed_kernel(scalar_ref, in_ref, *refs):
    outs, parts_ref = refs[:-1], refs[-1]
    count, size, column = parts_ref.shape
    for head in range(in_ref.shape[0] // column):
        part = in_ref[head * column : (head + 1) * column, :].T.astype(BF16)
        per_head = HD // size
        for i in range(per_head):
            parts_ref[head * per_head + i] = part[i * size : (i + 1) * size]
    for flip, out_ref in enumerate(outs):
        out_ref[...] = parts_ref[scalar_ref[0] ^ flip]


def mixed_members(base, heads_out, count, column):
    size = heads_out.shape[0] // column * HD // count
    return small_call(
        mixed_kernel,
        [((size, column), BF16)] * count,
        base.reshape(1).astype(jnp.int32),
        [heads_out],
        [((count, size, column), BF16)],
    )


def upstream_members(base, odd, pieces, rows):
    count = len(pieces)
    size, column = pieces[0].shape
    per_head = HD // size

    def kernel(scalar_ref, *refs):
        out_ref, parts_ref = refs[count:]
        put_in_order(parts_ref, scalar_ref, refs[:count], rows, lambda: None)
        for head in range(count // per_head):
            parts = [parts_ref[head * per_head + i] for i in range(per_head)]
            out_ref[head * column : (head + 1) * column, :] = (
                jnp.concatenate(parts, axis=0).astype(F32).T.astype(BF16)
            )

    return small_call(
        kernel,
        [((count // per_head * column, HD), BF16)],
        jnp.stack([base, odd]).astype(jnp.int32),
        pieces,
        [((count, size, column), BF16)],
    )[0]


def rope_back_kernel(query_rows, key_rows, count, scalar_ref, *refs):
    raw_ref, dq_ref, cos_ref, sin_ref, gain_ref, dk_ref, dv_ref = refs[:7]
    more = refs[7 : -2 - count]
    outs, gain_out, parts_ref = refs[-2 - count : -2], refs[-2], refs[-1]
    column = cos_ref.shape[1]
    cosine, sine = cos_ref[...], sin_ref[...]

    def back(parts, gain, upstream):
        heads = jnp.concatenate(parts, axis=0).astype(F32)
        scale = lax.rsqrt(jnp.mean(heads * heads, axis=0, keepdims=True) + EPSILON)
        low, high = upstream[:HALF], upstream[HALF:]
        turned = jnp.concatenate([low * cosine + high * sine, high * cosine - low * sine], axis=0)
        gain_grad = jnp.sum(turned * heads * scale, axis=1, keepdims=True)
        scaled = turned * gain
        mean = jnp.mean(scaled * heads, axis=0, keepdims=True)
        return (scale * scaled - heads * (scale * scale * scale * mean)).astype(BF16), gain_grad

    per_head = HD // query_rows
    total = jnp.zeros((HD, 1), F32)
    for head in range(count // per_head):
        at = [head * per_head + i for i in range(per_head)]
        grad, gain_grad = back(
            [raw_ref[i, :query_rows, :] for i in at],
            gain_ref[:, 0:1],
            dq_ref[head * column : (head + 1) * column, :].T,
        )
        total = total + gain_grad
        for place, i in enumerate(at):
            parts_ref[i, :query_rows, :] = grad[place * query_rows : (place + 1) * query_rows]
    gain_out[:, 0:1] = total
    key_grad, value_grad = dk_ref[...], dv_ref[...]
    for ref in more:
        key_grad = key_grad + ref[:, :HD].astype(F32)
        value_grad = value_grad + ref[:, HD:].astype(F32)
    grad, gain_grad = back(
        [raw_ref[i, query_rows : query_rows + key_rows, :] for i in range(count)],
        gain_ref[:, 1:2],
        key_grad.T,
    )
    gain_out[:, 1:2] = gain_grad
    value_grad = value_grad.T.astype(BF16)
    for i in range(count):
        cut = slice(i * key_rows, (i + 1) * key_rows)
        parts_ref[i, query_rows : query_rows + key_rows, :] = grad[cut]
        parts_ref[i, query_rows + key_rows :, :] = value_grad[cut]
    for flip, out_ref in enumerate(outs):
        out_ref[...] = parts_ref[scalar_ref[0] ^ flip]


def rope_back_members(base, raw, dq, cosine, sine, gains, dk, dv, more, query_rows, key_rows):
    count, size, column = raw.shape
    return small_call(
        functools.partial(rope_back_kernel, query_rows, key_rows, count),
        [((size, column), BF16)] * count + [((HD, 2), F32)],
        base.reshape(1).astype(jnp.int32),
        [raw, dq, cosine, sine, gains, dk, dv] + list(more),
        [((count, size, column), BF16)],
    )


def attend_kernel(first, last, *refs):
    refs = list(refs)
    q_ref, k_ref, v_ref, qpos_ref, qlow_ref, kpos_ref = refs[:6]
    outs = refs[6:] if first else refs[7:]
    kpos = kpos_ref[...]
    scores = col_inner(q_ref[...], k_ref[...])
    rows = q_ref.shape[0]
    qpos = jnp.broadcast_to(qpos_ref[...], (8, rows)).T[:, :1]
    qlow = jnp.broadcast_to(qlow_ref[...], (8, rows)).T[:, :1]
    allowed = (kpos <= qpos) & (kpos >= qlow)
    lifted = jnp.where(allowed, jnp.exp2(scores * EXP2_SCALE), 0.0).astype(BF16)
    values = jnp.concatenate([v_ref[...], jnp.ones(v_ref.shape, BF16)], axis=1)
    total = dot(lifted, values)
    if not first:
        total = total + refs[6][...]
    if last:
        weight = total[:, HD:]
        outs[0][...] = total[:, :HD] / weight
        outs[1][...] = jnp.log2(weight).T[:8, :]
    else:
        outs[0][...] = total


def attend(query, keys, values, qpos, qlow, kpos, total, last):
    rows, tokens = query.shape[0], keys.shape[0]
    value_at = values.shape[1] // HD - 1
    own = qpos.shape[1]
    block = 256
    wrap = own // block
    first = total is None
    cost = pl.CostEstimate(
        flops=20 * rows * tokens * HD, bytes_accessed=4 * tokens * HD, transcendentals=rows * tokens
    )
    whole = lambda i: (0, 0)
    return pl.pallas_call(
        functools.partial(attend_kernel, first, last),
        grid=(rows // block,),
        in_specs=[
            pl.BlockSpec((block, HD), lambda i: (i, 0)),
            pl.BlockSpec((tokens, HD), whole),
            pl.BlockSpec((tokens, HD), lambda i: (0, value_at)),
            pl.BlockSpec((1, block), lambda i: (0, i % wrap)),
            pl.BlockSpec((1, block), lambda i: (0, i % wrap)),
            pl.BlockSpec((1, tokens), whole),
        ]
        + ([] if first else [pl.BlockSpec((block, 2 * HD), lambda i: (i, 0))]),
        out_specs=[
            pl.BlockSpec((block, HD), lambda i: (i, 0)),
            pl.BlockSpec((8, block), lambda i: (0, i)),
        ]
        if last
        else pl.BlockSpec((block, 2 * HD), lambda i: (i, 0)),
        out_shape=[
            jax.ShapeDtypeStruct((rows, HD), F32),
            jax.ShapeDtypeStruct((8, rows), F32),
        ]
        if last
        else jax.ShapeDtypeStruct((rows, 2 * HD), F32),
        compiler_params=pltpu.CompilerParams(vmem_limit_bytes=VMEM_LIMIT),
        cost_estimate=cost,
    )(query, keys, values, qpos, qlow, kpos, *([] if first else [total]))


def attend_back_kernel(
    chunk, own, first, q_ref, g_ref, log_ref, qpos_ref, qlow_ref, k_ref, v_ref, kpos_ref,
    in_ref, extra_ref, dq_ref, dk_ref, dv_ref, *new_ref,
):
    rows = q_ref.shape[0]
    delta_ref = new_ref[0] if first else extra_ref

    @pl.when(pl.program_id(0) == 0)
    def _():
        if first:
            dq_ref[...] = jnp.zeros_like(dq_ref)
            for i in range(rows // chunk):
                at = pl.ds(i * chunk, chunk)
                product = g_ref[at, :].astype(F32) * in_ref[at, :]
                sums = jnp.sum(product.T, axis=0, keepdims=True)
                delta_ref[:, at] = jnp.broadcast_to(sums, (8, chunk))
        else:
            dq_ref[...] = in_ref[...]

    keys = k_ref[...]
    values = v_ref[...]
    kpos = jnp.broadcast_to(kpos_ref[...], (8, keys.shape[0])).T[:, :1]
    key_sum = jnp.zeros(keys.shape, F32)
    value_sum = jnp.zeros(keys.shape, F32)
    for i in range(rows // chunk):
        at = pl.ds(i * chunk, chunk)
        place = pl.ds((i * chunk) % own, chunk)
        query = q_ref[at, :]
        upstream = g_ref[at, :]
        scores = col_inner(keys, query)
        allowed = (kpos <= qpos_ref[:, place]) & (kpos >= qlow_ref[:, place])
        probs = jnp.where(allowed, jnp.exp2(scores * EXP2_SCALE - log_ref[0:1, at]), 0.0)
        prob_grad = col_inner(values, upstream)
        score_grad = (probs * (prob_grad - delta_ref[0:1, at])).astype(BF16)
        value_sum = value_sum + dot(probs.astype(BF16), upstream)
        key_sum = key_sum + dot(score_grad, query)
        dq_ref[at, :] += row_outer(score_grad, keys) * SCORE_SCALE
    dk_ref[...] = key_sum * SCORE_SCALE
    dv_ref[...] = value_sum


def attend_back(query, upstream, logs, qpos, qlow, keys, values, kpos, before, out):
    rows, tokens = query.shape[0], keys.shape[0]
    value_at = values.shape[1] // HD - 1
    own = qpos.shape[1]
    block = 512
    first = before is None
    cost = pl.CostEstimate(
        flops=32 * rows * tokens * HD, bytes_accessed=8 * tokens * HD, transcendentals=rows * tokens
    )
    whole = lambda i: (0, 0)
    taken = (out, logs) if first else before
    return pl.pallas_call(
        functools.partial(attend_back_kernel, 512, own, first),
        grid=(tokens // block,),
        in_specs=[
            pl.BlockSpec((rows, HD), whole),
            pl.BlockSpec((rows, HD), whole),
            pl.BlockSpec((8, rows), whole),
            pl.BlockSpec((1, own), whole),
            pl.BlockSpec((1, own), whole),
            pl.BlockSpec((block, HD), lambda i: (i, 0)),
            pl.BlockSpec((block, HD), lambda i: (i, value_at)),
            pl.BlockSpec((1, block), lambda i: (0, i)),
            pl.BlockSpec((rows, HD), whole),
            pl.BlockSpec((8, rows), whole),
        ],
        out_specs=[
            pl.BlockSpec((rows, HD), whole),
            pl.BlockSpec((block, HD), lambda i: (i, 0)),
            pl.BlockSpec((block, HD), lambda i: (i, 0)),
        ]
        + ([pl.BlockSpec((8, rows), whole)] if first else []),
        out_shape=[
            jax.ShapeDtypeStruct((rows, HD), F32),
            jax.ShapeDtypeStruct((tokens, HD), F32),
            jax.ShapeDtypeStruct((tokens, HD), F32),
        ]
        + ([jax.ShapeDtypeStruct((8, rows), F32)] if first else []),
        compiler_params=pltpu.CompilerParams(vmem_limit_bytes=VMEM_LIMIT),
        cost_estimate=cost,
    )(query, upstream, logs, qpos, qlow, keys, values, kpos, *taken)


def local(
    inputs,
    dealing,
    lengths,
    input_gain,
    w_query,
    w_key,
    w_value,
    query_gain,
    key_gain,
    w_out,
    hidden_gain,
    w_gate,
    w_up,
    w_down,
    cotangent,
):
    heads, blks = lax.axis_size("head"), lax.axis_size("blk")
    head, blk = lax.axis_index("head"), lax.axis_index("blk")
    shards = heads * blks
    chips = blks // 2
    chip, core = blk // 2, blk % 2
    shard = head * blks + blk
    rows, width = inputs.shape
    column = rows * blks
    pair = 2 * rows
    per_device = QH // blks
    query_rows, key_rows = w_query.shape[1], w_key.shape[1]
    qkv_rows = query_rows + 2 * key_rows
    in_pair = shards // KVH == heads and blks == 2 * heads

    gains = jnp.zeros((2 * width + 2 * HD,), F32)
    hidden_part = jnp.where(head == 0, hidden_gain.astype(F32), 0.0)
    for at, part in (
        (shard * input_gain.shape[0], input_gain),
        (width + blk * hidden_gain.shape[0], hidden_part),
        (2 * width + shard * query_gain.shape[0], query_gain),
        (2 * width + HD + shard * key_gain.shape[0], key_gain),
    ):
        gains = lax.dynamic_update_slice(gains, part.astype(F32), (at,))
    wire = Wire(inputs)

    index = jnp.stack(
        [
            (((chip - step) % chips) * 2 + (core ^ flip)) * heads + (head ^ place)
            for place in range(heads)
            for step in range(chips)
            for flip in range(2)
        ]
    )
    key_places, query_starts, cosine, sine = tables(
        index, lengths, dealing.reshape(blks * heads, rows), column, heads
    )
    query_places = key_places[:1]

    qkv_job = Job(
        plane_gather(jnp.concatenate([w_query.T, w_key.T, w_value.T], axis=0), False)
    )
    gain_job = Job(sum_everywhere(gains.reshape(-1, 128)))
    token_blocks = wire.drive(
        column_gather(inputs), riders=[qkv_job], hooks=[lambda: [gain_job]]
    )
    qkv_weights, gains = qkv_job.result, gain_job.result
    token_blocks = [part for parts in token_blocks for part in parts]
    gains = gains.reshape(-1)
    input_norm = gains[:width]
    hidden_norm = gains[width : 2 * width]
    query_norm = gains[2 * width : 2 * width + HD]
    key_norm = gains[2 * width + HD :]
    qkv_weights = jnp.concatenate(qkv_weights, axis=0)
    feed_rows, out_rows = w_down.shape[0], w_out.shape[0]
    out_weights = lax.all_gather(wire.tie(w_out)[0], "head", axis=0, tiled=True)
    column_values = jnp.concatenate(token_blocks, axis=0).astype(F32)
    normed_column = (column_values * rms_scale(column_values) * input_norm).astype(BF16)
    raw = col_inner(qkv_weights, normed_column).astype(BF16)
    norms = jnp.stack([query_norm, key_norm], axis=1)

    def reorder(value, index):
        cut = value.reshape(value.shape[:-1] + (blks, rows))
        return jnp.take(cut, index, axis=-2).reshape(value.shape)

    places = jnp.arange(blks)
    to_ring = ((chip - places // 2) % chips) * 2 + ((places % 2) ^ core)

    def gather_members(value):
        return reorder(lax.all_gather(reorder(value, to_ring), "blk", axis=0), to_ring)

    def exchange(pieces, behind=False):
        return [pieces[0]] + wire.phase(
            [(pieces[flip], member_move(flip)) for flip in range(1, heads)], behind
        )

    member = blk % heads
    odd = chip % 2
    if in_pair:
        pieces = exchange(split_blocks(head ^ member, [raw], heads))
        raw, query, key_value = rope_members(
            member, odd, pieces, cosine, sine, norms, rows, query_rows, key_rows
        )
    else:
        raw = raw.reshape(heads, qkv_rows, column)
        by_head = jnp.stack([pick(raw, head ^ place) for place in range(heads)])
        every = jnp.swapaxes(gather_members(by_head), 0, 1)
        every = every.reshape(shards, qkv_rows, column)
        query_all = every[:, :query_rows].reshape(QH, HD, column)
        key_all = every[:, query_rows : query_rows + key_rows].reshape(KVH, HD, column)
        value_all = every[:, query_rows + key_rows :].reshape(KVH, HD, column)
        query_raw = lax.dynamic_slice_in_dim(query_all, blk * per_device, per_device, 0)
        key_raw = pick(key_all, blk * KVH // blks)
        value_raw = pick(value_all, blk * KVH // blks)

        query = rope_forward(query_raw, query_norm, cosine, sine).astype(BF16)
        keys = rope_forward(key_raw, key_norm, cosine, sine).astype(BF16)
        query = jnp.swapaxes(query, 1, 2).reshape(per_device * column, HD)
        key_value = jnp.concatenate([keys.T, value_raw.T], axis=1)
    own_cotangent = lax.dynamic_slice_in_dim(cotangent, head * rows, rows, 0)
    cotangent_job = wire.add(column_gather(own_cotangent))

    pairs = {0: key_value}
    key_pieces, value_pieces = dict(pairs), dict(pairs)
    total = None

    def add_column(place, total):
        return attend(
            query,
            key_pieces[place],
            value_pieces[place],
            query_places,
            query_starts,
            key_places[place : place + 1],
            total,
            place == heads - 1,
        )

    ready = [0]
    for forward, backward in zip(plane_steps(False), plane_steps(True)):
        if forward == backward:
            items = [(pairs[source], head_move(bit)) for place, source, bit in forward]
        else:
            items = [
                (key_pieces[source][:, :HD], head_move(bit)) for place, source, bit in forward
            ] + [(value_pieces[source][:, -HD:], head_move(bit)) for place, source, bit in backward]
        got = wire.phase(items, behind=True)
        for place in ready:
            total = add_column(place, total)
        if ready == [0]:
            late = jnp.concatenate([w_gate.T, w_up.T, w_down], axis=0)
            total, late = wire.tie(total, late)
        else:
            total = wire.tie(total)[0]
        ready = [place for place, source, bit in forward]
        for index, place in enumerate(ready):
            key_pieces[place] = got[index]
            if forward == backward:
                value_pieces[place] = pairs[place] = got[index]
            else:
                value_pieces[backward[index][0]] = got[len(forward) + index]
    wire.phase([], behind=True)
    for place in ready:
        total = add_column(place, total)
    heads_out, logs = total

    if in_pair:
        pieces = exchange(mixed_members(member, heads_out, heads, column))
        mixed = join_members(member, odd, pieces, rows).reshape(heads * out_rows, column)
    else:
        mixed_heads = jnp.swapaxes(heads_out.astype(BF16).reshape(per_device, column, HD), 1, 2)
        every = gather_members(mixed_heads)
        every = every.reshape(heads, blks, out_rows, column)
        mixed = lax.dynamic_index_in_dim(every, blk, 1).reshape(heads * out_rows, column)
    wire.jobs.remove(cotangent_job)
    branch = wire.drive(
        column_scatter(
            lambda step: row_outer(mixed[:, step * pair : (step + 1) * pair], out_weights)
        ),
        riders=[cotangent_job],
    )
    token_values = inputs.astype(F32)
    middle = token_values + branch
    scale_two = rms_scale(middle)
    hidden_in = (middle * scale_two * hidden_norm).astype(BF16)

    late = lax.all_gather(late, "head", axis=0)
    gate_weights, up_weights, down_weights = (
        late[:, i * feed_rows : (i + 1) * feed_rows].reshape(-1, width) for i in range(3)
    )
    hidden_parts = []
    feed_halves = []
    feed_weights = [gate_weights, up_weights, down_weights]
    half_chips = chips // 2

    def feed_half(index):
        start = index * half_chips
        steps = range(start, start + half_chips)
        tokens, upstream = (
            jnp.concatenate([part for step in steps for part in parts[step]], axis=0)
            for parts in (hidden_parts, cotangent_job.result)
        )
        gate_weights, up_weights, down_weights = feed_weights
        act_grad = col_inner(upstream, down_weights)
        gate = col_inner(tokens, gate_weights)
        up_proj = col_inner(tokens, up_weights)
        sigmoid_gate = jax.nn.sigmoid(gate)
        silu_gate = gate * sigmoid_gate
        activated = (silu_gate * up_proj).astype(BF16)
        gate_grad = (
            act_grad * up_proj * sigmoid_gate * (1.0 + gate * (1.0 - sigmoid_gate))
        ).astype(BF16)
        up_grad = (act_grad * silu_gate).astype(BF16)
        back = dot(gate_grad, gate_weights) + dot(up_grad, up_weights)
        feed_halves.append((tokens, upstream, activated, gate_grad, up_grad, back))

    def feed_hook(step):
        def hook():
            if step == 0:
                feed_weights[:] = wire.tie(*feed_weights)
            if step == half_chips:
                feed_half(0)
                feed_halves[0] = tuple(wire.tie(*feed_halves[0]))

        return hook

    wire.drive(
        column_gather(hidden_in, hidden_parts), hooks=[feed_hook(step) for step in range(chips)]
    )
    feed_half(1)
    gate_weights, up_weights, down_weights = feed_weights

    def half_rows(index, step):
        at = (step % half_chips) * pair
        return feed_halves[step // half_chips][index][at : at + pair]

    grad_down, grad_gate, grad_up = (
        sum(row_outer(half[left], half[right]) for half in feed_halves).astype(BF16)
        for left, right in ((2, 1), (3, 0), (4, 0))
    )
    feed_grads = [grad_down, grad_gate, grad_up]

    def keep_grads(*indices):
        def hook():
            for index in indices:
                feed_grads[index] = wire.tie(feed_grads[index])[0]

        return hook

    hidden_grad = wire.drive(
        column_scatter(lambda step: half_rows(5, step), apart=True),
        hooks=[lambda: None, lambda: None, lambda: None, keep_grads(0), keep_grads(1)],
    )
    hidden_gain_grad = jnp.sum(hidden_grad * middle * scale_two, axis=0)
    middle_grad = own_cotangent.astype(F32) + norm_back(hidden_grad, middle, scale_two, hidden_norm)
    branch_grad = middle_grad.astype(BF16)
    down_parts = {}

    def keep_all():
        feed_grads[:] = [
            jnp.concatenate(
                [grad.reshape(heads, feed_rows, width) for grad in feed_grads], axis=1
            )
        ]
        for step in range(1, chips):
            down_parts[step] = dot(half_rows(2, step), down_weights)
        feed_grads[0], *parts = wire.tie(feed_grads[0], *down_parts.values())
        down_parts.update(zip(down_parts, parts))

    branch_blocks = join_blocks(
        wire.drive(column_gather(branch_grad), hooks=[keep_grads(2), keep_all])
    )
    down_parts[0] = dot(half_rows(2, 0), down_weights)
    feed_grads = lax.psum_scatter(feed_grads[0], "head", scatter_dimension=0).astype(F32)
    down_job = wire.add(column_scatter(lambda step: down_parts[step]))
    mixed_grads = [col_inner(out_weights, block).astype(BF16) for block in branch_blocks]
    grad_out = dot(mixed, jnp.concatenate(branch_blocks, axis=0)).reshape(heads, out_rows, width)
    if in_pair:
        pieces = exchange(split_blocks(member, mixed_grads, heads), True)
        upstream = upstream_members(member, odd, pieces, rows)
    else:
        mixed_grad = jnp.concatenate(mixed_grads, axis=1).reshape(heads, out_rows, column)
        every = gather_members(mixed_grad)
        every = jnp.swapaxes(every, 0, 1).reshape(blks, per_device, HD, column)
        upstream = jnp.swapaxes(pick(every, blk), 1, 2).reshape(per_device * column, HD)

    key_grads, value_grads = {}, {}
    carry = None
    wire.phase([], behind=True)
    for forward, backward in zip(plane_steps(False)[::-1] + [[]], plane_steps(True)[::-1] + [[]]):
        for place in [step[0] for step in forward] if forward else [0]:
            results = attend_back(
                query,
                upstream,
                logs,
                query_places,
                query_starts,
                key_pieces[place],
                value_pieces[place],
                key_places[place : place + 1],
                carry,
                heads_out,
            )
            key_grads[place] = key_grads.get(place, 0.0) + results[1]
            value_grads[place] = value_grads.get(place, 0.0) + results[2]
            carry = (results[0], carry[1] if carry else results[3])
        if not forward:
            break
        if forward == backward:
            items = [
                (
                    jnp.concatenate([key_grads[place], value_grads[place]], axis=1).astype(BF16),
                    head_move(bit),
                )
                for place, source, bit in forward
            ]
        else:
            items = [
                (key_grads[place].astype(BF16), head_move(bit)) for place, source, bit in forward
            ] + [
                (value_grads[place].astype(BF16), head_move(bit))
                for place, source, bit in backward
            ]
        tied = lax.optimization_barrier(tuple(value for value, move in items) + carry)
        items = [(value, move) for value, (ignored, move) in zip(tied, items)]
        carry = tied[len(items) :]
        got = wire.phase(items, behind=True)
        last_parts = got
        if forward[0][1] == 0:
            continue
        for index, (place, source, bit) in enumerate(forward):
            part = got[index][:, :HD].astype(F32)
            key_grads[source] = key_grads.get(source, 0.0) + part
        for index, (place, source, bit) in enumerate(backward):
            part = got[index if forward == backward else len(forward) + index]
            value_grads[source] = value_grads.get(source, 0.0) + part[:, -HD:].astype(F32)
    query_grad = carry[0]

    if in_pair:
        *pieces, gain_grads = rope_back_members(
            member, raw, query_grad, cosine, sine, norms, key_grads[0], value_grads[0], last_parts,
            query_rows, key_rows,
        )
        pieces = exchange(pieces, True)
        raw_grad = join_members(head ^ member, odd, pieces, rows).reshape(-1, column)
    else:
        key_grad = key_grads[0] + sum(part[:, :HD].astype(F32) for part in last_parts)
        value_grad = value_grads[0] + sum(part[:, HD:].astype(F32) for part in last_parts)
        query_grad = jnp.swapaxes(query_grad.reshape(per_device, column, HD), 1, 2)
        query_raw_grad, query_gain_grad = rope_backward(
            query_raw, query_norm, cosine, sine, query_grad
        )
        key_raw_grad, key_gain_grad = rope_backward(key_raw, key_norm, cosine, sine, key_grad.T)
        query_raw_grad = query_raw_grad.astype(BF16)
        key_raw_grad = key_raw_grad.astype(BF16)
        value_raw_grad = value_grad.T.astype(BF16)
        gain_grads = jnp.stack([jnp.sum(query_gain_grad, axis=0), key_gain_grad], axis=1)

        def spread(part, count, index):
            empty = jnp.zeros((count,) + part.shape[1:], BF16)
            return lax.dynamic_update_slice_in_dim(empty, part, index, 0)

        every = jnp.concatenate(
            [
                spread(query_raw_grad, QH, blk * per_device).reshape(shards, query_rows, column),
                spread(key_raw_grad[None], KVH, blk * KVH // blks).reshape(
                    shards, key_rows, column
                ),
                spread(value_raw_grad[None], KVH, blk * KVH // blks).reshape(
                    shards, key_rows, column
                ),
            ],
            axis=1,
        ).reshape(heads, blks, qkv_rows, column)
        every = reorder(jnp.swapaxes(every, 0, 1), to_ring)
        by_head = reorder(lax.psum_scatter(every, "blk", scatter_dimension=0), to_ring)
        raw_grad = jnp.concatenate(
            [pick(by_head, head ^ place) for place in range(heads)], axis=0
        )

    while wire.jobs:
        wire.phase([], behind=True)
    done = [feed_grads, (middle + down_job.result).astype(BF16)]
    tail = []

    def start_tail():
        qkv_grad = dot(wire.tie(raw_grad)[0], normed_column)
        input_gain_grad = jnp.sum(qkv_grad * qkv_weights.astype(F32), axis=0) / input_norm
        sums = jnp.concatenate(
            [input_gain_grad, hidden_gain_grad, gain_grads[:, 0], gain_grads[:, 1]]
        )
        qkv_grad = qkv_grad.reshape(heads, qkv_rows, width)
        tail.append(Job(sum_everywhere(sums.reshape(-1, 128))))
        parts = [
            jnp.concatenate([qkv_grad[place], pick(grad_out, head ^ place)], axis=0)
            for place in range(heads)
        ]
        tail.append(Job(plane_scatter(parts, False)))

    def keep_done():
        done[:] = wire.tie(*done)

    normed_grad = wire.drive(
        column_scatter(
            lambda step: row_outer(raw_grad[:, step * pair : (step + 1) * pair], qkv_weights)
        ),
        hooks=[start_tail, lambda: tail, keep_done],
    )
    sums, qkv_grad = tail[0].result.reshape(-1), tail[1].result
    feed_grads, layer_out = done
    grad_out = tail[1].result[qkv_rows:]
    grad_gate, grad_up, grad_down = (
        feed_grads[i * feed_rows : (i + 1) * feed_rows] for i in (1, 2, 0)
    )
    token_values = wire.token.astype(F32)
    grad_input = middle_grad + norm_back(
        normed_grad, token_values, rms_scale(token_values), input_norm
    )

    def own_part(at, size):
        return lax.dynamic_slice_in_dim(sums, at, size)

    return (
        layer_out,
        grad_input,
        own_part(shard * input_gain.shape[0], input_gain.shape[0]),
        qkv_grad[:query_rows].T,
        qkv_grad[query_rows : query_rows + key_rows].T,
        qkv_grad[query_rows + key_rows : qkv_rows].T,
        own_part(2 * width + shard * query_gain.shape[0], query_gain.shape[0]),
        own_part(2 * width + HD + shard * key_gain.shape[0], key_gain.shape[0]),
        grad_out,
        own_part(width + blk * hidden_gain.shape[0], hidden_gain.shape[0]),
        grad_gate.T,
        grad_up.T,
        grad_down,
    )


def solution(mesh):
    return jax.shard_map(
        local,
        mesh=mesh,
        in_specs=(
            P(("blk", "head"), None),
            P(),
            P(),
            P(("head", "blk")),
            P(None, ("head", "blk")),
            P(None, ("head", "blk")),
            P(None, ("head", "blk")),
            P(("head", "blk")),
            P(("head", "blk")),
            P(("head", "blk"), None),
            P("blk"),
            P(None, ("head", "blk")),
            P(None, ("head", "blk")),
            P(("head", "blk"), None),
            P("blk", None),
        ),
        out_specs=(
            P(("blk", "head"), None),
            P(("blk", "head"), None),
            P(("head", "blk")),
            P(None, ("head", "blk")),
            P(None, ("head", "blk")),
            P(None, ("head", "blk")),
            P(("head", "blk")),
            P(("head", "blk")),
            P(("head", "blk"), None),
            P("blk"),
            P(None, ("head", "blk")),
            P(None, ("head", "blk")),
            P(("head", "blk"), None),
        ),
        check_vma=False,
    )
```

time: 739 us -> 580 us (0.78)
  waiting for transfers between devices: 357 us -> 282 us
  other arithmetic: 70.5 us -> 31.3 us
  starting transfers between devices: 81.9 us -> 52.8 us
  local copies, waits for them, and re-layouts: 71.6 us -> 45.7 us
  between operations: 33.2 us -> 16.2 us
  Pallas kernels: 43.1 us -> 59.7 us
  matrix products: 73.9 us -> 82.5 us
    ppermute x120 -> x96, waiting for transfers between devices: 357 us -> 282 us  [phase(): lax.ppermute(value, move[0], move[1])]
    ppermute x120 -> x96, starting transfers between devices: 81.8 us -> 52.7 us  [phase(): lax.ppermute(value, move[0], move[1])]
    pallas_call x2 -> x17, Pallas kernels: 43.1 us -> 59.7 us  [the longest x4 30.1 us: attend_back(): pl.pallas_call(functools.partial(attend_back_kernel, 512, own, first), gr...]
    convert_element_type x22 -> x18, other arithmetic: 18.6 us -> 7.5 us  [the longest x11 2.63 us: column_scatter(): total.astype(BF16)]
    unnamed x294 -> x203, local copies, waits for them, and re-layouts: 37.6 us -> 28.2 us
    add x15 -> x6, other arithmetic: 9.78 us -> 0.34 us  [the longest x1 0.3 us: plane_scatter(): pieces[source] = pieces[source] + piece.astype(F32)]
    transpose x6 -> x0, other arithmetic: 8.5 us -> none  [the longest x1 3.34 us: local(): grad_up = head_scatter(grad_up.reshape((heads, -1, width)), True).T]
    another operation x11 -> x7, other arithmetic: 8.85 us -> 0.56 us
  transfers between devices with their start and end apart: 122 -> 99, of which waited for: 57 -> 46; matrix products, arithmetic and copies ran while one was open for 27% -> 23% of each run, Pallas kernels for 6% -> 10%
where the time goes in v2:
time: 580 us; the launch traced here: 571 us
  waiting for transfers between devices  282 us (49%)
  matrix products  82.5 us (14%)
  Pallas kernels  59.7 us (10%)
  starting transfers between devices  52.8 us (9%)
  local copies, waits for them, and re-layouts  45.7 us (8%)
  other arithmetic  31.3 us (5%)
  between operations  16.2 us (3%)
    ppermute x96, waiting for transfers between devices, phase(): lax.ppermute(value, move[0], move[1])  282 us
    ppermute x96, starting transfers between devices, phase(): lax.ppermute(value, move[0], move[1])  52.7 us
    dot_general x11, matrix products, col_inner(): lax.dot_general(left, right, CONTRACT_COLS, preferred_element_type=F32)  30.3 us
    pallas_call x4, Pallas kernels, attend_back(): pl.pallas_call(functools.partial(attend_back_kernel, 512, own, first), gr...  30.1 us
    dot_general x14, matrix products, row_outer(): lax.dot_general(left, right, CONTRACT_ROWS, preferred_element_type=F32)  29.4 us
    unnamed x203, local copies, waits for them, and re-layouts  28.2 us
    dot_general x10, matrix products, dot(): return jnp.dot(left, right, preferred_element_type=F32)  22.8 us
    pallas_call x4, Pallas kernels, attend(): pl.pallas_call(functools.partial(attend_kernel, first, last), grid=(rows...  22.1 us
  transfers between devices with their start and end apart: 99, of which 46 were waited for; matrix products, arithmetic and copies ran while one was open for 23% of the time, Pallas kernels for 10%

profile of v2, /device:TPU:0, one launch (start us, length us, event | category | flops | bytes accessed | tf_op | source)
XLA Modules:
  0.0 570.6 jit_solution(1561755151765119152)
XLA Ops:
  39.2 5.2 collective-permute-done.8
  51.4 9.3 %collective-permute-done.11 = bf16[128,2048]{1,0:T(8,128)(2,1)S(1)} collective-permute-done((bf16[128,2048]{1,0:T(8,128)(2,1)S(1)}, bf16[128,2048]{1,0:T(8,128)(2,1)S(1)}, u32[]{:S(2)}, u32[]{:S(2)}) %collective-permute-start.11) | collective-permute-done | bytes 524320 | tf_op jit(solution)/shard_map/ppermute | solution.py:119
  68.7 3.2 fusion
  72.5 4.1 convolution_convert_fusion.refs_0_
  79.1 6.9 %collective-permute-done.18.refs_2_ = bf16[128,1024]{1,0:T(8,128)(2,1)S(1)} collective-permute-done((bf16[128,1024]{1,0:T(8,128)(2,1)S(1)}, bf16[128,1024]{1,0:T(8,128)(2,1)S(1)}, u32[]{:S(2)}, u32[]{:S(2)}) %collective-permute-start.18) | collective-permute-done | bytes 262176 | tf_op jit(solution)/shard_map/ppermute | solution.py:119
  86.0 5.1 collective-permute-done.19.refs_3_
  96.6 5.5 shard_map.258.refs_6_
  103.4 3.6 collective-permute-done.20.refs_1_.refs_2_.k_ref.v_ref
  114.8 5.5 shard_map.259.refs_6_
  120.3 5.5 shard_map.260.refs_6_
  125.9 3.7 collective-permute-done.27
  129.7 5.7 shard_map.261
  135.7 10.2 %collective-permute-done.29 = bf16[128,2048]{1,0:T(8,128)(2,1)S(1)} collective-permute-done((bf16[128,2048]{1,0:T(8,128)(2,1)S(1)}, bf16[128,2048]{1,0:T(8,128)(2,1)S(1)}, u32[]{:S(2)}, u32[]{:S(2)}) %collective-permute-start.29) | collective-permute-done | bytes 524320 | tf_op jit(solution)/shard_map/ppermute | solution.py:119
  147.7 4.4 collective-permute-done.31.refs_2_
  161.0 14.5 %collective-permute-done.35 = bf16[128,2048]{1,0:T(8,128)(2,1)S(1)} collective-permute-done((bf16[128,2048]{1,0:T(8,128)(2,1)S(1)}, bf16[128,2048]{1,0:T(8,128)(2,1)S(1)}, u32[]{:S(2)}, u32[]{:S(2)}) %collective-permute-start.35) | collective-permute-done | bytes 524320 | tf_op jit(solution)/shard_map/ppermute | solution.py:119
  176.4 14.3 %collective-permute-done.37 = bf16[128,2048]{1,0:T(8,128)(2,1)S(1)} collective-permute-done((bf16[128,2048]{1,0:T(8,128)(2,1)S(1)}, bf16[128,2048]{1,0:T(8,128)(2,1)S(1)}, u32[]{:S(2)}, u32[]{:S(2)}) %collective-permute-start.37) | collective-permute-done | bytes 524320 | tf_op jit(solution)/shard_map/ppermute | solution.py:119
  194.1 11.0 %collective-permute-done.39 = bf16[128,2048]{1,0:T(8,128)(2,1)S(1)} collective-permute-done((bf16[128,2048]{1,0:T(8,128)(2,1)S(1)}, bf16[128,2048]{1,0:T(8,128)(2,1)S(1)}, u32[]{:S(2)}, u32[]{:S(2)}) %collective-permute-start.39) | collective-permute-done | bytes 524320 | tf_op jit(solution)/shard_map/ppermute | solution.py:119
  208.7 13.3 %collective-permute-done.42 = bf16[128,2048]{1,0:T(8,128)(2,1)} collective-permute-done((bf16[128,2048]{1,0:T(8,128)(2,1)S(1)}, bf16[128,2048]{1,0:T(8,128)(2,1)}, u32[]{:S(2)}, u32[]{:S(2)}) %collective-permute-start.42) | collective-permute-done | bytes 524320 | tf_op jit(solution)/shard_map/ppermute | solution.py:119
  222.0 4.3 fusion.85
  226.5 3.1 fusion.99
  229.6 13.2 %collective-permute-done.44 = bf16[128,2048]{1,0:T(8,128)(2,1)S(1)} collective-permute-done((bf16[128,2048]{1,0:T(8,128)(2,1)}, bf16[128,2048]{1,0:T(8,128)(2,1)S(1)}, u32[]{:S(2)}, u32[]{:S(2)}) %collective-permute-start.44) | collective-permute-done | bytes 524320 | tf_op jit(solution)/shard_map/ppermute | solution.py:119
  248.3 3.0 fusion.82
  251.3 3.4 multiply_convert_fusion.3
  262.4 4.5 fusion.97
  275.8 5.5 multiply_convert_fusion.2
  285.3 13.6 %collective-permute-done.49 = bf16[128,2048]{1,0:T(8,128)(2,1)S(1)} collective-permute-done((bf16[128,2048]{1,0:T(8,128)(2,1)S(1)}, bf16[128,2048]{1,0:T(8,128)(2,1)S(1)}, u32[]{:S(2)}, u32[]{:S(2)}) %collective-permute-start.49) | collective-permute-done | bytes 524320 | tf_op jit(solution)/shard_map/ppermute | solution.py:119
  305.2 4.7 add_convert_fusion.2
  309.9 10.3 %collective-permute-done.51 = bf16[128,2048]{1,0:T(8,128)(2,1)S(1)} collective-permute-done((bf16[128,2048]{1,0:T(8,128)(2,1)S(1)}, bf16[128,2048]{1,0:T(8,128)(2,1)S(1)}, u32[]{:S(2)}, u32[]{:S(2)}) %collective-permute-start.51) | collective-permute-done | bytes 524320 | tf_op jit(solution)/shard_map/ppermute | solution.py:119
  322.4 13.4 %collective-permute-done.53 = bf16[128,2048]{1,0:T(8,128)(2,1)S(1)} collective-permute-done((bf16[128,2048]{1,0:T(8,128)(2,1)S(1)}, bf16[128,2048]{1,0:T(8,128)(2,1)S(1)}, u32[]{:S(2)}, u32[]{:S(2)}) %collective-permute-start.53) | collective-permute-done | bytes 524320 | tf_op jit(solution)/shard_map/ppermute | solution.py:119
  341.1 14.2 %collective-permute-done.56 = bf16[128,2048]{1,0:T(8,128)(2,1)} collective-permute-done((bf16[128,2048]{1,0:T(8,128)(2,1)S(1)}, bf16[128,2048]{1,0:T(8,128)(2,1)}, u32[]{:S(2)}, u32[]{:S(2)}) %collective-permute-start.56) | collective-permute-done | bytes 524320 | tf_op jit(solution)/shard_map/ppermute | solution.py:119
  355.3 4.0 pad_maximum_fusion
  359.2 12.5 %collective-permute-done.58 = bf16[128,2048]{1,0:T(8,128)(2,1)} collective-permute-done((bf16[128,2048]{1,0:T(8,128)(2,1)}, bf16[128,2048]{1,0:T(8,128)(2,1)}, u32[]{:S(2)}, u32[]{:S(2)}) %collective-permute-start.58) | collective-permute-done | bytes 524320 | tf_op jit(solution)/shard_map/ppermute | solution.py:119
  371.8 3.1 fusion.54
  384.0 11.6 %collective-permute-done.60 = bf16[128,2048]{1,0:T(8,128)(2,1)S(1)} collective-permute-done((bf16[128,2048]{1,0:T(8,128)(2,1)}, bf16[128,2048]{1,0:T(8,128)(2,1)S(1)}, u32[]{:S(2)}, u32[]{:S(2)}) %collective-permute-start.60) | collective-permute-done | bytes 524320 | tf_op jit(solution)/shard_map/ppermute | solution.py:119
  402.6 3.7 collective-permute-done.63.refs_2_
  410.2 7.7 %shard_map.266 = (f32[2048,128]{1,0:T(8,128)S(1)}, f32[1024,128]{1,0:T(8,128)S(1)}, f32[1024,128]{1,0:T(8,128)S(1)}, f32[8,2048]{1,0:T(8,128)S(1)}) custom-call(bf16[2048,128]{1,0:T(8,128)(2,1)S(1)} %copy-done.12, bf16[2048,128]{1,0:T(8,128)(2,1)S(1)} %shard_map.265.g_ref, f32[8,2048]{1,0:T(8,128)S(1)} %get-tuple-element.588.log_ref.extra_ref, ...), custom_call_target="tpu_custom_call" | custom-call | flops 8589934592 | bytes 1048576 | tf_op jit(solution)/shard_map/pallas_call | solution.py:635
  418.0 7.5 %shard_map.267 = (f32[2048,128]{1,0:T(8,128)S(1)}, f32[1024,128]{1,0:T(8,128)S(1)}, f32[1024,128]{1,0:T(8,128)S(1)}) custom-call(bf16[2048,128]{1,0:T(8,128)(2,1)S(1)} %copy-done.12, bf16[2048,128]{1,0:T(8,128)(2,1)S(1)} %shard_map.265.g_ref, f32[8,2048]{1,0:T(8,128)S(1)} %get-tuple-element.588.log_ref.extra_ref, ...), custom_call_target="tpu_custom_call" | custom-call | flops 8589934592 | bytes 1048576 | tf_op jit(solution)/shard_map/pallas_call | solution.py:635
  428.4 7.5 %shard_map.268 = (f32[2048,128]{1,0:T(8,128)S(1)}, f32[1024,128]{1,0:T(8,128)S(1)}, f32[1024,128]{1,0:T(8,128)S(1)}) custom-call(bf16[2048,128]{1,0:T(8,128)(2,1)S(1)} %copy-done.12, bf16[2048,128]{1,0:T(8,128)(2,1)S(1)} %shard_map.265.g_ref, f32[8,2048]{1,0:T(8,128)S(1)} %get-tuple-element.588.log_ref.extra_ref, ...), custom_call_target="tpu_custom_call" | custom-call | flops 8589934592 | bytes 1048576 | tf_op jit(solution)/shard_map/pallas_call | solution.py:635
  436.0 7.4 %collective-permute-done.70 = bf16[128,2048]{1,0:T(8,128)(2,1)S(1)} collective-permute-done((bf16[128,2048]{1,0:T(8,128)(2,1)S(1)}, bf16[128,2048]{1,0:T(8,128)(2,1)S(1)}, u32[]{:S(2)}, u32[]{:S(2)}) %collective-permute-start.70) | collective-permute-done | bytes 524320 | tf_op jit(solution)/shard_map/ppermute | solution.py:119
  446.4 7.5 %shard_map.269 = (f32[2048,128]{1,0:T(8,128)S(1)}, f32[1024,128]{1,0:T(8,128)S(1)}, f32[1024,128]{1,0:T(8,128)S(1)}) custom-call(bf16[2048,128]{1,0:T(8,128)(2,1)S(1)} %copy-done.12, bf16[2048,128]{1,0:T(8,128)(2,1)S(1)} %shard_map.265.g_ref, f32[8,2048]{1,0:T(8,128)S(1)} %get-tuple-element.588.log_ref.extra_ref, ...), custom_call_target="tpu_custom_call" | custom-call | flops 8589934592 | bytes 1048576 | tf_op jit(solution)/shard_map/pallas_call | solution.py:635
  453.9 15.4 %collective-permute-done.72.refs_7_ = bf16[1024,256]{1,0:T(8,128)(2,1)S(1)} collective-permute-done((bf16[1024,256]{1,0:T(8,128)(2,1)S(1)}, bf16[1024,256]{1,0:T(8,128)(2,1)S(1)}, u32[]{:S(2)}, u32[]{:S(2)}) %collective-permute-start.72) | collective-permute-done | bytes 524320 | tf_op jit(solution)/shard_map/ppermute | solution.py:119
  475.7 6.1 %collective-permute-done.77.refs_2_ = bf16[128,1024]{1,0:T(8,128)(2,1)S(1)} collective-permute-done((bf16[128,1024]{1,0:T(8,128)(2,1)S(1)}, bf16[128,1024]{1,0:T(8,128)(2,1)S(1)}, u32[]{:S(2)}, u32[]{:S(2)}) %collective-permute-start.77) | collective-permute-done | bytes 262176 | tf_op jit(solution)/shard_map/ppermute | solution.py:119
  481.8 4.7 collective-permute-done.78.refs_3_
  495.6 4.2 fusion.88
  500.7 10.3 %collective-permute-done.80 = bf16[128,2048]{1,0:T(8,128)(2,1)S(1)} collective-permute-done((bf16[128,2048]{1,0:T(8,128)(2,1)S(1)}, bf16[128,2048]{1,0:T(8,128)(2,1)S(1)}, u32[]{:S(2)}, u32[]{:S(2)}) %collective-permute-start.80) | collective-permute-done | bytes 524320 | tf_op jit(solution)/shard_map/ppermute | solution.py:119
  520.9 10.0 %collective-permute-done.85 = f32[34,128]{1,0:T(8,128)S(1)} collective-permute-done((f32[34,128]{1,0:T(8,128)S(1)}, f32[34,128]{1,0:T(8,128)S(1)}, u32[]{:S(2)}, u32[]{:S(2)}) %collective-permute-start.85) | collective-permute-done | bytes 17440 | tf_op jit(solution)/shard_map/ppermute | solution.py:119
  540.7 13.2 %collective-permute-done.88 = bf16[128,2048]{1,0:T(8,128)(2,1)S(1)} collective-permute-done((bf16[128,2048]{1,0:T(8,128)(2,1)S(1)}, bf16[128,2048]{1,0:T(8,128)(2,1)S(1)}, u32[]{:S(2)}, u32[]{:S(2)}) %collective-permute-start.88) | collective-permute-done | bytes 524320 | tf_op jit(solution)/shard_map/ppermute | solution.py:119
  554.1 3.7 collective-permute-start.95
  (507 shorter events, 190.2 us)
Async XLA Ops:
  7.3 147.6 %all-gather.4.cloned.1.call-start = ((), (), s32[]{:S(2)}) async-start(), calls=%async_computation.1 | async-start | bytes 1310720 | tf_op jit(solution)/shard_map/all_gather | solution.py:738
  9.4 15.1 %collective-permute-start = (bf16[128,2048]{1,0:T(8,128)(2,1)}, bf16[128,2048]{1,0:T(8,128)(2,1)}, u32[]{:S(2)}, u32[]{:S(2)}) collective-permute-start(bf16[128,2048]{1,0:T(8,128)(2,1)} %param.16), channel_id=1, source_target_pairs={{0,1},{1,0},{2,3},{3,2},{4,5},{5,4},{6,7},{7,6},{8,9},{9,8},{10,11... | collective-permute-start | bytes 1572872 | tf_op jit(solution)/shard_map/ppermute | solution.py:119
  9.8 17.5 %collective-permute-start.1 = (bf16[128,2048]{1,0:T(8,128)(2,1)}, bf16[128,2048]{1,0:T(8,128)(2,1)}, u32[]{:S(2)}, u32[]{:S(2)}) collective-permute-start(bf16[128,2048]{1,0:T(8,128)(2,1)} %param.16), channel_id=1, source_target_pairs={{0,2},{1,3},{2,4},{3,5},{4,6},{5,7},{6,0},{7,1},{8,10},{9,11},{10,... | collective-permute-start | bytes 1572872 | tf_op jit(solution)/shard_map/ppermute | solution.py:119
  12.4 14.9 %collective-permute-start.2 = (bf16[128,2048]{1,0:T(8,128)(2,1)}, bf16[128,2048]{1,0:T(8,128)(2,1)S(1)}, u32[]{:S(2)}, u32[]{:S(2)}) collective-permute-start(bf16[128,2048]{1,0:T(8,128)(2,1)} %pad_maximum_fusion.6), channel_id=1, source_target_pairs={{0,8},{8,0},{16,24},{24,16},{1,9},{9,1},{17,25},{25,17},{2,10},{10... | collective-permute-start | bytes 1572872 | tf_op jit(solution)/shard_map/ppermute | solution.py:119
  28.0 16.5 %collective-permute-start.4 = (bf16[128,2048]{1,0:T(8,128)(2,1)}, bf16[128,2048]{1,0:T(8,128)(2,1)}, u32[]{:S(2)}, u32[]{:S(2)}) collective-permute-start(bf16[128,2048]{1,0:T(8,128)(2,1)} %collective-permute-done.1), channel_id=1, source_target_pairs={{0,1},{1,0},{2,3},{3,2},{4,5},{5,4},{6,7},{7,6},{8,9},{9,8},{10,11... | collective-permute-start | bytes 1572872 | tf_op jit(solution)/shard_map/ppermute | solution.py:119
  28.0 16.5 %collective-permute-start.5 = (bf16[128,2048]{1,0:T(8,128)(2,1)}, bf16[128,2048]{1,0:T(8,128)(2,1)S(1)}, u32[]{:S(2)}, u32[]{:S(2)}) collective-permute-start(bf16[128,2048]{1,0:T(8,128)(2,1)} %collective-permute-done.1), channel_id=1, source_target_pairs={{0,2},{1,3},{2,4},{3,5},{4,6},{5,7},{6,0},{7,1},{8,10},{9,11},{10,... | collective-permute-start | bytes 1572872 | tf_op jit(solution)/shard_map/ppermute | solution.py:119
  29.6 14.9 %collective-permute-start.6 = (bf16[128,2048]{1,0:T(8,128)(2,1)S(1)}, bf16[128,2048]{1,0:T(8,128)(2,1)S(1)}, u32[]{:S(2)}, u32[]{:S(2)}) collective-permute-start(bf16[128,2048]{1,0:T(8,128)(2,1)S(1)} %collective-permute-done.2), channel_id=1, source_target_pairs={{0,16},{8,24},{16,0},{24,8},{1,17},{9,25},{17,1},{25,9},{2,18},{10... | collective-permute-start | bytes 1572872 | tf_op jit(solution)/shard_map/ppermute | solution.py:119
  44.6 16.1 %collective-permute-start.11 = (bf16[128,2048]{1,0:T(8,128)(2,1)S(1)}, bf16[128,2048]{1,0:T(8,128)(2,1)S(1)}, u32[]{:S(2)}, u32[]{:S(2)}) collective-permute-start(bf16[128,2048]{1,0:T(8,128)(2,1)S(1)} %collective-permute-done.5), channel_id=1, source_target_pairs={{0,2},{1,3},{2,4},{3,5},{4,6},{5,7},{6,0},{7,1},{8,10},{9,11},{10,... | collective-permute-start | bytes 1572872 | tf_op jit(solution)/shard_map/ppermute | solution.py:119
  67.7 154.2 %all-gather.6.cloned.1.call-start = ((), (), s32[]{:S(2)}) async-start(), calls=%async_computation.2 | async-start | bytes 11796480 | tf_op jit(solution)/shard_map/all_gather | solution.py:849
  94.8 16.2 %collective-permute-start.23 = (bf16[128,2048]{1,0:T(8,128)(2,1)S(1)}, bf16[128,2048]{1,0:T(8,128)(2,1)}, u32[]{:S(2)}, u32[]{:S(2)}) collective-permute-start(bf16[128,2048]{1,0:T(8,128)(2,1)S(1)} %constant_dynamic-slice_fusion), channel_id=1, source_target_pairs={{0,2},{1,3},{2,4},{3,5},{4,6},{5,7},{6,0},{7,1},{8,10},{9,11},{10,... | collective-permute-start | bytes 1572872 | tf_op jit(solution)/shard_map/ppermute | solution.py:119
  111.1 422.0 %reduce-scatter.4.cloned.1.call-start = ((), (), s32[]{:S(2)}) async-start(), calls=%async_computation.3 | async-start | bytes 11796480
  111.2 14.6 %collective-permute-start.24 = (bf16[1024,128]{1,0:T(8,128)(2,1)S(1)}, bf16[1024,128]{1,0:T(8,128)(2,1)S(1)}, u32[]{:S(2)}, u32[]{:S(2)}) collective-permute-start(bf16[1024,128]{1,0:T(8,128)(2,1)S(1)} %slice.256), channel_id=1, source_target_pairs={{0,16},{8,24},{16,0},{24,8},{1,17},{9,25},{17,1},{25,9},{2,18},{10... | collective-permute-start | bytes 786440 | tf_op jit(solution)/shard_map/ppermute | solution.py:119
  113.2 16.3 %collective-permute-start.27 = (bf16[128,2048]{1,0:T(8,128)(2,1)}, bf16[128,2048]{1,0:T(8,128)(2,1)S(1)}, u32[]{:S(2)}, u32[]{:S(2)}) collective-permute-start(bf16[128,2048]{1,0:T(8,128)(2,1)} %collective-permute-done.23), channel_id=1, source_target_pairs={{0,2},{1,3},{2,4},{3,5},{4,6},{5,7},{6,0},{7,1},{8,10},{9,11},{10,... | collective-permute-start | bytes 1572872 | tf_op jit(solution)/shard_map/ppermute | solution.py:119
  129.5 16.3 %collective-permute-start.29 = (bf16[128,2048]{1,0:T(8,128)(2,1)S(1)}, bf16[128,2048]{1,0:T(8,128)(2,1)S(1)}, u32[]{:S(2)}, u32[]{:S(2)}) collective-permute-start(bf16[128,2048]{1,0:T(8,128)(2,1)S(1)} %collective-permute-done.27), channel_id=1, source_target_pairs={{0,2},{1,3},{2,4},{3,5},{4,6},{5,7},{6,0},{7,1},{8,10},{9,11},{10,... | collective-permute-start | bytes 1572872 | tf_op jit(solution)/shard_map/ppermute | solution.py:119
  159.6 15.9 %collective-permute-start.35 = (bf16[128,2048]{1,0:T(8,128)(2,1)S(1)}, bf16[128,2048]{1,0:T(8,128)(2,1)S(1)}, u32[]{:S(2)}, u32[]{:S(2)}) collective-permute-start(bf16[128,2048]{1,0:T(8,128)(2,1)S(1)} %fusion.31), channel_id=1, source_target_pairs={{0,2},{1,3},{2,4},{3,5},{4,6},{5,7},{6,0},{7,1},{8,10},{9,11},{10,... | collective-permute-start | bytes 1572872 | tf_op jit(solution)/shard_map/ppermute | solution.py:119
  160.4 15.0 %collective-permute-start.36 = (bf16[128,2048]{1,0:T(8,128)(2,1)S(1)}, bf16[128,2048]{1,0:T(8,128)(2,1)S(1)}, u32[]{:S(2)}, u32[]{:S(2)}) collective-permute-start(bf16[128,2048]{1,0:T(8,128)(2,1)S(1)} %slice.502), channel_id=1, source_target_pairs={{0,1},{1,0},{2,3},{3,2},{4,5},{5,4},{6,7},{7,6},{8,9},{9,8},{10,11... | collective-permute-start | bytes 1572872 | tf_op jit(solution)/shard_map/ppermute | solution.py:119
  175.7 15.1 %collective-permute-start.37 = (bf16[128,2048]{1,0:T(8,128)(2,1)S(1)}, bf16[128,2048]{1,0:T(8,128)(2,1)S(1)}, u32[]{:S(2)}, u32[]{:S(2)}) collective-permute-start(bf16[128,2048]{1,0:T(8,128)(2,1)S(1)} %fusion.33), channel_id=1, source_target_pairs={{0,2},{1,3},{2,4},{3,5},{4,6},{5,7},{6,0},{7,1},{8,10},{9,11},{10,... | collective-permute-start | bytes 1572872 | tf_op jit(solution)/shard_map/ppermute | solution.py:119
  175.7 15.0 %collective-permute-start.38 = (bf16[128,2048]{1,0:T(8,128)(2,1)S(1)}, bf16[128,2048]{1,0:T(8,128)(2,1)S(1)}, u32[]{:S(2)}, u32[]{:S(2)}) collective-permute-start(bf16[128,2048]{1,0:T(8,128)(2,1)S(1)} %slice.501), channel_id=1, source_target_pairs={{0,1},{1,0},{2,3},{3,2},{4,5},{5,4},{6,7},{7,6},{8,9},{9,8},{10,11... | collective-permute-start | bytes 1572872 | tf_op jit(solution)/shard_map/ppermute | solution.py:119
  205.8 16.2 %collective-permute-start.42 = (bf16[128,2048]{1,0:T(8,128)(2,1)S(1)}, bf16[128,2048]{1,0:T(8,128)(2,1)}, u32[]{:S(2)}, u32[]{:S(2)}) collective-permute-start(bf16[128,2048]{1,0:T(8,128)(2,1)S(1)} %multiply_convert_fusion.6), channel_id=1, source_target_pairs={{0,2},{1,3},{2,4},{3,5},{4,6},{5,7},{6,0},{7,1},{8,10},{9,11},{10,... | collective-permute-start | bytes 1572872 | tf_op jit(solution)/shard_map/ppermute | solution.py:119
  226.4 16.3 %collective-permute-start.44 = (bf16[128,2048]{1,0:T(8,128)(2,1)}, bf16[128,2048]{1,0:T(8,128)(2,1)S(1)}, u32[]{:S(2)}, u32[]{:S(2)}) collective-permute-start(bf16[128,2048]{1,0:T(8,128)(2,1)} %collective-permute-done.42), channel_id=1, source_target_pairs={{0,2},{1,3},{2,4},{3,5},{4,6},{5,7},{6,0},{7,1},{8,10},{9,11},{10,... | collective-permute-start | bytes 1572872 | tf_op jit(solution)/shard_map/ppermute | solution.py:119
  243.6 14.7 %collective-permute-start.45 = (bf16[128,2048]{1,0:T(8,128)(2,1)S(1)}, bf16[128,2048]{1,0:T(8,128)(2,1)S(1)}, u32[]{:S(2)}, u32[]{:S(2)}) collective-permute-start(bf16[128,2048]{1,0:T(8,128)(2,1)S(1)} %collective-permute-done.44), channel_id=1, source_target_pairs={{0,1},{1,0},{2,3},{3,2},{4,5},{5,4},{6,7},{7,6},{8,9},{9,8},{10,11... | collective-permute-start | bytes 1572872 | tf_op jit(solution)/shard_map/ppermute | solution.py:119
  243.6 16.5 %collective-permute-start.46 = (bf16[128,2048]{1,0:T(8,128)(2,1)S(1)}, bf16[128,2048]{1,0:T(8,128)(2,1)S(1)}, u32[]{:S(2)}, u32[]{:S(2)}) collective-permute-start(bf16[128,2048]{1,0:T(8,128)(2,1)S(1)} %collective-permute-done.44), channel_id=1, source_target_pairs={{0,2},{1,3},{2,4},{3,5},{4,6},{5,7},{6,0},{7,1},{8,10},{9,11},{10,... | collective-permute-start | bytes 1572872 | tf_op jit(solution)/shard_map/ppermute | solution.py:119
  283.3 15.6 %collective-permute-start.49 = (bf16[128,2048]{1,0:T(8,128)(2,1)S(1)}, bf16[128,2048]{1,0:T(8,128)(2,1)S(1)}, u32[]{:S(2)}, u32[]{:S(2)}) collective-permute-start(bf16[128,2048]{1,0:T(8,128)(2,1)S(1)} %add_convert_fusion.6), channel_id=1, source_target_pairs={{0,2},{1,3},{2,4},{3,5},{4,6},{5,7},{6,0},{7,1},{8,10},{9,11},{10,... | collective-permute-start | bytes 1572872 | tf_op jit(solution)/shard_map/ppermute | solution.py:119
  303.8 16.4 %collective-permute-start.51 = (bf16[128,2048]{1,0:T(8,128)(2,1)S(1)}, bf16[128,2048]{1,0:T(8,128)(2,1)S(1)}, u32[]{:S(2)}, u32[]{:S(2)}) collective-permute-start(bf16[128,2048]{1,0:T(8,128)(2,1)S(1)} %fusion.30), channel_id=1, source_target_pairs={{0,2},{1,3},{2,4},{3,5},{4,6},{5,7},{6,0},{7,1},{8,10},{9,11},{10,... | collective-permute-start | bytes 1572872 | tf_op jit(solution)/shard_map/ppermute | solution.py:119
  304.1 16.1 %collective-permute-start.52 = (bf16[128,2048]{1,0:T(8,128)(2,1)S(1)}, bf16[128,2048]{1,0:T(8,128)(2,1)S(1)}, u32[]{:S(2)}, u32[]{:S(2)}) collective-permute-start(bf16[128,2048]{1,0:T(8,128)(2,1)S(1)} %get-tuple-element.531), channel_id=1, source_target_pairs={{0,1},{1,0},{2,3},{3,2},{4,5},{5,4},{6,7},{7,6},{8,9},{9,8},{10,11... | collective-permute-start | bytes 1572872 | tf_op jit(solution)/shard_map/ppermute | solution.py:119
  320.4 15.4 %collective-permute-start.53 = (bf16[128,2048]{1,0:T(8,128)(2,1)S(1)}, bf16[128,2048]{1,0:T(8,128)(2,1)S(1)}, u32[]{:S(2)}, u32[]{:S(2)}) collective-permute-start(bf16[128,2048]{1,0:T(8,128)(2,1)S(1)} %fusion.28), channel_id=1, source_target_pairs={{0,2},{1,3},{2,4},{3,5},{4,6},{5,7},{6,0},{7,1},{8,10},{9,11},{10,... | collective-permute-start | bytes 1572872 | tf_op jit(solution)/shard_map/ppermute | solution.py:119
  320.5 15.3 %collective-permute-start.54 = (bf16[128,2048]{1,0:T(8,128)(2,1)S(1)}, bf16[128,2048]{1,0:T(8,128)(2,1)S(1)}, u32[]{:S(2)}, u32[]{:S(2)}) collective-permute-start(bf16[128,2048]{1,0:T(8,128)(2,1)S(1)} %copy-done.58), channel_id=1, source_target_pairs={{0,1},{1,0},{2,3},{3,2},{4,5},{5,4},{6,7},{7,6},{8,9},{9,8},{10,11... | collective-permute-start | bytes 1572872 | tf_op jit(solution)/shard_map/ppermute | solution.py:119
  339.0 16.2 %collective-permute-start.56 = (bf16[128,2048]{1,0:T(8,128)(2,1)S(1)}, bf16[128,2048]{1,0:T(8,128)(2,1)}, u32[]{:S(2)}, u32[]{:S(2)}) collective-permute-start(bf16[128,2048]{1,0:T(8,128)(2,1)S(1)} %get-tuple-element.550), channel_id=1, source_target_pairs={{0,2},{1,3},{2,4},{3,5},{4,6},{5,7},{6,0},{7,1},{8,10},{9,11},{10,... | collective-permute-start | bytes 1572872 | tf_op jit(solution)/shard_map/ppermute | solution.py:119
  355.3 16.4 %collective-permute-start.58 = (bf16[128,2048]{1,0:T(8,128)(2,1)}, bf16[128,2048]{1,0:T(8,128)(2,1)}, u32[]{:S(2)}, u32[]{:S(2)}) collective-permute-start(bf16[128,2048]{1,0:T(8,128)(2,1)} %collective-permute-done.56), channel_id=1, source_target_pairs={{0,2},{1,3},{2,4},{3,5},{4,6},{5,7},{6,0},{7,1},{8,10},{9,11},{10,... | collective-permute-start | bytes 1572872 | tf_op jit(solution)/shard_map/ppermute | solution.py:119
  379.3 16.3 %collective-permute-start.60 = (bf16[128,2048]{1,0:T(8,128)(2,1)}, bf16[128,2048]{1,0:T(8,128)(2,1)S(1)}, u32[]{:S(2)}, u32[]{:S(2)}) collective-permute-start(bf16[128,2048]{1,0:T(8,128)(2,1)} %collective-permute-done.58), channel_id=1, source_target_pairs={{0,2},{1,3},{2,4},{3,5},{4,6},{5,7},{6,0},{7,1},{8,10},{9,11},{10,... | collective-permute-start | bytes 1572872 | tf_op jit(solution)/shard_map/ppermute | solution.py:119
  407.9 17.6 %collective-permute-start.66 = (bf16[128,2048]{1,0:T(8,128)(2,1)S(1)}, bf16[128,2048]{1,0:T(8,128)(2,1)S(1)}, u32[]{:S(2)}, u32[]{:S(2)}) collective-permute-start(bf16[128,2048]{1,0:T(8,128)(2,1)S(1)} %add_convert_fusion.5), channel_id=1, source_target_pairs={{0,2},{1,3},{2,4},{3,5},{4,6},{5,7},{6,0},{7,1},{8,10},{9,11},{10,... | collective-permute-start | bytes 1572872 | tf_op jit(solution)/shard_map/ppermute | solution.py:119
  408.6 16.9 %collective-permute-start.67 = (bf16[128,2048]{1,0:T(8,128)(2,1)S(1)}, bf16[128,2048]{1,0:T(8,128)(2,1)S(1)}, u32[]{:S(2)}, u32[]{:S(2)}) collective-permute-start(bf16[128,2048]{1,0:T(8,128)(2,1)S(1)} %slice.498), channel_id=1, source_target_pairs={{0,1},{1,0},{2,3},{3,2},{4,5},{5,4},{6,7},{7,6},{8,9},{9,8},{10,11... | collective-permute-start | bytes 1572872 | tf_op jit(solution)/shard_map/ppermute | solution.py:119
  428.1 15.3 %collective-permute-start.70 = (bf16[128,2048]{1,0:T(8,128)(2,1)S(1)}, bf16[128,2048]{1,0:T(8,128)(2,1)S(1)}, u32[]{:S(2)}, u32[]{:S(2)}) collective-permute-start(bf16[128,2048]{1,0:T(8,128)(2,1)S(1)} %add_convert_fusion.4), channel_id=1, source_target_pairs={{0,2},{1,3},{2,4},{3,5},{4,6},{5,7},{6,0},{7,1},{8,10},{9,11},{10,... | collective-permute-start | bytes 1572872 | tf_op jit(solution)/shard_map/ppermute | solution.py:119
  428.4 15.0 %collective-permute-start.71 = (bf16[128,2048]{1,0:T(8,128)(2,1)S(1)}, bf16[128,2048]{1,0:T(8,128)(2,1)S(1)}, u32[]{:S(2)}, u32[]{:S(2)}) collective-permute-start(bf16[128,2048]{1,0:T(8,128)(2,1)S(1)} %slice.497), channel_id=1, source_target_pairs={{0,1},{1,0},{2,3},{3,2},{4,5},{5,4},{6,7},{7,6},{8,9},{9,8},{10,11... | collective-permute-start | bytes 1572872 | tf_op jit(solution)/shard_map/ppermute | solution.py:119
  443.9 25.3 %collective-permute-start.72 = (bf16[1024,256]{1,0:T(8,128)(2,1)S(1)}, bf16[1024,256]{1,0:T(8,128)(2,1)S(1)}, u32[]{:S(2)}, u32[]{:S(2)}) collective-permute-start(bf16[1024,256]{1,0:T(8,128)(2,1)S(1)} %pad_maximum_fusion.7), channel_id=1, source_target_pairs={{0,8},{8,0},{16,24},{24,16},{1,9},{9,1},{17,25},{25,17},{2,10},{10... | collective-permute-start | bytes 1572872 | tf_op jit(solution)/shard_map/ppermute | solution.py:119
  445.8 25.1 %collective-permute-start.73 = (bf16[1024,256]{1,0:T(8,128)(2,1)S(1)}, bf16[1024,256]{1,0:T(8,128)(2,1)S(1)}, u32[]{:S(2)}, u32[]{:S(2)}) collective-permute-start(bf16[1024,256]{1,0:T(8,128)(2,1)S(1)} %pad_maximum_fusion.8), channel_id=1, source_target_pairs={{0,16},{8,24},{16,0},{24,8},{1,17},{9,25},{17,1},{25,9},{2,18},{10... | collective-permute-start | bytes 1572872 | tf_op jit(solution)/shard_map/ppermute | solution.py:119
  446.1 24.8 %collective-permute-start.74 = (bf16[128,2048]{1,0:T(8,128)(2,1)S(1)}, bf16[128,2048]{1,0:T(8,128)(2,1)S(1)}, u32[]{:S(2)}, u32[]{:S(2)}) collective-permute-start(bf16[128,2048]{1,0:T(8,128)(2,1)S(1)} %add_convert_fusion.3), channel_id=1, source_target_pairs={{0,2},{1,3},{2,4},{3,5},{4,6},{5,7},{6,0},{7,1},{8,10},{9,11},{10,... | collective-permute-start | bytes 1572872 | tf_op jit(solution)/shard_map/ppermute | solution.py:119
  446.3 24.6 %collective-permute-start.75 = (bf16[128,2048]{1,0:T(8,128)(2,1)S(1)}, bf16[128,2048]{1,0:T(8,128)(2,1)S(1)}, u32[]{:S(2)}, u32[]{:S(2)}) collective-permute-start(bf16[128,2048]{1,0:T(8,128)(2,1)S(1)} %slice.496), channel_id=1, source_target_pairs={{0,1},{1,0},{2,3},{3,2},{4,5},{5,4},{6,7},{7,6},{8,9},{9,8},{10,11... | collective-permute-start | bytes 1572872 | tf_op jit(solution)/shard_map/ppermute | solution.py:119
  495.0 15.9 %collective-permute-start.80 = (bf16[128,2048]{1,0:T(8,128)(2,1)S(1)}, bf16[128,2048]{1,0:T(8,128)(2,1)S(1)}, u32[]{:S(2)}, u32[]{:S(2)}) collective-permute-start(bf16[128,2048]{1,0:T(8,128)(2,1)S(1)} %fusion.21), channel_id=1, source_target_pairs={{0,2},{1,3},{2,4},{3,5},{4,6},{5,7},{6,0},{7,1},{8,10},{9,11},{10,... | collective-permute-start | bytes 1572872 | tf_op jit(solution)/shard_map/ppermute | solution.py:119
  495.4 15.6 %collective-permute-start.81 = (bf16[128,2048]{1,0:T(8,128)(2,1)S(1)}, bf16[128,2048]{1,0:T(8,128)(2,1)S(1)}, u32[]{:S(2)}, u32[]{:S(2)}) collective-permute-start(bf16[128,2048]{1,0:T(8,128)(2,1)S(1)} %slice.494), channel_id=1, source_target_pairs={{0,1},{1,0},{2,3},{3,2},{4,5},{5,4},{6,7},{7,6},{8,9},{9,8},{10,11... | collective-permute-start | bytes 1572872 | tf_op jit(solution)/shard_map/ppermute | solution.py:119
  511.2 19.8 %collective-permute-start.87 = (bf16[192,2048]{1,0:T(8,128)(2,1)S(1)}, bf16[192,2048]{1,0:T(8,128)(2,1)S(1)}, u32[]{:S(2)}, u32[]{:S(2)}) collective-permute-start(bf16[192,2048]{1,0:T(8,128)(2,1)S(1)} %pad_maximum_fusion.4), channel_id=1, source_target_pairs={{0,16},{8,24},{16,0},{24,8},{1,17},{9,25},{17,1},{25,9},{2,18},{10... | collective-permute-start | bytes 2359304 | tf_op jit(solution)/shard_map/ppermute | solution.py:119
  515.8 15.1 %collective-permute-start.82 = (bf16[128,2048]{1,0:T(8,128)(2,1)S(1)}, bf16[128,2048]{1,0:T(8,128)(2,1)S(1)}, u32[]{:S(2)}, u32[]{:S(2)}) collective-permute-start(bf16[128,2048]{1,0:T(8,128)(2,1)S(1)} %fusion.23), channel_id=1, source_target_pairs={{0,2},{1,3},{2,4},{3,5},{4,6},{5,7},{6,0},{7,1},{8,10},{9,11},{10,... | collective-permute-start | bytes 1572872 | tf_op jit(solution)/shard_map/ppermute | solution.py:119
  516.0 14.9 %collective-permute-start.83 = (bf16[128,2048]{1,0:T(8,128)(2,1)S(1)}, bf16[128,2048]{1,0:T(8,128)(2,1)S(1)}, u32[]{:S(2)}, u32[]{:S(2)}) collective-permute-start(bf16[128,2048]{1,0:T(8,128)(2,1)S(1)} %slice.493), channel_id=1, source_target_pairs={{0,1},{1,0},{2,3},{3,2},{4,5},{5,4},{6,7},{7,6},{8,9},{9,8},{10,11... | collective-permute-start | bytes 1572872 | tf_op jit(solution)/shard_map/ppermute | solution.py:119
  516.3 14.7 %collective-permute-start.85 = (f32[34,128]{1,0:T(8,128)S(1)}, f32[34,128]{1,0:T(8,128)S(1)}, u32[]{:S(2)}, u32[]{:S(2)}) collective-permute-start(f32[34,128]{1,0:T(8,128)S(1)} %maximum_bitcast_fusion), channel_id=1, source_target_pairs={{0,16},{8,24},{16,0},{24,8},{1,17},{9,25},{17,1},{25,9},{2,18},{10... | collective-permute-start | bytes 52232 | tf_op jit(solution)/shard_map/ppermute | solution.py:119
  535.5 18.4 %collective-permute-start.91 = (bf16[192,2048]{1,0:T(8,128)(2,1)S(1)}, bf16[192,2048]{1,0:T(8,128)(2,1)S(1)}, u32[]{:S(2)}, u32[]{:S(2)}) collective-permute-start(bf16[192,2048]{1,0:T(8,128)(2,1)S(1)} %copy-done.48), channel_id=1, source_target_pairs={{0,8},{8,0},{16,24},{24,16},{1,9},{9,1},{17,25},{25,17},{2,10},{10... | collective-permute-start | bytes 2359304 | tf_op jit(solution)/shard_map/ppermute | solution.py:119
  536.2 17.7 %collective-permute-start.92 = (bf16[192,2048]{1,0:T(8,128)(2,1)S(1)}, bf16[192,2048]{1,0:T(8,128)(2,1)S(1)}, u32[]{:S(2)}, u32[]{:S(2)}) collective-permute-start(bf16[192,2048]{1,0:T(8,128)(2,1)S(1)} %copy-done.47), channel_id=1, source_target_pairs={{0,16},{8,24},{16,0},{24,8},{1,17},{9,25},{17,1},{25,9},{2,18},{10... | collective-permute-start | bytes 2359304 | tf_op jit(solution)/shard_map/ppermute | solution.py:119
  537.8 16.1 %collective-permute-start.88 = (bf16[128,2048]{1,0:T(8,128)(2,1)S(1)}, bf16[128,2048]{1,0:T(8,128)(2,1)S(1)}, u32[]{:S(2)}, u32[]{:S(2)}) collective-permute-start(bf16[128,2048]{1,0:T(8,128)(2,1)S(1)} %copy-done.50), channel_id=1, source_target_pairs={{0,2},{1,3},{2,4},{3,5},{4,6},{5,7},{6,0},{7,1},{8,10},{9,11},{10,... | collective-permute-start | bytes 1572872 | tf_op jit(solution)/shard_map/ppermute | solution.py:119
  537.8 16.1 %collective-permute-start.89 = (bf16[128,2048]{1,0:T(8,128)(2,1)S(1)}, bf16[128,2048]{1,0:T(8,128)(2,1)S(1)}, u32[]{:S(2)}, u32[]{:S(2)}) collective-permute-start(bf16[128,2048]{1,0:T(8,128)(2,1)S(1)} %copy-done.57), channel_id=1, source_target_pairs={{0,1},{1,0},{2,3},{3,2},{4,5},{5,4},{6,7},{7,6},{8,9},{9,8},{10,11... | collective-permute-start | bytes 1572872 | tf_op jit(solution)/shard_map/ppermute | solution.py:119
  (141 other events, 1372.3 us)
Sparse Core Ops, SparseCore 0:
  67.9 26.6 all-gather.3
  111.2 93.9 all-gather.5
  371.9 106.1 reduce-scatter.3

commit v3 on v2

--- a/solution.py
+++ b/solution.py
@@ -21,7 +21,7 @@
 CONTRACT_COLS = (((1,), (1,)), ((), ()))
 BF16 = jnp.bfloat16
 F32 = jnp.float32
-VMEM_LIMIT = 40 * 1024 * 1024
+MIB = 1024 * 1024
 
 
 def dot(left, right):
@@ -66,8 +66,8 @@
     return blk_move(0, 1, None)
 
 
-def ring_move():
-    return blk_move(1, 0, "z")
+def ring_move(steps):
+    return blk_move(steps, 0, "z")
 
 
 def member_move(flip):
@@ -104,56 +104,85 @@
         *arrays, self.token = lax.optimization_barrier(arrays + (self.token,))
         return arrays
 
-    def phase(self, items, behind=False, riders=()):
+    def phase(self, items, behind=False, riders=(), along=()):
         items = list(items)
         count = len(items)
         taken = []
-        for job in (self.jobs if behind else []) + list(riders):
+        for job in list(riders) + (self.jobs if behind else []):
             if job.wanted is not None:
                 taken.append((job, len(items), len(items) + len(job.wanted)))
                 items.extend(job.wanted)
         if not items:
+            for job, start, end in taken:
+                job.advance([])
             return []
         values = self.tie(*[value for value, move in items])
-        outs = self.tie(
-            *[lax.ppermute(value, move[0], move[1]) for value, (same, move) in zip(values, items)]
-        )
+        outs = [lax.ppermute(value, move[0], move[1]) for value, (same, move) in zip(values, items)]
+        outs = self.tie(*outs, *along)
+        self.along = outs[len(items) :]
         for job, start, end in taken:
             job.advance(outs[start:end])
         self.jobs = [job for job in self.jobs if job.wanted is not None]
         return outs[:count]
 
-    def drive(self, steps, hooks=(), riders=()):
+    def drive(self, steps, hooks=(), riders=(), behind=None, along=()):
         job = Job(steps)
         riders = list(riders)
         hooks = list(hooks)
+        count = 0
         while job.wanted is not None or any(rider.wanted is not None for rider in riders):
-            got = self.phase(job.wanted or [], riders=riders)
+            got = self.phase(
+                job.wanted or [],
+                riders=riders,
+                behind=behind is not None and count >= behind,
+                along=() if count else along,
+            )
             if job.wanted is not None:
                 job.advance(got)
             if hooks:
                 riders.extend(hooks.pop(0)() or [])
+            count += 1
         return job.result
 
 
 def column_gather(value, blocks=None):
     chips = lax.axis_size("blk") // 2
-    blocks = [] if blocks is None else blocks
+    near = chips // 2
+    blocks = {} if blocks is None else blocks
+    fresh = {0: value}
+    up = down = value
+    for hop in range(1, near + 2):
+        items = [(part, swap_move()) for part in fresh.values()]
+        if hop <= near:
+            items.append((up, ring_move(1)))
+        if hop <= chips - 1 - near:
+            items.append((down, ring_move(-1)))
+        got = yield items
+        for (step, part), other in zip(fresh.items(), got):
+            blocks[step] = [part, other]
+        got = got[len(fresh) :]
+        fresh = {}
+        if got:
+            up = fresh[hop] = got[0]
+        if len(got) > 1:
+            down = fresh[chips - hop] = got[1]
+    return [blocks[step] for step in range(chips)]
+
+
+def ring_gather(value):
+    chips = lax.axis_size("blk") // 2
+    blocks = []
     for step in range(chips):
         items = [(value, swap_move())]
         if step < chips - 1:
-            items.append((value, ring_move()))
+            items.append((value, ring_move(1)))
         got = yield items
         blocks.append([value, got[0]])
         value = got[-1]
     return blocks
 
 
-def join_blocks(blocks):
-    return [jnp.concatenate(block, axis=0) for block in blocks]
-
-
-def column_scatter(part_of, apart=False):
+def ring_scatter(part_of):
     chips = lax.axis_size("blk") // 2
     order = list(range(1, chips)) + [0]
 
@@ -164,18 +193,55 @@
 
     own, other = halves(order[0])
     got = yield [(other.astype(BF16), swap_move())]
-    total = own + got[0].astype(F32)
+    total = own.astype(F32) + got[0].astype(F32)
     for step in order[1:]:
+        own, other = halves(step)
+        got = yield [(total.astype(BF16), ring_move(1)), (other.astype(BF16), swap_move())]
+        total = own.astype(F32) + got[1].astype(F32) + got[0].astype(F32)
+    return total
+
+
+def join_blocks(blocks):
+    return [jnp.concatenate(block, axis=0) for block in blocks]
+
+
+def column_scatter(part_of, apart=False):
+    chips = lax.axis_size("blk") // 2
+    near = chips // 2
+    totals = {}
+
+    def swaps(steps):
+        parts = {step: part_of(step) for step in steps}
+        half = parts[steps[0]].shape[0] // 2
+        items = [(parts[step][half:].astype(BF16), swap_move()) for step in steps]
+        return items, {step: part[:half] for step, part in parts.items()}
+
+    def add(own, got):
+        for (step, part), other in zip(own.items(), got):
+            totals[step] = part.astype(F32) + other.astype(F32) + totals.get(step, 0.0)
+
+    items, own = swaps([near])
+    add(own, (yield items))
+    for hop in range(near, 0, -1):
+        both = hop <= chips - 1 - near
+        moves = [(totals[hop].astype(BF16), ring_move(-1))]
+        if both:
+            moves.append((totals[chips - hop].astype(BF16), ring_move(1)))
+        steps = sorted({hop - 1, (chips - hop + 1) % chips})
         if apart:
-            got = yield [(total.astype(BF16), ring_move())]
-            own, other = halves(step)
-            got = got + (yield [(other.astype(BF16), swap_move())])
+            got = yield moves
+            items, own = swaps(steps)
+            add(own, (yield items))
             apart = False
         else:
-            own, other = halves(step)
-            got = yield [(total.astype(BF16), ring_move()), (other.astype(BF16), swap_move())]
-        total = own + got[1].astype(F32) + got[0].astype(F32)
-    return total
+            items, own = swaps(steps)
+            got = yield moves + items
+            add(own, got[len(moves) :])
+        totals[hop - 1] = totals[hop - 1] + got[0].astype(F32)
+        if both:
+            step = (chips - hop + 1) % chips
+            totals[step] = totals[step] + got[1].astype(F32)
+    return totals[0]
 
 
 def plane_steps(backwards):
@@ -201,9 +267,11 @@
     return [pieces[i] for i in range(len(pieces))]
 
 
-def plane_scatter(parts, backwards):
+def plane_scatter(parts, backwards, pause=False):
     pieces = list(parts)
-    for step in plane_steps(backwards)[::-1]:
+    for index, step in enumerate(plane_steps(backwards)[::-1]):
+        if pause and index == 1:
+            yield []
         got = yield [(pieces[place].astype(BF16), head_move(bit)) for place, source, bit in step]
         for (place, source, bit), piece in zip(step, got):
             pieces[source] = pieces[source] + piece.astype(F32)
@@ -213,7 +281,7 @@
 def sum_everywhere(value):
     chips = lax.axis_size("blk") // 2
     for moves in (
-        [head_move(flip) for flip in range(1, lax.axis_size("head"))],
+        *([head_move(bit)] for bit in head_bits()),
         [swap_move()],
         [blk_move(steps, 0, None) for steps in range(1, chips)],
     ):
@@ -268,7 +336,7 @@
         out_specs=[vmem] * len(outs),
         out_shape=[jax.ShapeDtypeStruct(shape, dtype) for shape, dtype in outs],
         scratch_shapes=[pltpu.VMEM(shape, dtype) for shape, dtype in scratch],
-        compiler_params=pltpu.CompilerParams(vmem_limit_bytes=VMEM_LIMIT),
+        compiler_params=pltpu.CompilerParams(vmem_limit_bytes=10 * MIB),
         cost_estimate=pl.CostEstimate(
             flops=0,
             bytes_accessed=3 * sum(array.size * array.dtype.itemsize for array in arrays),
@@ -455,6 +523,55 @@
         pieces,
         [((count, size, column), BF16)],
     )[0]
+
+
+def light():
+    return pl.CostEstimate(flops=1, bytes_accessed=1, transcendentals=0)
+
+
+def weight_grad_kernel(count, groups, *refs):
+    pieces, lefts = refs[:count], refs[count : count + groups]
+    out_ref, right_ref = refs[-2:]
+    rows = pieces[0].shape[0]
+
+    @pl.when(pl.program_id(0) == 0)
+    def _():
+        for index in range(count):
+            right_ref[index * rows : (index + 1) * rows, :] = pieces[index][...]
+
+    size = out_ref.shape[1]
+    for head in range(lefts[0].shape[1] // size):
+
+        @pl.when(pl.program_id(0) == head)
+        def _(head=head):
+            cut = slice(head * size, (head + 1) * size)
+            left = jnp.concatenate([ref[:, cut] for ref in lefts], axis=0)
+            out_ref[0] = row_outer(left, right_ref[...]).astype(BF16)
+
+
+def weight_grads(lefts, pieces, heads, kind, into):
+    size = lefts[0].shape[1] // heads
+    piece, width = pieces[0].shape
+    count = len(pieces)
+    specs = [pl.BlockSpec((piece, width), lambda i: (0, 0))] * count
+    specs += [pl.BlockSpec(left.shape, lambda i: (0, 0)) for left in lefts]
+    operands = list(pieces) + list(lefts)
+    aliases = {}
+    if into is not None:
+        specs.append(pl.BlockSpec(memory_space=pl.ANY))
+        aliases = {len(operands): 0}
+        operands.append(into)
+    return pl.pallas_call(
+        functools.partial(weight_grad_kernel, count, len(lefts)),
+        grid=(heads,),
+        in_specs=specs,
+        out_specs=pl.BlockSpec((1, size, width), lambda i: (i, kind, 0)),
+        out_shape=jax.ShapeDtypeStruct((heads, 3 * size, width), BF16),
+        scratch_shapes=[pltpu.VMEM((count * piece, width), BF16)],
+        input_output_aliases=aliases,
+        compiler_params=pltpu.CompilerParams(vmem_limit_bytes=20 * MIB),
+        cost_estimate=light(),
+    )(*operands)
 
 
 def rope_back_kernel(query_rows, key_rows, count, scalar_ref, *refs):
@@ -575,7 +692,7 @@
         ]
         if last
         else jax.ShapeDtypeStruct((rows, 2 * HD), F32),
-        compiler_params=pltpu.CompilerParams(vmem_limit_bytes=VMEM_LIMIT),
+        compiler_params=pltpu.CompilerParams(vmem_limit_bytes=14 * MIB),
         cost_estimate=cost,
     )(query, keys, values, qpos, qlow, kpos, *([] if first else [total]))
 
@@ -659,7 +776,7 @@
             jax.ShapeDtypeStruct((tokens, HD), F32),
         ]
         + ([jax.ShapeDtypeStruct((8, rows), F32)] if first else []),
-        compiler_params=pltpu.CompilerParams(vmem_limit_bytes=VMEM_LIMIT),
+        compiler_params=pltpu.CompilerParams(vmem_limit_bytes=18 * MIB),
         cost_estimate=cost,
     )(query, upstream, logs, qpos, qlow, keys, values, kpos, *taken)
 
@@ -723,6 +840,8 @@
         plane_gather(jnp.concatenate([w_query.T, w_key.T, w_value.T], axis=0), False)
     )
     gain_job = Job(sum_everywhere(gains.reshape(-1, 128)))
+    own_cotangent = lax.dynamic_slice_in_dim(cotangent, head * rows, rows, 0)
+    cotangent_job = wire.add(ring_gather(own_cotangent))
     token_blocks = wire.drive(
         column_gather(inputs), riders=[qkv_job], hooks=[lambda: [gain_job]]
     )
@@ -739,6 +858,8 @@
     column_values = jnp.concatenate(token_blocks, axis=0).astype(F32)
     normed_column = (column_values * rms_scale(column_values) * input_norm).astype(BF16)
     raw = col_inner(qkv_weights, normed_column).astype(BF16)
+    wire.phase([], behind=True, along=[raw])
+    raw = wire.along[0]
     norms = jnp.stack([query_norm, key_norm], axis=1)
 
     def reorder(value, index):
@@ -779,8 +900,6 @@
         keys = rope_forward(key_raw, key_norm, cosine, sine).astype(BF16)
         query = jnp.swapaxes(query, 1, 2).reshape(per_device * column, HD)
         key_value = jnp.concatenate([keys.T, value_raw.T], axis=1)
-    own_cotangent = lax.dynamic_slice_in_dim(cotangent, head * rows, rows, 0)
-    cotangent_job = wire.add(column_gather(own_cotangent))
 
     pairs = {0: key_value}
     key_pieces, value_pieces = dict(pairs), dict(pairs)
@@ -806,14 +925,12 @@
             items = [
                 (key_pieces[source][:, :HD], head_move(bit)) for place, source, bit in forward
             ] + [(value_pieces[source][:, -HD:], head_move(bit)) for place, source, bit in backward]
-        got = wire.phase(items, behind=True)
         for place in ready:
             total = add_column(place, total)
+        got = wire.phase(items, behind=True, along=[total])
+        total = wire.along[0]
         if ready == [0]:
-            late = jnp.concatenate([w_gate.T, w_up.T, w_down], axis=0)
-            total, late = wire.tie(total, late)
-        else:
-            total = wire.tie(total)[0]
+            late = wire.tie(jnp.concatenate([w_gate.T, w_up.T, w_down], axis=0))[0]
         ready = [place for place, source, bit in forward]
         for index, place in enumerate(ready):
             key_pieces[place] = got[index]
@@ -821,47 +938,43 @@
                 value_pieces[place] = pairs[place] = got[index]
             else:
                 value_pieces[backward[index][0]] = got[len(forward) + index]
-    wire.phase([], behind=True)
     for place in ready:
         total = add_column(place, total)
     heads_out, logs = total
 
     if in_pair:
-        pieces = exchange(mixed_members(member, heads_out, heads, column))
+        pieces = exchange(mixed_members(member, heads_out, heads, column), True)
         mixed = join_members(member, odd, pieces, rows).reshape(heads * out_rows, column)
     else:
         mixed_heads = jnp.swapaxes(heads_out.astype(BF16).reshape(per_device, column, HD), 1, 2)
         every = gather_members(mixed_heads)
         every = every.reshape(heads, blks, out_rows, column)
         mixed = lax.dynamic_index_in_dim(every, blk, 1).reshape(heads * out_rows, column)
-    wire.jobs.remove(cotangent_job)
+    branch_parts = row_outer(mixed, out_weights)
     branch = wire.drive(
-        column_scatter(
-            lambda step: row_outer(mixed[:, step * pair : (step + 1) * pair], out_weights)
-        ),
-        riders=[cotangent_job],
-    )
+        column_scatter(lambda step: branch_parts[step * pair : (step + 1) * pair])
+    )
+    while wire.jobs:
+        wire.phase([], behind=True)
     token_values = inputs.astype(F32)
     middle = token_values + branch
     scale_two = rms_scale(middle)
     hidden_in = (middle * scale_two * hidden_norm).astype(BF16)
 
     late = lax.all_gather(late, "head", axis=0)
-    gate_weights, up_weights, down_weights = (
-        late[:, i * feed_rows : (i + 1) * feed_rows].reshape(-1, width) for i in range(3)
-    )
-    hidden_parts = []
-    feed_halves = []
-    feed_weights = [gate_weights, up_weights, down_weights]
-    half_chips = chips // 2
-
-    def feed_half(index):
-        start = index * half_chips
-        steps = range(start, start + half_chips)
-        tokens, upstream = (
-            jnp.concatenate([part for step in steps for part in parts[step]], axis=0)
-            for parts in (hidden_parts, cotangent_job.result)
-        )
+    hidden_parts = {}
+    feed_groups = []
+    near = chips // 2
+    groups = [sorted({hop, (chips - hop) % chips}) for hop in range(near + 1)]
+
+    def group_pieces(index, parts):
+        return [part for step in groups[index] for part in parts[step]]
+
+    feed_weights = []
+
+    def feed_group(index):
+        tokens = jnp.concatenate(group_pieces(index, hidden_parts), axis=0)
+        upstream = jnp.concatenate(group_pieces(index, cotangent_job.result), axis=0)
         gate_weights, up_weights, down_weights = feed_weights
         act_grad = col_inner(upstream, down_weights)
         gate = col_inner(tokens, gate_weights)
@@ -874,69 +987,63 @@
         ).astype(BF16)
         up_grad = (act_grad * silu_gate).astype(BF16)
         back = dot(gate_grad, gate_weights) + dot(up_grad, up_weights)
-        feed_halves.append((tokens, upstream, activated, gate_grad, up_grad, back))
-
-    def feed_hook(step):
-        def hook():
-            if step == 0:
-                feed_weights[:] = wire.tie(*feed_weights)
-            if step == half_chips:
-                feed_half(0)
-                feed_halves[0] = tuple(wire.tie(*feed_halves[0]))
-
-        return hook
+        down = dot(activated, down_weights)
+        feed_groups.append((activated, gate_grad, up_grad, back, down))
+
+    def start_feed():
+        feed_weights.extend(wire.along)
+
+    def keep_first():
+        feed_group(0)
+        feed_groups[0] = wire.tie(*feed_groups[0])
 
     wire.drive(
-        column_gather(hidden_in, hidden_parts), hooks=[feed_hook(step) for step in range(chips)]
-    )
-    feed_half(1)
-    gate_weights, up_weights, down_weights = feed_weights
-
-    def half_rows(index, step):
-        at = (step % half_chips) * pair
-        return feed_halves[step // half_chips][index][at : at + pair]
-
-    grad_down, grad_gate, grad_up = (
-        sum(row_outer(half[left], half[right]) for half in feed_halves).astype(BF16)
-        for left, right in ((2, 1), (3, 0), (4, 0))
-    )
-    feed_grads = [grad_down, grad_gate, grad_up]
-
-    def keep_grads(*indices):
-        def hook():
-            for index in indices:
-                feed_grads[index] = wire.tie(feed_grads[index])[0]
-
-        return hook
+        column_gather(hidden_in, hidden_parts),
+        hooks=[start_feed, keep_first],
+        along=[
+            late[:, i * feed_rows : (i + 1) * feed_rows].reshape(-1, width) for i in range(3)
+        ],
+    )
+    for index in range(1, near + 1):
+        feed_group(index)
+
+    def group_rows(index, step):
+        group = min(step, chips - step)
+        at = groups[group].index(step) * pair
+        return feed_groups[group][index][at : at + pair]
+
+    hidden_pieces = sum((group_pieces(index, hidden_parts) for index in range(near + 1)), [])
+    upstream_pieces = sum(
+        (group_pieces(index, cotangent_job.result) for index in range(near + 1)), []
+    )
+    down_grads = weight_grads([group[0] for group in feed_groups], upstream_pieces, heads, 2, None)
+    gate_grads = weight_grads([group[1] for group in feed_groups], hidden_pieces, heads, 0, down_grads)
+    feed_grads = [gate_grads]
+
+    def keep_grads():
+        downs = [group[4].astype(BF16) for group in feed_groups]
+        feed_grads[0], *downs = wire.tie(feed_grads[0], *downs)
+        for index, down in enumerate(downs):
+            feed_groups[index] = tuple(feed_groups[index][:4]) + (down,)
+
+    def keep_last():
+        feed_grads[0] = wire.tie(
+            weight_grads([group[2] for group in feed_groups], hidden_pieces, heads, 1, feed_grads[0])
+        )[0]
 
     hidden_grad = wire.drive(
-        column_scatter(lambda step: half_rows(5, step), apart=True),
-        hooks=[lambda: None, lambda: None, lambda: None, keep_grads(0), keep_grads(1)],
+        column_scatter(lambda step: group_rows(3, step), apart=True),
+        hooks=[lambda: None] * (near + 1) + [keep_grads],
     )
     hidden_gain_grad = jnp.sum(hidden_grad * middle * scale_two, axis=0)
     middle_grad = own_cotangent.astype(F32) + norm_back(hidden_grad, middle, scale_two, hidden_norm)
     branch_grad = middle_grad.astype(BF16)
-    down_parts = {}
-
-    def keep_all():
-        feed_grads[:] = [
-            jnp.concatenate(
-                [grad.reshape(heads, feed_rows, width) for grad in feed_grads], axis=1
-            )
-        ]
-        for step in range(1, chips):
-            down_parts[step] = dot(half_rows(2, step), down_weights)
-        feed_grads[0], *parts = wire.tie(feed_grads[0], *down_parts.values())
-        down_parts.update(zip(down_parts, parts))
-
-    branch_blocks = join_blocks(
-        wire.drive(column_gather(branch_grad), hooks=[keep_grads(2), keep_all])
-    )
-    down_parts[0] = dot(half_rows(2, 0), down_weights)
+    branch_blocks = join_blocks(wire.drive(column_gather(branch_grad), hooks=[keep_last]))
+    down_job = wire.add(column_scatter(lambda step: group_rows(4, step)))
     feed_grads = lax.psum_scatter(feed_grads[0], "head", scatter_dimension=0).astype(F32)
-    down_job = wire.add(column_scatter(lambda step: down_parts[step]))
     mixed_grads = [col_inner(out_weights, block).astype(BF16) for block in branch_blocks]
     grad_out = dot(mixed, jnp.concatenate(branch_blocks, axis=0)).reshape(heads, out_rows, width)
+    out_parts = [pick(grad_out, head ^ place) for place in range(heads)]
     if in_pair:
         pieces = exchange(split_blocks(member, mixed_grads, heads), True)
         upstream = upstream_members(member, odd, pieces, rows)
@@ -948,7 +1055,6 @@
 
     key_grads, value_grads = {}, {}
     carry = None
-    wire.phase([], behind=True)
     for forward, backward in zip(plane_steps(False)[::-1] + [[]], plane_steps(True)[::-1] + [[]]):
         for place in [step[0] for step in forward] if forward else [0]:
             results = attend_back(
@@ -1040,39 +1146,34 @@
             [pick(by_head, head ^ place) for place in range(heads)], axis=0
         )
 
-    while wire.jobs:
+    while down_job.wanted is not None:
         wire.phase([], behind=True)
     done = [feed_grads, (middle + down_job.result).astype(BF16)]
-    tail = []
-
-    def start_tail():
-        qkv_grad = dot(wire.tie(raw_grad)[0], normed_column)
-        input_gain_grad = jnp.sum(qkv_grad * qkv_weights.astype(F32), axis=0) / input_norm
-        sums = jnp.concatenate(
-            [input_gain_grad, hidden_gain_grad, gain_grads[:, 0], gain_grads[:, 1]]
-        )
-        qkv_grad = qkv_grad.reshape(heads, qkv_rows, width)
-        tail.append(Job(sum_everywhere(sums.reshape(-1, 128))))
-        parts = [
-            jnp.concatenate([qkv_grad[place], pick(grad_out, head ^ place)], axis=0)
-            for place in range(heads)
-        ]
-        tail.append(Job(plane_scatter(parts, False)))
+
+    qkv_grad = dot(raw_grad, normed_column)
+    input_gain_grad = jnp.sum(qkv_grad * qkv_weights.astype(F32), axis=0) / input_norm
+    sums = jnp.concatenate([input_gain_grad, hidden_gain_grad, gain_grads[:, 0], gain_grads[:, 1]])
+    qkv_grad = qkv_grad.reshape(heads, qkv_rows, width)
+    out_job = Job(plane_scatter(out_parts, True, pause=True))
+    tail = [
+        Job(sum_everywhere(sums.reshape(-1, 128))),
+        Job(plane_scatter(list(qkv_grad), False)),
+        out_job,
+    ]
 
     def keep_done():
         done[:] = wire.tie(*done)
 
     normed_grad = wire.drive(
-        column_scatter(
+        ring_scatter(
             lambda step: row_outer(raw_grad[:, step * pair : (step + 1) * pair], qkv_weights)
         ),
-        hooks=[start_tail, lambda: tail, keep_done],
-    )
-    sums, qkv_grad = tail[0].result.reshape(-1), tail[1].result
+        hooks=[lambda: tail] + [lambda: None] * (chips - 3) + [keep_done],
+    )
+    sums, grad_tail, grad_out = tail[0].result.reshape(-1), tail[1].result, out_job.result
     feed_grads, layer_out = done
-    grad_out = tail[1].result[qkv_rows:]
     grad_gate, grad_up, grad_down = (
-        feed_grads[i * feed_rows : (i + 1) * feed_rows] for i in (1, 2, 0)
+        feed_grads[i * feed_rows : (i + 1) * feed_rows] for i in range(3)
     )
     token_values = wire.token.astype(F32)
     grad_input = middle_grad + norm_back(
@@ -1086,9 +1187,9 @@
         layer_out,
         grad_input,
         own_part(shard * input_gain.shape[0], input_gain.shape[0]),
-        qkv_grad[:query_rows].T,
-        qkv_grad[query_rows : query_rows + key_rows].T,
-        qkv_grad[query_rows + key_rows : qkv_rows].T,
+        grad_tail[:query_rows].T,
+        grad_tail[query_rows : query_rows + key_rows].T,
+        grad_tail[query_rows + key_rows :].T,
         own_part(2 * width + shard * query_gain.shape[0], query_gain.shape[0]),
         own_part(2 * width + HD + shard * key_gain.shape[0], key_gain.shape[0]),
         grad_out,

time: 580 us -> 527 us (0.909)
  waiting for transfers between devices: 282 us -> 234 us
  matrix products: 82.5 us -> 47.9 us
  starting transfers between devices: 52.8 us -> 77.3 us
  Pallas kernels: 59.7 us -> 73.1 us
  other arithmetic: 31.3 us -> 24.5 us
    ppermute x96 -> x97, waiting for transfers between devices: 282 us -> 226 us  [phase(): lax.ppermute(value, move[0], move[1])]
    ppermute x96 -> x97, starting transfers between devices: 52.7 us -> 77.2 us  [phase(): lax.ppermute(value, move[0], move[1])]
    dot_general x14 -> x5, matrix products: 29.4 us -> 5.45 us  [row_outer(): lax.dot_general(left, right, CONTRACT_ROWS, preferred_element_type=F32)]
    pallas_call x0 -> x3, Pallas kernels: none -> 14.2 us  [weight_grads(): pl.pallas_call(functools.partial(weight_grad_kernel, count, len(lefts)),...]
    all_gather x1, waiting for transfers between devices: 0.01 us -> 8.13 us  [local(): late = lax.all_gather(late, 'head', axis=0)]
    concatenate x6 -> x1, other arithmetic: 10.9 us -> 3.5 us  [local(): late = wire.tie(jnp.concatenate([w_gate.T, w_up.T, w_down], axis=0))[0]]
    dot_general x11 -> x14, matrix products: 30.3 us -> 23.5 us  [col_inner(): lax.dot_general(left, right, CONTRACT_COLS, preferred_element_type=F32)]
    dot_general x10 -> x11, matrix products: 22.8 us -> 18.9 us  [dot(): return jnp.dot(left, right, preferred_element_type=F32)]
  transfers between devices with their start and end apart: 99 -> 100, of which waited for: 46 -> 45; matrix products, arithmetic and copies ran while one was open for 23% -> 17% of each run, Pallas kernels for 10% -> 14%
where the time goes in v3:
time: 527 us; the launch traced here: 519 us
  waiting for transfers between devices  234 us (44%)
  starting transfers between devices  77.3 us (15%)
  Pallas kernels  73.1 us (14%)
  matrix products  47.9 us (9%)
  local copies, waits for them, and re-layouts  46.2 us (9%)
  other arithmetic  24.5 us (5%)
  between operations  15.9 us (3%)
    ppermute x97, waiting for transfers between devices, phase(): lax.ppermute(value, move[0], move[1])  226 us
    ppermute x97, starting transfers between devices, phase(): lax.ppermute(value, move[0], move[1])  77.2 us
    unnamed x161, local copies, waits for them, and re-layouts  30 us
    pallas_call x4, Pallas kernels, attend_back(): pl.pallas_call(functools.partial(attend_back_kernel, 512, own, first), gr...  29.9 us
    dot_general x14, matrix products, col_inner(): lax.dot_general(left, right, CONTRACT_COLS, preferred_element_type=F32)  23.5 us
    pallas_call x4, Pallas kernels, attend(): pl.pallas_call(functools.partial(attend_kernel, first, last), grid=(rows...  22 us
    dot_general x11, matrix products, dot(): return jnp.dot(left, right, preferred_element_type=F32)  18.9 us
    pallas_call x3, Pallas kernels, weight_grads(): pl.pallas_call(functools.partial(weight_grad_kernel, count, len(lefts)),...  14.2 us
  transfers between devices with their start and end apart: 100, of which 45 were waited for; matrix products, arithmetic and copies ran while one was open for 17% of the time, Pallas kernels for 14%

profile of v3, /device:TPU:0, one launch (start us, length us, event | category | flops | bytes accessed | tf_op | source)
XLA Modules:
  0.0 518.7 jit_solution(3364258163344513051)
XLA Ops:
  24.7 3.5 pad_maximum_fusion
  28.3 9.6 %collective-permute-done.2 = bf16[128,2048]{1,0:T(8,128)(2,1)} collective-permute-done((bf16[128,2048]{1,0:T(8,128)(2,1)}, bf16[128,2048]{1,0:T(8,128)(2,1)}, u32[]{:S(2)}, u32[]{:S(2)}) %collective-permute-start.2) | collective-permute-done | bytes 524320 | tf_op jit(solution)/shard_map/ppermute | solution.py:120
  47.7 8.0 %collective-permute-done.7 = bf16[128,2048]{1,0:T(8,128)(2,1)S(1)} collective-permute-done((bf16[128,2048]{1,0:T(8,128)(2,1)}, bf16[128,2048]{1,0:T(8,128)(2,1)S(1)}, u32[]{:S(2)}, u32[]{:S(2)}) %collective-permute-start.7) | collective-permute-done | bytes 524320 | tf_op jit(solution)/shard_map/ppermute | solution.py:120
  63.3 3.1 fusion
  74.9 5.3 %convolution_convert_fusion.2.refs_0_ = bf16[512,1024]{1,0:T(8,128)(2,1)S(1)} fusion(bf16[512,2048]{1,0:T(8,128)(2,1)} %copy-done.41, bf16[1024,2048]{1,0:T(8,128)(2,1)} %constant_dynamic-update-slice_fusion.6, f32[2048]{0:T(1024)S(1)} %get-tuple-element.727, f32[1024]{0:T(1024)S(1)} %add_rsqrt_fusion), kind=kOutput, calls=%fused_computation.33 | convolution fusion | flops 2156396544 | bytes 7352320 | tf_op jit(solution)/shard_map/dot_general | solution.py:36
  80.2 8.7 %collective-permute-done.17.refs_2_ = bf16[128,2048]{1,0:T(8,128)(2,1)S(1)} collective-permute-done((bf16[128,2048]{1,0:T(8,128)(2,1)S(1)}, bf16[128,2048]{1,0:T(8,128)(2,1)S(1)}, u32[]{:S(2)}, u32[]{:S(2)}) %collective-permute-start.17) | collective-permute-done | bytes 524320 | tf_op jit(solution)/shard_map/ppermute | solution.py:120
  91.1 7.2 %collective-permute-done.19.refs_2_ = bf16[128,1024]{1,0:T(8,128)(2,1)S(1)} collective-permute-done((bf16[128,1024]{1,0:T(8,128)(2,1)S(1)}, bf16[128,1024]{1,0:T(8,128)(2,1)S(1)}, u32[]{:S(2)}, u32[]{:S(2)}) %collective-permute-start.19) | collective-permute-done | bytes 262176 | tf_op jit(solution)/shard_map/ppermute | solution.py:120
  98.2 4.7 collective-permute-done.20.refs_3_
  107.7 5.4 %shard_map.258.refs_6_ = f32[2048,256]{1,0:T(8,128)S(1)} custom-call(bf16[2048,128]{1,0:T(8,128)(2,1)S(1)} %get-tuple-element.405.refs_0_.q_ref, bf16[1024,256]{1,0:T(8,128)(2,1)S(1)} %get-tuple-element.410.refs_1_.refs_2_.k_ref.v_ref, bf16[1024,256]{1,0:T(8,128)(2,1)S(1)} %get-tuple-element.410.refs_1_.refs_2_.k_ref.v_ref, ...), custom_call_target="tpu_custom_call" | custom-call | flops 5368709120 | bytes 524288 | tf_op jit(solution)/shard_map/pallas_call | solution.py:671
  114.5 4.9 collective-permute-done.21.refs_1_.refs_2_.k_ref.v_ref
  119.7 3.8 collective-permute-done.24.refs_6_
  129.0 5.5 %shard_map.259.refs_6_ = f32[2048,256]{1,0:T(8,128)S(1)} custom-call(bf16[2048,128]{1,0:T(8,128)(2,1)S(1)} %copy-done.32, bf16[1024,256]{1,0:T(8,128)(2,1)S(1)} %collective-permute-done.21.refs_1_.refs_2_.k_ref.v_ref, bf16[1024,256]{1,0:T(8,128)(2,1)S(1)} %collective-permute-done.21.refs_1_.refs_2_.k_ref.v_ref, ...), custom_call_target="tpu_custom_call" | custom-call | flops 5368709120 | bytes 524288 | tf_op jit(solution)/shard_map/pallas_call | solution.py:671
  134.5 5.5 %shard_map.260.refs_6_ = f32[2048,256]{1,0:T(8,128)S(1)} custom-call(bf16[2048,128]{1,0:T(8,128)(2,1)S(1)} %copy-done.32, bf16[1024,256]{1,0:T(8,128)(2,1)S(1)} %copy-done.26, bf16[1024,256]{1,0:T(8,128)(2,1)S(1)} %copy-done.26, s32[1,1024]{1,0:T(1,128)S(1)} %get-tuple-element.733.refs_3_.refs_5_.qpos_ref.kpos_ref, ...), custom_call_target="tpu_custom_call" | custom-call | flops 5368709120 | bytes 524288 | tf_op jit(solution)/shard_map/pallas_call | solution.py:671
  142.1 5.6 %shard_map.261 = (f32[2048,128]{1,0:T(8,128)S(1)}, f32[8,2048]{1,0:T(8,128)S(1)}) custom-call(bf16[2048,128]{1,0:T(8,128)(2,1)S(1)} %copy-done.33, bf16[1024,128]{1,0:T(8,128)(2,1)S(1)} %collective-permute-done.25.refs_1_.k_ref, bf16[1024,128]{1,0:T(8,128)(2,1)S(1)} %collective-permute-done.26.refs_2_.v_ref, ...), custom_call_target="tpu_custom_call" | custom-call | flops 5368709120 | bytes 524288 | tf_op jit(solution)/shard_map/pallas_call | solution.py:671
  150.1 4.8 collective-permute-done.30.refs_2_
  164.7 11.7 %collective-permute-done.34 = bf16[128,2048]{1,0:T(8,128)(2,1)S(1)} collective-permute-done((bf16[128,2048]{1,0:T(8,128)(2,1)S(1)}, bf16[128,2048]{1,0:T(8,128)(2,1)S(1)}, u32[]{:S(2)}, u32[]{:S(2)}) %collective-permute-start.34) | collective-permute-done | bytes 524320 | tf_op jit(solution)/shard_map/ppermute | solution.py:120
  176.8 3.8 collective-permute-start.37
  180.6 12.4 %collective-permute-done.37 = bf16[128,2048]{1,0:T(8,128)(2,1)S(1)} collective-permute-done((bf16[128,2048]{1,0:T(8,128)(2,1)S(1)}, bf16[128,2048]{1,0:T(8,128)(2,1)S(1)}, u32[]{:S(2)}, u32[]{:S(2)}) %collective-permute-start.37) | collective-permute-done | bytes 524320 | tf_op jit(solution)/shard_map/ppermute | solution.py:120
  193.0 10.5 %collective-permute-done.38 = bf16[128,2048]{1,0:T(8,128)(2,1)S(1)} collective-permute-done((bf16[128,2048]{1,0:T(8,128)(2,1)S(1)}, bf16[128,2048]{1,0:T(8,128)(2,1)S(1)}, u32[]{:S(2)}, u32[]{:S(2)}) %collective-permute-start.38) | collective-permute-done | bytes 524320 | tf_op jit(solution)/shard_map/ppermute | solution.py:120
  209.1 8.1 %all-gather.6.cloned.1.call-done = bf16[2304,2048]{1,0:T(8,128)(2,1)} async-done(((bf16[576,2048]{1,0:T(8,128)(2,1)}), bf16[2304,2048]{1,0:T(8,128)(2,1)}) %all-gather.6.cloned.1.call-update) | async-done | bytes 9437200 | tf_op jit(solution)/shard_map/all_gather | solution.py:964
  217.3 4.1 fusion.90
  221.9 10.4 %collective-permute-done.42.refs_4_ = bf16[128,2048]{1,0:T(8,128)(2,1)S(1)} collective-permute-done((bf16[128,2048]{1,0:T(8,128)(2,1)S(1)}, bf16[128,2048]{1,0:T(8,128)(2,1)S(1)}, u32[]{:S(2)}, u32[]{:S(2)}) %collective-permute-start.42) | collective-permute-done | bytes 524320 | tf_op jit(solution)/shard_map/ppermute | solution.py:120
  244.5 4.4 collective-permute-done.45.refs_6_
  263.0 11.7 %collective-permute-done.48 = bf16[128,2048]{1,0:T(8,128)(2,1)S(1)} collective-permute-done((bf16[128,2048]{1,0:T(8,128)(2,1)S(1)}, bf16[128,2048]{1,0:T(8,128)(2,1)S(1)}, u32[]{:S(2)}, u32[]{:S(2)}) %collective-permute-start.48) | collective-permute-done | bytes 524320 | tf_op jit(solution)/shard_map/ppermute | solution.py:120
  280.2 3.2 convolution_convert_fusion
  283.4 4.7 shard_map.264.refs_11_
  288.1 4.7 shard_map.265.refs_11_
  294.8 8.6 %collective-permute-done.52 = bf16[128,2048]{1,0:T(8,128)(2,1)S(1)} collective-permute-done((bf16[128,2048]{1,0:T(8,128)(2,1)S(1)}, bf16[128,2048]{1,0:T(8,128)(2,1)S(1)}, u32[]{:S(2)}, u32[]{:S(2)}) %collective-permute-start.52) | collective-permute-done | bytes 524320 | tf_op jit(solution)/shard_map/ppermute | solution.py:120
  304.0 2.6 constant_dynamic-update-slice_fusion.27
  310.6 4.7 shard_map.266
  315.4 3.6 copy-done
  319.0 4.3 collective-permute-done.55
  323.3 10.7 %collective-permute-done.56 = bf16[128,2048]{1,0:T(8,128)(2,1)} collective-permute-done((bf16[128,2048]{1,0:T(8,128)(2,1)S(1)}, bf16[128,2048]{1,0:T(8,128)(2,1)}, u32[]{:S(2)}, u32[]{:S(2)}) %collective-permute-start.56) | collective-permute-done | bytes 524320 | tf_op jit(solution)/shard_map/ppermute | solution.py:120
  341.7 11.8 %collective-permute-done.59 = bf16[128,2048]{1,0:T(8,128)(2,1)S(1)} collective-permute-done((bf16[128,2048]{1,0:T(8,128)(2,1)}, bf16[128,2048]{1,0:T(8,128)(2,1)S(1)}, u32[]{:S(2)}, u32[]{:S(2)}) %collective-permute-start.59) | collective-permute-done | bytes 524320 | tf_op jit(solution)/shard_map/ppermute | solution.py:120
  362.4 3.3 collective-permute-done.62.refs_2_
  368.2 7.6 %shard_map.269 = (f32[2048,128]{1,0:T(8,128)S(1)}, f32[1024,128]{1,0:T(8,128)S(1)}, f32[1024,128]{1,0:T(8,128)S(1)}, f32[8,2048]{1,0:T(8,128)S(1)}) custom-call(bf16[2048,128]{1,0:T(8,128)(2,1)S(1)} %copy-done.34, bf16[2048,128]{1,0:T(8,128)(2,1)S(1)} %shard_map.268.g_ref, f32[8,2048]{1,0:T(8,128)S(1)} %get-tuple-element.561.log_ref.extra_ref, ...), custom_call_target="tpu_custom_call" | custom-call | flops 8589934592 | bytes 1048576 | tf_op jit(solution)/shard_map/pallas_call | solution.py:752
  379.1 7.4 %shard_map.270 = (f32[2048,128]{1,0:T(8,128)S(1)}, f32[1024,128]{1,0:T(8,128)S(1)}, f32[1024,128]{1,0:T(8,128)S(1)}) custom-call(bf16[2048,128]{1,0:T(8,128)(2,1)S(1)} %copy-done.34, bf16[2048,128]{1,0:T(8,128)(2,1)S(1)} %shard_map.268.g_ref, f32[8,2048]{1,0:T(8,128)S(1)} %get-tuple-element.561.log_ref.extra_ref, ...), custom_call_target="tpu_custom_call" | custom-call | flops 8589934592 | bytes 1048576 | tf_op jit(solution)/shard_map/pallas_call | solution.py:752
  386.5 7.4 %shard_map.271 = (f32[2048,128]{1,0:T(8,128)S(1)}, f32[1024,128]{1,0:T(8,128)S(1)}, f32[1024,128]{1,0:T(8,128)S(1)}) custom-call(bf16[2048,128]{1,0:T(8,128)(2,1)S(1)} %copy-done.34, bf16[2048,128]{1,0:T(8,128)(2,1)S(1)} %shard_map.268.g_ref, f32[8,2048]{1,0:T(8,128)S(1)} %get-tuple-element.561.log_ref.extra_ref, ...), custom_call_target="tpu_custom_call" | custom-call | flops 8589934592 | bytes 1048576 | tf_op jit(solution)/shard_map/pallas_call | solution.py:752
  400.5 7.4 %shard_map.272 = (f32[2048,128]{1,0:T(8,128)S(1)}, f32[1024,128]{1,0:T(8,128)S(1)}, f32[1024,128]{1,0:T(8,128)S(1)}) custom-call(bf16[2048,128]{1,0:T(8,128)(2,1)S(1)} %copy-done.34, bf16[2048,128]{1,0:T(8,128)(2,1)S(1)} %shard_map.268.g_ref, f32[8,2048]{1,0:T(8,128)S(1)} %get-tuple-element.561.log_ref.extra_ref, ...), custom_call_target="tpu_custom_call" | custom-call | flops 8589934592 | bytes 1048576 | tf_op jit(solution)/shard_map/pallas_call | solution.py:752
  407.9 5.0 collective-permute-done.70.refs_7_
  415.4 8.8 %collective-permute-done.73 = bf16[128,2048]{1,0:T(8,128)(2,1)S(1)} collective-permute-done((bf16[128,2048]{1,0:T(8,128)(2,1)S(1)}, bf16[128,2048]{1,0:T(8,128)(2,1)S(1)}, u32[]{:S(2)}, u32[]{:S(2)}) %collective-permute-start.73) | collective-permute-done | bytes 524320 | tf_op jit(solution)/shard_map/ppermute | solution.py:120
  428.1 7.1 %collective-permute-done.76.refs_2_ = bf16[128,1024]{1,0:T(8,128)(2,1)S(1)} collective-permute-done((bf16[128,1024]{1,0:T(8,128)(2,1)S(1)}, bf16[128,1024]{1,0:T(8,128)(2,1)S(1)}, u32[]{:S(2)}, u32[]{:S(2)}) %collective-permute-start.76) | collective-permute-done | bytes 262176 | tf_op jit(solution)/shard_map/ppermute | solution.py:120
  435.1 4.7 collective-permute-done.77.refs_3_
  454.4 4.9 collective-permute-done.83
  459.4 3.6 collective-permute-done.79
  467.9 10.8 %collective-permute-done.86 = f32[34,128]{1,0:T(8,128)S(1)} collective-permute-done((f32[34,128]{1,0:T(8,128)S(1)}, f32[34,128]{1,0:T(8,128)S(1)}, u32[]{:S(2)}, u32[]{:S(2)}) %collective-permute-start.86) | collective-permute-done | bytes 17440 | tf_op jit(solution)/shard_map/ppermute | solution.py:120
  489.0 3.0 collective-permute-done.92
  493.1 8.9 %collective-permute-done.89 = bf16[128,2048]{1,0:T(8,128)(2,1)S(1)} collective-permute-done((bf16[128,2048]{1,0:T(8,128)(2,1)S(1)}, bf16[128,2048]{1,0:T(8,128)(2,1)S(1)}, u32[]{:S(2)}, u32[]{:S(2)}) %collective-permute-start.89) | collective-permute-done | bytes 524320 | tf_op jit(solution)/shard_map/ppermute | solution.py:120
  (455 shorter events, 191.3 us)
Async XLA Ops:
  7.3 149.4 %all-gather.4.cloned.1.call-start = ((), (), s32[]{:S(2)}) async-start(), calls=%async_computation.1 | async-start | bytes 1310720 | tf_op jit(solution)/shard_map/all_gather | solution.py:857
  9.2 19.0 %collective-permute-start = (bf16[128,2048]{1,0:T(8,128)(2,1)}, bf16[128,2048]{1,0:T(8,128)(2,1)}, u32[]{:S(2)}, u32[]{:S(2)}) collective-permute-start(bf16[128,2048]{1,0:T(8,128)(2,1)} %param.16), channel_id=1, source_target_pairs={{0,1},{1,0},{2,3},{3,2},{4,5},{5,4},{6,7},{7,6},{8,9},{9,8},{10,11... | collective-permute-start | bytes 1572872 | tf_op jit(solution)/shard_map/ppermute | solution.py:120
  9.7 18.6 %collective-permute-start.1 = (bf16[128,2048]{1,0:T(8,128)(2,1)}, bf16[128,2048]{1,0:T(8,128)(2,1)}, u32[]{:S(2)}, u32[]{:S(2)}) collective-permute-start(bf16[128,2048]{1,0:T(8,128)(2,1)} %param.16), channel_id=1, source_target_pairs={{0,2},{1,3},{2,4},{3,5},{4,6},{5,7},{6,0},{7,1},{8,10},{9,11},{10,... | collective-permute-start | bytes 1572872 | tf_op jit(solution)/shard_map/ppermute | solution.py:120
  12.3 25.6 %collective-permute-start.2 = (bf16[128,2048]{1,0:T(8,128)(2,1)}, bf16[128,2048]{1,0:T(8,128)(2,1)}, u32[]{:S(2)}, u32[]{:S(2)}) collective-permute-start(bf16[128,2048]{1,0:T(8,128)(2,1)} %param.16), channel_id=1, source_target_pairs={{0,6},{1,7},{2,0},{3,1},{4,2},{5,3},{6,4},{7,5},{8,14},{9,15},{10,... | collective-permute-start | bytes 1572872 | tf_op jit(solution)/shard_map/ppermute | solution.py:120
  14.3 23.6 %collective-permute-start.3 = (bf16[128,2048]{1,0:T(8,128)(2,1)}, bf16[128,2048]{1,0:T(8,128)(2,1)}, u32[]{:S(2)}, u32[]{:S(2)}) collective-permute-start(bf16[128,2048]{1,0:T(8,128)(2,1)} %pad_maximum_fusion.4), channel_id=1, source_target_pairs={{0,8},{8,0},{16,24},{24,16},{1,9},{9,1},{17,25},{25,17},{2,10},{10... | collective-permute-start | bytes 1572872 | tf_op jit(solution)/shard_map/ppermute | solution.py:120
  16.0 21.9 %collective-permute-start.4 = (bf16[128,2048]{1,0:T(8,128)(2,1)}, bf16[128,2048]{1,0:T(8,128)(2,1)}, u32[]{:S(2)}, u32[]{:S(2)}) collective-permute-start(bf16[128,2048]{1,0:T(8,128)(2,1)} %pad_maximum_fusion.4), channel_id=1, source_target_pairs={{0,16},{8,24},{16,0},{24,8},{1,17},{9,25},{17,1},{25,9},{2,18},{10... | collective-permute-start | bytes 1572872 | tf_op jit(solution)/shard_map/ppermute | solution.py:120
  39.9 15.8 %collective-permute-start.7 = (bf16[128,2048]{1,0:T(8,128)(2,1)}, bf16[128,2048]{1,0:T(8,128)(2,1)S(1)}, u32[]{:S(2)}, u32[]{:S(2)}) collective-permute-start(bf16[128,2048]{1,0:T(8,128)(2,1)} %collective-permute-done.1), channel_id=1, source_target_pairs={{0,2},{1,3},{2,4},{3,5},{4,6},{5,7},{6,0},{7,1},{8,10},{9,11},{10,... | collective-permute-start | bytes 1572872 | tf_op jit(solution)/shard_map/ppermute | solution.py:120
  41.0 14.7 %collective-permute-start.8 = (bf16[128,2048]{1,0:T(8,128)(2,1)}, bf16[128,2048]{1,0:T(8,128)(2,1)S(1)}, u32[]{:S(2)}, u32[]{:S(2)}) collective-permute-start(bf16[128,2048]{1,0:T(8,128)(2,1)} %collective-permute-done.3), channel_id=1, source_target_pairs={{0,16},{8,24},{16,0},{24,8},{1,17},{9,25},{17,1},{25,9},{2,18},{10... | collective-permute-start | bytes 1572872 | tf_op jit(solution)/shard_map/ppermute | solution.py:120
  72.6 144.7 %all-gather.6.cloned.1.call-start = ((), (), s32[]{:S(2)}) async-start(), calls=%async_computation.2 | async-start | bytes 11796480 | tf_op jit(solution)/shard_map/all_gather | solution.py:964
  72.8 16.1 %collective-permute-start.17 = (bf16[128,2048]{1,0:T(8,128)(2,1)S(1)}, bf16[128,2048]{1,0:T(8,128)(2,1)S(1)}, u32[]{:S(2)}, u32[]{:S(2)}) collective-permute-start(bf16[128,2048]{1,0:T(8,128)(2,1)S(1)} %constant_dynamic-slice_fusion.refs_0_), channel_id=1, source_target_pairs={{0,2},{1,3},{2,4},{3,5},{4,6},{5,7},{6,0},{7,1},{8,10},{9,11},{10,... | collective-permute-start | bytes 1572872 | tf_op jit(solution)/shard_map/ppermute | solution.py:120
  107.4 16.1 %collective-permute-start.24 = (bf16[128,2048]{1,0:T(8,128)(2,1)S(1)}, bf16[128,2048]{1,0:T(8,128)(2,1)S(1)}, u32[]{:S(2)}, u32[]{:S(2)}) collective-permute-start(bf16[128,2048]{1,0:T(8,128)(2,1)S(1)} %collective-permute-done.17.refs_2_), channel_id=1, source_target_pairs={{0,2},{1,3},{2,4},{3,5},{4,6},{5,7},{6,0},{7,1},{8,10},{9,11},{10,... | collective-permute-start | bytes 1572872 | tf_op jit(solution)/shard_map/ppermute | solution.py:120
  123.5 357.3 %reduce-scatter.4.cloned.1.call-start = ((), (), s32[]{:S(2)}) async-start(), calls=%async_computation.3 | async-start | bytes 11796480
  123.6 16.3 %collective-permute-start.25 = (bf16[1024,128]{1,0:T(8,128)(2,1)S(1)}, bf16[1024,128]{1,0:T(8,128)(2,1)S(1)}, u32[]{:S(2)}, u32[]{:S(2)}) collective-permute-start(bf16[1024,128]{1,0:T(8,128)(2,1)S(1)} %slice.226), channel_id=1, source_target_pairs={{0,16},{8,24},{16,0},{24,8},{1,17},{9,25},{17,1},{25,9},{2,18},{10... | collective-permute-start | bytes 786440 | tf_op jit(solution)/shard_map/ppermute | solution.py:120
  124.2 15.7 %collective-permute-start.26 = (bf16[1024,128]{1,0:T(8,128)(2,1)S(1)}, bf16[1024,128]{1,0:T(8,128)(2,1)S(1)}, u32[]{:S(2)}, u32[]{:S(2)}) collective-permute-start(bf16[1024,128]{1,0:T(8,128)(2,1)S(1)} %slice.227), channel_id=1, source_target_pairs={{0,8},{8,0},{16,24},{24,16},{1,9},{9,1},{17,25},{25,17},{2,10},{10... | collective-permute-start | bytes 786440 | tf_op jit(solution)/shard_map/ppermute | solution.py:120
  125.7 14.3 %collective-permute-start.27 = (bf16[128,2048]{1,0:T(8,128)(2,1)S(1)}, bf16[128,2048]{1,0:T(8,128)(2,1)S(1)}, u32[]{:S(2)}, u32[]{:S(2)}) collective-permute-start(bf16[128,2048]{1,0:T(8,128)(2,1)S(1)} %collective-permute-done.24.refs_6_), channel_id=1, source_target_pairs={{0,1},{1,0},{2,3},{3,2},{4,5},{5,4},{6,7},{7,6},{8,9},{9,8},{10,11... | collective-permute-start | bytes 1572872 | tf_op jit(solution)/shard_map/ppermute | solution.py:120
  125.7 16.3 %collective-permute-start.28 = (bf16[128,2048]{1,0:T(8,128)(2,1)S(1)}, bf16[128,2048]{1,0:T(8,128)(2,1)S(1)}, u32[]{:S(2)}, u32[]{:S(2)}) collective-permute-start(bf16[128,2048]{1,0:T(8,128)(2,1)S(1)} %collective-permute-done.24.refs_6_), channel_id=1, source_target_pairs={{0,2},{1,3},{2,4},{3,5},{4,6},{5,7},{6,0},{7,1},{8,10},{9,11},{10,... | collective-permute-start | bytes 1572872 | tf_op jit(solution)/shard_map/ppermute | solution.py:120
  176.8 16.2 %collective-permute-start.37 = (bf16[128,2048]{1,0:T(8,128)(2,1)S(1)}, bf16[128,2048]{1,0:T(8,128)(2,1)S(1)}, u32[]{:S(2)}, u32[]{:S(2)}) collective-permute-start(bf16[128,2048]{1,0:T(8,128)(2,1)S(1)} %get-tuple-element.459), channel_id=1, source_target_pairs={{0,6},{1,7},{2,0},{3,1},{4,2},{5,3},{6,4},{7,5},{8,14},{9,15},{10,... | collective-permute-start | bytes 1572872 | tf_op jit(solution)/shard_map/ppermute | solution.py:120
  180.6 22.9 %collective-permute-start.38 = (bf16[128,2048]{1,0:T(8,128)(2,1)S(1)}, bf16[128,2048]{1,0:T(8,128)(2,1)S(1)}, u32[]{:S(2)}, u32[]{:S(2)}) collective-permute-start(bf16[128,2048]{1,0:T(8,128)(2,1)S(1)} %get-tuple-element.460), channel_id=1, source_target_pairs={{0,2},{1,3},{2,4},{3,5},{4,6},{5,7},{6,0},{7,1},{8,10},{9,11},{10,... | collective-permute-start | bytes 1572872 | tf_op jit(solution)/shard_map/ppermute | solution.py:120
  180.6 22.9 %collective-permute-start.39 = (bf16[128,2048]{1,0:T(8,128)(2,1)S(1)}, bf16[128,2048]{1,0:T(8,128)(2,1)S(1)}, u32[]{:S(2)}, u32[]{:S(2)}) collective-permute-start(bf16[128,2048]{1,0:T(8,128)(2,1)S(1)} %get-tuple-element.461), channel_id=1, source_target_pairs={{0,1},{1,0},{2,3},{3,2},{4,5},{5,4},{6,7},{7,6},{8,9},{9,8},{10,11... | collective-permute-start | bytes 1572872 | tf_op jit(solution)/shard_map/ppermute | solution.py:120
  205.2 16.2 %collective-permute-start.40 = (bf16[128,2048]{1,0:T(8,128)(2,1)S(1)}, bf16[128,2048]{1,0:T(8,128)(2,1)S(1)}, u32[]{:S(2)}, u32[]{:S(2)}) collective-permute-start(bf16[128,2048]{1,0:T(8,128)(2,1)S(1)} %multiply_convert_fusion.3.refs_0_), channel_id=1, source_target_pairs={{0,1},{1,0},{2,3},{3,2},{4,5},{5,4},{6,7},{7,6},{8,9},{9,8},{10,11... | collective-permute-start | bytes 1572872 | tf_op jit(solution)/shard_map/ppermute | solution.py:120
  205.3 16.6 %collective-permute-start.41 = (bf16[128,2048]{1,0:T(8,128)(2,1)S(1)}, bf16[128,2048]{1,0:T(8,128)(2,1)S(1)}, u32[]{:S(2)}, u32[]{:S(2)}) collective-permute-start(bf16[128,2048]{1,0:T(8,128)(2,1)S(1)} %multiply_convert_fusion.3.refs_0_), channel_id=1, source_target_pairs={{0,2},{1,3},{2,4},{3,5},{4,6},{5,7},{6,0},{7,1},{8,10},{9,11},{10,... | collective-permute-start | bytes 1572872 | tf_op jit(solution)/shard_map/ppermute | solution.py:120
  207.1 25.2 %collective-permute-start.42 = (bf16[128,2048]{1,0:T(8,128)(2,1)S(1)}, bf16[128,2048]{1,0:T(8,128)(2,1)S(1)}, u32[]{:S(2)}, u32[]{:S(2)}) collective-permute-start(bf16[128,2048]{1,0:T(8,128)(2,1)S(1)} %multiply_convert_fusion.3.refs_0_), channel_id=1, source_target_pairs={{0,6},{1,7},{2,0},{3,1},{4,2},{5,3},{6,4},{7,5},{8,14},{9,15},{10,... | collective-permute-start | bytes 1572872 | tf_op jit(solution)/shard_map/ppermute | solution.py:120
  233.0 15.9 %collective-permute-start.45 = (bf16[128,2048]{1,0:T(8,128)(2,1)S(1)}, bf16[128,2048]{1,0:T(8,128)(2,1)S(1)}, u32[]{:S(2)}, u32[]{:S(2)}) collective-permute-start(bf16[128,2048]{1,0:T(8,128)(2,1)S(1)} %collective-permute-done.41.refs_2_), channel_id=1, source_target_pairs={{0,2},{1,3},{2,4},{3,5},{4,6},{5,7},{6,0},{7,1},{8,10},{9,11},{10,... | collective-permute-start | bytes 1572872 | tf_op jit(solution)/shard_map/ppermute | solution.py:120
  277.8 17.0 %collective-permute-start.51 = (bf16[128,2048]{1,0:T(8,128)(2,1)S(1)}, bf16[128,2048]{1,0:T(8,128)(2,1)S(1)}, u32[]{:S(2)}, u32[]{:S(2)}) collective-permute-start(bf16[128,2048]{1,0:T(8,128)(2,1)S(1)} %get-tuple-element.515), channel_id=1, source_target_pairs={{0,6},{1,7},{2,0},{3,1},{4,2},{5,3},{6,4},{7,5},{8,14},{9,15},{10,... | collective-permute-start | bytes 1572872 | tf_op jit(solution)/shard_map/ppermute | solution.py:120
  280.0 23.5 %collective-permute-start.52 = (bf16[128,2048]{1,0:T(8,128)(2,1)S(1)}, bf16[128,2048]{1,0:T(8,128)(2,1)S(1)}, u32[]{:S(2)}, u32[]{:S(2)}) collective-permute-start(bf16[128,2048]{1,0:T(8,128)(2,1)S(1)} %get-tuple-element.516), channel_id=1, source_target_pairs={{0,2},{1,3},{2,4},{3,5},{4,6},{5,7},{6,0},{7,1},{8,10},{9,11},{10,... | collective-permute-start | bytes 1572872 | tf_op jit(solution)/shard_map/ppermute | solution.py:120
  280.1 23.3 %collective-permute-start.53 = (bf16[128,2048]{1,0:T(8,128)(2,1)S(1)}, bf16[128,2048]{1,0:T(8,128)(2,1)S(1)}, u32[]{:S(2)}, u32[]{:S(2)}) collective-permute-start(bf16[128,2048]{1,0:T(8,128)(2,1)S(1)} %slice.403), channel_id=1, source_target_pairs={{0,1},{1,0},{2,3},{3,2},{4,5},{5,4},{6,7},{7,6},{8,9},{9,8},{10,11... | collective-permute-start | bytes 1572872 | tf_op jit(solution)/shard_map/ppermute | solution.py:120
  306.6 16.7 %collective-permute-start.55 = (bf16[128,2048]{1,0:T(8,128)(2,1)S(1)}, bf16[128,2048]{1,0:T(8,128)(2,1)}, u32[]{:S(2)}, u32[]{:S(2)}) collective-permute-start(bf16[128,2048]{1,0:T(8,128)(2,1)S(1)} %get-tuple-element.527), channel_id=1, source_target_pairs={{0,2},{1,3},{2,4},{3,5},{4,6},{5,7},{6,0},{7,1},{8,10},{9,11},{10,... | collective-permute-start | bytes 1572872 | tf_op jit(solution)/shard_map/ppermute | solution.py:120
  308.4 25.6 %collective-permute-start.56 = (bf16[128,2048]{1,0:T(8,128)(2,1)S(1)}, bf16[128,2048]{1,0:T(8,128)(2,1)}, u32[]{:S(2)}, u32[]{:S(2)}) collective-permute-start(bf16[128,2048]{1,0:T(8,128)(2,1)S(1)} %get-tuple-element.527), channel_id=1, source_target_pairs={{0,6},{1,7},{2,0},{3,1},{4,2},{5,3},{6,4},{7,5},{8,14},{9,15},{10,... | collective-permute-start | bytes 1572872 | tf_op jit(solution)/shard_map/ppermute | solution.py:120
  337.5 15.9 %collective-permute-start.59 = (bf16[128,2048]{1,0:T(8,128)(2,1)}, bf16[128,2048]{1,0:T(8,128)(2,1)S(1)}, u32[]{:S(2)}, u32[]{:S(2)}) collective-permute-start(bf16[128,2048]{1,0:T(8,128)(2,1)} %collective-permute-done.55), channel_id=1, source_target_pairs={{0,2},{1,3},{2,4},{3,5},{4,6},{5,7},{6,0},{7,1},{8,10},{9,11},{10,... | collective-permute-start | bytes 1572872 | tf_op jit(solution)/shard_map/ppermute | solution.py:120
  376.1 17.9 %collective-permute-start.65 = (bf16[1024,128]{1,0:T(8,128)(2,1)S(1)}, bf16[1024,128]{1,0:T(8,128)(2,1)S(1)}, u32[]{:S(2)}, u32[]{:S(2)}) collective-permute-start(bf16[1024,128]{1,0:T(8,128)(2,1)S(1)} %convert_element_type.342), channel_id=1, source_target_pairs={{0,16},{8,24},{16,0},{24,8},{1,17},{9,25},{17,1},{25,9},{2,18},{10... | collective-permute-start | bytes 786440 | tf_op jit(solution)/shard_map/ppermute | solution.py:120
  377.8 16.3 %collective-permute-start.66 = (bf16[1024,128]{1,0:T(8,128)(2,1)S(1)}, bf16[1024,128]{1,0:T(8,128)(2,1)S(1)}, u32[]{:S(2)}, u32[]{:S(2)}) collective-permute-start(bf16[1024,128]{1,0:T(8,128)(2,1)S(1)} %convert_element_type.343), channel_id=1, source_target_pairs={{0,8},{8,0},{16,24},{24,16},{1,9},{9,1},{17,25},{25,17},{2,10},{10... | collective-permute-start | bytes 786440 | tf_op jit(solution)/shard_map/ppermute | solution.py:120
  378.1 16.0 %collective-permute-start.67 = (bf16[128,2048]{1,0:T(8,128)(2,1)S(1)}, bf16[128,2048]{1,0:T(8,128)(2,1)S(1)}, u32[]{:S(2)}, u32[]{:S(2)}) collective-permute-start(bf16[128,2048]{1,0:T(8,128)(2,1)S(1)} %add_convert_fusion.3), channel_id=1, source_target_pairs={{0,6},{1,7},{2,0},{3,1},{4,2},{5,3},{6,4},{7,5},{8,14},{9,15},{10,... | collective-permute-start | bytes 1572872 | tf_op jit(solution)/shard_map/ppermute | solution.py:120
  378.6 15.5 %collective-permute-start.68 = (bf16[128,2048]{1,0:T(8,128)(2,1)S(1)}, bf16[128,2048]{1,0:T(8,128)(2,1)S(1)}, u32[]{:S(2)}, u32[]{:S(2)}) collective-permute-start(bf16[128,2048]{1,0:T(8,128)(2,1)S(1)} %get-tuple-element.574), channel_id=1, source_target_pairs={{0,1},{1,0},{2,3},{3,2},{4,5},{5,4},{6,7},{7,6},{8,9},{9,8},{10,11... | collective-permute-start | bytes 1572872 | tf_op jit(solution)/shard_map/ppermute | solution.py:120
  378.8 15.3 %collective-permute-start.69 = (bf16[128,2048]{1,0:T(8,128)(2,1)S(1)}, bf16[128,2048]{1,0:T(8,128)(2,1)S(1)}, u32[]{:S(2)}, u32[]{:S(2)}) collective-permute-start(bf16[128,2048]{1,0:T(8,128)(2,1)S(1)} %get-tuple-element.575), channel_id=1, source_target_pairs={{0,1},{1,0},{2,3},{3,2},{4,5},{5,4},{6,7},{7,6},{8,9},{9,8},{10,11... | collective-permute-start | bytes 1572872 | tf_op jit(solution)/shard_map/ppermute | solution.py:120
  396.1 16.8 %collective-permute-start.70 = (bf16[1024,256]{1,0:T(8,128)(2,1)S(1)}, bf16[1024,256]{1,0:T(8,128)(2,1)S(1)}, u32[]{:S(2)}, u32[]{:S(2)}) collective-permute-start(bf16[1024,256]{1,0:T(8,128)(2,1)S(1)} %pad_maximum_fusion.5), channel_id=1, source_target_pairs={{0,8},{8,0},{16,24},{24,16},{1,9},{9,1},{17,25},{25,17},{2,10},{10... | collective-permute-start | bytes 1572872 | tf_op jit(solution)/shard_map/ppermute | solution.py:120
  397.9 17.6 %collective-permute-start.71 = (bf16[1024,256]{1,0:T(8,128)(2,1)S(1)}, bf16[1024,256]{1,0:T(8,128)(2,1)S(1)}, u32[]{:S(2)}, u32[]{:S(2)}) collective-permute-start(bf16[1024,256]{1,0:T(8,128)(2,1)S(1)} %pad_maximum_fusion.6), channel_id=1, source_target_pairs={{0,16},{8,24},{16,0},{24,8},{1,17},{9,25},{17,1},{25,9},{2,18},{10... | collective-permute-start | bytes 1572872 | tf_op jit(solution)/shard_map/ppermute | solution.py:120
  398.3 17.2 %collective-permute-start.72 = (bf16[128,2048]{1,0:T(8,128)(2,1)S(1)}, bf16[128,2048]{1,0:T(8,128)(2,1)S(1)}, u32[]{:S(2)}, u32[]{:S(2)}) collective-permute-start(bf16[128,2048]{1,0:T(8,128)(2,1)S(1)} %get-tuple-element.595), channel_id=1, source_target_pairs={{0,6},{1,7},{2,0},{3,1},{4,2},{5,3},{6,4},{7,5},{8,14},{9,15},{10,... | collective-permute-start | bytes 1572872 | tf_op jit(solution)/shard_map/ppermute | solution.py:120
  398.7 25.5 %collective-permute-start.73 = (bf16[128,2048]{1,0:T(8,128)(2,1)S(1)}, bf16[128,2048]{1,0:T(8,128)(2,1)S(1)}, u32[]{:S(2)}, u32[]{:S(2)}) collective-permute-start(bf16[128,2048]{1,0:T(8,128)(2,1)S(1)} %get-tuple-element.596), channel_id=1, source_target_pairs={{0,2},{1,3},{2,4},{3,5},{4,6},{5,7},{6,0},{7,1},{8,10},{9,11},{10,... | collective-permute-start | bytes 1572872 | tf_op jit(solution)/shard_map/ppermute | solution.py:120
  400.5 23.8 %collective-permute-start.74 = (bf16[128,2048]{1,0:T(8,128)(2,1)S(1)}, bf16[128,2048]{1,0:T(8,128)(2,1)S(1)}, u32[]{:S(2)}, u32[]{:S(2)}) collective-permute-start(bf16[128,2048]{1,0:T(8,128)(2,1)S(1)} %slice.258), channel_id=1, source_target_pairs={{0,1},{1,0},{2,3},{3,2},{4,5},{5,4},{6,7},{7,6},{8,9},{9,8},{10,11... | collective-permute-start | bytes 1572872 | tf_op jit(solution)/shard_map/ppermute | solution.py:120
  447.0 16.0 %collective-permute-start.79 = (bf16[128,2048]{1,0:T(8,128)(2,1)S(1)}, bf16[128,2048]{1,0:T(8,128)(2,1)S(1)}, u32[]{:S(2)}, u32[]{:S(2)}) collective-permute-start(bf16[128,2048]{1,0:T(8,128)(2,1)S(1)} %fusion.28), channel_id=1, source_target_pairs={{0,2},{1,3},{2,4},{3,5},{4,6},{5,7},{6,0},{7,1},{8,10},{9,11},{10,... | collective-permute-start | bytes 1572872 | tf_op jit(solution)/shard_map/ppermute | solution.py:120
  447.5 15.4 %collective-permute-start.80 = (bf16[128,2048]{1,0:T(8,128)(2,1)S(1)}, bf16[128,2048]{1,0:T(8,128)(2,1)S(1)}, u32[]{:S(2)}, u32[]{:S(2)}) collective-permute-start(bf16[128,2048]{1,0:T(8,128)(2,1)S(1)} %slice.401), channel_id=1, source_target_pairs={{0,1},{1,0},{2,3},{3,2},{4,5},{5,4},{6,7},{7,6},{8,9},{9,8},{10,11... | collective-permute-start | bytes 1572872 | tf_op jit(solution)/shard_map/ppermute | solution.py:120
  447.5 15.4 %collective-permute-start.82 = (bf16[128,2048]{1,0:T(8,128)(2,1)S(1)}, bf16[128,2048]{1,0:T(8,128)(2,1)S(1)}, u32[]{:S(2)}, u32[]{:S(2)}) collective-permute-start(bf16[128,2048]{1,0:T(8,128)(2,1)S(1)} %get-tuple-element.631), channel_id=1, source_target_pairs={{0,16},{8,24},{16,0},{24,8},{1,17},{9,25},{17,1},{25,9},{2,18},{10... | collective-permute-start | bytes 1572872 | tf_op jit(solution)/shard_map/ppermute | solution.py:120
  463.3 15.4 %collective-permute-start.84 = (bf16[128,2048]{1,0:T(8,128)(2,1)S(1)}, bf16[128,2048]{1,0:T(8,128)(2,1)S(1)}, u32[]{:S(2)}, u32[]{:S(2)}) collective-permute-start(bf16[128,2048]{1,0:T(8,128)(2,1)S(1)} %fusion.30), channel_id=1, source_target_pairs={{0,2},{1,3},{2,4},{3,5},{4,6},{5,7},{6,0},{7,1},{8,10},{9,11},{10,... | collective-permute-start | bytes 1572872 | tf_op jit(solution)/shard_map/ppermute | solution.py:120
  463.6 15.2 %collective-permute-start.85 = (bf16[128,2048]{1,0:T(8,128)(2,1)S(1)}, bf16[128,2048]{1,0:T(8,128)(2,1)S(1)}, u32[]{:S(2)}, u32[]{:S(2)}) collective-permute-start(bf16[128,2048]{1,0:T(8,128)(2,1)S(1)} %slice.400), channel_id=1, source_target_pairs={{0,1},{1,0},{2,3},{3,2},{4,5},{5,4},{6,7},{7,6},{8,9},{9,8},{10,11... | collective-permute-start | bytes 1572872 | tf_op jit(solution)/shard_map/ppermute | solution.py:120
  463.7 15.1 %collective-permute-start.87 = (bf16[128,2048]{1,0:T(8,128)(2,1)S(1)}, bf16[128,2048]{1,0:T(8,128)(2,1)S(1)}, u32[]{:S(2)}, u32[]{:S(2)}) collective-permute-start(bf16[128,2048]{1,0:T(8,128)(2,1)S(1)} %fusion.27), channel_id=1, source_target_pairs={{0,8},{8,0},{16,24},{24,16},{1,9},{9,1},{17,25},{25,17},{2,10},{10... | collective-permute-start | bytes 1572872 | tf_op jit(solution)/shard_map/ppermute | solution.py:120
  464.3 14.4 %collective-permute-start.88 = (bf16[128,2048]{1,0:T(8,128)(2,1)S(1)}, bf16[128,2048]{1,0:T(8,128)(2,1)S(1)}, u32[]{:S(2)}, u32[]{:S(2)}) collective-permute-start(bf16[128,2048]{1,0:T(8,128)(2,1)S(1)} %get-tuple-element.643), channel_id=1, source_target_pairs={{0,16},{8,24},{16,0},{24,8},{1,17},{9,25},{17,1},{25,9},{2,18},{10... | collective-permute-start | bytes 1572872 | tf_op jit(solution)/shard_map/ppermute | solution.py:120
  486.3 15.7 %collective-permute-start.89 = (bf16[128,2048]{1,0:T(8,128)(2,1)S(1)}, bf16[128,2048]{1,0:T(8,128)(2,1)S(1)}, u32[]{:S(2)}, u32[]{:S(2)}) collective-permute-start(bf16[128,2048]{1,0:T(8,128)(2,1)S(1)} %fusion.26), channel_id=1, source_target_pairs={{0,2},{1,3},{2,4},{3,5},{4,6},{5,7},{6,0},{7,1},{8,10},{9,11},{10,... | collective-permute-start | bytes 1572872 | tf_op jit(solution)/shard_map/ppermute | solution.py:120
  486.7 15.4 %collective-permute-start.90 = (bf16[128,2048]{1,0:T(8,128)(2,1)S(1)}, bf16[128,2048]{1,0:T(8,128)(2,1)S(1)}, u32[]{:S(2)}, u32[]{:S(2)}) collective-permute-start(bf16[128,2048]{1,0:T(8,128)(2,1)S(1)} %slice.399), channel_id=1, source_target_pairs={{0,1},{1,0},{2,3},{3,2},{4,5},{5,4},{6,7},{7,6},{8,9},{9,8},{10,11... | collective-permute-start | bytes 1572872 | tf_op jit(solution)/shard_map/ppermute | solution.py:120
  (122 other events, 1327.6 us)
Sparse Core Ops, SparseCore 0:
  72.7 26.5 all-gather.3
  123.7 93.5 all-gather.5
  334.1 104.2 reduce-scatter.3

commit v4 on v3

--- a/solution.py
+++ b/solution.py
@@ -453,14 +453,15 @@
         normed = heads * scale * gain
         low, high = normed[:HALF], normed[HALF:]
         turned = jnp.concatenate([low * cosine - high * sine, high * cosine + low * sine], axis=0)
-        return turned.T.astype(BF16)
+        return turned
 
     per_head = HD // query_rows
     for head in range(count // per_head):
         parts = [raw_ref[head * per_head + i, :query_rows, :] for i in range(per_head)]
-        query_ref[head * column : (head + 1) * column, :] = rotate(parts, gain_ref[:, 0:1])
+        turned = rotate(parts, gain_ref[:, 0:1]) * EXP2_SCALE
+        query_ref[head * column : (head + 1) * column, :] = turned.T.astype(BF16)
     parts = [raw_ref[i, query_rows : query_rows + key_rows, :] for i in range(count)]
-    pair_ref[:, :HD] = rotate(parts, gain_ref[:, 1:2])
+    pair_ref[:, :HD] = rotate(parts, gain_ref[:, 1:2]).T.astype(BF16)
     parts = [raw_ref[i, query_rows + key_rows :, :] for i in range(count)]
     pair_ref[:, HD:] = jnp.concatenate(parts, axis=0).astype(F32).T.astype(BF16)
 
@@ -644,7 +645,7 @@
     qpos = jnp.broadcast_to(qpos_ref[...], (8, rows)).T[:, :1]
     qlow = jnp.broadcast_to(qlow_ref[...], (8, rows)).T[:, :1]
     allowed = (kpos <= qpos) & (kpos >= qlow)
-    lifted = jnp.where(allowed, jnp.exp2(scores * EXP2_SCALE), 0.0).astype(BF16)
+    lifted = jnp.where(allowed, jnp.exp2(scores), 0.0).astype(BF16)
     values = jnp.concatenate([v_ref[...], jnp.ones(v_ref.shape, BF16)], axis=1)
     total = dot(lifted, values)
     if not first:
@@ -728,13 +729,13 @@
         upstream = g_ref[at, :]
         scores = col_inner(keys, query)
         allowed = (kpos <= qpos_ref[:, place]) & (kpos >= qlow_ref[:, place])
-        probs = jnp.where(allowed, jnp.exp2(scores * EXP2_SCALE - log_ref[0:1, at]), 0.0)
+        probs = jnp.where(allowed, jnp.exp2(scores - log_ref[0:1, at]), 0.0)
         prob_grad = col_inner(values, upstream)
         score_grad = (probs * (prob_grad - delta_ref[0:1, at])).astype(BF16)
         value_sum = value_sum + dot(probs.astype(BF16), upstream)
         key_sum = key_sum + dot(score_grad, query)
         dq_ref[at, :] += row_outer(score_grad, keys) * SCORE_SCALE
-    dk_ref[...] = key_sum * SCORE_SCALE
+    dk_ref[...] = key_sum * (SCORE_SCALE / EXP2_SCALE)
     dv_ref[...] = value_sum
 
 
@@ -847,6 +848,7 @@
     )
     qkv_weights, gains = qkv_job.result, gain_job.result
     token_blocks = [part for parts in token_blocks for part in parts]
+    token_blocks[chips:] = wire.tie(*token_blocks[chips:])
     gains = gains.reshape(-1)
     input_norm = gains[:width]
     hidden_norm = gains[width : 2 * width]
@@ -896,7 +898,7 @@
         key_raw = pick(key_all, blk * KVH // blks)
         value_raw = pick(value_all, blk * KVH // blks)
 
-        query = rope_forward(query_raw, query_norm, cosine, sine).astype(BF16)
+        query = (rope_forward(query_raw, query_norm, cosine, sine) * EXP2_SCALE).astype(BF16)
         keys = rope_forward(key_raw, key_norm, cosine, sine).astype(BF16)
         query = jnp.swapaxes(query, 1, 2).reshape(per_device * column, HD)
         key_value = jnp.concatenate([keys.T, value_raw.T], axis=1)
@@ -1154,10 +1156,10 @@
     input_gain_grad = jnp.sum(qkv_grad * qkv_weights.astype(F32), axis=0) / input_norm
     sums = jnp.concatenate([input_gain_grad, hidden_gain_grad, gain_grads[:, 0], gain_grads[:, 1]])
     qkv_grad = qkv_grad.reshape(heads, qkv_rows, width)
-    out_job = Job(plane_scatter(out_parts, True, pause=True))
+    out_job = Job(plane_scatter(out_parts, True))
     tail = [
         Job(sum_everywhere(sums.reshape(-1, 128))),
-        Job(plane_scatter(list(qkv_grad), False)),
+        Job(plane_scatter(list(qkv_grad), False, pause=True)),
         out_job,
     ]
 

time: 527 us -> 522 us (level)
  waiting for transfers between devices: 234 us -> 224 us
  local copies, waits for them, and re-layouts: 46.2 us -> 52.5 us
    ppermute x97, waiting for transfers between devices: 226 us -> 216 us  [phase(): lax.ppermute(value, move[0], move[1])]
    unnamed x161 -> x171, local copies, waits for them, and re-layouts: 30 us -> 32.3 us
  transfers between devices with their start and end apart: 100 -> 100, of which waited for: 45 -> 46; matrix products, arithmetic and copies ran while one was open for 17% -> 18% of each run, Pallas kernels for 14% -> 14%
where the time goes in v4:
time: 522 us; the launch traced here: 513 us
  waiting for transfers between devices  224 us (43%)
  starting transfers between devices  78.4 us (15%)
  Pallas kernels  72.6 us (14%)
  local copies, waits for them, and re-layouts  52.5 us (10%)
  matrix products  45 us (9%)
  other arithmetic  24 us (5%)
  between operations  16 us (3%)
    ppermute x97, waiting for transfers between devices, phase(): lax.ppermute(value, move[0], move[1])  216 us
    ppermute x97, starting transfers between devices, phase(): lax.ppermute(value, move[0], move[1])  78.3 us
    unnamed x171, local copies, waits for them, and re-layouts  32.3 us
    pallas_call x4, Pallas kernels, attend_back(): pl.pallas_call(functools.partial(attend_back_kernel, 512, own, first), gr...  29.5 us
    pallas_call x4, Pallas kernels, attend(): pl.pallas_call(functools.partial(attend_kernel, first, last), grid=(rows...  22 us
    dot_general x14, matrix products, col_inner(): lax.dot_general(left, right, CONTRACT_COLS, preferred_element_type=F32)  20.7 us
    dot_general x11, matrix products, dot(): return jnp.dot(left, right, preferred_element_type=F32)  18.8 us
    pallas_call x3, Pallas kernels, weight_grads(): pl.pallas_call(functools.partial(weight_grad_kernel, count, len(lefts)),...  14.2 us
  transfers between devices with their start and end apart: 100, of which 46 were waited for; matrix products, arithmetic and copies ran while one was open for 18% of the time, Pallas kernels for 14%

profile of v4, /device:TPU:0, one launch (start us, length us, event | category | flops | bytes accessed | tf_op | source)
XLA Modules:
  0.0 512.8 jit_solution(14832621012594218806)
XLA Ops:
  8.9 2.6 collective-permute-start.1
  21.2 3.3 pad_maximum_fusion
  26.7 10.4 %collective-permute-done.2 = bf16[128,2048]{1,0:T(8,128)(2,1)} collective-permute-done((bf16[128,2048]{1,0:T(8,128)(2,1)}, bf16[128,2048]{1,0:T(8,128)(2,1)}, u32[]{:S(2)}, u32[]{:S(2)}) %collective-permute-start.2) | collective-permute-done | bytes 524320 | tf_op jit(solution)/shard_map/ppermute | solution.py:120
  44.1 9.5 %collective-permute-done.7 = bf16[128,2048]{1,0:T(8,128)(2,1)} collective-permute-done((bf16[128,2048]{1,0:T(8,128)(2,1)}, bf16[128,2048]{1,0:T(8,128)(2,1)}, u32[]{:S(2)}, u32[]{:S(2)}) %collective-permute-start.7) | collective-permute-done | bytes 524320 | tf_op jit(solution)/shard_map/ppermute | solution.py:120
  78.3 3.2 fusion
  86.8 7.2 %collective-permute-done.19.refs_2_ = bf16[128,1024]{1,0:T(8,128)(2,1)S(1)} collective-permute-done((bf16[128,1024]{1,0:T(8,128)(2,1)S(1)}, bf16[128,1024]{1,0:T(8,128)(2,1)S(1)}, u32[]{:S(2)}, u32[]{:S(2)}) %collective-permute-start.19) | collective-permute-done | bytes 262176 | tf_op jit(solution)/shard_map/ppermute | solution.py:120
  93.9 4.7 collective-permute-done.20.refs_3_
  104.4 5.4 %shard_map.258.refs_6_ = f32[2048,256]{1,0:T(8,128)S(1)} custom-call(bf16[2048,128]{1,0:T(8,128)(2,1)S(1)} %get-tuple-element.415.refs_0_.q_ref, bf16[1024,256]{1,0:T(8,128)(2,1)S(1)} %get-tuple-element.420.refs_1_.refs_2_.k_ref.v_ref, bf16[1024,256]{1,0:T(8,128)(2,1)S(1)} %get-tuple-element.420.refs_1_.refs_2_.k_ref.v_ref, ...), custom_call_target="tpu_custom_call" | custom-call | flops 5368709120 | bytes 524288 | tf_op jit(solution)/shard_map/pallas_call | solution.py:672
  111.3 3.9 collective-permute-done.21.refs_1_.refs_2_.k_ref.v_ref
  116.4 3.8 collective-permute-done.24.refs_6_
  124.7 5.5 %shard_map.259.refs_6_ = f32[2048,256]{1,0:T(8,128)S(1)} custom-call(bf16[2048,128]{1,0:T(8,128)(2,1)S(1)} %copy-done.32, bf16[1024,256]{1,0:T(8,128)(2,1)S(1)} %collective-permute-done.21.refs_1_.refs_2_.k_ref.v_ref, bf16[1024,256]{1,0:T(8,128)(2,1)S(1)} %collective-permute-done.21.refs_1_.refs_2_.k_ref.v_ref, ...), custom_call_target="tpu_custom_call" | custom-call | flops 5368709120 | bytes 524288 | tf_op jit(solution)/shard_map/pallas_call | solution.py:672
  130.2 5.5 %shard_map.260.refs_6_ = f32[2048,256]{1,0:T(8,128)S(1)} custom-call(bf16[2048,128]{1,0:T(8,128)(2,1)S(1)} %copy-done.32, bf16[1024,256]{1,0:T(8,128)(2,1)S(1)} %copy-done.26, bf16[1024,256]{1,0:T(8,128)(2,1)S(1)} %copy-done.26, s32[1,1024]{1,0:T(1,128)S(1)} %get-tuple-element.743.refs_3_.refs_5_.qpos_ref.kpos_ref, ...), custom_call_target="tpu_custom_call" | custom-call | flops 5368709120 | bytes 524288 | tf_op jit(solution)/shard_map/pallas_call | solution.py:672
  137.8 5.6 %shard_map.261 = (f32[2048,128]{1,0:T(8,128)S(1)}, f32[8,2048]{1,0:T(8,128)S(1)}) custom-call(bf16[2048,128]{1,0:T(8,128)(2,1)S(1)} %copy-done.33, bf16[1024,128]{1,0:T(8,128)(2,1)S(1)} %collective-permute-done.25.refs_1_.k_ref, bf16[1024,128]{1,0:T(8,128)(2,1)S(1)} %collective-permute-done.26.refs_2_.v_ref, ...), custom_call_target="tpu_custom_call" | custom-call | flops 5368709120 | bytes 524288 | tf_op jit(solution)/shard_map/pallas_call | solution.py:672
  145.9 4.8 collective-permute-done.30.refs_2_
  152.4 2.5 fusion.99
  160.4 11.7 %collective-permute-done.34 = bf16[128,2048]{1,0:T(8,128)(2,1)S(1)} collective-permute-done((bf16[128,2048]{1,0:T(8,128)(2,1)S(1)}, bf16[128,2048]{1,0:T(8,128)(2,1)S(1)}, u32[]{:S(2)}, u32[]{:S(2)}) %collective-permute-start.34) | collective-permute-done | bytes 524320 | tf_op jit(solution)/shard_map/ppermute | solution.py:120
  172.6 3.8 collective-permute-start.37
  176.4 12.4 %collective-permute-done.37 = bf16[128,2048]{1,0:T(8,128)(2,1)S(1)} collective-permute-done((bf16[128,2048]{1,0:T(8,128)(2,1)S(1)}, bf16[128,2048]{1,0:T(8,128)(2,1)S(1)}, u32[]{:S(2)}, u32[]{:S(2)}) %collective-permute-start.37) | collective-permute-done | bytes 524320 | tf_op jit(solution)/shard_map/ppermute | solution.py:120
  188.8 10.5 %collective-permute-done.38 = bf16[128,2048]{1,0:T(8,128)(2,1)S(1)} collective-permute-done((bf16[128,2048]{1,0:T(8,128)(2,1)S(1)}, bf16[128,2048]{1,0:T(8,128)(2,1)S(1)}, u32[]{:S(2)}, u32[]{:S(2)}) %collective-permute-start.38) | collective-permute-done | bytes 524320 | tf_op jit(solution)/shard_map/ppermute | solution.py:120
  204.9 8.2 %all-gather.6.cloned.1.call-done = bf16[2304,2048]{1,0:T(8,128)(2,1)} async-done(((bf16[576,2048]{1,0:T(8,128)(2,1)}), bf16[2304,2048]{1,0:T(8,128)(2,1)}) %all-gather.6.cloned.1.call-update) | async-done | bytes 9437200 | tf_op jit(solution)/shard_map/all_gather | solution.py:966
  213.1 4.1 fusion.90
  217.7 10.4 %collective-permute-done.42.refs_4_ = bf16[128,2048]{1,0:T(8,128)(2,1)S(1)} collective-permute-done((bf16[128,2048]{1,0:T(8,128)(2,1)S(1)}, bf16[128,2048]{1,0:T(8,128)(2,1)S(1)}, u32[]{:S(2)}, u32[]{:S(2)}) %collective-permute-start.42) | collective-permute-done | bytes 524320 | tf_op jit(solution)/shard_map/ppermute | solution.py:120
  240.3 4.4 collective-permute-done.45.refs_6_
  258.8 11.7 %collective-permute-done.48 = bf16[128,2048]{1,0:T(8,128)(2,1)S(1)} collective-permute-done((bf16[128,2048]{1,0:T(8,128)(2,1)S(1)}, bf16[128,2048]{1,0:T(8,128)(2,1)S(1)}, u32[]{:S(2)}, u32[]{:S(2)}) %collective-permute-start.48) | collective-permute-done | bytes 524320 | tf_op jit(solution)/shard_map/ppermute | solution.py:120
  276.0 3.2 convolution_convert_fusion
  279.1 4.7 shard_map.264.refs_11_
  283.9 4.7 shard_map.265.refs_11_
  290.6 8.6 %collective-permute-done.52 = bf16[128,2048]{1,0:T(8,128)(2,1)S(1)} collective-permute-done((bf16[128,2048]{1,0:T(8,128)(2,1)S(1)}, bf16[128,2048]{1,0:T(8,128)(2,1)S(1)}, u32[]{:S(2)}, u32[]{:S(2)}) %collective-permute-start.52) | collective-permute-done | bytes 524320 | tf_op jit(solution)/shard_map/ppermute | solution.py:120
  299.8 2.6 constant_dynamic-update-slice_fusion.27
  306.4 4.7 shard_map.266
  311.2 3.6 copy-done
  314.8 4.3 collective-permute-done.55
  319.1 10.7 %collective-permute-done.56 = bf16[128,2048]{1,0:T(8,128)(2,1)} collective-permute-done((bf16[128,2048]{1,0:T(8,128)(2,1)S(1)}, bf16[128,2048]{1,0:T(8,128)(2,1)}, u32[]{:S(2)}, u32[]{:S(2)}) %collective-permute-start.56) | collective-permute-done | bytes 524320 | tf_op jit(solution)/shard_map/ppermute | solution.py:120
  337.6 11.8 %collective-permute-done.59 = bf16[128,2048]{1,0:T(8,128)(2,1)S(1)} collective-permute-done((bf16[128,2048]{1,0:T(8,128)(2,1)}, bf16[128,2048]{1,0:T(8,128)(2,1)S(1)}, u32[]{:S(2)}, u32[]{:S(2)}) %collective-permute-start.59) | collective-permute-done | bytes 524320 | tf_op jit(solution)/shard_map/ppermute | solution.py:120
  358.2 3.2 collective-permute-done.62.refs_2_
  364.2 7.5 %shard_map.269 = (f32[2048,128]{1,0:T(8,128)S(1)}, f32[1024,128]{1,0:T(8,128)S(1)}, f32[1024,128]{1,0:T(8,128)S(1)}, f32[8,2048]{1,0:T(8,128)S(1)}) custom-call(bf16[2048,128]{1,0:T(8,128)(2,1)S(1)} %copy-done.34, bf16[2048,128]{1,0:T(8,128)(2,1)S(1)} %shard_map.268.g_ref, f32[8,2048]{1,0:T(8,128)S(1)} %get-tuple-element.571.log_ref.extra_ref, ...), custom_call_target="tpu_custom_call" | custom-call | flops 8589934592 | bytes 1048576 | tf_op jit(solution)/shard_map/pallas_call | solution.py:753
  375.9 7.3 %shard_map.270 = (f32[2048,128]{1,0:T(8,128)S(1)}, f32[1024,128]{1,0:T(8,128)S(1)}, f32[1024,128]{1,0:T(8,128)S(1)}) custom-call(bf16[2048,128]{1,0:T(8,128)(2,1)S(1)} %copy-done.34, bf16[2048,128]{1,0:T(8,128)(2,1)S(1)} %shard_map.268.g_ref, f32[8,2048]{1,0:T(8,128)S(1)} %get-tuple-element.571.log_ref.extra_ref, ...), custom_call_target="tpu_custom_call" | custom-call | flops 8589934592 | bytes 1048576 | tf_op jit(solution)/shard_map/pallas_call | solution.py:753
  383.2 7.3 %shard_map.271 = (f32[2048,128]{1,0:T(8,128)S(1)}, f32[1024,128]{1,0:T(8,128)S(1)}, f32[1024,128]{1,0:T(8,128)S(1)}) custom-call(bf16[2048,128]{1,0:T(8,128)(2,1)S(1)} %copy-done.34, bf16[2048,128]{1,0:T(8,128)(2,1)S(1)} %shard_map.268.g_ref, f32[8,2048]{1,0:T(8,128)S(1)} %get-tuple-element.571.log_ref.extra_ref, ...), custom_call_target="tpu_custom_call" | custom-call | flops 8589934592 | bytes 1048576 | tf_op jit(solution)/shard_map/pallas_call | solution.py:753
  396.2 7.3 %shard_map.272 = (f32[2048,128]{1,0:T(8,128)S(1)}, f32[1024,128]{1,0:T(8,128)S(1)}, f32[1024,128]{1,0:T(8,128)S(1)}) custom-call(bf16[2048,128]{1,0:T(8,128)(2,1)S(1)} %copy-done.34, bf16[2048,128]{1,0:T(8,128)(2,1)S(1)} %shard_map.268.g_ref, f32[8,2048]{1,0:T(8,128)S(1)} %get-tuple-element.571.log_ref.extra_ref, ...), custom_call_target="tpu_custom_call" | custom-call | flops 8589934592 | bytes 1048576 | tf_op jit(solution)/shard_map/pallas_call | solution.py:753
  403.5 4.9 collective-permute-done.70.refs_7_
  409.5 10.4 %collective-permute-done.73 = bf16[128,2048]{1,0:T(8,128)(2,1)S(1)} collective-permute-done((bf16[128,2048]{1,0:T(8,128)(2,1)S(1)}, bf16[128,2048]{1,0:T(8,128)(2,1)S(1)}, u32[]{:S(2)}, u32[]{:S(2)}) %collective-permute-start.73) | collective-permute-done | bytes 524320 | tf_op jit(solution)/shard_map/ppermute | solution.py:120
  423.6 7.1 %collective-permute-done.76.refs_2_ = bf16[128,1024]{1,0:T(8,128)(2,1)S(1)} collective-permute-done((bf16[128,1024]{1,0:T(8,128)(2,1)S(1)}, bf16[128,1024]{1,0:T(8,128)(2,1)S(1)}, u32[]{:S(2)}, u32[]{:S(2)}) %collective-permute-start.76) | collective-permute-done | bytes 262176 | tf_op jit(solution)/shard_map/ppermute | solution.py:120
  430.6 4.7 collective-permute-done.77.refs_3_
  450.5 5.6 %collective-permute-done.83 = bf16[64,2048]{1,0:T(8,128)(2,1)S(1)} collective-permute-done((bf16[64,2048]{1,0:T(8,128)(2,1)S(1)}, bf16[64,2048]{1,0:T(8,128)(2,1)S(1)}, u32[]{:S(2)}, u32[]{:S(2)}) %collective-permute-start.83) | collective-permute-done | bytes 262176 | tf_op jit(solution)/shard_map/ppermute | solution.py:120
  456.1 3.2 collective-permute-done.79
  465.9 5.5 %collective-permute-done.87 = bf16[64,2048]{1,0:T(8,128)(2,1)S(1)} collective-permute-done((bf16[64,2048]{1,0:T(8,128)(2,1)S(1)}, bf16[64,2048]{1,0:T(8,128)(2,1)S(1)}, u32[]{:S(2)}, u32[]{:S(2)}) %collective-permute-start.87) | collective-permute-done | bytes 262176 | tf_op jit(solution)/shard_map/ppermute | solution.py:120
  484.0 10.4 %collective-permute-done.89 = bf16[128,2048]{1,0:T(8,128)(2,1)S(1)} collective-permute-done((bf16[128,2048]{1,0:T(8,128)(2,1)S(1)}, bf16[128,2048]{1,0:T(8,128)(2,1)S(1)}, u32[]{:S(2)}, u32[]{:S(2)}) %collective-permute-start.89) | collective-permute-done | bytes 524320 | tf_op jit(solution)/shard_map/ppermute | solution.py:120
  494.6 4.0 collective-permute-start.95
  (465 shorter events, 194.3 us)
Async XLA Ops:
  7.2 145.2 %all-gather.4.cloned.1.call-start = ((), (), s32[]{:S(2)}) async-start(), calls=%async_computation.1 | async-start | bytes 1310720 | tf_op jit(solution)/shard_map/all_gather | solution.py:859
  8.4 16.3 %collective-permute-start = (bf16[128,2048]{1,0:T(8,128)(2,1)}, bf16[128,2048]{1,0:T(8,128)(2,1)}, u32[]{:S(2)}, u32[]{:S(2)}) collective-permute-start(bf16[128,2048]{1,0:T(8,128)(2,1)} %param.16), channel_id=1, source_target_pairs={{0,1},{1,0},{2,3},{3,2},{4,5},{5,4},{6,7},{7,6},{8,9},{9,8},{10,11... | collective-permute-start | bytes 1572872 | tf_op jit(solution)/shard_map/ppermute | solution.py:120
  8.9 17.8 %collective-permute-start.1 = (bf16[128,2048]{1,0:T(8,128)(2,1)}, bf16[128,2048]{1,0:T(8,128)(2,1)}, u32[]{:S(2)}, u32[]{:S(2)}) collective-permute-start(bf16[128,2048]{1,0:T(8,128)(2,1)} %param.16), channel_id=1, source_target_pairs={{0,2},{1,3},{2,4},{3,5},{4,6},{5,7},{6,0},{7,1},{8,10},{9,11},{10,... | collective-permute-start | bytes 1572872 | tf_op jit(solution)/shard_map/ppermute | solution.py:120
  11.5 25.5 %collective-permute-start.2 = (bf16[128,2048]{1,0:T(8,128)(2,1)}, bf16[128,2048]{1,0:T(8,128)(2,1)}, u32[]{:S(2)}, u32[]{:S(2)}) collective-permute-start(bf16[128,2048]{1,0:T(8,128)(2,1)} %param.16), channel_id=1, source_target_pairs={{0,6},{1,7},{2,0},{3,1},{4,2},{5,3},{6,4},{7,5},{8,14},{9,15},{10,... | collective-permute-start | bytes 1572872 | tf_op jit(solution)/shard_map/ppermute | solution.py:120
  13.6 23.4 %collective-permute-start.3 = (bf16[128,2048]{1,0:T(8,128)(2,1)S(1)}, bf16[128,2048]{1,0:T(8,128)(2,1)}, u32[]{:S(2)}, u32[]{:S(2)}) collective-permute-start(bf16[128,2048]{1,0:T(8,128)(2,1)S(1)} %pad_maximum_fusion.4), channel_id=1, source_target_pairs={{0,8},{8,0},{16,24},{24,16},{1,9},{9,1},{17,25},{25,17},{2,10},{10... | collective-permute-start | bytes 1572872 | tf_op jit(solution)/shard_map/ppermute | solution.py:120
  15.3 21.8 %collective-permute-start.4 = (bf16[128,2048]{1,0:T(8,128)(2,1)S(1)}, bf16[128,2048]{1,0:T(8,128)(2,1)}, u32[]{:S(2)}, u32[]{:S(2)}) collective-permute-start(bf16[128,2048]{1,0:T(8,128)(2,1)S(1)} %pad_maximum_fusion.4), channel_id=1, source_target_pairs={{0,16},{8,24},{16,0},{24,8},{1,17},{9,25},{17,1},{25,9},{2,18},{10... | collective-permute-start | bytes 1572872 | tf_op jit(solution)/shard_map/ppermute | solution.py:120
  37.6 16.0 %collective-permute-start.7 = (bf16[128,2048]{1,0:T(8,128)(2,1)}, bf16[128,2048]{1,0:T(8,128)(2,1)}, u32[]{:S(2)}, u32[]{:S(2)}) collective-permute-start(bf16[128,2048]{1,0:T(8,128)(2,1)} %collective-permute-done.1), channel_id=1, source_target_pairs={{0,2},{1,3},{2,4},{3,5},{4,6},{5,7},{6,0},{7,1},{8,10},{9,11},{10,... | collective-permute-start | bytes 1572872 | tf_op jit(solution)/shard_map/ppermute | solution.py:120
  38.7 14.9 %collective-permute-start.8 = (bf16[128,2048]{1,0:T(8,128)(2,1)}, bf16[128,2048]{1,0:T(8,128)(2,1)}, u32[]{:S(2)}, u32[]{:S(2)}) collective-permute-start(bf16[128,2048]{1,0:T(8,128)(2,1)} %collective-permute-done.3), channel_id=1, source_target_pairs={{0,16},{8,24},{16,0},{24,8},{1,17},{9,25},{17,1},{25,9},{2,18},{10... | collective-permute-start | bytes 1572872 | tf_op jit(solution)/shard_map/ppermute | solution.py:120
  68.3 144.8 %all-gather.6.cloned.1.call-start = ((), (), s32[]{:S(2)}) async-start(), calls=%async_computation.2 | async-start | bytes 11796480 | tf_op jit(solution)/shard_map/all_gather | solution.py:966
  68.4 15.8 %collective-permute-start.16 = (bf16[128,2048]{1,0:T(8,128)(2,1)S(1)}, bf16[128,2048]{1,0:T(8,128)(2,1)S(1)}, u32[]{:S(2)}, u32[]{:S(2)}) collective-permute-start(bf16[128,2048]{1,0:T(8,128)(2,1)S(1)} %constant_dynamic-slice_fusion.refs_0_), channel_id=1, source_target_pairs={{0,1},{1,0},{2,3},{3,2},{4,5},{5,4},{6,7},{7,6},{8,9},{9,8},{10,11... | collective-permute-start | bytes 1572872 | tf_op jit(solution)/shard_map/ppermute | solution.py:120
  68.5 16.1 %collective-permute-start.17 = (bf16[128,2048]{1,0:T(8,128)(2,1)S(1)}, bf16[128,2048]{1,0:T(8,128)(2,1)S(1)}, u32[]{:S(2)}, u32[]{:S(2)}) collective-permute-start(bf16[128,2048]{1,0:T(8,128)(2,1)S(1)} %constant_dynamic-slice_fusion.refs_0_), channel_id=1, source_target_pairs={{0,2},{1,3},{2,4},{3,5},{4,6},{5,7},{6,0},{7,1},{8,10},{9,11},{10,... | collective-permute-start | bytes 1572872 | tf_op jit(solution)/shard_map/ppermute | solution.py:120
  104.1 16.1 %collective-permute-start.24 = (bf16[128,2048]{1,0:T(8,128)(2,1)S(1)}, bf16[128,2048]{1,0:T(8,128)(2,1)S(1)}, u32[]{:S(2)}, u32[]{:S(2)}) collective-permute-start(bf16[128,2048]{1,0:T(8,128)(2,1)S(1)} %collective-permute-done.17.refs_2_), channel_id=1, source_target_pairs={{0,2},{1,3},{2,4},{3,5},{4,6},{5,7},{6,0},{7,1},{8,10},{9,11},{10,... | collective-permute-start | bytes 1572872 | tf_op jit(solution)/shard_map/ppermute | solution.py:120
  120.3 355.7 %reduce-scatter.4.cloned.1.call-start = ((), (), s32[]{:S(2)}) async-start(), calls=%async_computation.3 | async-start | bytes 11796480
  120.4 15.4 %collective-permute-start.25 = (bf16[1024,128]{1,0:T(8,128)(2,1)S(1)}, bf16[1024,128]{1,0:T(8,128)(2,1)S(1)}, u32[]{:S(2)}, u32[]{:S(2)}) collective-permute-start(bf16[1024,128]{1,0:T(8,128)(2,1)S(1)} %slice.226), channel_id=1, source_target_pairs={{0,16},{8,24},{16,0},{24,8},{1,17},{9,25},{17,1},{25,9},{2,18},{10... | collective-permute-start | bytes 786440 | tf_op jit(solution)/shard_map/ppermute | solution.py:120
  120.9 14.8 %collective-permute-start.26 = (bf16[1024,128]{1,0:T(8,128)(2,1)S(1)}, bf16[1024,128]{1,0:T(8,128)(2,1)S(1)}, u32[]{:S(2)}, u32[]{:S(2)}) collective-permute-start(bf16[1024,128]{1,0:T(8,128)(2,1)S(1)} %slice.227), channel_id=1, source_target_pairs={{0,8},{8,0},{16,24},{24,16},{1,9},{9,1},{17,25},{25,17},{2,10},{10... | collective-permute-start | bytes 786440 | tf_op jit(solution)/shard_map/ppermute | solution.py:120
  121.5 14.3 %collective-permute-start.27 = (bf16[128,2048]{1,0:T(8,128)(2,1)S(1)}, bf16[128,2048]{1,0:T(8,128)(2,1)S(1)}, u32[]{:S(2)}, u32[]{:S(2)}) collective-permute-start(bf16[128,2048]{1,0:T(8,128)(2,1)S(1)} %collective-permute-done.24.refs_6_), channel_id=1, source_target_pairs={{0,1},{1,0},{2,3},{3,2},{4,5},{5,4},{6,7},{7,6},{8,9},{9,8},{10,11... | collective-permute-start | bytes 1572872 | tf_op jit(solution)/shard_map/ppermute | solution.py:120
  121.5 16.3 %collective-permute-start.28 = (bf16[128,2048]{1,0:T(8,128)(2,1)S(1)}, bf16[128,2048]{1,0:T(8,128)(2,1)S(1)}, u32[]{:S(2)}, u32[]{:S(2)}) collective-permute-start(bf16[128,2048]{1,0:T(8,128)(2,1)S(1)} %collective-permute-done.24.refs_6_), channel_id=1, source_target_pairs={{0,2},{1,3},{2,4},{3,5},{4,6},{5,7},{6,0},{7,1},{8,10},{9,11},{10,... | collective-permute-start | bytes 1572872 | tf_op jit(solution)/shard_map/ppermute | solution.py:120
  172.6 16.2 %collective-permute-start.37 = (bf16[128,2048]{1,0:T(8,128)(2,1)S(1)}, bf16[128,2048]{1,0:T(8,128)(2,1)S(1)}, u32[]{:S(2)}, u32[]{:S(2)}) collective-permute-start(bf16[128,2048]{1,0:T(8,128)(2,1)S(1)} %get-tuple-element.469), channel_id=1, source_target_pairs={{0,6},{1,7},{2,0},{3,1},{4,2},{5,3},{6,4},{7,5},{8,14},{9,15},{10,... | collective-permute-start | bytes 1572872 | tf_op jit(solution)/shard_map/ppermute | solution.py:120
  176.4 22.9 %collective-permute-start.38 = (bf16[128,2048]{1,0:T(8,128)(2,1)S(1)}, bf16[128,2048]{1,0:T(8,128)(2,1)S(1)}, u32[]{:S(2)}, u32[]{:S(2)}) collective-permute-start(bf16[128,2048]{1,0:T(8,128)(2,1)S(1)} %get-tuple-element.470), channel_id=1, source_target_pairs={{0,2},{1,3},{2,4},{3,5},{4,6},{5,7},{6,0},{7,1},{8,10},{9,11},{10,... | collective-permute-start | bytes 1572872 | tf_op jit(solution)/shard_map/ppermute | solution.py:120
  176.4 22.9 %collective-permute-start.39 = (bf16[128,2048]{1,0:T(8,128)(2,1)S(1)}, bf16[128,2048]{1,0:T(8,128)(2,1)S(1)}, u32[]{:S(2)}, u32[]{:S(2)}) collective-permute-start(bf16[128,2048]{1,0:T(8,128)(2,1)S(1)} %get-tuple-element.471), channel_id=1, source_target_pairs={{0,1},{1,0},{2,3},{3,2},{4,5},{5,4},{6,7},{7,6},{8,9},{9,8},{10,11... | collective-permute-start | bytes 1572872 | tf_op jit(solution)/shard_map/ppermute | solution.py:120
  201.0 16.3 %collective-permute-start.40 = (bf16[128,2048]{1,0:T(8,128)(2,1)S(1)}, bf16[128,2048]{1,0:T(8,128)(2,1)S(1)}, u32[]{:S(2)}, u32[]{:S(2)}) collective-permute-start(bf16[128,2048]{1,0:T(8,128)(2,1)S(1)} %multiply_convert_fusion.3.refs_0_), channel_id=1, source_target_pairs={{0,1},{1,0},{2,3},{3,2},{4,5},{5,4},{6,7},{7,6},{8,9},{9,8},{10,11... | collective-permute-start | bytes 1572872 | tf_op jit(solution)/shard_map/ppermute | solution.py:120
  201.0 16.6 %collective-permute-start.41 = (bf16[128,2048]{1,0:T(8,128)(2,1)S(1)}, bf16[128,2048]{1,0:T(8,128)(2,1)S(1)}, u32[]{:S(2)}, u32[]{:S(2)}) collective-permute-start(bf16[128,2048]{1,0:T(8,128)(2,1)S(1)} %multiply_convert_fusion.3.refs_0_), channel_id=1, source_target_pairs={{0,2},{1,3},{2,4},{3,5},{4,6},{5,7},{6,0},{7,1},{8,10},{9,11},{10,... | collective-permute-start | bytes 1572872 | tf_op jit(solution)/shard_map/ppermute | solution.py:120
  202.9 25.2 %collective-permute-start.42 = (bf16[128,2048]{1,0:T(8,128)(2,1)S(1)}, bf16[128,2048]{1,0:T(8,128)(2,1)S(1)}, u32[]{:S(2)}, u32[]{:S(2)}) collective-permute-start(bf16[128,2048]{1,0:T(8,128)(2,1)S(1)} %multiply_convert_fusion.3.refs_0_), channel_id=1, source_target_pairs={{0,6},{1,7},{2,0},{3,1},{4,2},{5,3},{6,4},{7,5},{8,14},{9,15},{10,... | collective-permute-start | bytes 1572872 | tf_op jit(solution)/shard_map/ppermute | solution.py:120
  228.7 15.9 %collective-permute-start.45 = (bf16[128,2048]{1,0:T(8,128)(2,1)S(1)}, bf16[128,2048]{1,0:T(8,128)(2,1)S(1)}, u32[]{:S(2)}, u32[]{:S(2)}) collective-permute-start(bf16[128,2048]{1,0:T(8,128)(2,1)S(1)} %collective-permute-done.41.refs_2_), channel_id=1, source_target_pairs={{0,2},{1,3},{2,4},{3,5},{4,6},{5,7},{6,0},{7,1},{8,10},{9,11},{10,... | collective-permute-start | bytes 1572872 | tf_op jit(solution)/shard_map/ppermute | solution.py:120
  273.6 17.0 %collective-permute-start.51 = (bf16[128,2048]{1,0:T(8,128)(2,1)S(1)}, bf16[128,2048]{1,0:T(8,128)(2,1)S(1)}, u32[]{:S(2)}, u32[]{:S(2)}) collective-permute-start(bf16[128,2048]{1,0:T(8,128)(2,1)S(1)} %get-tuple-element.525), channel_id=1, source_target_pairs={{0,6},{1,7},{2,0},{3,1},{4,2},{5,3},{6,4},{7,5},{8,14},{9,15},{10,... | collective-permute-start | bytes 1572872 | tf_op jit(solution)/shard_map/ppermute | solution.py:120
  275.7 23.5 %collective-permute-start.52 = (bf16[128,2048]{1,0:T(8,128)(2,1)S(1)}, bf16[128,2048]{1,0:T(8,128)(2,1)S(1)}, u32[]{:S(2)}, u32[]{:S(2)}) collective-permute-start(bf16[128,2048]{1,0:T(8,128)(2,1)S(1)} %get-tuple-element.526), channel_id=1, source_target_pairs={{0,2},{1,3},{2,4},{3,5},{4,6},{5,7},{6,0},{7,1},{8,10},{9,11},{10,... | collective-permute-start | bytes 1572872 | tf_op jit(solution)/shard_map/ppermute | solution.py:120
  275.9 23.3 %collective-permute-start.53 = (bf16[128,2048]{1,0:T(8,128)(2,1)S(1)}, bf16[128,2048]{1,0:T(8,128)(2,1)S(1)}, u32[]{:S(2)}, u32[]{:S(2)}) collective-permute-start(bf16[128,2048]{1,0:T(8,128)(2,1)S(1)} %slice.403), channel_id=1, source_target_pairs={{0,1},{1,0},{2,3},{3,2},{4,5},{5,4},{6,7},{7,6},{8,9},{9,8},{10,11... | collective-permute-start | bytes 1572872 | tf_op jit(solution)/shard_map/ppermute | solution.py:120
  302.4 16.7 %collective-permute-start.55 = (bf16[128,2048]{1,0:T(8,128)(2,1)S(1)}, bf16[128,2048]{1,0:T(8,128)(2,1)}, u32[]{:S(2)}, u32[]{:S(2)}) collective-permute-start(bf16[128,2048]{1,0:T(8,128)(2,1)S(1)} %get-tuple-element.537), channel_id=1, source_target_pairs={{0,2},{1,3},{2,4},{3,5},{4,6},{5,7},{6,0},{7,1},{8,10},{9,11},{10,... | collective-permute-start | bytes 1572872 | tf_op jit(solution)/shard_map/ppermute | solution.py:120
  304.2 25.6 %collective-permute-start.56 = (bf16[128,2048]{1,0:T(8,128)(2,1)S(1)}, bf16[128,2048]{1,0:T(8,128)(2,1)}, u32[]{:S(2)}, u32[]{:S(2)}) collective-permute-start(bf16[128,2048]{1,0:T(8,128)(2,1)S(1)} %get-tuple-element.537), channel_id=1, source_target_pairs={{0,6},{1,7},{2,0},{3,1},{4,2},{5,3},{6,4},{7,5},{8,14},{9,15},{10,... | collective-permute-start | bytes 1572872 | tf_op jit(solution)/shard_map/ppermute | solution.py:120
  333.5 15.9 %collective-permute-start.59 = (bf16[128,2048]{1,0:T(8,128)(2,1)}, bf16[128,2048]{1,0:T(8,128)(2,1)S(1)}, u32[]{:S(2)}, u32[]{:S(2)}) collective-permute-start(bf16[128,2048]{1,0:T(8,128)(2,1)} %collective-permute-done.55), channel_id=1, source_target_pairs={{0,2},{1,3},{2,4},{3,5},{4,6},{5,7},{6,0},{7,1},{8,10},{9,11},{10,... | collective-permute-start | bytes 1572872 | tf_op jit(solution)/shard_map/ppermute | solution.py:120
  372.0 18.6 %collective-permute-start.65 = (bf16[1024,128]{1,0:T(8,128)(2,1)S(1)}, bf16[1024,128]{1,0:T(8,128)(2,1)S(1)}, u32[]{:S(2)}, u32[]{:S(2)}) collective-permute-start(bf16[1024,128]{1,0:T(8,128)(2,1)S(1)} %convert_element_type.342), channel_id=1, source_target_pairs={{0,16},{8,24},{16,0},{24,8},{1,17},{9,25},{17,1},{25,9},{2,18},{10... | collective-permute-start | bytes 786440 | tf_op jit(solution)/shard_map/ppermute | solution.py:120
  373.6 17.1 %collective-permute-start.66 = (bf16[1024,128]{1,0:T(8,128)(2,1)S(1)}, bf16[1024,128]{1,0:T(8,128)(2,1)S(1)}, u32[]{:S(2)}, u32[]{:S(2)}) collective-permute-start(bf16[1024,128]{1,0:T(8,128)(2,1)S(1)} %convert_element_type.343), channel_id=1, source_target_pairs={{0,8},{8,0},{16,24},{24,16},{1,9},{9,1},{17,25},{25,17},{2,10},{10... | collective-permute-start | bytes 786440 | tf_op jit(solution)/shard_map/ppermute | solution.py:120
  374.9 15.7 %collective-permute-start.67 = (bf16[128,2048]{1,0:T(8,128)(2,1)S(1)}, bf16[128,2048]{1,0:T(8,128)(2,1)S(1)}, u32[]{:S(2)}, u32[]{:S(2)}) collective-permute-start(bf16[128,2048]{1,0:T(8,128)(2,1)S(1)} %add_convert_fusion.3), channel_id=1, source_target_pairs={{0,6},{1,7},{2,0},{3,1},{4,2},{5,3},{6,4},{7,5},{8,14},{9,15},{10,... | collective-permute-start | bytes 1572872 | tf_op jit(solution)/shard_map/ppermute | solution.py:120
  375.3 15.3 %collective-permute-start.68 = (bf16[128,2048]{1,0:T(8,128)(2,1)S(1)}, bf16[128,2048]{1,0:T(8,128)(2,1)S(1)}, u32[]{:S(2)}, u32[]{:S(2)}) collective-permute-start(bf16[128,2048]{1,0:T(8,128)(2,1)S(1)} %get-tuple-element.584), channel_id=1, source_target_pairs={{0,1},{1,0},{2,3},{3,2},{4,5},{5,4},{6,7},{7,6},{8,9},{9,8},{10,11... | collective-permute-start | bytes 1572872 | tf_op jit(solution)/shard_map/ppermute | solution.py:120
  375.6 15.1 %collective-permute-start.69 = (bf16[128,2048]{1,0:T(8,128)(2,1)S(1)}, bf16[128,2048]{1,0:T(8,128)(2,1)S(1)}, u32[]{:S(2)}, u32[]{:S(2)}) collective-permute-start(bf16[128,2048]{1,0:T(8,128)(2,1)S(1)} %get-tuple-element.585), channel_id=1, source_target_pairs={{0,1},{1,0},{2,3},{3,2},{4,5},{5,4},{6,7},{7,6},{8,9},{9,8},{10,11... | collective-permute-start | bytes 1572872 | tf_op jit(solution)/shard_map/ppermute | solution.py:120
  392.7 15.7 %collective-permute-start.70 = (bf16[1024,256]{1,0:T(8,128)(2,1)S(1)}, bf16[1024,256]{1,0:T(8,128)(2,1)S(1)}, u32[]{:S(2)}, u32[]{:S(2)}) collective-permute-start(bf16[1024,256]{1,0:T(8,128)(2,1)S(1)} %pad_maximum_fusion.5), channel_id=1, source_target_pairs={{0,8},{8,0},{16,24},{24,16},{1,9},{9,1},{17,25},{25,17},{2,10},{10... | collective-permute-start | bytes 1572872 | tf_op jit(solution)/shard_map/ppermute | solution.py:120
  393.5 16.0 %collective-permute-start.71 = (bf16[1024,256]{1,0:T(8,128)(2,1)S(1)}, bf16[1024,256]{1,0:T(8,128)(2,1)S(1)}, u32[]{:S(2)}, u32[]{:S(2)}) collective-permute-start(bf16[1024,256]{1,0:T(8,128)(2,1)S(1)} %pad_maximum_fusion.6), channel_id=1, source_target_pairs={{0,16},{8,24},{16,0},{24,8},{1,17},{9,25},{17,1},{25,9},{2,18},{10... | collective-permute-start | bytes 1572872 | tf_op jit(solution)/shard_map/ppermute | solution.py:120
  394.0 15.5 %collective-permute-start.72 = (bf16[128,2048]{1,0:T(8,128)(2,1)S(1)}, bf16[128,2048]{1,0:T(8,128)(2,1)S(1)}, u32[]{:S(2)}, u32[]{:S(2)}) collective-permute-start(bf16[128,2048]{1,0:T(8,128)(2,1)S(1)} %get-tuple-element.605), channel_id=1, source_target_pairs={{0,6},{1,7},{2,0},{3,1},{4,2},{5,3},{6,4},{7,5},{8,14},{9,15},{10,... | collective-permute-start | bytes 1572872 | tf_op jit(solution)/shard_map/ppermute | solution.py:120
  394.3 25.6 %collective-permute-start.73 = (bf16[128,2048]{1,0:T(8,128)(2,1)S(1)}, bf16[128,2048]{1,0:T(8,128)(2,1)S(1)}, u32[]{:S(2)}, u32[]{:S(2)}) collective-permute-start(bf16[128,2048]{1,0:T(8,128)(2,1)S(1)} %get-tuple-element.606), channel_id=1, source_target_pairs={{0,2},{1,3},{2,4},{3,5},{4,6},{5,7},{6,0},{7,1},{8,10},{9,11},{10,... | collective-permute-start | bytes 1572872 | tf_op jit(solution)/shard_map/ppermute | solution.py:120
  396.1 23.7 %collective-permute-start.74 = (bf16[128,2048]{1,0:T(8,128)(2,1)S(1)}, bf16[128,2048]{1,0:T(8,128)(2,1)S(1)}, u32[]{:S(2)}, u32[]{:S(2)}) collective-permute-start(bf16[128,2048]{1,0:T(8,128)(2,1)S(1)} %slice.258), channel_id=1, source_target_pairs={{0,1},{1,0},{2,3},{3,2},{4,5},{5,4},{6,7},{7,6},{8,9},{9,8},{10,11... | collective-permute-start | bytes 1572872 | tf_op jit(solution)/shard_map/ppermute | solution.py:120
  443.3 16.0 %collective-permute-start.79 = (bf16[128,2048]{1,0:T(8,128)(2,1)S(1)}, bf16[128,2048]{1,0:T(8,128)(2,1)S(1)}, u32[]{:S(2)}, u32[]{:S(2)}) collective-permute-start(bf16[128,2048]{1,0:T(8,128)(2,1)S(1)} %fusion.28), channel_id=1, source_target_pairs={{0,2},{1,3},{2,4},{3,5},{4,6},{5,7},{6,0},{7,1},{8,10},{9,11},{10,... | collective-permute-start | bytes 1572872 | tf_op jit(solution)/shard_map/ppermute | solution.py:120
  443.9 15.3 %collective-permute-start.80 = (bf16[128,2048]{1,0:T(8,128)(2,1)S(1)}, bf16[128,2048]{1,0:T(8,128)(2,1)S(1)}, u32[]{:S(2)}, u32[]{:S(2)}) collective-permute-start(bf16[128,2048]{1,0:T(8,128)(2,1)S(1)} %slice.401), channel_id=1, source_target_pairs={{0,1},{1,0},{2,3},{3,2},{4,5},{5,4},{6,7},{7,6},{8,9},{9,8},{10,11... | collective-permute-start | bytes 1572872 | tf_op jit(solution)/shard_map/ppermute | solution.py:120
  443.9 15.3 %collective-permute-start.82 = (bf16[128,2048]{1,0:T(8,128)(2,1)S(1)}, bf16[128,2048]{1,0:T(8,128)(2,1)S(1)}, u32[]{:S(2)}, u32[]{:S(2)}) collective-permute-start(bf16[128,2048]{1,0:T(8,128)(2,1)S(1)} %get-tuple-element.641), channel_id=1, source_target_pairs={{0,16},{8,24},{16,0},{24,8},{1,17},{9,25},{17,1},{25,9},{2,18},{10... | collective-permute-start | bytes 1572872 | tf_op jit(solution)/shard_map/ppermute | solution.py:120
  459.5 15.4 %collective-permute-start.84 = (bf16[128,2048]{1,0:T(8,128)(2,1)S(1)}, bf16[128,2048]{1,0:T(8,128)(2,1)S(1)}, u32[]{:S(2)}, u32[]{:S(2)}) collective-permute-start(bf16[128,2048]{1,0:T(8,128)(2,1)S(1)} %fusion.30), channel_id=1, source_target_pairs={{0,2},{1,3},{2,4},{3,5},{4,6},{5,7},{6,0},{7,1},{8,10},{9,11},{10,... | collective-permute-start | bytes 1572872 | tf_op jit(solution)/shard_map/ppermute | solution.py:120
  459.8 15.1 %collective-permute-start.85 = (bf16[128,2048]{1,0:T(8,128)(2,1)S(1)}, bf16[128,2048]{1,0:T(8,128)(2,1)S(1)}, u32[]{:S(2)}, u32[]{:S(2)}) collective-permute-start(bf16[128,2048]{1,0:T(8,128)(2,1)S(1)} %slice.400), channel_id=1, source_target_pairs={{0,1},{1,0},{2,3},{3,2},{4,5},{5,4},{6,7},{7,6},{8,9},{9,8},{10,11... | collective-permute-start | bytes 1572872 | tf_op jit(solution)/shard_map/ppermute | solution.py:120
  478.3 16.1 %collective-permute-start.89 = (bf16[128,2048]{1,0:T(8,128)(2,1)S(1)}, bf16[128,2048]{1,0:T(8,128)(2,1)S(1)}, u32[]{:S(2)}, u32[]{:S(2)}) collective-permute-start(bf16[128,2048]{1,0:T(8,128)(2,1)S(1)} %fusion.27), channel_id=1, source_target_pairs={{0,2},{1,3},{2,4},{3,5},{4,6},{5,7},{6,0},{7,1},{8,10},{9,11},{10,... | collective-permute-start | bytes 1572872 | tf_op jit(solution)/shard_map/ppermute | solution.py:120
  478.4 16.1 %collective-permute-start.90 = (bf16[128,2048]{1,0:T(8,128)(2,1)}, bf16[128,2048]{1,0:T(8,128)(2,1)S(1)}, u32[]{:S(2)}, u32[]{:S(2)}) collective-permute-start(bf16[128,2048]{1,0:T(8,128)(2,1)} %slice.399), channel_id=1, source_target_pairs={{0,1},{1,0},{2,3},{3,2},{4,5},{5,4},{6,7},{7,6},{8,9},{9,8},{10,11... | collective-permute-start | bytes 1572872 | tf_op jit(solution)/shard_map/ppermute | solution.py:120
  478.9 15.6 %collective-permute-start.92 = (bf16[128,2048]{1,0:T(8,128)(2,1)}, bf16[128,2048]{1,0:T(8,128)(2,1)S(1)}, u32[]{:S(2)}, u32[]{:S(2)}) collective-permute-start(bf16[128,2048]{1,0:T(8,128)(2,1)} %fusion.25), channel_id=1, source_target_pairs={{0,8},{8,0},{16,24},{24,16},{1,9},{9,1},{17,25},{25,17},{2,10},{10... | collective-permute-start | bytes 1572872 | tf_op jit(solution)/shard_map/ppermute | solution.py:120
  (127 other events, 1196.8 us)
Sparse Core Ops, SparseCore 0:
  68.4 27.5 all-gather.3
  120.4 92.6 all-gather.5
  329.9 103.9 reduce-scatter.3

commit v5 on v4

--- a/solution.py
+++ b/solution.py
@@ -125,7 +125,7 @@
         self.jobs = [job for job in self.jobs if job.wanted is not None]
         return outs[:count]
 
-    def drive(self, steps, hooks=(), riders=(), behind=None, along=()):
+    def drive(self, steps, hooks=(), riders=(), behind=None, along=(), beside=0):
         job = Job(steps)
         riders = list(riders)
         hooks = list(hooks)
@@ -135,7 +135,7 @@
                 job.wanted or [],
                 riders=riders,
                 behind=behind is not None and count >= behind,
-                along=() if count else along,
+                along=along if count == beside else (),
             )
             if job.wanted is not None:
                 job.advance(got)
@@ -528,6 +528,59 @@
 
 def light():
     return pl.CostEstimate(flops=1, bytes_accessed=1, transcendentals=0)
+
+
+def feed_kernel(count, *refs):
+    tokens = refs[:count]
+    grad_ref, gate_ref, up_ref, act_out, gate_out, up_out, back_out, token_ref, total_ref = refs[
+        count:
+    ]
+    step = pl.program_id(0)
+
+    @pl.when(step == 0)
+    def _():
+        rows = tokens[0].shape[0]
+        for index in range(count):
+            token_ref[index * rows : (index + 1) * rows, :] = tokens[index][...]
+        total_ref[...] = jnp.zeros_like(total_ref)
+
+    gate = col_inner(token_ref[...], gate_ref[...])
+    up_proj = col_inner(token_ref[...], up_ref[...])
+    act_grad = grad_ref[...]
+    sigmoid_gate = jax.nn.sigmoid(gate)
+    silu_gate = gate * sigmoid_gate
+    gate_grad = (act_grad * up_proj * sigmoid_gate * (1.0 + gate * (1.0 - sigmoid_gate))).astype(
+        BF16
+    )
+    up_grad = (act_grad * silu_gate).astype(BF16)
+    act_out[...] = (silu_gate * up_proj).astype(BF16)
+    gate_out[...] = gate_grad
+    up_out[...] = up_grad
+    total_ref[...] += dot(gate_grad, gate_ref[...]) + dot(up_grad, up_ref[...])
+
+    @pl.when(step == pl.num_programs(0) - 1)
+    def _():
+        back_out[...] = total_ref[...].astype(BF16)
+
+
+def feed_beside(tokens, act_grad, gate_weights, up_weights):
+    piece, width = tokens[0].shape
+    rows, hidden = act_grad.shape
+    tile = hidden // 3
+    part = pl.BlockSpec((rows, tile), lambda i: (0, i))
+    weight = pl.BlockSpec((tile, width), lambda i: (i, 0))
+    whole = lambda i: (0, 0)
+    return pl.pallas_call(
+        functools.partial(feed_kernel, len(tokens)),
+        grid=(3,),
+        in_specs=[pl.BlockSpec((piece, width), whole)] * len(tokens) + [part, weight, weight],
+        out_specs=[part] * 3 + [pl.BlockSpec((rows, width), whole)],
+        out_shape=[jax.ShapeDtypeStruct((rows, hidden), BF16)] * 3
+        + [jax.ShapeDtypeStruct((rows, width), BF16)],
+        scratch_shapes=[pltpu.VMEM((rows, width), BF16), pltpu.VMEM((rows, width), F32)],
+        compiler_params=pltpu.CompilerParams(vmem_limit_bytes=24 * MIB),
+        cost_estimate=light(),
+    )(*tokens, act_grad, gate_weights, up_weights)
 
 
 def weight_grad_kernel(count, groups, *refs):
@@ -662,7 +715,7 @@
     rows, tokens = query.shape[0], keys.shape[0]
     value_at = values.shape[1] // HD - 1
     own = qpos.shape[1]
-    block = 256
+    block = 512
     wrap = own // block
     first = total is None
     cost = pl.CostEstimate(
@@ -693,7 +746,7 @@
         ]
         if last
         else jax.ShapeDtypeStruct((rows, 2 * HD), F32),
-        compiler_params=pltpu.CompilerParams(vmem_limit_bytes=14 * MIB),
+        compiler_params=pltpu.CompilerParams(vmem_limit_bytes=20 * MIB),
         cost_estimate=cost,
     )(query, keys, values, qpos, qlow, kpos, *([] if first else [total]))
 
@@ -743,7 +796,7 @@
     rows, tokens = query.shape[0], keys.shape[0]
     value_at = values.shape[1] // HD - 1
     own = qpos.shape[1]
-    block = 512
+    block = 1024
     first = before is None
     cost = pl.CostEstimate(
         flops=32 * rows * tokens * HD, bytes_accessed=8 * tokens * HD, transcendentals=rows * tokens
@@ -777,7 +830,7 @@
             jax.ShapeDtypeStruct((tokens, HD), F32),
         ]
         + ([jax.ShapeDtypeStruct((8, rows), F32)] if first else []),
-        compiler_params=pltpu.CompilerParams(vmem_limit_bytes=18 * MIB),
+        compiler_params=pltpu.CompilerParams(vmem_limit_bytes=28 * MIB),
         cost_estimate=cost,
     )(query, upstream, logs, qpos, qlow, keys, values, kpos, *taken)
 
@@ -979,6 +1032,13 @@
         upstream = jnp.concatenate(group_pieces(index, cotangent_job.result), axis=0)
         gate_weights, up_weights, down_weights = feed_weights
         act_grad = col_inner(upstream, down_weights)
+        if 0 < index < near:
+            activated, gate_grad, up_grad, back = feed_beside(
+                group_pieces(index, hidden_parts), act_grad, gate_weights, up_weights
+            )
+            down = dot(activated, down_weights)
+            feed_groups.append((activated, gate_grad, up_grad, back, down))
+            return
         gate = col_inner(tokens, gate_weights)
         up_proj = col_inner(tokens, up_weights)
         sigmoid_gate = jax.nn.sigmoid(gate)
@@ -1164,13 +1224,15 @@
     ]
 
     def keep_done():
-        done[:] = wire.tie(*done)
+        done[:] = wire.along
 
     normed_grad = wire.drive(
         ring_scatter(
             lambda step: row_outer(raw_grad[:, step * pair : (step + 1) * pair], qkv_weights)
         ),
         hooks=[lambda: tail] + [lambda: None] * (chips - 3) + [keep_done],
+        along=done,
+        beside=chips - 2,
     )
     sums, grad_tail, grad_out = tail[0].result.reshape(-1), tail[1].result, out_job.result
     feed_grads, layer_out = done

time: 522 us -> 518 us (level)
  matrix products: 45 us -> 37.1 us
    pallas_call x0 -> x1, Pallas kernels: none -> 8.63 us  [feed_beside(): pl.pallas_call(functools.partial(feed_kernel, len(tokens)), grid=(3,), in...]
    dot_general x14 -> x12, matrix products: 20.7 us -> 16.6 us  [col_inner(): lax.dot_general(left, right, CONTRACT_COLS, preferred_element_type=F32)]
    dot_general x11 -> x9, matrix products: 18.8 us -> 15.1 us  [dot(): return jnp.dot(left, right, preferred_element_type=F32)]
    unnamed x171 -> x174, local copies, waits for them, and re-layouts: 32.3 us -> 33.4 us
  transfers between devices with their start and end apart: 100 -> 100, of which waited for: 46 -> 45; matrix products, arithmetic and copies ran while one was open for 18% -> 18% of each run, Pallas kernels for 14% -> 15%
where the time goes in v5:
time: 518 us; the launch traced here: 509 us
  waiting for transfers between devices  219 us (42%)
  Pallas kernels  76.7 us (15%)
  starting transfers between devices  75.2 us (15%)
  local copies, waits for them, and re-layouts  57.5 us (11%)
  matrix products  37.1 us (7%)
  other arithmetic  27.2 us (5%)
  between operations  16 us (3%)
    ppermute x97, waiting for transfers between devices, phase(): lax.ppermute(value, move[0], move[1])  212 us
    ppermute x97, starting transfers between devices, phase(): lax.ppermute(value, move[0], move[1])  75.1 us
    unnamed x174, local copies, waits for them, and re-layouts  33.4 us
    pallas_call x4, Pallas kernels, attend_back(): pl.pallas_call(functools.partial(attend_back_kernel, 512, own, first), gr...  28.1 us
    pallas_call x4, Pallas kernels, attend(): pl.pallas_call(functools.partial(attend_kernel, first, last), grid=(rows...  17.4 us
    dot_general x12, matrix products, col_inner(): lax.dot_general(left, right, CONTRACT_COLS, preferred_element_type=F32)  16.6 us
    dot_general x9, matrix products, dot(): return jnp.dot(left, right, preferred_element_type=F32)  15.1 us
    pallas_call x3, Pallas kernels, weight_grads(): pl.pallas_call(functools.partial(weight_grad_kernel, count, len(lefts)),...  14.3 us
  transfers between devices with their start and end apart: 100, of which 45 were waited for; matrix products, arithmetic and copies ran while one was open for 18% of the time, Pallas kernels for 15%

profile of v5, /device:TPU:0, one launch (start us, length us, event | category | flops | bytes accessed | tf_op | source)
XLA Modules:
  0.0 509.2 jit_solution(15400917977020533786)
XLA Ops:
  8.9 2.6 collective-permute-start.1
  21.2 3.3 pad_maximum_fusion
  26.7 10.4 %collective-permute-done.2 = bf16[128,2048]{1,0:T(8,128)(2,1)} collective-permute-done((bf16[128,2048]{1,0:T(8,128)(2,1)}, bf16[128,2048]{1,0:T(8,128)(2,1)}, u32[]{:S(2)}, u32[]{:S(2)}) %collective-permute-start.2) | collective-permute-done | bytes 524320 | tf_op jit(solution)/shard_map/ppermute | solution.py:120
  44.1 9.5 %collective-permute-done.7 = bf16[128,2048]{1,0:T(8,128)(2,1)} collective-permute-done((bf16[128,2048]{1,0:T(8,128)(2,1)}, bf16[128,2048]{1,0:T(8,128)(2,1)}, u32[]{:S(2)}, u32[]{:S(2)}) %collective-permute-start.7) | collective-permute-done | bytes 524320 | tf_op jit(solution)/shard_map/ppermute | solution.py:120
  78.3 3.2 fusion
  87.6 7.3 %collective-permute-done.19.refs_2_ = bf16[128,1024]{1,0:T(8,128)(2,1)S(1)} collective-permute-done((bf16[128,1024]{1,0:T(8,128)(2,1)}, bf16[128,1024]{1,0:T(8,128)(2,1)S(1)}, u32[]{:S(2)}, u32[]{:S(2)}) %collective-permute-start.19) | collective-permute-done | bytes 262176 | tf_op jit(solution)/shard_map/ppermute | solution.py:120
  94.9 4.8 collective-permute-done.20.refs_3_
  105.5 4.3 shard_map.258.refs_6_
  111.2 5.0 collective-permute-done.21.refs_1_.refs_2_.k_ref.v_ref
  118.3 3.1 collective-permute-done.24.refs_6_
  129.0 4.3 shard_map.259.refs_6_
  133.3 4.3 shard_map.260.refs_6_
  137.7 3.2 collective-permute-done.28.refs_4_
  141.0 4.4 shard_map.261
  148.4 4.8 collective-permute-done.30.refs_2_
  162.5 13.0 %collective-permute-done.34 = bf16[128,2048]{1,0:T(8,128)(2,1)S(1)} collective-permute-done((bf16[128,2048]{1,0:T(8,128)(2,1)S(1)}, bf16[128,2048]{1,0:T(8,128)(2,1)S(1)}, u32[]{:S(2)}, u32[]{:S(2)}) %collective-permute-start.34) | collective-permute-done | bytes 524320 | tf_op jit(solution)/shard_map/ppermute | solution.py:120
  178.5 12.4 %collective-permute-done.37 = bf16[128,2048]{1,0:T(8,128)(2,1)S(1)} collective-permute-done((bf16[128,2048]{1,0:T(8,128)(2,1)S(1)}, bf16[128,2048]{1,0:T(8,128)(2,1)S(1)}, u32[]{:S(2)}, u32[]{:S(2)}) %collective-permute-start.37) | collective-permute-done | bytes 524320 | tf_op jit(solution)/shard_map/ppermute | solution.py:120
  190.8 10.5 %collective-permute-done.38 = bf16[128,2048]{1,0:T(8,128)(2,1)S(1)} collective-permute-done((bf16[128,2048]{1,0:T(8,128)(2,1)S(1)}, bf16[128,2048]{1,0:T(8,128)(2,1)S(1)}, u32[]{:S(2)}, u32[]{:S(2)}) %collective-permute-start.38) | collective-permute-done | bytes 524320 | tf_op jit(solution)/shard_map/ppermute | solution.py:120
  207.0 7.2 %all-gather.6.cloned.1.call-done = bf16[2304,2048]{1,0:T(8,128)(2,1)} async-done(((bf16[576,2048]{1,0:T(8,128)(2,1)}), bf16[2304,2048]{1,0:T(8,128)(2,1)}) %all-gather.6.cloned.1.call-update) | async-done | bytes 9437200 | tf_op jit(solution)/shard_map/all_gather | solution.py:1019
  214.2 4.5 fusion.86
  219.7 10.5 %collective-permute-done.42.refs_2_.refs_4_ = bf16[128,2048]{1,0:T(8,128)(2,1)S(1)} collective-permute-done((bf16[128,2048]{1,0:T(8,128)(2,1)S(1)}, bf16[128,2048]{1,0:T(8,128)(2,1)S(1)}, u32[]{:S(2)}, u32[]{:S(2)}) %collective-permute-start.42) | collective-permute-done | bytes 524320 | tf_op jit(solution)/shard_map/ppermute | solution.py:120
  239.0 7.7 %collective-permute-done.45.refs_6_ = bf16[128,2048]{1,0:T(8,128)(2,1)S(1)} collective-permute-done((bf16[128,2048]{1,0:T(8,128)(2,1)S(1)}, bf16[128,2048]{1,0:T(8,128)(2,1)S(1)}, u32[]{:S(2)}, u32[]{:S(2)}) %collective-permute-start.45) | collective-permute-done | bytes 524320 | tf_op jit(solution)/shard_map/ppermute | solution.py:120
  257.8 8.6 %shard_map.264 = (bf16[512,768]{1,0:T(8,128)(2,1)S(1)}, bf16[512,768]{1,0:T(8,128)(2,1)S(1)}, bf16[512,768]{1,0:T(8,128)(2,1)S(1)}, bf16[512,2048]{1,0:T(8,128)(2,1)S(1)}) custom-call(bf16[128,2048]{1,0:T(8,128)(2,1)S(1)} %collective-permute-done.41.refs_0_.refs_2_, bf16[128,2048]{1,0:T(8,128)(2,1)S(1)} %collective-permute-done.43.refs_1_.refs_3_, ...), custom_call_target="tpu_custom_call" | custom-call | flops 1 | bytes 1 | tf_op jit(solution)/shard_map/pallas_call | solution.py:573
  266.6 3.1 collective-permute-done.48
  275.0 3.2 convolution_convert_fusion
  278.2 4.8 shard_map.265.refs_11_
  282.9 4.8 shard_map.266.refs_11_
  289.7 8.7 %collective-permute-done.52 = bf16[128,2048]{1,0:T(8,128)(2,1)S(1)} collective-permute-done((bf16[128,2048]{1,0:T(8,128)(2,1)S(1)}, bf16[128,2048]{1,0:T(8,128)(2,1)S(1)}, u32[]{:S(2)}, u32[]{:S(2)}) %collective-permute-start.52) | collective-permute-done | bytes 524320 | tf_op jit(solution)/shard_map/ppermute | solution.py:120
  299.1 2.6 constant_dynamic-update-slice_fusion.23
  305.9 4.8 shard_map.267
  310.7 3.6 copy-done
  314.3 4.1 collective-permute-done.55
  318.4 10.8 %collective-permute-done.56 = bf16[128,2048]{1,0:T(8,128)(2,1)} collective-permute-done((bf16[128,2048]{1,0:T(8,128)(2,1)S(1)}, bf16[128,2048]{1,0:T(8,128)(2,1)}, u32[]{:S(2)}, u32[]{:S(2)}) %collective-permute-start.56) | collective-permute-done | bytes 524320 | tf_op jit(solution)/shard_map/ppermute | solution.py:120
  336.9 11.8 %collective-permute-done.59 = bf16[128,2048]{1,0:T(8,128)(2,1)S(1)} collective-permute-done((bf16[128,2048]{1,0:T(8,128)(2,1)}, bf16[128,2048]{1,0:T(8,128)(2,1)S(1)}, u32[]{:S(2)}, u32[]{:S(2)}) %collective-permute-start.59) | collective-permute-done | bytes 524320 | tf_op jit(solution)/shard_map/ppermute | solution.py:120
  361.4 7.0 %shard_map.270 = (f32[2048,128]{1,0:T(8,128)S(1)}, f32[1024,128]{1,0:T(8,128)S(1)}, f32[1024,128]{1,0:T(8,128)S(1)}, f32[8,2048]{1,0:T(8,128)S(1)}) custom-call(bf16[2048,128]{1,0:T(8,128)(2,1)S(1)} %copy-done.30, bf16[2048,128]{1,0:T(8,128)(2,1)S(1)} %shard_map.269.g_ref, f32[8,2048]{1,0:T(8,128)S(1)} %copy-done.40, ...), custom_call_target="tpu_custom_call" | custom-call | flops 8589934592 | bytes 1048576 | tf_op jit(solution)/shard_map/pallas_call | solution.py:806
  372.5 7.0 %shard_map.271 = (f32[2048,128]{1,0:T(8,128)S(1)}, f32[1024,128]{1,0:T(8,128)S(1)}, f32[1024,128]{1,0:T(8,128)S(1)}) custom-call(bf16[2048,128]{1,0:T(8,128)(2,1)S(1)} %copy-done.30, bf16[2048,128]{1,0:T(8,128)(2,1)S(1)} %shard_map.269.g_ref, f32[8,2048]{1,0:T(8,128)S(1)} %copy-done.40, s32[1,1024]{1,0:T(1,128)S(1)} %get-tuple-element.746.refs_3_.refs_5_.qpos_ref.kpos_ref, ...), custom_call_target="tpu_custom_call" | custom-call | flops 8589934592 | bytes 1048576 | tf_op jit(solution)/shard_map/pallas_call | solution.py:806
  379.4 7.2 %shard_map.272 = (f32[2048,128]{1,0:T(8,128)S(1)}, f32[1024,128]{1,0:T(8,128)S(1)}, f32[1024,128]{1,0:T(8,128)S(1)}) custom-call(bf16[2048,128]{1,0:T(8,128)(2,1)S(1)} %copy-done.30, bf16[2048,128]{1,0:T(8,128)(2,1)S(1)} %shard_map.269.g_ref, f32[8,2048]{1,0:T(8,128)S(1)} %copy-done.40, s32[1,1024]{1,0:T(1,128)S(1)} %get-tuple-element.746.refs_3_.refs_5_.qpos_ref.kpos_ref, ...), custom_call_target="tpu_custom_call" | custom-call | flops 8589934592 | bytes 1048576 | tf_op jit(solution)/shard_map/pallas_call | solution.py:806
  390.7 7.0 %shard_map.273 = (f32[2048,128]{1,0:T(8,128)S(1)}, f32[1024,128]{1,0:T(8,128)S(1)}, f32[1024,128]{1,0:T(8,128)S(1)}) custom-call(bf16[2048,128]{1,0:T(8,128)(2,1)S(1)} %copy-done.30, bf16[2048,128]{1,0:T(8,128)(2,1)S(1)} %shard_map.269.g_ref, f32[8,2048]{1,0:T(8,128)S(1)} %copy-done.40, s32[1,1024]{1,0:T(1,128)S(1)} %get-tuple-element.746.refs_3_.refs_5_.qpos_ref.kpos_ref, ...), custom_call_target="tpu_custom_call" | custom-call | flops 8589934592 | bytes 1048576 | tf_op jit(solution)/shard_map/pallas_call | solution.py:806
  397.7 7.0 %collective-permute-done.70.refs_7_ = bf16[1024,256]{1,0:T(8,128)(2,1)S(1)} collective-permute-done((bf16[1024,256]{1,0:T(8,128)(2,1)S(1)}, bf16[1024,256]{1,0:T(8,128)(2,1)S(1)}, u32[]{:S(2)}, u32[]{:S(2)}) %collective-permute-start.70) | collective-permute-done | bytes 524320 | tf_op jit(solution)/shard_map/ppermute | solution.py:120
  404.8 9.9 %collective-permute-done.73 = bf16[128,2048]{1,0:T(8,128)(2,1)S(1)} collective-permute-done((bf16[128,2048]{1,0:T(8,128)(2,1)S(1)}, bf16[128,2048]{1,0:T(8,128)(2,1)S(1)}, u32[]{:S(2)}, u32[]{:S(2)}) %collective-permute-start.73) | collective-permute-done | bytes 524320 | tf_op jit(solution)/shard_map/ppermute | solution.py:120
  419.6 5.9 %collective-permute-done.76.refs_2_ = bf16[128,1024]{1,0:T(8,128)(2,1)S(1)} collective-permute-done((bf16[128,1024]{1,0:T(8,128)(2,1)S(1)}, bf16[128,1024]{1,0:T(8,128)(2,1)S(1)}, u32[]{:S(2)}, u32[]{:S(2)}) %collective-permute-start.76) | collective-permute-done | bytes 262176 | tf_op jit(solution)/shard_map/ppermute | solution.py:120
  425.5 4.7 collective-permute-done.77.refs_3_
  433.5 2.6 fusion.88
  446.7 4.8 collective-permute-done.83
  451.5 3.4 collective-permute-done.79
  466.7 7.4 %collective-permute-done.84 = bf16[128,2048]{1,0:T(8,128)(2,1)S(1)} collective-permute-done((bf16[128,2048]{1,0:T(8,128)(2,1)S(1)}, bf16[128,2048]{1,0:T(8,128)(2,1)S(1)}, u32[]{:S(2)}, u32[]{:S(2)}) %collective-permute-start.84) | collective-permute-done | bytes 524320 | tf_op jit(solution)/shard_map/ppermute | solution.py:120
  482.4 9.2 %collective-permute-done.89 = bf16[128,2048]{1,0:T(8,128)(2,1)S(1)} collective-permute-done((bf16[128,2048]{1,0:T(8,128)(2,1)S(1)}, bf16[128,2048]{1,0:T(8,128)(2,1)S(1)}, u32[]{:S(2)}, u32[]{:S(2)}) %collective-permute-start.89) | collective-permute-done | bytes 524320 | tf_op jit(solution)/shard_map/ppermute | solution.py:120
  491.6 2.9 collective-permute-start.95
  (464 shorter events, 195.9 us)
Async XLA Ops:
  7.2 148.5 %all-gather.4.cloned.1.call-start = ((), (), s32[]{:S(2)}) async-start(), calls=%async_computation.1 | async-start | bytes 1310720 | tf_op jit(solution)/shard_map/all_gather | solution.py:912
  8.4 16.3 %collective-permute-start = (bf16[128,2048]{1,0:T(8,128)(2,1)}, bf16[128,2048]{1,0:T(8,128)(2,1)}, u32[]{:S(2)}, u32[]{:S(2)}) collective-permute-start(bf16[128,2048]{1,0:T(8,128)(2,1)} %param.16), channel_id=1, source_target_pairs={{0,1},{1,0},{2,3},{3,2},{4,5},{5,4},{6,7},{7,6},{8,9},{9,8},{10,11... | collective-permute-start | bytes 1572872 | tf_op jit(solution)/shard_map/ppermute | solution.py:120
  8.9 17.8 %collective-permute-start.1 = (bf16[128,2048]{1,0:T(8,128)(2,1)}, bf16[128,2048]{1,0:T(8,128)(2,1)}, u32[]{:S(2)}, u32[]{:S(2)}) collective-permute-start(bf16[128,2048]{1,0:T(8,128)(2,1)} %param.16), channel_id=1, source_target_pairs={{0,2},{1,3},{2,4},{3,5},{4,6},{5,7},{6,0},{7,1},{8,10},{9,11},{10,... | collective-permute-start | bytes 1572872 | tf_op jit(solution)/shard_map/ppermute | solution.py:120
  11.5 25.5 %collective-permute-start.2 = (bf16[128,2048]{1,0:T(8,128)(2,1)}, bf16[128,2048]{1,0:T(8,128)(2,1)}, u32[]{:S(2)}, u32[]{:S(2)}) collective-permute-start(bf16[128,2048]{1,0:T(8,128)(2,1)} %param.16), channel_id=1, source_target_pairs={{0,6},{1,7},{2,0},{3,1},{4,2},{5,3},{6,4},{7,5},{8,14},{9,15},{10,... | collective-permute-start | bytes 1572872 | tf_op jit(solution)/shard_map/ppermute | solution.py:120
  13.7 23.4 %collective-permute-start.3 = (bf16[128,2048]{1,0:T(8,128)(2,1)S(1)}, bf16[128,2048]{1,0:T(8,128)(2,1)}, u32[]{:S(2)}, u32[]{:S(2)}) collective-permute-start(bf16[128,2048]{1,0:T(8,128)(2,1)S(1)} %pad_maximum_fusion.4), channel_id=1, source_target_pairs={{0,8},{8,0},{16,24},{24,16},{1,9},{9,1},{17,25},{25,17},{2,10},{10... | collective-permute-start | bytes 1572872 | tf_op jit(solution)/shard_map/ppermute | solution.py:120
  15.3 21.8 %collective-permute-start.4 = (bf16[128,2048]{1,0:T(8,128)(2,1)S(1)}, bf16[128,2048]{1,0:T(8,128)(2,1)}, u32[]{:S(2)}, u32[]{:S(2)}) collective-permute-start(bf16[128,2048]{1,0:T(8,128)(2,1)S(1)} %pad_maximum_fusion.4), channel_id=1, source_target_pairs={{0,16},{8,24},{16,0},{24,8},{1,17},{9,25},{17,1},{25,9},{2,18},{10... | collective-permute-start | bytes 1572872 | tf_op jit(solution)/shard_map/ppermute | solution.py:120
  37.6 16.0 %collective-permute-start.7 = (bf16[128,2048]{1,0:T(8,128)(2,1)}, bf16[128,2048]{1,0:T(8,128)(2,1)}, u32[]{:S(2)}, u32[]{:S(2)}) collective-permute-start(bf16[128,2048]{1,0:T(8,128)(2,1)} %collective-permute-done.1), channel_id=1, source_target_pairs={{0,2},{1,3},{2,4},{3,5},{4,6},{5,7},{6,0},{7,1},{8,10},{9,11},{10,... | collective-permute-start | bytes 1572872 | tf_op jit(solution)/shard_map/ppermute | solution.py:120
  38.7 14.9 %collective-permute-start.8 = (bf16[128,2048]{1,0:T(8,128)(2,1)}, bf16[128,2048]{1,0:T(8,128)(2,1)}, u32[]{:S(2)}, u32[]{:S(2)}) collective-permute-start(bf16[128,2048]{1,0:T(8,128)(2,1)} %collective-permute-done.3), channel_id=1, source_target_pairs={{0,16},{8,24},{16,0},{24,8},{1,17},{9,25},{17,1},{25,9},{2,18},{10... | collective-permute-start | bytes 1572872 | tf_op jit(solution)/shard_map/ppermute | solution.py:120
  68.3 145.9 %all-gather.6.cloned.1.call-start = ((), (), s32[]{:S(2)}) async-start(), calls=%async_computation.2 | async-start | bytes 11796480 | tf_op jit(solution)/shard_map/all_gather | solution.py:1019
  68.4 15.9 %collective-permute-start.16 = (bf16[128,2048]{1,0:T(8,128)(2,1)S(1)}, bf16[128,2048]{1,0:T(8,128)(2,1)S(1)}, u32[]{:S(2)}, u32[]{:S(2)}) collective-permute-start(bf16[128,2048]{1,0:T(8,128)(2,1)S(1)} %constant_dynamic-slice_fusion.refs_0_), channel_id=1, source_target_pairs={{0,1},{1,0},{2,3},{3,2},{4,5},{5,4},{6,7},{7,6},{8,9},{9,8},{10,11... | collective-permute-start | bytes 1572872 | tf_op jit(solution)/shard_map/ppermute | solution.py:120
  68.5 16.1 %collective-permute-start.17 = (bf16[128,2048]{1,0:T(8,128)(2,1)S(1)}, bf16[128,2048]{1,0:T(8,128)(2,1)S(1)}, u32[]{:S(2)}, u32[]{:S(2)}) collective-permute-start(bf16[128,2048]{1,0:T(8,128)(2,1)S(1)} %constant_dynamic-slice_fusion.refs_0_), channel_id=1, source_target_pairs={{0,2},{1,3},{2,4},{3,5},{4,6},{5,7},{6,0},{7,1},{8,10},{9,11},{10,... | collective-permute-start | bytes 1572872 | tf_op jit(solution)/shard_map/ppermute | solution.py:120
  105.3 16.1 %collective-permute-start.24 = (bf16[128,2048]{1,0:T(8,128)(2,1)S(1)}, bf16[128,2048]{1,0:T(8,128)(2,1)S(1)}, u32[]{:S(2)}, u32[]{:S(2)}) collective-permute-start(bf16[128,2048]{1,0:T(8,128)(2,1)S(1)} %collective-permute-done.17.refs_2_), channel_id=1, source_target_pairs={{0,2},{1,3},{2,4},{3,5},{4,6},{5,7},{6,0},{7,1},{8,10},{9,11},{10,... | collective-permute-start | bytes 1572872 | tf_op jit(solution)/shard_map/ppermute | solution.py:120
  121.4 339.0 %reduce-scatter.4.cloned.1.call-start = ((), (), s32[]{:S(2)}) async-start(), calls=%async_computation.3 | async-start | bytes 11796480
  124.6 16.3 %collective-permute-start.28 = (bf16[128,2048]{1,0:T(8,128)(2,1)S(1)}, bf16[128,2048]{1,0:T(8,128)(2,1)S(1)}, u32[]{:S(2)}, u32[]{:S(2)}) collective-permute-start(bf16[128,2048]{1,0:T(8,128)(2,1)S(1)} %collective-permute-done.24.refs_6_), channel_id=1, source_target_pairs={{0,2},{1,3},{2,4},{3,5},{4,6},{5,7},{6,0},{7,1},{8,10},{9,11},{10,... | collective-permute-start | bytes 1572872 | tf_op jit(solution)/shard_map/ppermute | solution.py:120
  161.2 14.3 %collective-permute-start.34 = (bf16[128,2048]{1,0:T(8,128)(2,1)S(1)}, bf16[128,2048]{1,0:T(8,128)(2,1)S(1)}, u32[]{:S(2)}, u32[]{:S(2)}) collective-permute-start(bf16[128,2048]{1,0:T(8,128)(2,1)S(1)} %fusion.32), channel_id=1, source_target_pairs={{0,6},{1,7},{2,0},{3,1},{4,2},{5,3},{6,4},{7,5},{8,14},{9,15},{10,... | collective-permute-start | bytes 1572872 | tf_op jit(solution)/shard_map/ppermute | solution.py:120
  175.9 14.9 %collective-permute-start.37 = (bf16[128,2048]{1,0:T(8,128)(2,1)S(1)}, bf16[128,2048]{1,0:T(8,128)(2,1)S(1)}, u32[]{:S(2)}, u32[]{:S(2)}) collective-permute-start(bf16[128,2048]{1,0:T(8,128)(2,1)S(1)} %get-tuple-element.473), channel_id=1, source_target_pairs={{0,6},{1,7},{2,0},{3,1},{4,2},{5,3},{6,4},{7,5},{8,14},{9,15},{10,... | collective-permute-start | bytes 1572872 | tf_op jit(solution)/shard_map/ppermute | solution.py:120
  178.5 22.9 %collective-permute-start.38 = (bf16[128,2048]{1,0:T(8,128)(2,1)S(1)}, bf16[128,2048]{1,0:T(8,128)(2,1)S(1)}, u32[]{:S(2)}, u32[]{:S(2)}) collective-permute-start(bf16[128,2048]{1,0:T(8,128)(2,1)S(1)} %get-tuple-element.474), channel_id=1, source_target_pairs={{0,2},{1,3},{2,4},{3,5},{4,6},{5,7},{6,0},{7,1},{8,10},{9,11},{10,... | collective-permute-start | bytes 1572872 | tf_op jit(solution)/shard_map/ppermute | solution.py:120
  178.5 22.9 %collective-permute-start.39 = (bf16[128,2048]{1,0:T(8,128)(2,1)S(1)}, bf16[128,2048]{1,0:T(8,128)(2,1)S(1)}, u32[]{:S(2)}, u32[]{:S(2)}) collective-permute-start(bf16[128,2048]{1,0:T(8,128)(2,1)S(1)} %get-tuple-element.475), channel_id=1, source_target_pairs={{0,1},{1,0},{2,3},{3,2},{4,5},{5,4},{6,7},{7,6},{8,9},{9,8},{10,11... | collective-permute-start | bytes 1572872 | tf_op jit(solution)/shard_map/ppermute | solution.py:120
  203.0 15.7 %collective-permute-start.40 = (bf16[128,2048]{1,0:T(8,128)(2,1)S(1)}, bf16[128,2048]{1,0:T(8,128)(2,1)S(1)}, u32[]{:S(2)}, u32[]{:S(2)}) collective-permute-start(bf16[128,2048]{1,0:T(8,128)(2,1)S(1)} %multiply_convert_fusion.refs_0_), channel_id=1, source_target_pairs={{0,1},{1,0},{2,3},{3,2},{4,5},{5,4},{6,7},{7,6},{8,9},{9,8},{10,11... | collective-permute-start | bytes 1572872 | tf_op jit(solution)/shard_map/ppermute | solution.py:120
  203.1 16.6 %collective-permute-start.41 = (bf16[128,2048]{1,0:T(8,128)(2,1)S(1)}, bf16[128,2048]{1,0:T(8,128)(2,1)S(1)}, u32[]{:S(2)}, u32[]{:S(2)}) collective-permute-start(bf16[128,2048]{1,0:T(8,128)(2,1)S(1)} %multiply_convert_fusion.refs_0_), channel_id=1, source_target_pairs={{0,2},{1,3},{2,4},{3,5},{4,6},{5,7},{6,0},{7,1},{8,10},{9,11},{10,... | collective-permute-start | bytes 1572872 | tf_op jit(solution)/shard_map/ppermute | solution.py:120
  204.9 25.2 %collective-permute-start.42 = (bf16[128,2048]{1,0:T(8,128)(2,1)S(1)}, bf16[128,2048]{1,0:T(8,128)(2,1)S(1)}, u32[]{:S(2)}, u32[]{:S(2)}) collective-permute-start(bf16[128,2048]{1,0:T(8,128)(2,1)S(1)} %multiply_convert_fusion.refs_0_), channel_id=1, source_target_pairs={{0,6},{1,7},{2,0},{3,1},{4,2},{5,3},{6,4},{7,5},{8,14},{9,15},{10,... | collective-permute-start | bytes 1572872 | tf_op jit(solution)/shard_map/ppermute | solution.py:120
  230.7 16.0 %collective-permute-start.45 = (bf16[128,2048]{1,0:T(8,128)(2,1)S(1)}, bf16[128,2048]{1,0:T(8,128)(2,1)S(1)}, u32[]{:S(2)}, u32[]{:S(2)}) collective-permute-start(bf16[128,2048]{1,0:T(8,128)(2,1)S(1)} %collective-permute-done.41.refs_0_.refs_2_), channel_id=1, source_target_pairs={{0,2},{1,3},{2,4},{3,5},{4,6},{5,7},{6,0},{7,1},{8,10},{9,11},{10,... | collective-permute-start | bytes 1572872 | tf_op jit(solution)/shard_map/ppermute | solution.py:120
  255.5 14.2 %collective-permute-start.48 = (bf16[128,2048]{1,0:T(8,128)(2,1)S(1)}, bf16[128,2048]{1,0:T(8,128)(2,1)S(1)}, u32[]{:S(2)}, u32[]{:S(2)}) collective-permute-start(bf16[128,2048]{1,0:T(8,128)(2,1)S(1)} %fusion.30), channel_id=1, source_target_pairs={{0,6},{1,7},{2,0},{3,1},{4,2},{5,3},{6,4},{7,5},{8,14},{9,15},{10,... | collective-permute-start | bytes 1572872 | tf_op jit(solution)/shard_map/ppermute | solution.py:120
  272.8 16.9 %collective-permute-start.51 = (bf16[128,2048]{1,0:T(8,128)(2,1)S(1)}, bf16[128,2048]{1,0:T(8,128)(2,1)S(1)}, u32[]{:S(2)}, u32[]{:S(2)}) collective-permute-start(bf16[128,2048]{1,0:T(8,128)(2,1)S(1)} %get-tuple-element.526), channel_id=1, source_target_pairs={{0,6},{1,7},{2,0},{3,1},{4,2},{5,3},{6,4},{7,5},{8,14},{9,15},{10,... | collective-permute-start | bytes 1572872 | tf_op jit(solution)/shard_map/ppermute | solution.py:120
  275.0 23.5 %collective-permute-start.52 = (bf16[128,2048]{1,0:T(8,128)(2,1)S(1)}, bf16[128,2048]{1,0:T(8,128)(2,1)S(1)}, u32[]{:S(2)}, u32[]{:S(2)}) collective-permute-start(bf16[128,2048]{1,0:T(8,128)(2,1)S(1)} %get-tuple-element.527), channel_id=1, source_target_pairs={{0,2},{1,3},{2,4},{3,5},{4,6},{5,7},{6,0},{7,1},{8,10},{9,11},{10,... | collective-permute-start | bytes 1572872 | tf_op jit(solution)/shard_map/ppermute | solution.py:120
  275.0 23.5 %collective-permute-start.53 = (bf16[128,2048]{1,0:T(8,128)(2,1)S(1)}, bf16[128,2048]{1,0:T(8,128)(2,1)S(1)}, u32[]{:S(2)}, u32[]{:S(2)}) collective-permute-start(bf16[128,2048]{1,0:T(8,128)(2,1)S(1)} %slice.391), channel_id=1, source_target_pairs={{0,1},{1,0},{2,3},{3,2},{4,5},{5,4},{6,7},{7,6},{8,9},{9,8},{10,11... | collective-permute-start | bytes 1572872 | tf_op jit(solution)/shard_map/ppermute | solution.py:120
  301.7 16.7 %collective-permute-start.55 = (bf16[128,2048]{1,0:T(8,128)(2,1)S(1)}, bf16[128,2048]{1,0:T(8,128)(2,1)}, u32[]{:S(2)}, u32[]{:S(2)}) collective-permute-start(bf16[128,2048]{1,0:T(8,128)(2,1)S(1)} %get-tuple-element.542), channel_id=1, source_target_pairs={{0,2},{1,3},{2,4},{3,5},{4,6},{5,7},{6,0},{7,1},{8,10},{9,11},{10,... | collective-permute-start | bytes 1572872 | tf_op jit(solution)/shard_map/ppermute | solution.py:120
  303.5 25.8 %collective-permute-start.56 = (bf16[128,2048]{1,0:T(8,128)(2,1)S(1)}, bf16[128,2048]{1,0:T(8,128)(2,1)}, u32[]{:S(2)}, u32[]{:S(2)}) collective-permute-start(bf16[128,2048]{1,0:T(8,128)(2,1)S(1)} %get-tuple-element.542), channel_id=1, source_target_pairs={{0,6},{1,7},{2,0},{3,1},{4,2},{5,3},{6,4},{7,5},{8,14},{9,15},{10,... | collective-permute-start | bytes 1572872 | tf_op jit(solution)/shard_map/ppermute | solution.py:120
  332.8 15.9 %collective-permute-start.59 = (bf16[128,2048]{1,0:T(8,128)(2,1)}, bf16[128,2048]{1,0:T(8,128)(2,1)S(1)}, u32[]{:S(2)}, u32[]{:S(2)}) collective-permute-start(bf16[128,2048]{1,0:T(8,128)(2,1)} %collective-permute-done.55), channel_id=1, source_target_pairs={{0,2},{1,3},{2,4},{3,5},{4,6},{5,7},{6,0},{7,1},{8,10},{9,11},{10,... | collective-permute-start | bytes 1572872 | tf_op jit(solution)/shard_map/ppermute | solution.py:120
  368.6 18.1 %collective-permute-start.65 = (bf16[1024,128]{1,0:T(8,128)(2,1)S(1)}, bf16[1024,128]{1,0:T(8,128)(2,1)S(1)}, u32[]{:S(2)}, u32[]{:S(2)}) collective-permute-start(bf16[1024,128]{1,0:T(8,128)(2,1)S(1)} %convert_element_type.333), channel_id=1, source_target_pairs={{0,16},{8,24},{16,0},{24,8},{1,17},{9,25},{17,1},{25,9},{2,18},{10... | collective-permute-start | bytes 786440 | tf_op jit(solution)/shard_map/ppermute | solution.py:120
  370.2 16.5 %collective-permute-start.66 = (bf16[1024,128]{1,0:T(8,128)(2,1)S(1)}, bf16[1024,128]{1,0:T(8,128)(2,1)S(1)}, u32[]{:S(2)}, u32[]{:S(2)}) collective-permute-start(bf16[1024,128]{1,0:T(8,128)(2,1)S(1)} %convert_element_type.334), channel_id=1, source_target_pairs={{0,8},{8,0},{16,24},{24,16},{1,9},{9,1},{17,25},{25,17},{2,10},{10... | collective-permute-start | bytes 786440 | tf_op jit(solution)/shard_map/ppermute | solution.py:120
  371.6 15.1 %collective-permute-start.67 = (bf16[128,2048]{1,0:T(8,128)(2,1)S(1)}, bf16[128,2048]{1,0:T(8,128)(2,1)S(1)}, u32[]{:S(2)}, u32[]{:S(2)}) collective-permute-start(bf16[128,2048]{1,0:T(8,128)(2,1)S(1)} %add_convert_fusion.3), channel_id=1, source_target_pairs={{0,6},{1,7},{2,0},{3,1},{4,2},{5,3},{6,4},{7,5},{8,14},{9,15},{10,... | collective-permute-start | bytes 1572872 | tf_op jit(solution)/shard_map/ppermute | solution.py:120
  371.8 14.9 %collective-permute-start.68 = (bf16[128,2048]{1,0:T(8,128)(2,1)S(1)}, bf16[128,2048]{1,0:T(8,128)(2,1)S(1)}, u32[]{:S(2)}, u32[]{:S(2)}) collective-permute-start(bf16[128,2048]{1,0:T(8,128)(2,1)S(1)} %get-tuple-element.590), channel_id=1, source_target_pairs={{0,1},{1,0},{2,3},{3,2},{4,5},{5,4},{6,7},{7,6},{8,9},{9,8},{10,11... | collective-permute-start | bytes 1572872 | tf_op jit(solution)/shard_map/ppermute | solution.py:120
  372.4 14.4 %collective-permute-start.69 = (bf16[128,2048]{1,0:T(8,128)(2,1)S(1)}, bf16[128,2048]{1,0:T(8,128)(2,1)S(1)}, u32[]{:S(2)}, u32[]{:S(2)}) collective-permute-start(bf16[128,2048]{1,0:T(8,128)(2,1)S(1)} %get-tuple-element.591), channel_id=1, source_target_pairs={{0,1},{1,0},{2,3},{3,2},{4,5},{5,4},{6,7},{7,6},{8,9},{9,8},{10,11... | collective-permute-start | bytes 1572872 | tf_op jit(solution)/shard_map/ppermute | solution.py:120
  387.5 17.2 %collective-permute-start.70 = (bf16[1024,256]{1,0:T(8,128)(2,1)S(1)}, bf16[1024,256]{1,0:T(8,128)(2,1)S(1)}, u32[]{:S(2)}, u32[]{:S(2)}) collective-permute-start(bf16[1024,256]{1,0:T(8,128)(2,1)S(1)} %pad_maximum_fusion.5), channel_id=1, source_target_pairs={{0,8},{8,0},{16,24},{24,16},{1,9},{9,1},{17,25},{25,17},{2,10},{10... | collective-permute-start | bytes 1572872 | tf_op jit(solution)/shard_map/ppermute | solution.py:120
  388.2 16.6 %collective-permute-start.71 = (bf16[1024,256]{1,0:T(8,128)(2,1)S(1)}, bf16[1024,256]{1,0:T(8,128)(2,1)S(1)}, u32[]{:S(2)}, u32[]{:S(2)}) collective-permute-start(bf16[1024,256]{1,0:T(8,128)(2,1)S(1)} %pad_maximum_fusion.6), channel_id=1, source_target_pairs={{0,16},{8,24},{16,0},{24,8},{1,17},{9,25},{17,1},{25,9},{2,18},{10... | collective-permute-start | bytes 1572872 | tf_op jit(solution)/shard_map/ppermute | solution.py:120
  388.7 16.1 %collective-permute-start.72 = (bf16[128,2048]{1,0:T(8,128)(2,1)S(1)}, bf16[128,2048]{1,0:T(8,128)(2,1)S(1)}, u32[]{:S(2)}, u32[]{:S(2)}) collective-permute-start(bf16[128,2048]{1,0:T(8,128)(2,1)S(1)} %get-tuple-element.617), channel_id=1, source_target_pairs={{0,6},{1,7},{2,0},{3,1},{4,2},{5,3},{6,4},{7,5},{8,14},{9,15},{10,... | collective-permute-start | bytes 1572872 | tf_op jit(solution)/shard_map/ppermute | solution.py:120
  390.2 24.5 %collective-permute-start.73 = (bf16[128,2048]{1,0:T(8,128)(2,1)S(1)}, bf16[128,2048]{1,0:T(8,128)(2,1)S(1)}, u32[]{:S(2)}, u32[]{:S(2)}) collective-permute-start(bf16[128,2048]{1,0:T(8,128)(2,1)S(1)} %get-tuple-element.618), channel_id=1, source_target_pairs={{0,2},{1,3},{2,4},{3,5},{4,6},{5,7},{6,0},{7,1},{8,10},{9,11},{10,... | collective-permute-start | bytes 1572872 | tf_op jit(solution)/shard_map/ppermute | solution.py:120
  390.7 23.9 %collective-permute-start.74 = (bf16[128,2048]{1,0:T(8,128)(2,1)S(1)}, bf16[128,2048]{1,0:T(8,128)(2,1)S(1)}, u32[]{:S(2)}, u32[]{:S(2)}) collective-permute-start(bf16[128,2048]{1,0:T(8,128)(2,1)S(1)} %slice.255), channel_id=1, source_target_pairs={{0,1},{1,0},{2,3},{3,2},{4,5},{5,4},{6,7},{7,6},{8,9},{9,8},{10,11... | collective-permute-start | bytes 1572872 | tf_op jit(solution)/shard_map/ppermute | solution.py:120
  438.7 16.3 %collective-permute-start.79 = (bf16[128,2048]{1,0:T(8,128)(2,1)S(1)}, bf16[128,2048]{1,0:T(8,128)(2,1)S(1)}, u32[]{:S(2)}, u32[]{:S(2)}) collective-permute-start(bf16[128,2048]{1,0:T(8,128)(2,1)S(1)} %fusion.27), channel_id=1, source_target_pairs={{0,2},{1,3},{2,4},{3,5},{4,6},{5,7},{6,0},{7,1},{8,10},{9,11},{10,... | collective-permute-start | bytes 1572872 | tf_op jit(solution)/shard_map/ppermute | solution.py:120
  439.3 15.6 %collective-permute-start.80 = (bf16[128,2048]{1,0:T(8,128)(2,1)S(1)}, bf16[128,2048]{1,0:T(8,128)(2,1)S(1)}, u32[]{:S(2)}, u32[]{:S(2)}) collective-permute-start(bf16[128,2048]{1,0:T(8,128)(2,1)S(1)} %slice.389), channel_id=1, source_target_pairs={{0,1},{1,0},{2,3},{3,2},{4,5},{5,4},{6,7},{7,6},{8,9},{9,8},{10,11... | collective-permute-start | bytes 1572872 | tf_op jit(solution)/shard_map/ppermute | solution.py:120
  439.8 15.1 %collective-permute-start.82 = (bf16[128,2048]{1,0:T(8,128)(2,1)S(1)}, bf16[128,2048]{1,0:T(8,128)(2,1)S(1)}, u32[]{:S(2)}, u32[]{:S(2)}) collective-permute-start(bf16[128,2048]{1,0:T(8,128)(2,1)S(1)} %get-tuple-element.644), channel_id=1, source_target_pairs={{0,16},{8,24},{16,0},{24,8},{1,17},{9,25},{17,1},{25,9},{2,18},{10... | collective-permute-start | bytes 1572872 | tf_op jit(solution)/shard_map/ppermute | solution.py:120
  459.5 14.6 %collective-permute-start.84 = (bf16[128,2048]{1,0:T(8,128)(2,1)S(1)}, bf16[128,2048]{1,0:T(8,128)(2,1)S(1)}, u32[]{:S(2)}, u32[]{:S(2)}) collective-permute-start(bf16[128,2048]{1,0:T(8,128)(2,1)S(1)} %fusion.29), channel_id=1, source_target_pairs={{0,2},{1,3},{2,4},{3,5},{4,6},{5,7},{6,0},{7,1},{8,10},{9,11},{10,... | collective-permute-start | bytes 1572872 | tf_op jit(solution)/shard_map/ppermute | solution.py:120
  459.5 14.6 %collective-permute-start.85 = (bf16[128,2048]{1,0:T(8,128)(2,1)}, bf16[128,2048]{1,0:T(8,128)(2,1)}, u32[]{:S(2)}, u32[]{:S(2)}) collective-permute-start(bf16[128,2048]{1,0:T(8,128)(2,1)} %slice.388), channel_id=1, source_target_pairs={{0,1},{1,0},{2,3},{3,2},{4,5},{5,4},{6,7},{7,6},{8,9},{9,8},{10,11... | collective-permute-start | bytes 1572872 | tf_op jit(solution)/shard_map/ppermute | solution.py:120
  475.4 16.1 %collective-permute-start.89 = (bf16[128,2048]{1,0:T(8,128)(2,1)S(1)}, bf16[128,2048]{1,0:T(8,128)(2,1)S(1)}, u32[]{:S(2)}, u32[]{:S(2)}) collective-permute-start(bf16[128,2048]{1,0:T(8,128)(2,1)S(1)} %fusion.26), channel_id=1, source_target_pairs={{0,2},{1,3},{2,4},{3,5},{4,6},{5,7},{6,0},{7,1},{8,10},{9,11},{10,... | collective-permute-start | bytes 1572872 | tf_op jit(solution)/shard_map/ppermute | solution.py:120
  475.5 16.1 %collective-permute-start.90 = (bf16[128,2048]{1,0:T(8,128)(2,1)S(1)}, bf16[128,2048]{1,0:T(8,128)(2,1)S(1)}, u32[]{:S(2)}, u32[]{:S(2)}) collective-permute-start(bf16[128,2048]{1,0:T(8,128)(2,1)S(1)} %copy-done.61), channel_id=1, source_target_pairs={{0,1},{1,0},{2,3},{3,2},{4,5},{5,4},{6,7},{7,6},{8,9},{9,8},{10,11... | collective-permute-start | bytes 1572872 | tf_op jit(solution)/shard_map/ppermute | solution.py:120
  475.9 15.6 %collective-permute-start.92 = (bf16[128,2048]{1,0:T(8,128)(2,1)S(1)}, bf16[128,2048]{1,0:T(8,128)(2,1)S(1)}, u32[]{:S(2)}, u32[]{:S(2)}) collective-permute-start(bf16[128,2048]{1,0:T(8,128)(2,1)S(1)} %copy-done.64), channel_id=1, source_target_pairs={{0,8},{8,0},{16,24},{24,16},{1,9},{9,1},{17,25},{25,17},{2,10},{10... | collective-permute-start | bytes 1572872 | tf_op jit(solution)/shard_map/ppermute | solution.py:120
  476.5 15.1 %collective-permute-start.93 = (bf16[128,2048]{1,0:T(8,128)(2,1)S(1)}, bf16[128,2048]{1,0:T(8,128)(2,1)S(1)}, u32[]{:S(2)}, u32[]{:S(2)}) collective-permute-start(bf16[128,2048]{1,0:T(8,128)(2,1)S(1)} %copy-done.63), channel_id=1, source_target_pairs={{0,16},{8,24},{16,0},{24,8},{1,17},{9,25},{17,1},{25,9},{2,18},{10... | collective-permute-start | bytes 1572872 | tf_op jit(solution)/shard_map/ppermute | solution.py:120
  (130 other events, 1262.6 us)
Sparse Core Ops, SparseCore 0:
  68.4 27.5 all-gather.3
  121.5 92.6 all-gather.5
  329.4 105.8 reduce-scatter.3

commit v6 on v5

--- a/solution.py
+++ b/solution.py
@@ -715,7 +715,7 @@
     rows, tokens = query.shape[0], keys.shape[0]
     value_at = values.shape[1] // HD - 1
     own = qpos.shape[1]
-    block = 512
+    block = 1024
     wrap = own // block
     first = total is None
     cost = pl.CostEstimate(
@@ -746,7 +746,7 @@
         ]
         if last
         else jax.ShapeDtypeStruct((rows, 2 * HD), F32),
-        compiler_params=pltpu.CompilerParams(vmem_limit_bytes=20 * MIB),
+        compiler_params=pltpu.CompilerParams(vmem_limit_bytes=40 * MIB),
         cost_estimate=cost,
     )(query, keys, values, qpos, qlow, kpos, *([] if first else [total]))
 

time: 518 us -> 518 us (level)
  transfers between devices with their start and end apart: 100 -> 100, of which waited for: 45 -> 44; matrix products, arithmetic and copies ran while one was open for 18% -> 18% of each run, Pallas kernels for 15% -> 15%
where the time goes in v6:
time: 518 us; the launch traced here: 508 us
  waiting for transfers between devices  223 us (43%)
  starting transfers between devices  74.2 us (14%)
  Pallas kernels  73.8 us (14%)
  local copies, waits for them, and re-layouts  57.5 us (11%)
  matrix products  37.1 us (7%)
  other arithmetic  27.2 us (5%)
  between operations  16 us (3%)
    ppermute x97, waiting for transfers between devices, phase(): lax.ppermute(value, move[0], move[1])  214 us
    ppermute x97, starting transfers between devices, phase(): lax.ppermute(value, move[0], move[1])  74.1 us
    unnamed x174, local copies, waits for them, and re-layouts  33.4 us
    pallas_call x4, Pallas kernels, attend_back(): pl.pallas_call(functools.partial(attend_back_kernel, 512, own, first), gr...  28.1 us
    dot_general x12, matrix products, col_inner(): lax.dot_general(left, right, CONTRACT_COLS, preferred_element_type=F32)  16.6 us
    dot_general x9, matrix products, dot(): return jnp.dot(left, right, preferred_element_type=F32)  15.1 us
    pallas_call x4, Pallas kernels, attend(): pl.pallas_call(functools.partial(attend_kernel, first, last), grid=(rows...  14.4 us
    pallas_call x3, Pallas kernels, weight_grads(): pl.pallas_call(functools.partial(weight_grad_kernel, count, len(lefts)),...  14.4 us
  transfers between devices with their start and end apart: 100, of which 44 were waited for; matrix products, arithmetic and copies ran while one was open for 18% of the time, Pallas kernels for 15%

profile of v6, /device:TPU:0, one launch (start us, length us, event | category | flops | bytes accessed | tf_op | source)
XLA Modules:
  0.0 508.3 jit_solution(5589520347701319444)
XLA Ops:
  8.9 2.6 collective-permute-start.1
  21.2 3.3 pad_maximum_fusion
  26.7 10.4 %collective-permute-done.2 = bf16[128,2048]{1,0:T(8,128)(2,1)} collective-permute-done((bf16[128,2048]{1,0:T(8,128)(2,1)}, bf16[128,2048]{1,0:T(8,128)(2,1)}, u32[]{:S(2)}, u32[]{:S(2)}) %collective-permute-start.2) | collective-permute-done | bytes 524320 | tf_op jit(solution)/shard_map/ppermute | solution.py:120
  44.1 9.5 %collective-permute-done.7 = bf16[128,2048]{1,0:T(8,128)(2,1)} collective-permute-done((bf16[128,2048]{1,0:T(8,128)(2,1)}, bf16[128,2048]{1,0:T(8,128)(2,1)}, u32[]{:S(2)}, u32[]{:S(2)}) %collective-permute-start.7) | collective-permute-done | bytes 524320 | tf_op jit(solution)/shard_map/ppermute | solution.py:120
  78.3 3.2 fusion
  87.6 7.3 %collective-permute-done.19.refs_2_ = bf16[128,1024]{1,0:T(8,128)(2,1)S(1)} collective-permute-done((bf16[128,1024]{1,0:T(8,128)(2,1)}, bf16[128,1024]{1,0:T(8,128)(2,1)S(1)}, u32[]{:S(2)}, u32[]{:S(2)}) %collective-permute-start.19) | collective-permute-done | bytes 262176 | tf_op jit(solution)/shard_map/ppermute | solution.py:120
  94.9 4.8 collective-permute-done.20.refs_3_
  105.6 3.6 shard_map.258.refs_6_
  110.5 5.8 %collective-permute-done.21.refs_1_.refs_2_.k_ref.v_ref = bf16[1024,256]{1,0:T(8,128)(2,1)S(1)} collective-permute-done((bf16[1024,256]{1,0:T(8,128)(2,1)S(1)}, bf16[1024,256]{1,0:T(8,128)(2,1)S(1)}, u32[]{:S(2)}, u32[]{:S(2)}) %collective-permute-start.21) | collective-permute-done | bytes 524320 | tf_op jit(solution)/shard_map/ppermute | solution.py:120
  118.3 3.1 collective-permute-done.24.refs_6_
  129.0 3.6 shard_map.259.refs_6_
  132.6 3.6 shard_map.260.refs_6_
  136.3 4.7 collective-permute-done.28.refs_4_
  141.0 3.6 shard_map.261
  147.6 4.8 collective-permute-done.30.refs_2_
  161.1 13.6 %collective-permute-done.34 = bf16[128,2048]{1,0:T(8,128)(2,1)S(1)} collective-permute-done((bf16[128,2048]{1,0:T(8,128)(2,1)S(1)}, bf16[128,2048]{1,0:T(8,128)(2,1)S(1)}, u32[]{:S(2)}, u32[]{:S(2)}) %collective-permute-start.34) | collective-permute-done | bytes 524320 | tf_op jit(solution)/shard_map/ppermute | solution.py:120
  177.3 12.3 %collective-permute-done.37 = bf16[128,2048]{1,0:T(8,128)(2,1)S(1)} collective-permute-done((bf16[128,2048]{1,0:T(8,128)(2,1)S(1)}, bf16[128,2048]{1,0:T(8,128)(2,1)S(1)}, u32[]{:S(2)}, u32[]{:S(2)}) %collective-permute-start.37) | collective-permute-done | bytes 524320 | tf_op jit(solution)/shard_map/ppermute | solution.py:120
  189.6 10.8 %collective-permute-done.38 = bf16[128,2048]{1,0:T(8,128)(2,1)S(1)} collective-permute-done((bf16[128,2048]{1,0:T(8,128)(2,1)S(1)}, bf16[128,2048]{1,0:T(8,128)(2,1)S(1)}, u32[]{:S(2)}, u32[]{:S(2)}) %collective-permute-start.38) | collective-permute-done | bytes 524320 | tf_op jit(solution)/shard_map/ppermute | solution.py:120
  206.0 8.2 %all-gather.6.cloned.1.call-done = bf16[2304,2048]{1,0:T(8,128)(2,1)} async-done(((bf16[576,2048]{1,0:T(8,128)(2,1)}), bf16[2304,2048]{1,0:T(8,128)(2,1)}) %all-gather.6.cloned.1.call-update) | async-done | bytes 9437200 | tf_op jit(solution)/shard_map/all_gather | solution.py:1019
  214.2 4.5 fusion.86
  218.7 10.4 %collective-permute-done.42.refs_2_.refs_4_ = bf16[128,2048]{1,0:T(8,128)(2,1)S(1)} collective-permute-done((bf16[128,2048]{1,0:T(8,128)(2,1)S(1)}, bf16[128,2048]{1,0:T(8,128)(2,1)S(1)}, u32[]{:S(2)}, u32[]{:S(2)}) %collective-permute-start.42) | collective-permute-done | bytes 524320 | tf_op jit(solution)/shard_map/ppermute | solution.py:120
  238.0 7.7 %collective-permute-done.45.refs_6_ = bf16[128,2048]{1,0:T(8,128)(2,1)S(1)} collective-permute-done((bf16[128,2048]{1,0:T(8,128)(2,1)S(1)}, bf16[128,2048]{1,0:T(8,128)(2,1)S(1)}, u32[]{:S(2)}, u32[]{:S(2)}) %collective-permute-start.45) | collective-permute-done | bytes 524320 | tf_op jit(solution)/shard_map/ppermute | solution.py:120
  256.9 8.6 %shard_map.264 = (bf16[512,768]{1,0:T(8,128)(2,1)S(1)}, bf16[512,768]{1,0:T(8,128)(2,1)S(1)}, bf16[512,768]{1,0:T(8,128)(2,1)S(1)}, bf16[512,2048]{1,0:T(8,128)(2,1)S(1)}) custom-call(bf16[128,2048]{1,0:T(8,128)(2,1)S(1)} %collective-permute-done.41.refs_0_.refs_2_, bf16[128,2048]{1,0:T(8,128)(2,1)S(1)} %collective-permute-done.43.refs_1_.refs_3_, ...), custom_call_target="tpu_custom_call" | custom-call | flops 1 | bytes 1 | tf_op jit(solution)/shard_map/pallas_call | solution.py:573
  265.6 3.1 collective-permute-done.48
  274.0 3.2 convolution_convert_fusion
  277.2 4.8 shard_map.265.refs_11_
  282.0 4.8 shard_map.266.refs_11_
  288.7 8.7 %collective-permute-done.52 = bf16[128,2048]{1,0:T(8,128)(2,1)S(1)} collective-permute-done((bf16[128,2048]{1,0:T(8,128)(2,1)S(1)}, bf16[128,2048]{1,0:T(8,128)(2,1)S(1)}, u32[]{:S(2)}, u32[]{:S(2)}) %collective-permute-start.52) | collective-permute-done | bytes 524320 | tf_op jit(solution)/shard_map/ppermute | solution.py:120
  298.1 2.6 constant_dynamic-update-slice_fusion.23
  304.9 4.8 shard_map.267
  309.7 3.6 copy-done
  313.3 4.1 collective-permute-done.55
  317.5 10.8 %collective-permute-done.56 = bf16[128,2048]{1,0:T(8,128)(2,1)} collective-permute-done((bf16[128,2048]{1,0:T(8,128)(2,1)S(1)}, bf16[128,2048]{1,0:T(8,128)(2,1)}, u32[]{:S(2)}, u32[]{:S(2)}) %collective-permute-start.56) | collective-permute-done | bytes 524320 | tf_op jit(solution)/shard_map/ppermute | solution.py:120
  336.0 11.8 %collective-permute-done.59 = bf16[128,2048]{1,0:T(8,128)(2,1)S(1)} collective-permute-done((bf16[128,2048]{1,0:T(8,128)(2,1)}, bf16[128,2048]{1,0:T(8,128)(2,1)S(1)}, u32[]{:S(2)}, u32[]{:S(2)}) %collective-permute-start.59) | collective-permute-done | bytes 524320 | tf_op jit(solution)/shard_map/ppermute | solution.py:120
  360.4 7.0 %shard_map.270 = (f32[2048,128]{1,0:T(8,128)S(1)}, f32[1024,128]{1,0:T(8,128)S(1)}, f32[1024,128]{1,0:T(8,128)S(1)}, f32[8,2048]{1,0:T(8,128)S(1)}) custom-call(bf16[2048,128]{1,0:T(8,128)(2,1)S(1)} %copy-done.30, bf16[2048,128]{1,0:T(8,128)(2,1)S(1)} %shard_map.269.g_ref, f32[8,2048]{1,0:T(8,128)S(1)} %copy-done.40, ...), custom_call_target="tpu_custom_call" | custom-call | flops 8589934592 | bytes 1048576 | tf_op jit(solution)/shard_map/pallas_call | solution.py:806
  371.5 7.0 %shard_map.271 = (f32[2048,128]{1,0:T(8,128)S(1)}, f32[1024,128]{1,0:T(8,128)S(1)}, f32[1024,128]{1,0:T(8,128)S(1)}) custom-call(bf16[2048,128]{1,0:T(8,128)(2,1)S(1)} %copy-done.30, bf16[2048,128]{1,0:T(8,128)(2,1)S(1)} %shard_map.269.g_ref, f32[8,2048]{1,0:T(8,128)S(1)} %copy-done.40, s32[1,1024]{1,0:T(1,128)S(1)} %get-tuple-element.746.refs_3_.refs_5_.qpos_ref.kpos_ref, ...), custom_call_target="tpu_custom_call" | custom-call | flops 8589934592 | bytes 1048576 | tf_op jit(solution)/shard_map/pallas_call | solution.py:806
  378.5 7.2 %shard_map.272 = (f32[2048,128]{1,0:T(8,128)S(1)}, f32[1024,128]{1,0:T(8,128)S(1)}, f32[1024,128]{1,0:T(8,128)S(1)}) custom-call(bf16[2048,128]{1,0:T(8,128)(2,1)S(1)} %copy-done.30, bf16[2048,128]{1,0:T(8,128)(2,1)S(1)} %shard_map.269.g_ref, f32[8,2048]{1,0:T(8,128)S(1)} %copy-done.40, s32[1,1024]{1,0:T(1,128)S(1)} %get-tuple-element.746.refs_3_.refs_5_.qpos_ref.kpos_ref, ...), custom_call_target="tpu_custom_call" | custom-call | flops 8589934592 | bytes 1048576 | tf_op jit(solution)/shard_map/pallas_call | solution.py:806
  389.8 7.0 %shard_map.273 = (f32[2048,128]{1,0:T(8,128)S(1)}, f32[1024,128]{1,0:T(8,128)S(1)}, f32[1024,128]{1,0:T(8,128)S(1)}) custom-call(bf16[2048,128]{1,0:T(8,128)(2,1)S(1)} %copy-done.30, bf16[2048,128]{1,0:T(8,128)(2,1)S(1)} %shard_map.269.g_ref, f32[8,2048]{1,0:T(8,128)S(1)} %copy-done.40, s32[1,1024]{1,0:T(1,128)S(1)} %get-tuple-element.746.refs_3_.refs_5_.qpos_ref.kpos_ref, ...), custom_call_target="tpu_custom_call" | custom-call | flops 8589934592 | bytes 1048576 | tf_op jit(solution)/shard_map/pallas_call | solution.py:806
  396.7 7.0 %collective-permute-done.70.refs_7_ = bf16[1024,256]{1,0:T(8,128)(2,1)S(1)} collective-permute-done((bf16[1024,256]{1,0:T(8,128)(2,1)S(1)}, bf16[1024,256]{1,0:T(8,128)(2,1)S(1)}, u32[]{:S(2)}, u32[]{:S(2)}) %collective-permute-start.70) | collective-permute-done | bytes 524320 | tf_op jit(solution)/shard_map/ppermute | solution.py:120
  403.8 9.9 %collective-permute-done.73 = bf16[128,2048]{1,0:T(8,128)(2,1)S(1)} collective-permute-done((bf16[128,2048]{1,0:T(8,128)(2,1)S(1)}, bf16[128,2048]{1,0:T(8,128)(2,1)S(1)}, u32[]{:S(2)}, u32[]{:S(2)}) %collective-permute-start.73) | collective-permute-done | bytes 524320 | tf_op jit(solution)/shard_map/ppermute | solution.py:120
  418.6 5.9 %collective-permute-done.76.refs_2_ = bf16[128,1024]{1,0:T(8,128)(2,1)S(1)} collective-permute-done((bf16[128,1024]{1,0:T(8,128)(2,1)S(1)}, bf16[128,1024]{1,0:T(8,128)(2,1)S(1)}, u32[]{:S(2)}, u32[]{:S(2)}) %collective-permute-start.76) | collective-permute-done | bytes 262176 | tf_op jit(solution)/shard_map/ppermute | solution.py:120
  424.5 4.7 collective-permute-done.77.refs_3_
  432.5 2.6 fusion.88
  445.7 4.8 collective-permute-done.83
  450.5 3.4 collective-permute-done.79
  465.7 7.4 %collective-permute-done.84 = bf16[128,2048]{1,0:T(8,128)(2,1)S(1)} collective-permute-done((bf16[128,2048]{1,0:T(8,128)(2,1)S(1)}, bf16[128,2048]{1,0:T(8,128)(2,1)S(1)}, u32[]{:S(2)}, u32[]{:S(2)}) %collective-permute-start.84) | collective-permute-done | bytes 524320 | tf_op jit(solution)/shard_map/ppermute | solution.py:120
  481.4 9.2 %collective-permute-done.89 = bf16[128,2048]{1,0:T(8,128)(2,1)S(1)} collective-permute-done((bf16[128,2048]{1,0:T(8,128)(2,1)S(1)}, bf16[128,2048]{1,0:T(8,128)(2,1)S(1)}, u32[]{:S(2)}, u32[]{:S(2)}) %collective-permute-start.89) | collective-permute-done | bytes 524320 | tf_op jit(solution)/shard_map/ppermute | solution.py:120
  490.6 2.9 collective-permute-start.95
  (464 shorter events, 193.9 us)
Async XLA Ops:
  7.2 147.7 %all-gather.4.cloned.1.call-start = ((), (), s32[]{:S(2)}) async-start(), calls=%async_computation.1 | async-start | bytes 1310720 | tf_op jit(solution)/shard_map/all_gather | solution.py:912
  8.4 16.3 %collective-permute-start = (bf16[128,2048]{1,0:T(8,128)(2,1)}, bf16[128,2048]{1,0:T(8,128)(2,1)}, u32[]{:S(2)}, u32[]{:S(2)}) collective-permute-start(bf16[128,2048]{1,0:T(8,128)(2,1)} %param.16), channel_id=1, source_target_pairs={{0,1},{1,0},{2,3},{3,2},{4,5},{5,4},{6,7},{7,6},{8,9},{9,8},{10,11... | collective-permute-start | bytes 1572872 | tf_op jit(solution)/shard_map/ppermute | solution.py:120
  8.9 17.8 %collective-permute-start.1 = (bf16[128,2048]{1,0:T(8,128)(2,1)}, bf16[128,2048]{1,0:T(8,128)(2,1)}, u32[]{:S(2)}, u32[]{:S(2)}) collective-permute-start(bf16[128,2048]{1,0:T(8,128)(2,1)} %param.16), channel_id=1, source_target_pairs={{0,2},{1,3},{2,4},{3,5},{4,6},{5,7},{6,0},{7,1},{8,10},{9,11},{10,... | collective-permute-start | bytes 1572872 | tf_op jit(solution)/shard_map/ppermute | solution.py:120
  11.5 25.5 %collective-permute-start.2 = (bf16[128,2048]{1,0:T(8,128)(2,1)}, bf16[128,2048]{1,0:T(8,128)(2,1)}, u32[]{:S(2)}, u32[]{:S(2)}) collective-permute-start(bf16[128,2048]{1,0:T(8,128)(2,1)} %param.16), channel_id=1, source_target_pairs={{0,6},{1,7},{2,0},{3,1},{4,2},{5,3},{6,4},{7,5},{8,14},{9,15},{10,... | collective-permute-start | bytes 1572872 | tf_op jit(solution)/shard_map/ppermute | solution.py:120
  13.7 23.4 %collective-permute-start.3 = (bf16[128,2048]{1,0:T(8,128)(2,1)S(1)}, bf16[128,2048]{1,0:T(8,128)(2,1)}, u32[]{:S(2)}, u32[]{:S(2)}) collective-permute-start(bf16[128,2048]{1,0:T(8,128)(2,1)S(1)} %pad_maximum_fusion.4), channel_id=1, source_target_pairs={{0,8},{8,0},{16,24},{24,16},{1,9},{9,1},{17,25},{25,17},{2,10},{10... | collective-permute-start | bytes 1572872 | tf_op jit(solution)/shard_map/ppermute | solution.py:120
  15.3 21.8 %collective-permute-start.4 = (bf16[128,2048]{1,0:T(8,128)(2,1)S(1)}, bf16[128,2048]{1,0:T(8,128)(2,1)}, u32[]{:S(2)}, u32[]{:S(2)}) collective-permute-start(bf16[128,2048]{1,0:T(8,128)(2,1)S(1)} %pad_maximum_fusion.4), channel_id=1, source_target_pairs={{0,16},{8,24},{16,0},{24,8},{1,17},{9,25},{17,1},{25,9},{2,18},{10... | collective-permute-start | bytes 1572872 | tf_op jit(solution)/shard_map/ppermute | solution.py:120
  37.6 16.0 %collective-permute-start.7 = (bf16[128,2048]{1,0:T(8,128)(2,1)}, bf16[128,2048]{1,0:T(8,128)(2,1)}, u32[]{:S(2)}, u32[]{:S(2)}) collective-permute-start(bf16[128,2048]{1,0:T(8,128)(2,1)} %collective-permute-done.1), channel_id=1, source_target_pairs={{0,2},{1,3},{2,4},{3,5},{4,6},{5,7},{6,0},{7,1},{8,10},{9,11},{10,... | collective-permute-start | bytes 1572872 | tf_op jit(solution)/shard_map/ppermute | solution.py:120
  38.7 14.9 %collective-permute-start.8 = (bf16[128,2048]{1,0:T(8,128)(2,1)}, bf16[128,2048]{1,0:T(8,128)(2,1)}, u32[]{:S(2)}, u32[]{:S(2)}) collective-permute-start(bf16[128,2048]{1,0:T(8,128)(2,1)} %collective-permute-done.3), channel_id=1, source_target_pairs={{0,16},{8,24},{16,0},{24,8},{1,17},{9,25},{17,1},{25,9},{2,18},{10... | collective-permute-start | bytes 1572872 | tf_op jit(solution)/shard_map/ppermute | solution.py:120
  68.3 145.9 %all-gather.6.cloned.1.call-start = ((), (), s32[]{:S(2)}) async-start(), calls=%async_computation.2 | async-start | bytes 11796480 | tf_op jit(solution)/shard_map/all_gather | solution.py:1019
  68.4 15.9 %collective-permute-start.16 = (bf16[128,2048]{1,0:T(8,128)(2,1)S(1)}, bf16[128,2048]{1,0:T(8,128)(2,1)S(1)}, u32[]{:S(2)}, u32[]{:S(2)}) collective-permute-start(bf16[128,2048]{1,0:T(8,128)(2,1)S(1)} %constant_dynamic-slice_fusion.refs_0_), channel_id=1, source_target_pairs={{0,1},{1,0},{2,3},{3,2},{4,5},{5,4},{6,7},{7,6},{8,9},{9,8},{10,11... | collective-permute-start | bytes 1572872 | tf_op jit(solution)/shard_map/ppermute | solution.py:120
  68.5 16.1 %collective-permute-start.17 = (bf16[128,2048]{1,0:T(8,128)(2,1)S(1)}, bf16[128,2048]{1,0:T(8,128)(2,1)S(1)}, u32[]{:S(2)}, u32[]{:S(2)}) collective-permute-start(bf16[128,2048]{1,0:T(8,128)(2,1)S(1)} %constant_dynamic-slice_fusion.refs_0_), channel_id=1, source_target_pairs={{0,2},{1,3},{2,4},{3,5},{4,6},{5,7},{6,0},{7,1},{8,10},{9,11},{10,... | collective-permute-start | bytes 1572872 | tf_op jit(solution)/shard_map/ppermute | solution.py:120
  105.3 16.1 %collective-permute-start.24 = (bf16[128,2048]{1,0:T(8,128)(2,1)S(1)}, bf16[128,2048]{1,0:T(8,128)(2,1)S(1)}, u32[]{:S(2)}, u32[]{:S(2)}) collective-permute-start(bf16[128,2048]{1,0:T(8,128)(2,1)S(1)} %collective-permute-done.17.refs_2_), channel_id=1, source_target_pairs={{0,2},{1,3},{2,4},{3,5},{4,6},{5,7},{6,0},{7,1},{8,10},{9,11},{10,... | collective-permute-start | bytes 1572872 | tf_op jit(solution)/shard_map/ppermute | solution.py:120
  121.4 338.0 %reduce-scatter.4.cloned.1.call-start = ((), (), s32[]{:S(2)}) async-start(), calls=%async_computation.3 | async-start | bytes 11796480
  124.7 16.3 %collective-permute-start.28 = (bf16[128,2048]{1,0:T(8,128)(2,1)S(1)}, bf16[128,2048]{1,0:T(8,128)(2,1)S(1)}, u32[]{:S(2)}, u32[]{:S(2)}) collective-permute-start(bf16[128,2048]{1,0:T(8,128)(2,1)S(1)} %collective-permute-done.24.refs_6_), channel_id=1, source_target_pairs={{0,2},{1,3},{2,4},{3,5},{4,6},{5,7},{6,0},{7,1},{8,10},{9,11},{10,... | collective-permute-start | bytes 1572872 | tf_op jit(solution)/shard_map/ppermute | solution.py:120
  160.4 14.3 %collective-permute-start.34 = (bf16[128,2048]{1,0:T(8,128)(2,1)S(1)}, bf16[128,2048]{1,0:T(8,128)(2,1)S(1)}, u32[]{:S(2)}, u32[]{:S(2)}) collective-permute-start(bf16[128,2048]{1,0:T(8,128)(2,1)S(1)} %fusion.32), channel_id=1, source_target_pairs={{0,6},{1,7},{2,0},{3,1},{4,2},{5,3},{6,4},{7,5},{8,14},{9,15},{10,... | collective-permute-start | bytes 1572872 | tf_op jit(solution)/shard_map/ppermute | solution.py:120
  175.1 14.5 %collective-permute-start.37 = (bf16[128,2048]{1,0:T(8,128)(2,1)S(1)}, bf16[128,2048]{1,0:T(8,128)(2,1)S(1)}, u32[]{:S(2)}, u32[]{:S(2)}) collective-permute-start(bf16[128,2048]{1,0:T(8,128)(2,1)S(1)} %get-tuple-element.473), channel_id=1, source_target_pairs={{0,6},{1,7},{2,0},{3,1},{4,2},{5,3},{6,4},{7,5},{8,14},{9,15},{10,... | collective-permute-start | bytes 1572872 | tf_op jit(solution)/shard_map/ppermute | solution.py:120
  177.3 23.1 %collective-permute-start.38 = (bf16[128,2048]{1,0:T(8,128)(2,1)S(1)}, bf16[128,2048]{1,0:T(8,128)(2,1)S(1)}, u32[]{:S(2)}, u32[]{:S(2)}) collective-permute-start(bf16[128,2048]{1,0:T(8,128)(2,1)S(1)} %get-tuple-element.474), channel_id=1, source_target_pairs={{0,2},{1,3},{2,4},{3,5},{4,6},{5,7},{6,0},{7,1},{8,10},{9,11},{10,... | collective-permute-start | bytes 1572872 | tf_op jit(solution)/shard_map/ppermute | solution.py:120
  177.3 23.1 %collective-permute-start.39 = (bf16[128,2048]{1,0:T(8,128)(2,1)S(1)}, bf16[128,2048]{1,0:T(8,128)(2,1)S(1)}, u32[]{:S(2)}, u32[]{:S(2)}) collective-permute-start(bf16[128,2048]{1,0:T(8,128)(2,1)S(1)} %get-tuple-element.475), channel_id=1, source_target_pairs={{0,1},{1,0},{2,3},{3,2},{4,5},{5,4},{6,7},{7,6},{8,9},{9,8},{10,11... | collective-permute-start | bytes 1572872 | tf_op jit(solution)/shard_map/ppermute | solution.py:120
  202.0 16.7 %collective-permute-start.40 = (bf16[128,2048]{1,0:T(8,128)(2,1)S(1)}, bf16[128,2048]{1,0:T(8,128)(2,1)S(1)}, u32[]{:S(2)}, u32[]{:S(2)}) collective-permute-start(bf16[128,2048]{1,0:T(8,128)(2,1)S(1)} %multiply_convert_fusion.refs_0_), channel_id=1, source_target_pairs={{0,1},{1,0},{2,3},{3,2},{4,5},{5,4},{6,7},{7,6},{8,9},{9,8},{10,11... | collective-permute-start | bytes 1572872 | tf_op jit(solution)/shard_map/ppermute | solution.py:120
  202.1 16.6 %collective-permute-start.41 = (bf16[128,2048]{1,0:T(8,128)(2,1)S(1)}, bf16[128,2048]{1,0:T(8,128)(2,1)S(1)}, u32[]{:S(2)}, u32[]{:S(2)}) collective-permute-start(bf16[128,2048]{1,0:T(8,128)(2,1)S(1)} %multiply_convert_fusion.refs_0_), channel_id=1, source_target_pairs={{0,2},{1,3},{2,4},{3,5},{4,6},{5,7},{6,0},{7,1},{8,10},{9,11},{10,... | collective-permute-start | bytes 1572872 | tf_op jit(solution)/shard_map/ppermute | solution.py:120
  204.0 25.2 %collective-permute-start.42 = (bf16[128,2048]{1,0:T(8,128)(2,1)S(1)}, bf16[128,2048]{1,0:T(8,128)(2,1)S(1)}, u32[]{:S(2)}, u32[]{:S(2)}) collective-permute-start(bf16[128,2048]{1,0:T(8,128)(2,1)S(1)} %multiply_convert_fusion.refs_0_), channel_id=1, source_target_pairs={{0,6},{1,7},{2,0},{3,1},{4,2},{5,3},{6,4},{7,5},{8,14},{9,15},{10,... | collective-permute-start | bytes 1572872 | tf_op jit(solution)/shard_map/ppermute | solution.py:120
  229.7 16.0 %collective-permute-start.45 = (bf16[128,2048]{1,0:T(8,128)(2,1)S(1)}, bf16[128,2048]{1,0:T(8,128)(2,1)S(1)}, u32[]{:S(2)}, u32[]{:S(2)}) collective-permute-start(bf16[128,2048]{1,0:T(8,128)(2,1)S(1)} %collective-permute-done.41.refs_0_.refs_2_), channel_id=1, source_target_pairs={{0,2},{1,3},{2,4},{3,5},{4,6},{5,7},{6,0},{7,1},{8,10},{9,11},{10,... | collective-permute-start | bytes 1572872 | tf_op jit(solution)/shard_map/ppermute | solution.py:120
  254.5 14.2 %collective-permute-start.48 = (bf16[128,2048]{1,0:T(8,128)(2,1)S(1)}, bf16[128,2048]{1,0:T(8,128)(2,1)S(1)}, u32[]{:S(2)}, u32[]{:S(2)}) collective-permute-start(bf16[128,2048]{1,0:T(8,128)(2,1)S(1)} %fusion.30), channel_id=1, source_target_pairs={{0,6},{1,7},{2,0},{3,1},{4,2},{5,3},{6,4},{7,5},{8,14},{9,15},{10,... | collective-permute-start | bytes 1572872 | tf_op jit(solution)/shard_map/ppermute | solution.py:120
  271.8 16.9 %collective-permute-start.51 = (bf16[128,2048]{1,0:T(8,128)(2,1)S(1)}, bf16[128,2048]{1,0:T(8,128)(2,1)S(1)}, u32[]{:S(2)}, u32[]{:S(2)}) collective-permute-start(bf16[128,2048]{1,0:T(8,128)(2,1)S(1)} %get-tuple-element.526), channel_id=1, source_target_pairs={{0,6},{1,7},{2,0},{3,1},{4,2},{5,3},{6,4},{7,5},{8,14},{9,15},{10,... | collective-permute-start | bytes 1572872 | tf_op jit(solution)/shard_map/ppermute | solution.py:120
  274.0 23.5 %collective-permute-start.52 = (bf16[128,2048]{1,0:T(8,128)(2,1)S(1)}, bf16[128,2048]{1,0:T(8,128)(2,1)S(1)}, u32[]{:S(2)}, u32[]{:S(2)}) collective-permute-start(bf16[128,2048]{1,0:T(8,128)(2,1)S(1)} %get-tuple-element.527), channel_id=1, source_target_pairs={{0,2},{1,3},{2,4},{3,5},{4,6},{5,7},{6,0},{7,1},{8,10},{9,11},{10,... | collective-permute-start | bytes 1572872 | tf_op jit(solution)/shard_map/ppermute | solution.py:120
  274.0 23.5 %collective-permute-start.53 = (bf16[128,2048]{1,0:T(8,128)(2,1)S(1)}, bf16[128,2048]{1,0:T(8,128)(2,1)S(1)}, u32[]{:S(2)}, u32[]{:S(2)}) collective-permute-start(bf16[128,2048]{1,0:T(8,128)(2,1)S(1)} %slice.391), channel_id=1, source_target_pairs={{0,1},{1,0},{2,3},{3,2},{4,5},{5,4},{6,7},{7,6},{8,9},{9,8},{10,11... | collective-permute-start | bytes 1572872 | tf_op jit(solution)/shard_map/ppermute | solution.py:120
  300.7 16.7 %collective-permute-start.55 = (bf16[128,2048]{1,0:T(8,128)(2,1)S(1)}, bf16[128,2048]{1,0:T(8,128)(2,1)}, u32[]{:S(2)}, u32[]{:S(2)}) collective-permute-start(bf16[128,2048]{1,0:T(8,128)(2,1)S(1)} %get-tuple-element.542), channel_id=1, source_target_pairs={{0,2},{1,3},{2,4},{3,5},{4,6},{5,7},{6,0},{7,1},{8,10},{9,11},{10,... | collective-permute-start | bytes 1572872 | tf_op jit(solution)/shard_map/ppermute | solution.py:120
  302.5 25.8 %collective-permute-start.56 = (bf16[128,2048]{1,0:T(8,128)(2,1)S(1)}, bf16[128,2048]{1,0:T(8,128)(2,1)}, u32[]{:S(2)}, u32[]{:S(2)}) collective-permute-start(bf16[128,2048]{1,0:T(8,128)(2,1)S(1)} %get-tuple-element.542), channel_id=1, source_target_pairs={{0,6},{1,7},{2,0},{3,1},{4,2},{5,3},{6,4},{7,5},{8,14},{9,15},{10,... | collective-permute-start | bytes 1572872 | tf_op jit(solution)/shard_map/ppermute | solution.py:120
  331.9 15.9 %collective-permute-start.59 = (bf16[128,2048]{1,0:T(8,128)(2,1)}, bf16[128,2048]{1,0:T(8,128)(2,1)S(1)}, u32[]{:S(2)}, u32[]{:S(2)}) collective-permute-start(bf16[128,2048]{1,0:T(8,128)(2,1)} %collective-permute-done.55), channel_id=1, source_target_pairs={{0,2},{1,3},{2,4},{3,5},{4,6},{5,7},{6,0},{7,1},{8,10},{9,11},{10,... | collective-permute-start | bytes 1572872 | tf_op jit(solution)/shard_map/ppermute | solution.py:120
  367.7 18.1 %collective-permute-start.65 = (bf16[1024,128]{1,0:T(8,128)(2,1)S(1)}, bf16[1024,128]{1,0:T(8,128)(2,1)S(1)}, u32[]{:S(2)}, u32[]{:S(2)}) collective-permute-start(bf16[1024,128]{1,0:T(8,128)(2,1)S(1)} %convert_element_type.333), channel_id=1, source_target_pairs={{0,16},{8,24},{16,0},{24,8},{1,17},{9,25},{17,1},{25,9},{2,18},{10... | collective-permute-start | bytes 786440 | tf_op jit(solution)/shard_map/ppermute | solution.py:120
  369.2 16.5 %collective-permute-start.66 = (bf16[1024,128]{1,0:T(8,128)(2,1)S(1)}, bf16[1024,128]{1,0:T(8,128)(2,1)S(1)}, u32[]{:S(2)}, u32[]{:S(2)}) collective-permute-start(bf16[1024,128]{1,0:T(8,128)(2,1)S(1)} %convert_element_type.334), channel_id=1, source_target_pairs={{0,8},{8,0},{16,24},{24,16},{1,9},{9,1},{17,25},{25,17},{2,10},{10... | collective-permute-start | bytes 786440 | tf_op jit(solution)/shard_map/ppermute | solution.py:120
  370.6 15.1 %collective-permute-start.67 = (bf16[128,2048]{1,0:T(8,128)(2,1)S(1)}, bf16[128,2048]{1,0:T(8,128)(2,1)S(1)}, u32[]{:S(2)}, u32[]{:S(2)}) collective-permute-start(bf16[128,2048]{1,0:T(8,128)(2,1)S(1)} %add_convert_fusion.3), channel_id=1, source_target_pairs={{0,6},{1,7},{2,0},{3,1},{4,2},{5,3},{6,4},{7,5},{8,14},{9,15},{10,... | collective-permute-start | bytes 1572872 | tf_op jit(solution)/shard_map/ppermute | solution.py:120
  370.8 14.9 %collective-permute-start.68 = (bf16[128,2048]{1,0:T(8,128)(2,1)S(1)}, bf16[128,2048]{1,0:T(8,128)(2,1)S(1)}, u32[]{:S(2)}, u32[]{:S(2)}) collective-permute-start(bf16[128,2048]{1,0:T(8,128)(2,1)S(1)} %get-tuple-element.590), channel_id=1, source_target_pairs={{0,1},{1,0},{2,3},{3,2},{4,5},{5,4},{6,7},{7,6},{8,9},{9,8},{10,11... | collective-permute-start | bytes 1572872 | tf_op jit(solution)/shard_map/ppermute | solution.py:120
  371.4 14.4 %collective-permute-start.69 = (bf16[128,2048]{1,0:T(8,128)(2,1)S(1)}, bf16[128,2048]{1,0:T(8,128)(2,1)S(1)}, u32[]{:S(2)}, u32[]{:S(2)}) collective-permute-start(bf16[128,2048]{1,0:T(8,128)(2,1)S(1)} %get-tuple-element.591), channel_id=1, source_target_pairs={{0,1},{1,0},{2,3},{3,2},{4,5},{5,4},{6,7},{7,6},{8,9},{9,8},{10,11... | collective-permute-start | bytes 1572872 | tf_op jit(solution)/shard_map/ppermute | solution.py:120
  386.5 17.2 %collective-permute-start.70 = (bf16[1024,256]{1,0:T(8,128)(2,1)S(1)}, bf16[1024,256]{1,0:T(8,128)(2,1)S(1)}, u32[]{:S(2)}, u32[]{:S(2)}) collective-permute-start(bf16[1024,256]{1,0:T(8,128)(2,1)S(1)} %pad_maximum_fusion.5), channel_id=1, source_target_pairs={{0,8},{8,0},{16,24},{24,16},{1,9},{9,1},{17,25},{25,17},{2,10},{10... | collective-permute-start | bytes 1572872 | tf_op jit(solution)/shard_map/ppermute | solution.py:120
  387.2 16.6 %collective-permute-start.71 = (bf16[1024,256]{1,0:T(8,128)(2,1)S(1)}, bf16[1024,256]{1,0:T(8,128)(2,1)S(1)}, u32[]{:S(2)}, u32[]{:S(2)}) collective-permute-start(bf16[1024,256]{1,0:T(8,128)(2,1)S(1)} %pad_maximum_fusion.6), channel_id=1, source_target_pairs={{0,16},{8,24},{16,0},{24,8},{1,17},{9,25},{17,1},{25,9},{2,18},{10... | collective-permute-start | bytes 1572872 | tf_op jit(solution)/shard_map/ppermute | solution.py:120
  387.7 16.1 %collective-permute-start.72 = (bf16[128,2048]{1,0:T(8,128)(2,1)S(1)}, bf16[128,2048]{1,0:T(8,128)(2,1)S(1)}, u32[]{:S(2)}, u32[]{:S(2)}) collective-permute-start(bf16[128,2048]{1,0:T(8,128)(2,1)S(1)} %get-tuple-element.617), channel_id=1, source_target_pairs={{0,6},{1,7},{2,0},{3,1},{4,2},{5,3},{6,4},{7,5},{8,14},{9,15},{10,... | collective-permute-start | bytes 1572872 | tf_op jit(solution)/shard_map/ppermute | solution.py:120
  389.2 24.5 %collective-permute-start.73 = (bf16[128,2048]{1,0:T(8,128)(2,1)S(1)}, bf16[128,2048]{1,0:T(8,128)(2,1)S(1)}, u32[]{:S(2)}, u32[]{:S(2)}) collective-permute-start(bf16[128,2048]{1,0:T(8,128)(2,1)S(1)} %get-tuple-element.618), channel_id=1, source_target_pairs={{0,2},{1,3},{2,4},{3,5},{4,6},{5,7},{6,0},{7,1},{8,10},{9,11},{10,... | collective-permute-start | bytes 1572872 | tf_op jit(solution)/shard_map/ppermute | solution.py:120
  389.8 23.9 %collective-permute-start.74 = (bf16[128,2048]{1,0:T(8,128)(2,1)S(1)}, bf16[128,2048]{1,0:T(8,128)(2,1)S(1)}, u32[]{:S(2)}, u32[]{:S(2)}) collective-permute-start(bf16[128,2048]{1,0:T(8,128)(2,1)S(1)} %slice.255), channel_id=1, source_target_pairs={{0,1},{1,0},{2,3},{3,2},{4,5},{5,4},{6,7},{7,6},{8,9},{9,8},{10,11... | collective-permute-start | bytes 1572872 | tf_op jit(solution)/shard_map/ppermute | solution.py:120
  437.7 16.3 %collective-permute-start.79 = (bf16[128,2048]{1,0:T(8,128)(2,1)S(1)}, bf16[128,2048]{1,0:T(8,128)(2,1)S(1)}, u32[]{:S(2)}, u32[]{:S(2)}) collective-permute-start(bf16[128,2048]{1,0:T(8,128)(2,1)S(1)} %fusion.27), channel_id=1, source_target_pairs={{0,2},{1,3},{2,4},{3,5},{4,6},{5,7},{6,0},{7,1},{8,10},{9,11},{10,... | collective-permute-start | bytes 1572872 | tf_op jit(solution)/shard_map/ppermute | solution.py:120
  438.4 15.6 %collective-permute-start.80 = (bf16[128,2048]{1,0:T(8,128)(2,1)S(1)}, bf16[128,2048]{1,0:T(8,128)(2,1)S(1)}, u32[]{:S(2)}, u32[]{:S(2)}) collective-permute-start(bf16[128,2048]{1,0:T(8,128)(2,1)S(1)} %slice.389), channel_id=1, source_target_pairs={{0,1},{1,0},{2,3},{3,2},{4,5},{5,4},{6,7},{7,6},{8,9},{9,8},{10,11... | collective-permute-start | bytes 1572872 | tf_op jit(solution)/shard_map/ppermute | solution.py:120
  438.8 15.1 %collective-permute-start.82 = (bf16[128,2048]{1,0:T(8,128)(2,1)S(1)}, bf16[128,2048]{1,0:T(8,128)(2,1)S(1)}, u32[]{:S(2)}, u32[]{:S(2)}) collective-permute-start(bf16[128,2048]{1,0:T(8,128)(2,1)S(1)} %get-tuple-element.644), channel_id=1, source_target_pairs={{0,16},{8,24},{16,0},{24,8},{1,17},{9,25},{17,1},{25,9},{2,18},{10... | collective-permute-start | bytes 1572872 | tf_op jit(solution)/shard_map/ppermute | solution.py:120
  458.5 14.6 %collective-permute-start.84 = (bf16[128,2048]{1,0:T(8,128)(2,1)S(1)}, bf16[128,2048]{1,0:T(8,128)(2,1)S(1)}, u32[]{:S(2)}, u32[]{:S(2)}) collective-permute-start(bf16[128,2048]{1,0:T(8,128)(2,1)S(1)} %fusion.29), channel_id=1, source_target_pairs={{0,2},{1,3},{2,4},{3,5},{4,6},{5,7},{6,0},{7,1},{8,10},{9,11},{10,... | collective-permute-start | bytes 1572872 | tf_op jit(solution)/shard_map/ppermute | solution.py:120
  458.5 14.6 %collective-permute-start.85 = (bf16[128,2048]{1,0:T(8,128)(2,1)}, bf16[128,2048]{1,0:T(8,128)(2,1)}, u32[]{:S(2)}, u32[]{:S(2)}) collective-permute-start(bf16[128,2048]{1,0:T(8,128)(2,1)} %slice.388), channel_id=1, source_target_pairs={{0,1},{1,0},{2,3},{3,2},{4,5},{5,4},{6,7},{7,6},{8,9},{9,8},{10,11... | collective-permute-start | bytes 1572872 | tf_op jit(solution)/shard_map/ppermute | solution.py:120
  474.4 16.1 %collective-permute-start.89 = (bf16[128,2048]{1,0:T(8,128)(2,1)S(1)}, bf16[128,2048]{1,0:T(8,128)(2,1)S(1)}, u32[]{:S(2)}, u32[]{:S(2)}) collective-permute-start(bf16[128,2048]{1,0:T(8,128)(2,1)S(1)} %fusion.26), channel_id=1, source_target_pairs={{0,2},{1,3},{2,4},{3,5},{4,6},{5,7},{6,0},{7,1},{8,10},{9,11},{10,... | collective-permute-start | bytes 1572872 | tf_op jit(solution)/shard_map/ppermute | solution.py:120
  474.5 16.1 %collective-permute-start.90 = (bf16[128,2048]{1,0:T(8,128)(2,1)S(1)}, bf16[128,2048]{1,0:T(8,128)(2,1)S(1)}, u32[]{:S(2)}, u32[]{:S(2)}) collective-permute-start(bf16[128,2048]{1,0:T(8,128)(2,1)S(1)} %copy-done.61), channel_id=1, source_target_pairs={{0,1},{1,0},{2,3},{3,2},{4,5},{5,4},{6,7},{7,6},{8,9},{9,8},{10,11... | collective-permute-start | bytes 1572872 | tf_op jit(solution)/shard_map/ppermute | solution.py:120
  474.9 15.6 %collective-permute-start.92 = (bf16[128,2048]{1,0:T(8,128)(2,1)S(1)}, bf16[128,2048]{1,0:T(8,128)(2,1)S(1)}, u32[]{:S(2)}, u32[]{:S(2)}) collective-permute-start(bf16[128,2048]{1,0:T(8,128)(2,1)S(1)} %copy-done.64), channel_id=1, source_target_pairs={{0,8},{8,0},{16,24},{24,16},{1,9},{9,1},{17,25},{25,17},{2,10},{10... | collective-permute-start | bytes 1572872 | tf_op jit(solution)/shard_map/ppermute | solution.py:120
  475.5 15.1 %collective-permute-start.93 = (bf16[128,2048]{1,0:T(8,128)(2,1)S(1)}, bf16[128,2048]{1,0:T(8,128)(2,1)S(1)}, u32[]{:S(2)}, u32[]{:S(2)}) collective-permute-start(bf16[128,2048]{1,0:T(8,128)(2,1)S(1)} %copy-done.63), channel_id=1, source_target_pairs={{0,16},{8,24},{16,0},{24,8},{1,17},{9,25},{17,1},{25,9},{2,18},{10... | collective-permute-start | bytes 1572872 | tf_op jit(solution)/shard_map/ppermute | solution.py:120
  (130 other events, 1255.4 us)
Sparse Core Ops, SparseCore 0:
  68.4 27.5 all-gather.3
  121.5 92.6 all-gather.5
  328.4 105.8 reduce-scatter.3
